TPU v7x, 512 devices: a whole 4x4x16 slice. The times are simulated.
512 devices in a mesh: draw: 16 (over y_hi, x, core), blk: 32 (over y_lo, z).
Axes of the slice: x: 4, y: 4 (y_hi: 2, y_lo: 2; y = y_hi * 2 + y_lo), z: 16, core: 2. Of those that a mesh axis runs over, the one named last changes fastest.
Arguments:
- field: bfloat16 [12288, 4096], P('draw', 'blk'), may hold values from -8 to 8
- backward: bfloat16 [12288, 4096], P('draw', 'blk'), may hold values from -6 to 6
Outputs:
- feature_kernel: float32 [4096, 4096], P('blk', 'draw')
- gradient_kernel: float32 [4096, 4096], P('blk', 'draw')
All inputs are finite; a program needn't handle non-finite values.
Results may differ from a plain program's by a relative error of at most 0.002.
Values may be sent and summed in bfloat16 or wider, within the bound.
No kernel may reach another device: no remote copies, remote signals or barrier semaphores. Data moves between devices by JAX's collectives and lax.ppermute only.
A program may use at most 64 MiB of HBM per device.

v0:
```python
import jax
import jax.numpy as jnp
from jax import lax
from jax.sharding import PartitionSpec as P


def on_device(field, backward):
    wide = jnp.tanh(field.astype(jnp.float32))
    activity = wide.astype(jnp.bfloat16)
    signal = ((1.0 - wide * wide) * backward.astype(jnp.float32)).astype(jnp.bfloat16)
    stacked = jnp.stack([activity, signal])
    total_draws = field.shape[0] * lax.axis_size("draw")
    terms = jnp.einsum(
        "kdi,kdj->kij",
        stacked,
        lax.all_gather(stacked, "blk", axis=2, tiled=True),
        preferred_element_type=jnp.float32,
    )
    kernels = lax.psum_scatter(terms, "draw", scatter_dimension=2, tiled=True)
    kernels = kernels / total_draws
    return (kernels[0], kernels[1])


def solution(mesh):
    return jax.shard_map(
        on_device,
        mesh=mesh,
        in_specs=(P("draw", "blk"), P("draw", "blk")),
        out_specs=(P("blk", "draw"), P("blk", "draw")),
        check_vma=False,
    )
```

profile of v0, /device:TPU:7, one launch (start us, length us, event | category | flops | bytes accessed | tf_op | source)
XLA Modules:
  0.0 343.6 jit_solution(199593910198985426)
XLA Ops:
  7.2 0.0 all-gather.2.cloned.1.call-start
  7.2 1.1 fusion.1
  8.3 0.8 pad_maximum_fusion
  9.1 0.0 all-gather.2.cloned.1.call-update
  9.2 0.0 reduce-scatter.2.cloned.1.call-start
  9.2 197.7 %all-gather.2.cloned.1.call-done = bf16[2,768,4096]{2,1,0:T(8,128)(2,1)} async-done(((bf16[2,768,128]{2,1,0:T(8,128)(2,1)}), bf16[2,768,4096]{2,1,0:T(8,128)(2,1)}) %all-gather.2.cloned.1.call-update) | async-done | bytes 12582928 | tf_op jit(solution)/shard_map/all_gather | solution.py:16
  206.9 8.4 %fusion.3 = f32[2,128,4096]{2,1,0:T(8,128)} fusion(bf16[2,768,4096]{2,1,0:T(8,128)(2,1)} %all-gather.2.cloned.1.call-done, bf16[1,768,128]{2,1,0:T(8,128)(2,1)S(1)} %get-tuple-element.5, bf16[1,768,128]{2,1,0:T(8,128)(2,1)S(1)} %get-tuple-element.4), kind=kOutput, calls=%fused_computation.9 | convolution fusion | flops 1610809344 | bytes 17170432 | tf_op jit(solution)/shard_map/kdi,kdj->kij/dot_general | solution.py:13
  215.3 0.0 reduce-scatter.2.cloned.1.call-update
  215.3 119.7 %reduce-scatter.2.cloned.1.call-done = f32[2,128,256]{2,1,0:T(8,128)} async-done(((f32[2,128,4096]{2,1,0:T(8,128)}), f32[2,128,256]{2,1,0:T(8,128)}) %reduce-scatter.2.cloned.1.call-update) | async-done | bytes 262160 | tf_op jit(solution)/shard_map/reduce_scatter | solution.py:19
  335.0 1.0 broadcast_multiply_fusion
  336.0 0.7 slice_bitcast_fusion
Async XLA Ops:
  7.2 199.8 %all-gather.2.cloned.1.call-start = ((), (), s32[]{:S(2)}) async-start(), calls=%async_computation.1 | async-start | bytes 12976128 | tf_op jit(solution)/shard_map/all_gather | solution.py:16
  9.2 325.9 %reduce-scatter.2.cloned.1.call-start = ((), (), s32[]{:S(2)}) async-start(), calls=%async_computation.2 | async-start | bytes 4456448 | tf_op jit(solution)/shard_map/reduce_scatter | solution.py:19
Sparse Core Ops, SparseCore 0:
  10.0 196.8 all-gather.1
  215.4 119.5 reduce-scatter.1
where the time goes:
time: 346 us; the launch traced here: 344 us
  waiting for transfers between devices  317 us (92%)
  between operations  14 us (4%)
  matrix products  8.38 us (2%)
    all_gather x1, waiting for transfers between devices, on_device(): lax.all_gather(stacked, 'blk', axis=2, tiled=True)  198 us
    reduce_scatter x1, waiting for transfers between devices, on_device(): kernels = lax.psum_scatter(terms, 'draw', scatter_dimension=2, tiled=True)  120 us
    dot_general x1, matrix products, on_device(): jnp.einsum('kdi,kdj->kij', stacked, lax.all_gather(stacked, 'blk', axis=2...  8.38 us
  transfers between devices with their start and end apart: 2, of which 2 were waited for; matrix products, arithmetic and copies ran while one was open for 0% of the time, Pallas kernels for 0%

commit v1 on v0

v1 whole, which is shorter than its diff:
```python
import functools

import jax
import jax.numpy as jnp
import numpy as np
from jax import lax
from jax.experimental import pallas as pl
from jax.experimental.pallas import tpu as pltpu
from jax.sharding import Mesh, PartitionSpec as P

AXES = ("yh", "x", "c", "yl", "z")
SIZES = (2, 4, 2, 2, 16)
EXTRA = 16
VMEM = pl.BlockSpec(memory_space=pltpu.VMEM)
SMEM = pl.BlockSpec(memory_space=pltpu.SMEM)
PARAMS = pltpu.CompilerParams(vmem_limit_bytes=40 * 1024 * 1024)


def device_index(yh, x, c, yl, z):
    return (((yh * 4 + x) * 2 + c) * 2 + yl) * 16 + z


def home(row_y, row_z, col_y, col_z):
    return device_index(col_y, col_z // 4, col_z % 4 // 2, row_y, row_z), col_z % 2


def homes(yh, x, c, yl, z):
    top, bottom = yl, yh
    if c == 0:
        left, right = [(z + 4, z - 1), (z + 4, z - 2), (z, z - 3), (z, z - 4)][x]
    elif x < 3:
        left, right = [(z, z + 1), (z, z + 2), (z - 4, z + 3)][x]
    elif yl == 0:
        left, right = z - 4, z + 4
        if yh == 0:
            top = bottom = 0 if z < 8 else 1
    elif yh == 1:
        return [home(0, z, 0, z) + (2,), home(1, z, 1, z) + (3,)]
    else:
        left = right = z
        top, bottom = 0, 1
    left, right = left % 16, right % 16
    return [home(top, left, bottom, right) + (0,), home(bottom, right, top, left) + (1,)]


def routes():
    edges = []
    for place in np.ndindex(*SIZES):
        for to, half, mode in homes(*place):
            edges.append((device_index(*place), to, half, mode))
    into = [[] for _ in range(512)]
    for e, edge in enumerate(edges):
        into[edge[1]].append(e)
    turn = [-1] * len(edges)
    for first in range(len(edges)):
        e = first
        while turn[e] < 0:
            turn[e] = 0
            pair = into[edges[e][1]]
            other = pair[0] + pair[1] - e
            turn[other] = 1
            e = other ^ 1
    perms = [[], []]
    table = np.zeros((512, 4), np.int32)
    for e, (source, to, half, mode) in enumerate(edges):
        perms[turn[e]].append((source, to))
        table[to, 2 * half] = turn[e]
        table[to, 2 * half + 1] = mode
    return perms, table


def features_kernel(place, field, backward, keep, send):
    rows = field.shape[0] // 2
    mine = place[1]
    for out, half in ((keep, mine), (send, 1 - mine)):
        part = pl.ds(pl.multiple_of(half * rows, rows), rows)
        wide = jnp.tanh(field[part, :].astype(jnp.float32))
        out[0] = wide.astype(jnp.bfloat16)
        out[1] = ((1.0 - wide * wide) * backward[part, :].astype(jnp.float32)).astype(
            jnp.bfloat16
        )


def products_kernel(place, *refs):
    walk, far, out, scratch = refs[:10], refs[10:12], refs[12], refs[13]
    core, y, z = place[0], place[1], place[2]
    n = out.shape[-1]
    w = [(walk[2 * j], walk[2 * j + 1]) for j in range(5)]

    def product(left, right, kernel):
        total = None
        for c in range(2):
            lhs = jnp.concatenate([left[0][c, kernel], left[1][c, kernel]], axis=1)
            rhs = jnp.concatenate([right[0][c, kernel], right[1][c, kernel]], axis=1)
            term = lax.dot_general(
                lhs, rhs, (((0,), (0,)), ((), ())), preferred_element_type=jnp.float32
            )
            total = term if total is None else total + term
        return total

    def store(x, kernel, total):
        for p in range(2):
            for q in range(2):
                out[q ^ y, x, p ^ y, kernel, 0:n] = total[
                    p * n : (p + 1) * n, q * n : (q + 1) * n
                ].astype(jnp.bfloat16)

    def keep(at, total):
        for p in range(2):
            for q in range(2):
                scratch[at, p ^ y, q ^ y] = total[
                    p * n : (p + 1) * n, q * n : (q + 1) * n
                ]

    for yh in range(2):
        for x in range(4):
            for yl in range(2):
                for kernel in range(2):
                    out[yh, x, yl, kernel, n : n + EXTRA] = jnp.zeros(
                        (EXTRA, n), jnp.bfloat16
                    )

    @pl.when(core == 0)
    def _():
        for kernel in range(2):
            store(0, kernel, product(far, w[1], kernel))
            store(1, kernel, product(far, w[2], kernel))
            store(2, kernel, product(w[0], w[3], kernel))
            store(3, kernel, product(w[0], w[4], kernel))

    @pl.when(core == 1)
    def _():
        row = lax.broadcasted_iota(jnp.int32, (n, n), 0)
        col = lax.broadcasted_iota(jnp.int32, (n, n), 1)
        for kernel in range(2):
            store(0, kernel, product(w[0], w[1], kernel))
            store(1, kernel, product(w[0], w[2], kernel))
            store(2, kernel, product(far, w[3], kernel))
            keep(0, product(far, w[4], kernel))
            keep(1, product(w[0], w[0], kernel))
            side = jnp.where(z < 8, 0, 1)
            out[1, 3, 0, kernel, 0:n] = scratch[0, 0, 1].astype(jnp.bfloat16)
            out[0, 3, 0, kernel, 0:n] = scratch[0, side, side].astype(jnp.bfloat16)
            out[0, 3, 1, kernel, 0:n] = scratch[1, 0, 1].astype(jnp.bfloat16)
            low = scratch[1, 1, 1]
            out[1, 3, 1, kernel, 0:n] = jnp.where(
                row <= col, scratch[1, 0, 0], low
            ).astype(jnp.bfloat16)
            diagonal = jnp.sum(jnp.where(row == col, low, 0.0), axis=0, keepdims=True)
            out[1, 3, 1, kernel, n : n + EXTRA] = jnp.broadcast_to(
                diagonal, (EXTRA, n)
            ).astype(jnp.bfloat16)


def place_kernel(total_draws, todo, a, b, feature, gradient):
    n = feature.shape[0]
    row = lax.broadcasted_iota(jnp.int32, (n, n), 0)
    col = lax.broadcasted_iota(jnp.int32, (n, n), 1)
    for kernel, out in enumerate((feature, gradient)):
        for half in range(2):
            second, mode = todo[2 * half] == 1, todo[2 * half + 1]
            got = jnp.where(second, b[kernel, 0:n], a[kernel, 0:n])
            extra = jnp.where(second, b[kernel, n : n + 1], a[kernel, n : n + 1])
            turned = got.T
            lower = row > col
            plain = (mode == 0) | ((mode == 2) & (row <= col)) | ((mode == 3) & lower)
            value = jnp.where(plain, got, turned)
            value = jnp.where((mode == 3) & (row == col), extra, value)
            out[:, half * n : (half + 1) * n] = value / total_draws


def on_device(field, backward):
    draws, n = field.shape
    total_draws = draws * 16
    place = jnp.stack([lax.axis_index("c"), lax.axis_index("yl"), lax.axis_index("z")])
    half = jax.ShapeDtypeStruct((2, draws // 2, n), jnp.bfloat16)
    keep, send = pl.pallas_call(
        features_kernel,
        out_shape=(half, half),
        in_specs=[SMEM, VMEM, VMEM],
        out_specs=(VMEM, VMEM),
        compiler_params=PARAMS,
    )(place, field, backward)

    swap = [(0, 1), (1, 0)]
    other = lax.ppermute(send, "yl", swap)
    chains = [lax.all_gather(keep, "c"), lax.all_gather(other, "c")]
    step = [
        (c * 16 + z, c * 16 + (z + 1 - 2 * c) % 16) for c in range(2) for z in range(16)
    ]
    walk = list(chains)
    for _ in range(4):
        chains = [lax.ppermute(chain, ("c", "z"), step) for chain in chains]
        walk += chains
    far = [lax.ppermute(chain, "c", swap) for chain in chains]

    partial = pl.pallas_call(
        products_kernel,
        out_shape=jax.ShapeDtypeStruct((2, 4, 2, 2, n + EXTRA, n), jnp.bfloat16),
        in_specs=[SMEM] + [VMEM] * 12,
        out_specs=VMEM,
        scratch_shapes=[pltpu.VMEM((2, 2, 2, n, n), jnp.float32)],
        compiler_params=PARAMS,
    )(place, *walk, *far)
    partial = partial.reshape(16, 2, n + EXTRA, n)
    partial = lax.all_to_all(partial, ("yh", "x", "yl"), 0, 0, tiled=True)
    block = jnp.sum(partial.astype(jnp.float32), axis=0)

    perms, table = routes()
    a = lax.ppermute(block, AXES, perms[0])
    b = lax.ppermute(block, AXES, perms[1])
    todo = lax.dynamic_index_in_dim(
        jnp.asarray(table), lax.axis_index(AXES), 0, keepdims=False
    )
    out = jax.ShapeDtypeStruct((n, 2 * n), jnp.float32)
    return pl.pallas_call(
        functools.partial(place_kernel, total_draws),
        out_shape=(out, out),
        in_specs=[SMEM, VMEM, VMEM],
        out_specs=(VMEM, VMEM),
        compiler_params=PARAMS,
    )(todo, a, b)


def solution(mesh):
    grid = Mesh(mesh.devices.reshape(SIZES), AXES)
    return jax.shard_map(
        on_device,
        mesh=grid,
        in_specs=(P(("yh", "x", "c"), ("yl", "z")),) * 2,
        out_specs=(P(("yl", "z"), ("yh", "x", "c")),) * 2,
        check_vma=False,
    )
```

time: 346 us -> 120 us (0.35)
  the two profiles are of different devices: /device:TPU:7 before, /device:TPU:10 now
where the time goes in v1:
time: 120 us; the launch traced here: 119 us
  waiting for transfers between devices  44.1 us (37%)
  blocking collectives  35.6 us (30%)
  starting transfers between devices  32.3 us (27%)
  Pallas kernels  3.87 us (3%)
  local copies, waits for them, and re-layouts  2.55 us (2%)
    ppermute x8, waiting for transfers between devices, on_device(): chains = [lax.ppermute(chain, ('c', 'z'), step) for chain in chains]  28.1 us
    all_to_all x1, blocking collectives, on_device(): partial = lax.all_to_all(partial, ('yh', 'x', 'yl'), 0, 0, tiled=True)  24.6 us
    ppermute x8, starting transfers between devices, on_device(): chains = [lax.ppermute(chain, ('c', 'z'), step) for chain in chains]  17.2 us
    ppermute x1, waiting for transfers between devices, on_device(): a = lax.ppermute(block, AXES, perms[0])  11.4 us
    all_gather x2, blocking collectives, on_device(): chains = [lax.all_gather(keep, 'c'), lax.all_gather(other, 'c')]  11 us
    ppermute x1, starting transfers between devices, on_device(): a = lax.ppermute(block, AXES, perms[0])  7.01 us
    ppermute x2, starting transfers between devices, on_device(): far = [lax.ppermute(chain, 'c', swap) for chain in chains]  3.82 us
    ppermute x1, waiting for transfers between devices, on_device(): b = lax.ppermute(block, AXES, perms[1])  2.59 us
  transfers between devices with their start and end apart: 13, of which 12 were waited for; matrix products, arithmetic and copies ran while one was open for 1% of the time, Pallas kernels for 0%

profile of v1, /device:TPU:10, one launch (start us, length us, event | category | flops | bytes accessed | tf_op | source)
XLA Modules:
  0.0 119.4 jit_solution(5253330418894627500)
XLA Ops:
  0.7 0.9 copy-done
  1.6 0.9 copy-done.1
  3.2 2.4 %collective-permute-start = (bf16[2,384,128]{2,1,0:T(8,128)(2,1)S(1)}, bf16[2,384,128]{2,1,0:T(8,128)(2,1)S(1)}, u32[]{:S(2)}, u32[]{:S(2)}) collective-permute-start(bf16[2,384,128]{2,1,0:T(8,128)(2,1)S(1)} %get-tuple-element.5), channel_id=1, source_target_pairs={{0,16},{16,0},{1,17},{17,1},{2,18},{18,2},{3,19},{19,3},{4,20},{20... | collective-permute-start | bytes 589832 | tf_op jit(solution)/shard_map/ppermute | solution.py:186
  5.6 2.1 %all-gather = bf16[4,384,128]{2,1,0:T(8,128)(2,1)S(1)} all-gather(bf16[2,384,128]{2,1,0:T(8,128)(2,1)S(1)} %get-tuple-element.4), channel_id=2, replica_groups=mesh['yh'=2,'x'=4,'c'=2,'yl'=2,'z'=16] {'c'}, dimensions={0}, use_global_device_ids=true | all-gather | bytes 589824 | tf_op jit(solution)/shard_map/all_gather | solution.py:187
  7.7 3.8 %collective-permute-start.1 = (bf16[2,2,384,128]{3,2,1,0:T(8,128)(2,1)S(1)}, bf16[2,2,384,128]{3,2,1,0:T(8,128)(2,1)S(1)}, u32[]{:S(2)}, u32[]{:S(2)}) collective-permute-start(bf16[2,2,384,128]{3,2,1,0:T(8,128)(2,1)S(1)} %bitcast.9), channel_id=1, source_target_pairs={{0,1},{1,2},{2,3},{3,4},{4,5},{5,6},{6,7},{7,8},{8,9},{9,10},{10,1... | collective-permute-start | bytes 1179656 | tf_op jit(solution)/shard_map/ppermute | solution.py:193
  11.7 8.9 %all-gather.1 = bf16[4,384,128]{2,1,0:T(8,128)(2,1)S(1)} all-gather(bf16[2,384,128]{2,1,0:T(8,128)(2,1)S(1)} %collective-permute-done), channel_id=3, replica_groups=mesh['yh'=2,'x'=4,'c'=2,'yl'=2,'z'=16] {'c'}, dimensions={0}, use_global_device_ids=true | all-gather | bytes 589824 | tf_op jit(solution)/shard_map/all_gather | solution.py:187
  20.7 1.9 %collective-permute-start.2 = (bf16[2,2,384,128]{3,2,1,0:T(8,128)(2,1)S(1)}, bf16[2,2,384,128]{3,2,1,0:T(8,128)(2,1)S(1)}, u32[]{:S(2)}, u32[]{:S(2)}) collective-permute-start(bf16[2,2,384,128]{3,2,1,0:T(8,128)(2,1)S(1)} %bitcast.11), channel_id=1, source_target_pairs={{0,1},{1,2},{2,3},{3,4},{4,5},{5,6},{6,7},{7,8},{8,9},{9,10},{10,1... | collective-permute-start | bytes 1179656 | tf_op jit(solution)/shard_map/ppermute | solution.py:193
  22.6 2.2 %collective-permute-done.1.refs_2_ = bf16[2,2,384,128]{3,2,1,0:T(8,128)(2,1)S(1)} collective-permute-done((bf16[2,2,384,128]{3,2,1,0:T(8,128)(2,1)S(1)}, bf16[2,2,384,128]{3,2,1,0:T(8,128)(2,1)S(1)}, u32[]{:S(2)}, u32[]{:S(2)}) %collective-permute-start.1) | collective-permute-done | bytes 393248 | tf_op jit(solution)/shard_map/ppermute | solution.py:193
  24.8 1.9 %collective-permute-start.3 = (bf16[2,2,384,128]{3,2,1,0:T(8,128)(2,1)S(1)}, bf16[2,2,384,128]{3,2,1,0:T(8,128)(2,1)S(1)}, u32[]{:S(2)}, u32[]{:S(2)}) collective-permute-start(bf16[2,2,384,128]{3,2,1,0:T(8,128)(2,1)S(1)} %collective-permute-done.1.refs_2_), channel_id=1, source_target_pairs={{0,1},{1,2},{2,3},{3,4},{4,5},{5,6},{6,7},{7,8},{8,9},{9,10},{10,1... | collective-permute-start | bytes 1179656 | tf_op jit(solution)/shard_map/ppermute | solution.py:193
  26.7 4.8 %collective-permute-done.2.refs_3_ = bf16[2,2,384,128]{3,2,1,0:T(8,128)(2,1)S(1)} collective-permute-done((bf16[2,2,384,128]{3,2,1,0:T(8,128)(2,1)S(1)}, bf16[2,2,384,128]{3,2,1,0:T(8,128)(2,1)S(1)}, u32[]{:S(2)}, u32[]{:S(2)}) %collective-permute-start.2) | collective-permute-done | bytes 393248 | tf_op jit(solution)/shard_map/ppermute | solution.py:193
  31.5 1.9 %collective-permute-start.4 = (bf16[2,2,384,128]{3,2,1,0:T(8,128)(2,1)S(1)}, bf16[2,2,384,128]{3,2,1,0:T(8,128)(2,1)S(1)}, u32[]{:S(2)}, u32[]{:S(2)}) collective-permute-start(bf16[2,2,384,128]{3,2,1,0:T(8,128)(2,1)S(1)} %collective-permute-done.2.refs_3_), channel_id=1, source_target_pairs={{0,1},{1,2},{2,3},{3,4},{4,5},{5,6},{6,7},{7,8},{8,9},{9,10},{10,1... | collective-permute-start | bytes 1179656 | tf_op jit(solution)/shard_map/ppermute | solution.py:193
  33.4 2.3 %collective-permute-done.3.refs_4_ = bf16[2,2,384,128]{3,2,1,0:T(8,128)(2,1)S(1)} collective-permute-done((bf16[2,2,384,128]{3,2,1,0:T(8,128)(2,1)S(1)}, bf16[2,2,384,128]{3,2,1,0:T(8,128)(2,1)S(1)}, u32[]{:S(2)}, u32[]{:S(2)}) %collective-permute-start.3) | collective-permute-done | bytes 393248 | tf_op jit(solution)/shard_map/ppermute | solution.py:193
  35.7 1.9 %collective-permute-start.5 = (bf16[2,2,384,128]{3,2,1,0:T(8,128)(2,1)S(1)}, bf16[2,2,384,128]{3,2,1,0:T(8,128)(2,1)S(1)}, u32[]{:S(2)}, u32[]{:S(2)}) collective-permute-start(bf16[2,2,384,128]{3,2,1,0:T(8,128)(2,1)S(1)} %collective-permute-done.3.refs_4_), channel_id=1, source_target_pairs={{0,1},{1,2},{2,3},{3,4},{4,5},{5,6},{6,7},{7,8},{8,9},{9,10},{10,1... | collective-permute-start | bytes 1179656 | tf_op jit(solution)/shard_map/ppermute | solution.py:193
  37.7 4.7 %collective-permute-done.4.refs_5_ = bf16[2,2,384,128]{3,2,1,0:T(8,128)(2,1)S(1)} collective-permute-done((bf16[2,2,384,128]{3,2,1,0:T(8,128)(2,1)S(1)}, bf16[2,2,384,128]{3,2,1,0:T(8,128)(2,1)S(1)}, u32[]{:S(2)}, u32[]{:S(2)}) %collective-permute-start.4) | collective-permute-done | bytes 393248 | tf_op jit(solution)/shard_map/ppermute | solution.py:193
  42.4 1.9 %collective-permute-start.6 = (bf16[2,2,384,128]{3,2,1,0:T(8,128)(2,1)S(1)}, bf16[2,2,384,128]{3,2,1,0:T(8,128)(2,1)S(1)}, u32[]{:S(2)}, u32[]{:S(2)}) collective-permute-start(bf16[2,2,384,128]{3,2,1,0:T(8,128)(2,1)S(1)} %collective-permute-done.4.refs_5_), channel_id=1, source_target_pairs={{0,1},{1,2},{2,3},{3,4},{4,5},{5,6},{6,7},{7,8},{8,9},{9,10},{10,1... | collective-permute-start | bytes 1179656 | tf_op jit(solution)/shard_map/ppermute | solution.py:193
  44.3 2.3 %collective-permute-done.5.refs_6_ = bf16[2,2,384,128]{3,2,1,0:T(8,128)(2,1)S(1)} collective-permute-done((bf16[2,2,384,128]{3,2,1,0:T(8,128)(2,1)S(1)}, bf16[2,2,384,128]{3,2,1,0:T(8,128)(2,1)S(1)}, u32[]{:S(2)}, u32[]{:S(2)}) %collective-permute-start.5) | collective-permute-done | bytes 393248 | tf_op jit(solution)/shard_map/ppermute | solution.py:193
  46.6 1.9 %collective-permute-start.7 = (bf16[2,2,384,128]{3,2,1,0:T(8,128)(2,1)S(1)}, bf16[2,2,384,128]{3,2,1,0:T(8,128)(2,1)S(1)}, u32[]{:S(2)}, u32[]{:S(2)}) collective-permute-start(bf16[2,2,384,128]{3,2,1,0:T(8,128)(2,1)S(1)} %collective-permute-done.5.refs_6_), channel_id=1, source_target_pairs={{0,1},{1,2},{2,3},{3,4},{4,5},{5,6},{6,7},{7,8},{8,9},{9,10},{10,1... | collective-permute-start | bytes 1179656 | tf_op jit(solution)/shard_map/ppermute | solution.py:193
  48.5 4.7 %collective-permute-done.6.refs_7_ = bf16[2,2,384,128]{3,2,1,0:T(8,128)(2,1)S(1)} collective-permute-done((bf16[2,2,384,128]{3,2,1,0:T(8,128)(2,1)S(1)}, bf16[2,2,384,128]{3,2,1,0:T(8,128)(2,1)S(1)}, u32[]{:S(2)}, u32[]{:S(2)}) %collective-permute-start.6) | collective-permute-done | bytes 393248 | tf_op jit(solution)/shard_map/ppermute | solution.py:193
  53.3 1.9 %collective-permute-start.8 = (bf16[2,2,384,128]{3,2,1,0:T(8,128)(2,1)S(1)}, bf16[2,2,384,128]{3,2,1,0:T(8,128)(2,1)S(1)}, u32[]{:S(2)}, u32[]{:S(2)}) collective-permute-start(bf16[2,2,384,128]{3,2,1,0:T(8,128)(2,1)S(1)} %collective-permute-done.6.refs_7_), channel_id=1, source_target_pairs={{0,1},{1,2},{2,3},{3,4},{4,5},{5,6},{6,7},{7,8},{8,9},{9,10},{10,1... | collective-permute-start | bytes 1179656 | tf_op jit(solution)/shard_map/ppermute | solution.py:193
  55.2 2.3 %collective-permute-done.7.refs_8_ = bf16[2,2,384,128]{3,2,1,0:T(8,128)(2,1)S(1)} collective-permute-done((bf16[2,2,384,128]{3,2,1,0:T(8,128)(2,1)S(1)}, bf16[2,2,384,128]{3,2,1,0:T(8,128)(2,1)S(1)}, u32[]{:S(2)}, u32[]{:S(2)}) %collective-permute-start.7) | collective-permute-done | bytes 393248 | tf_op jit(solution)/shard_map/ppermute | solution.py:193
  57.5 1.9 %collective-permute-start.9 = (bf16[2,2,384,128]{3,2,1,0:T(8,128)(2,1)S(1)}, bf16[2,2,384,128]{3,2,1,0:T(8,128)(2,1)S(1)}, u32[]{:S(2)}, u32[]{:S(2)}) collective-permute-start(bf16[2,2,384,128]{3,2,1,0:T(8,128)(2,1)S(1)} %collective-permute-done.7.refs_8_), channel_id=1, source_target_pairs={{0,32},{32,0},{1,33},{33,1},{2,34},{34,2},{3,35},{35,3},{4,36},{36... | collective-permute-start | bytes 1179656 | tf_op jit(solution)/shard_map/ppermute | solution.py:195
  59.4 4.7 %collective-permute-done.8.refs_9_ = bf16[2,2,384,128]{3,2,1,0:T(8,128)(2,1)S(1)} collective-permute-done((bf16[2,2,384,128]{3,2,1,0:T(8,128)(2,1)S(1)}, bf16[2,2,384,128]{3,2,1,0:T(8,128)(2,1)S(1)}, u32[]{:S(2)}, u32[]{:S(2)}) %collective-permute-start.8) | collective-permute-done | bytes 393248 | tf_op jit(solution)/shard_map/ppermute | solution.py:193
  64.1 1.9 %collective-permute-start.10 = (bf16[2,2,384,128]{3,2,1,0:T(8,128)(2,1)S(1)}, bf16[2,2,384,128]{3,2,1,0:T(8,128)(2,1)S(1)}, u32[]{:S(2)}, u32[]{:S(2)}) collective-permute-start(bf16[2,2,384,128]{3,2,1,0:T(8,128)(2,1)S(1)} %collective-permute-done.8.refs_9_), channel_id=1, source_target_pairs={{0,32},{32,0},{1,33},{33,1},{2,34},{34,2},{3,35},{35,3},{4,36},{36... | collective-permute-start | bytes 1179656 | tf_op jit(solution)/shard_map/ppermute | solution.py:195
  66.1 1.7 %collective-permute-done.10.refs_11_ = bf16[2,2,384,128]{3,2,1,0:T(8,128)(2,1)S(1)} collective-permute-done((bf16[2,2,384,128]{3,2,1,0:T(8,128)(2,1)S(1)}, bf16[2,2,384,128]{3,2,1,0:T(8,128)(2,1)S(1)}, u32[]{:S(2)}, u32[]{:S(2)}) %collective-permute-start.10) | collective-permute-done | bytes 393248 | tf_op jit(solution)/shard_map/ppermute | solution.py:195
  67.7 1.9 %shard_map.51 = bf16[2,4,2,2,144,128]{5,4,3,2,1,0:T(8,128)(2,1)S(1)} custom-call(s32[3]{0:T(128)S(1)} %pad_add_fusion.place, bf16[2,2,384,128]{3,2,1,0:T(8,128)(2,1)S(1)} %bitcast.10, bf16[2,2,384,128]{3,2,1,0:T(8,128)(2,1)S(1)} %bitcast.12, bf16[2,2,384,128]{3,2,1,0:T(8,128)(2,1)S(1)} %collective-permute-done.1.refs_2_, ...), custom_call_target="tpu_custom_call" | custom-call | tf_op jit(solution)/shard_map/pallas_call | solution.py:197
  69.6 24.6 %all_to_all.5 = bf16[16,2,144,128]{3,2,1,0:T(8,128)(2,1)S(1)} all-to-all(bf16[16,2,144,128]{3,2,1,0:T(8,128)(2,1)S(1)} %bitcast.8), channel_id=1, replica_groups=mesh['yh'=2,'x'=4,'c'=2,'yl'=2,'z'=16] {'yh','x','yl'}, dimensions={0} | all-to-all | bytes 2359296 | tf_op jit(solution)/shard_map/all_to_all | solution.py:206
  94.3 1.9 %collective-permute-start.12 = (f32[2,144,128]{2,1,0:T(8,128)S(1)}, f32[2,144,128]{2,1,0:T(8,128)S(1)}, u32[]{:S(2)}, u32[]{:S(2)}) collective-permute-start(f32[2,144,128]{2,1,0:T(8,128)S(1)} %convert_reduce_fusion), channel_id=1, source_target_pairs={{0,79},{1,64},{2,97},{3,98},{4,131},{5,132},{6,165},{7,166},{8,199... | collective-permute-start | bytes 442376 | tf_op jit(solution)/shard_map/ppermute | solution.py:211
  96.3 7.0 %collective-permute-start.11 = (f32[2,144,128]{2,1,0:T(8,128)S(1)}, f32[2,144,128]{2,1,0:T(8,128)S(1)}, u32[]{:S(2)}, u32[]{:S(2)}) collective-permute-start(f32[2,144,128]{2,1,0:T(8,128)S(1)} %convert_reduce_fusion), channel_id=1, source_target_pairs={{0,228},{1,5},{2,6},{3,39},{4,40},{5,73},{6,74},{7,107},{8,108},{9... | collective-permute-start | bytes 442376 | tf_op jit(solution)/shard_map/ppermute | solution.py:210
  103.3 0.7 dynamic-slice_bitcast_fusion.todo
  104.0 2.6 %collective-permute-done.12.b = f32[2,144,128]{2,1,0:T(8,128)S(1)} collective-permute-done((f32[2,144,128]{2,1,0:T(8,128)S(1)}, f32[2,144,128]{2,1,0:T(8,128)S(1)}, u32[]{:S(2)}, u32[]{:S(2)}) %collective-permute-start.12) | collective-permute-done | bytes 147488 | tf_op jit(solution)/shard_map/ppermute | solution.py:211
  106.6 11.4 %collective-permute-done.11.a = f32[2,144,128]{2,1,0:T(8,128)S(1)} collective-permute-done((f32[2,144,128]{2,1,0:T(8,128)S(1)}, f32[2,144,128]{2,1,0:T(8,128)S(1)}, u32[]{:S(2)}, u32[]{:S(2)}) %collective-permute-start.11) | collective-permute-done | bytes 147488 | tf_op jit(solution)/shard_map/ppermute | solution.py:210
  118.0 1.4 %shard_map.52 = (f32[128,256]{1,0:T(8,128)}, f32[128,256]{1,0:T(8,128)}) custom-call(s32[4]{0:T(128)S(1)} %dynamic-slice_bitcast_fusion.todo, f32[2,144,128]{2,1,0:T(8,128)S(1)} %collective-permute-done.11.a, f32[2,144,128]{2,1,0:T(8,128)S(1)} %collective-permute-done.12.b), custom_call_target="tpu_custom_call" | custom-call | tf_op jit(solution)/shard_map/pallas_call | solution.py:216
  (7 shorter events, 1.1 us)
Async XLA Ops:
  0.7 0.9 copy-start
  1.6 0.9 copy-start.1
  3.2 8.5 %collective-permute-start = (bf16[2,384,128]{2,1,0:T(8,128)(2,1)S(1)}, bf16[2,384,128]{2,1,0:T(8,128)(2,1)S(1)}, u32[]{:S(2)}, u32[]{:S(2)}) collective-permute-start(bf16[2,384,128]{2,1,0:T(8,128)(2,1)S(1)} %get-tuple-element.5), channel_id=1, source_target_pairs={{0,16},{16,0},{1,17},{17,1},{2,18},{18,2},{3,19},{19,3},{4,20},{20... | collective-permute-start | bytes 589832 | tf_op jit(solution)/shard_map/ppermute | solution.py:186
  7.7 17.1 %collective-permute-start.1 = (bf16[2,2,384,128]{3,2,1,0:T(8,128)(2,1)S(1)}, bf16[2,2,384,128]{3,2,1,0:T(8,128)(2,1)S(1)}, u32[]{:S(2)}, u32[]{:S(2)}) collective-permute-start(bf16[2,2,384,128]{3,2,1,0:T(8,128)(2,1)S(1)} %bitcast.9), channel_id=1, source_target_pairs={{0,1},{1,2},{2,3},{3,4},{4,5},{5,6},{6,7},{7,8},{8,9},{9,10},{10,1... | collective-permute-start | bytes 1179656 | tf_op jit(solution)/shard_map/ppermute | solution.py:193
  20.7 10.9 %collective-permute-start.2 = (bf16[2,2,384,128]{3,2,1,0:T(8,128)(2,1)S(1)}, bf16[2,2,384,128]{3,2,1,0:T(8,128)(2,1)S(1)}, u32[]{:S(2)}, u32[]{:S(2)}) collective-permute-start(bf16[2,2,384,128]{3,2,1,0:T(8,128)(2,1)S(1)} %bitcast.11), channel_id=1, source_target_pairs={{0,1},{1,2},{2,3},{3,4},{4,5},{5,6},{6,7},{7,8},{8,9},{9,10},{10,1... | collective-permute-start | bytes 1179656 | tf_op jit(solution)/shard_map/ppermute | solution.py:193
  24.8 10.9 %collective-permute-start.3 = (bf16[2,2,384,128]{3,2,1,0:T(8,128)(2,1)S(1)}, bf16[2,2,384,128]{3,2,1,0:T(8,128)(2,1)S(1)}, u32[]{:S(2)}, u32[]{:S(2)}) collective-permute-start(bf16[2,2,384,128]{3,2,1,0:T(8,128)(2,1)S(1)} %collective-permute-done.1.refs_2_), channel_id=1, source_target_pairs={{0,1},{1,2},{2,3},{3,4},{4,5},{5,6},{6,7},{7,8},{8,9},{9,10},{10,1... | collective-permute-start | bytes 1179656 | tf_op jit(solution)/shard_map/ppermute | solution.py:193
  31.5 10.9 %collective-permute-start.4 = (bf16[2,2,384,128]{3,2,1,0:T(8,128)(2,1)S(1)}, bf16[2,2,384,128]{3,2,1,0:T(8,128)(2,1)S(1)}, u32[]{:S(2)}, u32[]{:S(2)}) collective-permute-start(bf16[2,2,384,128]{3,2,1,0:T(8,128)(2,1)S(1)} %collective-permute-done.2.refs_3_), channel_id=1, source_target_pairs={{0,1},{1,2},{2,3},{3,4},{4,5},{5,6},{6,7},{7,8},{8,9},{9,10},{10,1... | collective-permute-start | bytes 1179656 | tf_op jit(solution)/shard_map/ppermute | solution.py:193
  35.7 10.9 %collective-permute-start.5 = (bf16[2,2,384,128]{3,2,1,0:T(8,128)(2,1)S(1)}, bf16[2,2,384,128]{3,2,1,0:T(8,128)(2,1)S(1)}, u32[]{:S(2)}, u32[]{:S(2)}) collective-permute-start(bf16[2,2,384,128]{3,2,1,0:T(8,128)(2,1)S(1)} %collective-permute-done.3.refs_4_), channel_id=1, source_target_pairs={{0,1},{1,2},{2,3},{3,4},{4,5},{5,6},{6,7},{7,8},{8,9},{9,10},{10,1... | collective-permute-start | bytes 1179656 | tf_op jit(solution)/shard_map/ppermute | solution.py:193
  42.4 10.9 %collective-permute-start.6 = (bf16[2,2,384,128]{3,2,1,0:T(8,128)(2,1)S(1)}, bf16[2,2,384,128]{3,2,1,0:T(8,128)(2,1)S(1)}, u32[]{:S(2)}, u32[]{:S(2)}) collective-permute-start(bf16[2,2,384,128]{3,2,1,0:T(8,128)(2,1)S(1)} %collective-permute-done.4.refs_5_), channel_id=1, source_target_pairs={{0,1},{1,2},{2,3},{3,4},{4,5},{5,6},{6,7},{7,8},{8,9},{9,10},{10,1... | collective-permute-start | bytes 1179656 | tf_op jit(solution)/shard_map/ppermute | solution.py:193
  46.6 10.9 %collective-permute-start.7 = (bf16[2,2,384,128]{3,2,1,0:T(8,128)(2,1)S(1)}, bf16[2,2,384,128]{3,2,1,0:T(8,128)(2,1)S(1)}, u32[]{:S(2)}, u32[]{:S(2)}) collective-permute-start(bf16[2,2,384,128]{3,2,1,0:T(8,128)(2,1)S(1)} %collective-permute-done.5.refs_6_), channel_id=1, source_target_pairs={{0,1},{1,2},{2,3},{3,4},{4,5},{5,6},{6,7},{7,8},{8,9},{9,10},{10,1... | collective-permute-start | bytes 1179656 | tf_op jit(solution)/shard_map/ppermute | solution.py:193
  53.3 10.9 %collective-permute-start.8 = (bf16[2,2,384,128]{3,2,1,0:T(8,128)(2,1)S(1)}, bf16[2,2,384,128]{3,2,1,0:T(8,128)(2,1)S(1)}, u32[]{:S(2)}, u32[]{:S(2)}) collective-permute-start(bf16[2,2,384,128]{3,2,1,0:T(8,128)(2,1)S(1)} %collective-permute-done.6.refs_7_), channel_id=1, source_target_pairs={{0,1},{1,2},{2,3},{3,4},{4,5},{5,6},{6,7},{7,8},{8,9},{9,10},{10,1... | collective-permute-start | bytes 1179656 | tf_op jit(solution)/shard_map/ppermute | solution.py:193
  57.5 8.6 %collective-permute-start.9 = (bf16[2,2,384,128]{3,2,1,0:T(8,128)(2,1)S(1)}, bf16[2,2,384,128]{3,2,1,0:T(8,128)(2,1)S(1)}, u32[]{:S(2)}, u32[]{:S(2)}) collective-permute-start(bf16[2,2,384,128]{3,2,1,0:T(8,128)(2,1)S(1)} %collective-permute-done.7.refs_8_), channel_id=1, source_target_pairs={{0,32},{32,0},{1,33},{33,1},{2,34},{34,2},{3,35},{35,3},{4,36},{36... | collective-permute-start | bytes 1179656 | tf_op jit(solution)/shard_map/ppermute | solution.py:195
  64.1 3.6 %collective-permute-start.10 = (bf16[2,2,384,128]{3,2,1,0:T(8,128)(2,1)S(1)}, bf16[2,2,384,128]{3,2,1,0:T(8,128)(2,1)S(1)}, u32[]{:S(2)}, u32[]{:S(2)}) collective-permute-start(bf16[2,2,384,128]{3,2,1,0:T(8,128)(2,1)S(1)} %collective-permute-done.8.refs_9_), channel_id=1, source_target_pairs={{0,32},{32,0},{1,33},{33,1},{2,34},{34,2},{3,35},{35,3},{4,36},{36... | collective-permute-start | bytes 1179656 | tf_op jit(solution)/shard_map/ppermute | solution.py:195
  94.3 12.3 %collective-permute-start.12 = (f32[2,144,128]{2,1,0:T(8,128)S(1)}, f32[2,144,128]{2,1,0:T(8,128)S(1)}, u32[]{:S(2)}, u32[]{:S(2)}) collective-permute-start(f32[2,144,128]{2,1,0:T(8,128)S(1)} %convert_reduce_fusion), channel_id=1, source_target_pairs={{0,79},{1,64},{2,97},{3,98},{4,131},{5,132},{6,165},{7,166},{8,199... | collective-permute-start | bytes 442376 | tf_op jit(solution)/shard_map/ppermute | solution.py:211
  96.3 21.8 %collective-permute-start.11 = (f32[2,144,128]{2,1,0:T(8,128)S(1)}, f32[2,144,128]{2,1,0:T(8,128)S(1)}, u32[]{:S(2)}, u32[]{:S(2)}) collective-permute-start(f32[2,144,128]{2,1,0:T(8,128)S(1)} %convert_reduce_fusion), channel_id=1, source_target_pairs={{0,228},{1,5},{2,6},{3,39},{4,40},{5,73},{6,74},{7,107},{8,108},{9... | collective-permute-start | bytes 442376 | tf_op jit(solution)/shard_map/ppermute | solution.py:210

commit v2 on v1

v2 whole, which is shorter than its diff:
```python
import functools

import jax
import jax.numpy as jnp
import numpy as np
from jax import lax
from jax.experimental import pallas as pl
from jax.experimental.pallas import tpu as pltpu
from jax.sharding import Mesh, PartitionSpec as P

AXES = ("yh", "x", "c", "yl", "z")
SIZES = (2, 4, 2, 2, 16)
EXTRA = 16
VMEM = pl.BlockSpec(memory_space=pltpu.VMEM)
SMEM = pl.BlockSpec(memory_space=pltpu.SMEM)
PARAMS = pltpu.CompilerParams(vmem_limit_bytes=40 * 1024 * 1024)


def device_index(yh, x, c, yl, z):
    return (((yh * 4 + x) * 2 + c) * 2 + yl) * 16 + z


def home(row_y, row_z, col_y, col_z):
    return device_index(col_y, col_z // 4, col_z % 4 // 2, row_y, row_z), col_z % 2


def homes(yh, x, c, yl, z):
    slot = yh * 4 + x
    if c == 0:
        left, right = (1 - yl, z if slot > 3 else z + 4), (yl, z - slot % 4 - 1)
        if slot == 3 and yl == 1:
            left, right = (0, z), (1, z)
    else:
        left, right = (yl, z if slot > 3 else z - 4), (yl, z + slot % 4 + 1)
        if slot == 3 and (z < 8) != (yl == 0):
            return [home(0, z, 0, z) + (2,), home(1, z, 1, z) + (3,)]
    left, right = (left[0], left[1] % 16), (right[0], right[1] % 16)
    return [home(*left, *right) + (0,), home(*right, *left) + (1,)]


def routes():
    edges = []
    for place in np.ndindex(*SIZES):
        for to, half, mode in homes(*place):
            edges.append((device_index(*place), to, half, mode))
    into = [[] for _ in range(512)]
    for e, edge in enumerate(edges):
        into[edge[1]].append(e)
    turn = [-1] * len(edges)
    for first in range(len(edges)):
        e = first
        while turn[e] < 0:
            turn[e] = 0
            pair = into[edges[e][1]]
            other = pair[0] + pair[1] - e
            turn[other] = 1
            e = other ^ 1
    perms = [[], []]
    table = np.zeros((512, 4), np.int32)
    for e, (source, to, half, mode) in enumerate(edges):
        perms[turn[e]].append((source, to))
        table[to, 2 * half] = turn[e]
        table[to, 2 * half + 1] = mode
    return perms, table


def features_kernel(field, backward, activity, signal, f, b, sems):
    copies = [
        pltpu.make_async_copy(field, f, sems.at[0]),
        pltpu.make_async_copy(backward, b, sems.at[1]),
    ]
    for copy in copies:
        copy.start()
    for copy in copies:
        copy.wait()
    wide = jnp.tanh(f[...].astype(jnp.float32))
    activity[...] = wide.astype(jnp.bfloat16)
    signal[...] = ((1.0 - wide * wide) * b[...].astype(jnp.float32)).astype(
        jnp.bfloat16
    )


def products_kernel(place, scale, *refs):
    out = refs[-1]
    core, y, z = place[0], place[1], place[2]
    n = out.shape[-1]
    row = lax.broadcasted_iota(jnp.int32, (n, n), 0)
    col = lax.broadcasted_iota(jnp.int32, (n, n), 1)

    def product(left, right):
        return lax.dot_general(
            left, right, (((0,), (0,)), ((), ())), preferred_element_type=jnp.float32
        )

    def store(slot, kernel, total):
        out[slot, kernel * n : (kernel + 1) * n] = (total * scale[0]).astype(
            jnp.bfloat16
        )

    for slot in range(8):
        out[slot, 2 * n : 2 * n + EXTRA] = jnp.zeros((EXTRA, n), jnp.bfloat16)
    packed = (core == 1) & ((z < 8) != (y == 0))
    for kernel in range(2):
        walk, near, far = refs[kernel : 10 + kernel : 2], refs[10 + kernel], refs[12 + kernel]
        steps = jnp.concatenate([w[...] for w in walk[1:]], axis=1)

        def four(first, left):
            total = product(left, steps)
            for j in range(4):
                store(first + j, kernel, total[:, j * n : (j + 1) * n])

        four(0, far[...])

        @pl.when(core == 0)
        def _():
            four(4, near[...])

        @pl.when(core == 1)
        def _():
            four(4, walk[0][...])

        @pl.when((core == 0) & (y == 1))
        def _():
            store(3, kernel, product(near[...], walk[0][...]))

        @pl.when(packed)
        def _():
            own = product(walk[0][...], walk[0][...])
            other = product(near[...], near[...])
            high = jnp.where(y == 0, own, other)
            low = jnp.where(y == 0, other, own)
            store(3, kernel, jnp.where(row <= col, high, low))
            diagonal = jnp.sum(jnp.where(row == col, low, 0.0), axis=0, keepdims=True)
            line = lax.broadcasted_iota(jnp.int32, (EXTRA, n), 0)
            extra = out[3, 2 * n : 2 * n + EXTRA].astype(jnp.float32)
            extra = jnp.where(line == kernel, diagonal * scale[0], extra)
            out[3, 2 * n : 2 * n + EXTRA] = extra.astype(jnp.bfloat16)


def place_kernel(total_draws, todo, a, b, feature, gradient):
    n = feature.shape[0]
    row = lax.broadcasted_iota(jnp.int32, (n, n), 0)
    col = lax.broadcasted_iota(jnp.int32, (n, n), 1)
    for kernel, out in enumerate((feature, gradient)):
        block, line = pl.ds(kernel * n, n), pl.ds(2 * n + kernel, 1)
        for half in range(2):
            second, mode = todo[2 * half] == 1, todo[2 * half + 1]
            got = jnp.where(second, b[block, :], a[block, :])
            extra = jnp.where(second, b[line, :], a[line, :])
            turned = got.T
            lower = row > col
            plain = (mode == 0) | ((mode == 2) & (row <= col)) | ((mode == 3) & lower)
            value = jnp.where(plain, got, turned)
            value = jnp.where((mode == 3) & (row == col), extra, value)
            out[:, half * n : (half + 1) * n] = value / total_draws


def on_device(field, backward):
    draws, n = field.shape
    total_draws = draws * 16
    values = jax.ShapeDtypeStruct((draws, n), jnp.bfloat16)
    own = pl.pallas_call(
        features_kernel,
        out_shape=(values, values),
        in_specs=[pl.BlockSpec(memory_space=pl.ANY)] * 2,
        out_specs=(VMEM, VMEM),
        scratch_shapes=[
            pltpu.VMEM((draws, n), jnp.bfloat16),
            pltpu.VMEM((draws, n), jnp.bfloat16),
            pltpu.SemaphoreType.DMA((2,)),
        ],
        compiler_params=PARAMS,
    )(field, backward)

    step = [
        (c * 16 + z, c * 16 + (z + 1 - 2 * c) % 16) for c in range(2) for z in range(16)
    ]
    chains = [lax.all_gather(part, "c", axis=0, tiled=True) for part in own]
    start, walk = chains, list(chains)
    for j in range(4):
        chains = [lax.ppermute(chain, ("c", "z"), step) for chain in chains]
        walk += chains
        if j == 0:
            start = lax.optimization_barrier((start, chains))[0]
    near = [lax.ppermute(part, "yl", [(0, 1), (1, 0)]) for part in start]
    cross = [(0, 2), (1, 3), (2, 1), (3, 0)]
    far = [lax.ppermute(chain, ("c", "yl"), cross) for chain in chains]

    place = jnp.stack([lax.axis_index("c"), lax.axis_index("yl"), lax.axis_index("z")])
    scales = np.exp2(np.arange(8) / 8).astype(np.float32)
    scale = lax.dynamic_slice_in_dim(
        jnp.asarray(scales), lax.axis_index(("yh", "x")), 1
    )
    partial = pl.pallas_call(
        products_kernel,
        out_shape=jax.ShapeDtypeStruct((8, 2 * n + EXTRA, n), jnp.bfloat16),
        in_specs=[SMEM, SMEM] + [VMEM] * 14,
        out_specs=VMEM,
        compiler_params=PARAMS,
    )(place, scale, *walk, *near, *far)
    partial = lax.all_to_all(partial, ("yh", "x"), 0, 0, tiled=True)
    block = jnp.sum(partial.astype(jnp.float32) / scales[:, None, None], axis=0)
    block = block[: 2 * n + 8]

    perms, table = routes()
    a = lax.ppermute(block, AXES, perms[0])
    b = lax.ppermute(block, AXES, perms[1])
    todo = lax.dynamic_index_in_dim(
        jnp.asarray(table), lax.axis_index(AXES), 0, keepdims=False
    )
    out = jax.ShapeDtypeStruct((n, 2 * n), jnp.float32)
    return pl.pallas_call(
        functools.partial(place_kernel, total_draws),
        out_shape=(out, out),
        in_specs=[SMEM, VMEM, VMEM],
        out_specs=(VMEM, VMEM),
        compiler_params=PARAMS,
    )(todo, a, b)


def solution(mesh):
    grid = Mesh(mesh.devices.reshape(SIZES), AXES)
    return jax.shard_map(
        on_device,
        mesh=grid,
        in_specs=(P(("yh", "x", "c"), ("yl", "z")),) * 2,
        out_specs=(P(("yl", "z"), ("yh", "x", "c")),) * 2,
        check_vma=False,
    )
```

time: 120 us -> 124 us (1.033)
  the two profiles are of different devices: /device:TPU:10 before, /device:TPU:7 now
where the time goes in v2:
time: 124 us; the launch traced here: 123 us
  starting transfers between devices  71.1 us (57%)
  waiting for transfers between devices  22.8 us (18%)
  blocking collectives  19.1 us (15%)
  Pallas kernels  5.73 us (5%)
  local copies, waits for them, and re-layouts  3.21 us (3%)
    ppermute x8, starting transfers between devices, on_device(): chains = [lax.ppermute(chain, ('c', 'z'), step) for chain in chains]  40.7 us
    all_to_all x1, blocking collectives, on_device(): partial = lax.all_to_all(partial, ('yh', 'x'), 0, 0, tiled=True)  14.6 us
    ppermute x2, waiting for transfers between devices, on_device(): far = [lax.ppermute(chain, ('c', 'yl'), cross) for chain in chains]  10.9 us
    ppermute x1, starting transfers between devices, on_device(): b = lax.ppermute(block, AXES, perms[1])  10.9 us
    ppermute x2, starting transfers between devices, on_device(): far = [lax.ppermute(chain, ('c', 'yl'), cross) for chain in chains]  9.68 us
    ppermute x2, starting transfers between devices, on_device(): near = [lax.ppermute(part, 'yl', [(0, 1), (1, 0)]) for part in start]  5.28 us
    ppermute x1, starting transfers between devices, on_device(): a = lax.ppermute(block, AXES, perms[0])  4.56 us
    all_gather x2, blocking collectives, on_device(): chains = [lax.all_gather(part, 'c', axis=0, tiled=True) for part in own]  4.48 us
  transfers between devices with their start and end apart: 14, of which 8 were waited for; matrix products, arithmetic and copies ran while one was open for 1% of the time, Pallas kernels for 0%

profile of v2, /device:TPU:7, one launch (start us, length us, event | category | flops | bytes accessed | tf_op | source)
XLA Modules:
  0.0 123.1 jit_solution(13981768472309150597)
XLA Ops:
  0.6 0.9 copy-done
  1.6 0.9 copy-done.1
  2.5 0.6 shard_map.68
  3.1 2.4 %all_gather.7.refs_1_ = bf16[1536,128]{1,0:T(8,128)(2,1)S(1)} all-gather(bf16[768,128]{1,0:T(8,128)(2,1)S(1)} %get-tuple-element.7), channel_id=1, replica_groups=mesh['yh'=2,'x'=4,'c'=2,'yl'=2,'z'=16] {'c'}, dimensions={0}, use_global_device_ids=true | all-gather | bytes 589824 | tf_op jit(solution)/shard_map/all_gather | solution.py:178
  5.5 11.1 %collective-permute-start.1 = (bf16[1536,128]{1,0:T(8,128)(2,1)S(1)}, bf16[1536,128]{1,0:T(8,128)(2,1)S(1)}, u32[]{:S(2)}, u32[]{:S(2)}) collective-permute-start(bf16[1536,128]{1,0:T(8,128)(2,1)S(1)} %all_gather.7.refs_1_), channel_id=1, source_target_pairs={{0,1},{1,2},{2,3},{3,4},{4,5},{5,6},{6,7},{7,8},{8,9},{9,10},{10,1... | collective-permute-start | bytes 1179656 | tf_op jit(solution)/shard_map/ppermute | solution.py:181
  16.6 2.1 %all_gather.6.refs_0_ = bf16[1536,128]{1,0:T(8,128)(2,1)S(1)} all-gather(bf16[768,128]{1,0:T(8,128)(2,1)S(1)} %get-tuple-element.6), channel_id=1, replica_groups=mesh['yh'=2,'x'=4,'c'=2,'yl'=2,'z'=16] {'c'}, dimensions={0}, use_global_device_ids=true | all-gather | bytes 589824 | tf_op jit(solution)/shard_map/all_gather | solution.py:178
  18.7 2.6 %collective-permute-start = (bf16[1536,128]{1,0:T(8,128)(2,1)S(1)}, bf16[1536,128]{1,0:T(8,128)(2,1)S(1)}, u32[]{:S(2)}, u32[]{:S(2)}) collective-permute-start(bf16[1536,128]{1,0:T(8,128)(2,1)S(1)} %all_gather.6.refs_0_), channel_id=1, source_target_pairs={{0,1},{1,2},{2,3},{3,4},{4,5},{5,6},{6,7},{7,8},{8,9},{9,10},{10,1... | collective-permute-start | bytes 1179656 | tf_op jit(solution)/shard_map/ppermute | solution.py:181
  21.3 5.0 %collective-permute-start.3 = (bf16[1536,128]{1,0:T(8,128)(2,1)S(1)}, bf16[1536,128]{1,0:T(8,128)(2,1)S(1)}, u32[]{:S(2)}, u32[]{:S(2)}) collective-permute-start(bf16[1536,128]{1,0:T(8,128)(2,1)S(1)} %collective-permute-done.1.refs_3_), channel_id=1, source_target_pairs={{0,1},{1,2},{2,3},{3,4},{4,5},{5,6},{6,7},{7,8},{8,9},{9,10},{10,1... | collective-permute-start | bytes 1179656 | tf_op jit(solution)/shard_map/ppermute | solution.py:181
  26.3 1.2 collective-permute-done.refs_2_
  27.5 3.5 %collective-permute-start.2 = (bf16[1536,128]{1,0:T(8,128)(2,1)S(1)}, bf16[1536,128]{1,0:T(8,128)(2,1)S(1)}, u32[]{:S(2)}, u32[]{:S(2)}) collective-permute-start(bf16[1536,128]{1,0:T(8,128)(2,1)S(1)} %collective-permute-done.refs_2_), channel_id=1, source_target_pairs={{0,1},{1,2},{2,3},{3,4},{4,5},{5,6},{6,7},{7,8},{8,9},{9,10},{10,1... | collective-permute-start | bytes 1179656 | tf_op jit(solution)/shard_map/ppermute | solution.py:181
  31.0 0.7 collective-permute-done.3.refs_5_
  31.7 4.3 %collective-permute-start.5 = (bf16[1536,128]{1,0:T(8,128)(2,1)S(1)}, bf16[1536,128]{1,0:T(8,128)(2,1)S(1)}, u32[]{:S(2)}, u32[]{:S(2)}) collective-permute-start(bf16[1536,128]{1,0:T(8,128)(2,1)S(1)} %collective-permute-done.3.refs_5_), channel_id=1, source_target_pairs={{0,1},{1,2},{2,3},{3,4},{4,5},{5,6},{6,7},{7,8},{8,9},{9,10},{10,1... | collective-permute-start | bytes 1179656 | tf_op jit(solution)/shard_map/ppermute | solution.py:181
  36.0 0.3 collective-permute-done.2.refs_4_
  36.3 4.5 %collective-permute-start.4 = (bf16[1536,128]{1,0:T(8,128)(2,1)S(1)}, bf16[1536,128]{1,0:T(8,128)(2,1)S(1)}, u32[]{:S(2)}, u32[]{:S(2)}) collective-permute-start(bf16[1536,128]{1,0:T(8,128)(2,1)S(1)} %collective-permute-done.2.refs_4_), channel_id=1, source_target_pairs={{0,1},{1,2},{2,3},{3,4},{4,5},{5,6},{6,7},{7,8},{8,9},{9,10},{10,1... | collective-permute-start | bytes 1179656 | tf_op jit(solution)/shard_map/ppermute | solution.py:181
  40.8 5.0 %collective-permute-start.7 = (bf16[1536,128]{1,0:T(8,128)(2,1)S(1)}, bf16[1536,128]{1,0:T(8,128)(2,1)S(1)}, u32[]{:S(2)}, u32[]{:S(2)}) collective-permute-start(bf16[1536,128]{1,0:T(8,128)(2,1)S(1)} %collective-permute-done.5.refs_7_), channel_id=1, source_target_pairs={{0,1},{1,2},{2,3},{3,4},{4,5},{5,6},{6,7},{7,8},{8,9},{9,10},{10,1... | collective-permute-start | bytes 1179656 | tf_op jit(solution)/shard_map/ppermute | solution.py:181
  45.8 4.7 %collective-permute-start.6 = (bf16[1536,128]{1,0:T(8,128)(2,1)S(1)}, bf16[1536,128]{1,0:T(8,128)(2,1)}, u32[]{:S(2)}, u32[]{:S(2)}) collective-permute-start(bf16[1536,128]{1,0:T(8,128)(2,1)S(1)} %collective-permute-done.4.refs_6_), channel_id=1, source_target_pairs={{0,1},{1,2},{2,3},{3,4},{4,5},{5,6},{6,7},{7,8},{8,9},{9,10},{10,1... | collective-permute-start | bytes 1179656 | tf_op jit(solution)/shard_map/ppermute | solution.py:181
  50.5 3.2 %collective-permute-start.8 = (bf16[1536,128]{1,0:T(8,128)(2,1)S(1)}, bf16[1536,128]{1,0:T(8,128)(2,1)}, u32[]{:S(2)}, u32[]{:S(2)}) collective-permute-start(bf16[1536,128]{1,0:T(8,128)(2,1)S(1)} %all_gather.6.refs_0_), channel_id=1, source_target_pairs={{0,16},{16,0},{1,17},{17,1},{2,18},{18,2},{3,19},{19,3},{4,20},{20... | collective-permute-start | bytes 1179656 | tf_op jit(solution)/shard_map/ppermute | solution.py:185
  53.7 2.1 %collective-permute-start.9 = (bf16[1536,128]{1,0:T(8,128)(2,1)S(1)}, bf16[1536,128]{1,0:T(8,128)(2,1)}, u32[]{:S(2)}, u32[]{:S(2)}) collective-permute-start(bf16[1536,128]{1,0:T(8,128)(2,1)S(1)} %all_gather.7.refs_1_), channel_id=1, source_target_pairs={{0,16},{16,0},{1,17},{17,1},{2,18},{18,2},{3,19},{19,3},{4,20},{20... | collective-permute-start | bytes 1179656 | tf_op jit(solution)/shard_map/ppermute | solution.py:185
  55.8 6.5 %collective-permute-start.11 = (bf16[1536,128]{1,0:T(8,128)(2,1)S(1)}, bf16[1536,128]{1,0:T(8,128)(2,1)}, u32[]{:S(2)}, u32[]{:S(2)}) collective-permute-start(bf16[1536,128]{1,0:T(8,128)(2,1)S(1)} %collective-permute-done.7.refs_9_), channel_id=1, source_target_pairs={{0,32},{16,48},{32,16},{48,0},{1,33},{17,49},{33,17},{49,1},{2,34}... | collective-permute-start | bytes 1179656 | tf_op jit(solution)/shard_map/ppermute | solution.py:187
  62.3 3.2 %collective-permute-start.10 = (bf16[1536,128]{1,0:T(8,128)(2,1)}, bf16[1536,128]{1,0:T(8,128)(2,1)}, u32[]{:S(2)}, u32[]{:S(2)}) collective-permute-start(bf16[1536,128]{1,0:T(8,128)(2,1)} %collective-permute-done.6.refs_8_), channel_id=1, source_target_pairs={{0,32},{16,48},{32,16},{48,0},{1,33},{17,49},{33,17},{49,1},{2,34}... | collective-permute-start | bytes 1179656 | tf_op jit(solution)/shard_map/ppermute | solution.py:187
  65.5 0.6 dynamic_slice.8.scale
  66.2 2.4 %collective-permute-done.9.refs_11_ = bf16[1536,128]{1,0:T(8,128)(2,1)} collective-permute-done((bf16[1536,128]{1,0:T(8,128)(2,1)S(1)}, bf16[1536,128]{1,0:T(8,128)(2,1)}, u32[]{:S(2)}, u32[]{:S(2)}) %collective-permute-start.9) | collective-permute-done | bytes 393248 | tf_op jit(solution)/shard_map/ppermute | solution.py:185
  68.6 6.6 %collective-permute-done.11.refs_13_ = bf16[1536,128]{1,0:T(8,128)(2,1)} collective-permute-done((bf16[1536,128]{1,0:T(8,128)(2,1)S(1)}, bf16[1536,128]{1,0:T(8,128)(2,1)}, u32[]{:S(2)}, u32[]{:S(2)}) %collective-permute-start.11) | collective-permute-done | bytes 393248 | tf_op jit(solution)/shard_map/ppermute | solution.py:187
  75.3 4.3 %collective-permute-done.10.refs_12_ = bf16[1536,128]{1,0:T(8,128)(2,1)} collective-permute-done((bf16[1536,128]{1,0:T(8,128)(2,1)}, bf16[1536,128]{1,0:T(8,128)(2,1)}, u32[]{:S(2)}, u32[]{:S(2)}) %collective-permute-start.10) | collective-permute-done | bytes 393248 | tf_op jit(solution)/shard_map/ppermute | solution.py:187
  79.6 3.8 %shard_map.69 = bf16[8,272,128]{2,1,0:T(8,128)(2,1)S(1)} custom-call(s32[3]{0:T(128)S(1)} %pad_add_fusion.place, f32[1]{0:T(128)} %dynamic_slice.8.scale, bf16[1536,128]{1,0:T(8,128)(2,1)S(1)} %all_gather.6.refs_0_, bf16[1536,128]{1,0:T(8,128)(2,1)S(1)} %all_gather.7.refs_1_, bf16[1536,128]{1,0:T(8,128)(2,1)S(1)} %collective-permute-done.refs_2_, ...), custom_call_target="tpu_custom_call" | custom-call | tf_op jit(solution)/shard_map/pallas_call | solution.py:194
  83.4 14.6 %all_to_all.5 = bf16[8,272,128]{2,1,0:T(8,128)(2,1)S(1)} all-to-all(bf16[8,272,128]{2,1,0:T(8,128)(2,1)S(1)} %shard_map.69), channel_id=1, replica_groups=mesh['yh'=2,'x'=4,'c'=2,'yl'=2,'z'=16] {'yh','x'}, dimensions={0} | all-to-all | bytes 1114112 | tf_op jit(solution)/shard_map/all_to_all | solution.py:201
  98.1 10.9 %collective-permute-start.13 = (f32[264,128]{1,0:T(8,128)S(1)}, f32[264,128]{1,0:T(8,128)S(1)}, u32[]{:S(2)}, u32[]{:S(2)}) collective-permute-start(f32[264,128]{1,0:T(8,128)S(1)} %slice.4), channel_id=1, source_target_pairs={{0,335},{1,320},{2,353},{3,354},{4,387},{5,388},{6,421},{7,422},{8... | collective-permute-start | bytes 405512 | tf_op jit(solution)/shard_map/ppermute | solution.py:207
  109.0 4.6 %collective-permute-start.12 = (f32[264,128]{1,0:T(8,128)S(1)}, f32[264,128]{1,0:T(8,128)S(1)}, u32[]{:S(2)}, u32[]{:S(2)}) collective-permute-start(f32[264,128]{1,0:T(8,128)S(1)} %slice.4), channel_id=1, source_target_pairs={{0,244},{1,21},{2,22},{3,55},{4,56},{5,89},{6,90},{7,123},{8,124},... | collective-permute-start | bytes 405512 | tf_op jit(solution)/shard_map/ppermute | solution.py:206
  113.6 0.7 dynamic-slice_bitcast_fusion.todo
  114.3 3.1 %collective-permute-done.13.b = f32[264,128]{1,0:T(8,128)S(1)} collective-permute-done((f32[264,128]{1,0:T(8,128)S(1)}, f32[264,128]{1,0:T(8,128)S(1)}, u32[]{:S(2)}, u32[]{:S(2)}) %collective-permute-start.13) | collective-permute-done | bytes 135200 | tf_op jit(solution)/shard_map/ppermute | solution.py:207
  117.4 4.3 %collective-permute-done.12.a = f32[264,128]{1,0:T(8,128)S(1)} collective-permute-done((f32[264,128]{1,0:T(8,128)S(1)}, f32[264,128]{1,0:T(8,128)S(1)}, u32[]{:S(2)}, u32[]{:S(2)}) %collective-permute-start.12) | collective-permute-done | bytes 135200 | tf_op jit(solution)/shard_map/ppermute | solution.py:206
  121.7 1.4 %shard_map.70 = (f32[128,256]{1,0:T(8,128)}, f32[128,256]{1,0:T(8,128)}) custom-call(s32[4]{0:T(128)S(1)} %dynamic-slice_bitcast_fusion.todo, f32[264,128]{1,0:T(8,128)S(1)} %collective-permute-done.12.a, f32[264,128]{1,0:T(8,128)S(1)} %collective-permute-done.13.b), custom_call_target="tpu_custom_call" | custom-call | tf_op jit(solution)/shard_map/pallas_call | solution.py:212
  (15 shorter events, 0.3 us)
Async XLA Ops:
  0.6 0.9 copy-start
  1.6 0.9 copy-start.1
  3.1 62.4 %copy-start.3 = (f32[8]{0:T(128)S(1)}, f32[8]{0:T(128)}, u32[]{:S(2)}) copy-start(f32[8]{0:T(128)} %constant.50.clone) | copy-start | bytes 100
  5.5 15.8 %collective-permute-start.1 = (bf16[1536,128]{1,0:T(8,128)(2,1)S(1)}, bf16[1536,128]{1,0:T(8,128)(2,1)S(1)}, u32[]{:S(2)}, u32[]{:S(2)}) collective-permute-start(bf16[1536,128]{1,0:T(8,128)(2,1)S(1)} %all_gather.7.refs_1_), channel_id=1, source_target_pairs={{0,1},{1,2},{2,3},{3,4},{4,5},{5,6},{6,7},{7,8},{8,9},{9,10},{10,1... | collective-permute-start | bytes 1179656 | tf_op jit(solution)/shard_map/ppermute | solution.py:181
  18.7 8.8 %collective-permute-start = (bf16[1536,128]{1,0:T(8,128)(2,1)S(1)}, bf16[1536,128]{1,0:T(8,128)(2,1)S(1)}, u32[]{:S(2)}, u32[]{:S(2)}) collective-permute-start(bf16[1536,128]{1,0:T(8,128)(2,1)S(1)} %all_gather.6.refs_0_), channel_id=1, source_target_pairs={{0,1},{1,2},{2,3},{3,4},{4,5},{5,6},{6,7},{7,8},{8,9},{9,10},{10,1... | collective-permute-start | bytes 1179656 | tf_op jit(solution)/shard_map/ppermute | solution.py:181
  21.3 10.4 %collective-permute-start.3 = (bf16[1536,128]{1,0:T(8,128)(2,1)S(1)}, bf16[1536,128]{1,0:T(8,128)(2,1)S(1)}, u32[]{:S(2)}, u32[]{:S(2)}) collective-permute-start(bf16[1536,128]{1,0:T(8,128)(2,1)S(1)} %collective-permute-done.1.refs_3_), channel_id=1, source_target_pairs={{0,1},{1,2},{2,3},{3,4},{4,5},{5,6},{6,7},{7,8},{8,9},{9,10},{10,1... | collective-permute-start | bytes 1179656 | tf_op jit(solution)/shard_map/ppermute | solution.py:181
  27.5 8.8 %collective-permute-start.2 = (bf16[1536,128]{1,0:T(8,128)(2,1)S(1)}, bf16[1536,128]{1,0:T(8,128)(2,1)S(1)}, u32[]{:S(2)}, u32[]{:S(2)}) collective-permute-start(bf16[1536,128]{1,0:T(8,128)(2,1)S(1)} %collective-permute-done.refs_2_), channel_id=1, source_target_pairs={{0,1},{1,2},{2,3},{3,4},{4,5},{5,6},{6,7},{7,8},{8,9},{9,10},{10,1... | collective-permute-start | bytes 1179656 | tf_op jit(solution)/shard_map/ppermute | solution.py:181
  31.7 9.1 %collective-permute-start.5 = (bf16[1536,128]{1,0:T(8,128)(2,1)S(1)}, bf16[1536,128]{1,0:T(8,128)(2,1)S(1)}, u32[]{:S(2)}, u32[]{:S(2)}) collective-permute-start(bf16[1536,128]{1,0:T(8,128)(2,1)S(1)} %collective-permute-done.3.refs_5_), channel_id=1, source_target_pairs={{0,1},{1,2},{2,3},{3,4},{4,5},{5,6},{6,7},{7,8},{8,9},{9,10},{10,1... | collective-permute-start | bytes 1179656 | tf_op jit(solution)/shard_map/ppermute | solution.py:181
  36.3 9.5 %collective-permute-start.4 = (bf16[1536,128]{1,0:T(8,128)(2,1)S(1)}, bf16[1536,128]{1,0:T(8,128)(2,1)S(1)}, u32[]{:S(2)}, u32[]{:S(2)}) collective-permute-start(bf16[1536,128]{1,0:T(8,128)(2,1)S(1)} %collective-permute-done.2.refs_4_), channel_id=1, source_target_pairs={{0,1},{1,2},{2,3},{3,4},{4,5},{5,6},{6,7},{7,8},{8,9},{9,10},{10,1... | collective-permute-start | bytes 1179656 | tf_op jit(solution)/shard_map/ppermute | solution.py:181
  40.8 15.0 %collective-permute-start.7 = (bf16[1536,128]{1,0:T(8,128)(2,1)S(1)}, bf16[1536,128]{1,0:T(8,128)(2,1)S(1)}, u32[]{:S(2)}, u32[]{:S(2)}) collective-permute-start(bf16[1536,128]{1,0:T(8,128)(2,1)S(1)} %collective-permute-done.5.refs_7_), channel_id=1, source_target_pairs={{0,1},{1,2},{2,3},{3,4},{4,5},{5,6},{6,7},{7,8},{8,9},{9,10},{10,1... | collective-permute-start | bytes 1179656 | tf_op jit(solution)/shard_map/ppermute | solution.py:181
  45.8 16.6 %collective-permute-start.6 = (bf16[1536,128]{1,0:T(8,128)(2,1)S(1)}, bf16[1536,128]{1,0:T(8,128)(2,1)}, u32[]{:S(2)}, u32[]{:S(2)}) collective-permute-start(bf16[1536,128]{1,0:T(8,128)(2,1)S(1)} %collective-permute-done.4.refs_6_), channel_id=1, source_target_pairs={{0,1},{1,2},{2,3},{3,4},{4,5},{5,6},{6,7},{7,8},{8,9},{9,10},{10,1... | collective-permute-start | bytes 1179656 | tf_op jit(solution)/shard_map/ppermute | solution.py:181
  50.5 15.8 %collective-permute-start.8 = (bf16[1536,128]{1,0:T(8,128)(2,1)S(1)}, bf16[1536,128]{1,0:T(8,128)(2,1)}, u32[]{:S(2)}, u32[]{:S(2)}) collective-permute-start(bf16[1536,128]{1,0:T(8,128)(2,1)S(1)} %all_gather.6.refs_0_), channel_id=1, source_target_pairs={{0,16},{16,0},{1,17},{17,1},{2,18},{18,2},{3,19},{19,3},{4,20},{20... | collective-permute-start | bytes 1179656 | tf_op jit(solution)/shard_map/ppermute | solution.py:185
  53.7 14.9 %collective-permute-start.9 = (bf16[1536,128]{1,0:T(8,128)(2,1)S(1)}, bf16[1536,128]{1,0:T(8,128)(2,1)}, u32[]{:S(2)}, u32[]{:S(2)}) collective-permute-start(bf16[1536,128]{1,0:T(8,128)(2,1)S(1)} %all_gather.7.refs_1_), channel_id=1, source_target_pairs={{0,16},{16,0},{1,17},{17,1},{2,18},{18,2},{3,19},{19,3},{4,20},{20... | collective-permute-start | bytes 1179656 | tf_op jit(solution)/shard_map/ppermute | solution.py:185
  55.8 19.5 %collective-permute-start.11 = (bf16[1536,128]{1,0:T(8,128)(2,1)S(1)}, bf16[1536,128]{1,0:T(8,128)(2,1)}, u32[]{:S(2)}, u32[]{:S(2)}) collective-permute-start(bf16[1536,128]{1,0:T(8,128)(2,1)S(1)} %collective-permute-done.7.refs_9_), channel_id=1, source_target_pairs={{0,32},{16,48},{32,16},{48,0},{1,33},{17,49},{33,17},{49,1},{2,34}... | collective-permute-start | bytes 1179656 | tf_op jit(solution)/shard_map/ppermute | solution.py:187
  62.3 17.2 %collective-permute-start.10 = (bf16[1536,128]{1,0:T(8,128)(2,1)}, bf16[1536,128]{1,0:T(8,128)(2,1)}, u32[]{:S(2)}, u32[]{:S(2)}) collective-permute-start(bf16[1536,128]{1,0:T(8,128)(2,1)} %collective-permute-done.6.refs_8_), channel_id=1, source_target_pairs={{0,32},{16,48},{32,16},{48,0},{1,33},{17,49},{33,17},{49,1},{2,34}... | collective-permute-start | bytes 1179656 | tf_op jit(solution)/shard_map/ppermute | solution.py:187
  83.3 14.6 %copy-start.2 = (f32[8]{0:T(128)S(1)}, f32[8]{0:T(128)}, u32[]{:S(2)}) copy-start(f32[8]{0:T(128)} %constant.54) | copy-start | bytes 100
  98.1 19.3 %collective-permute-start.13 = (f32[264,128]{1,0:T(8,128)S(1)}, f32[264,128]{1,0:T(8,128)S(1)}, u32[]{:S(2)}, u32[]{:S(2)}) collective-permute-start(f32[264,128]{1,0:T(8,128)S(1)} %slice.4), channel_id=1, source_target_pairs={{0,335},{1,320},{2,353},{3,354},{4,387},{5,388},{6,421},{7,422},{8... | collective-permute-start | bytes 405512 | tf_op jit(solution)/shard_map/ppermute | solution.py:207
  109.0 12.7 %collective-permute-start.12 = (f32[264,128]{1,0:T(8,128)S(1)}, f32[264,128]{1,0:T(8,128)S(1)}, u32[]{:S(2)}, u32[]{:S(2)}) collective-permute-start(f32[264,128]{1,0:T(8,128)S(1)} %slice.4), channel_id=1, source_target_pairs={{0,244},{1,21},{2,22},{3,55},{4,56},{5,89},{6,90},{7,123},{8,124},... | collective-permute-start | bytes 405512 | tf_op jit(solution)/shard_map/ppermute | solution.py:206

commit v3 on v2

--- a/solution.py
+++ b/solution.py
@@ -10,6 +10,7 @@
 
 AXES = ("yh", "x", "c", "yl", "z")
 SIZES = (2, 4, 2, 2, 16)
+PIECES = 4
 EXTRA = 16
 VMEM = pl.BlockSpec(memory_space=pltpu.VMEM)
 SMEM = pl.BlockSpec(memory_space=pltpu.SMEM)
@@ -65,22 +66,30 @@
 
 
 def features_kernel(field, backward, activity, signal, f, b, sems):
-    copies = [
-        pltpu.make_async_copy(field, f, sems.at[0]),
-        pltpu.make_async_copy(backward, b, sems.at[1]),
-    ]
-    for copy in copies:
-        copy.start()
-    for copy in copies:
-        copy.wait()
-    wide = jnp.tanh(f[...].astype(jnp.float32))
-    activity[...] = wide.astype(jnp.bfloat16)
-    signal[...] = ((1.0 - wide * wide) * b[...].astype(jnp.float32)).astype(
-        jnp.bfloat16
-    )
-
-
-def products_kernel(place, scale, *refs):
+    rows = field.shape[0] // PIECES
+    copies = []
+    for piece in range(PIECES):
+        part = pl.ds(piece * rows, rows)
+        copies.append(
+            [
+                pltpu.make_async_copy(src.at[part], dst.at[part], sems.at[i, piece])
+                for i, (src, dst) in enumerate(((field, f), (backward, b)))
+            ]
+        )
+        for copy in copies[-1]:
+            copy.start()
+    for piece in range(PIECES):
+        part = pl.ds(piece * rows, rows)
+        for copy in copies[piece]:
+            copy.wait()
+        wide = jnp.tanh(f[part, :].astype(jnp.float32))
+        activity[part, :] = wide.astype(jnp.bfloat16)
+        signal[part, :] = (
+            (1.0 - wide * wide) * b[part, :].astype(jnp.float32)
+        ).astype(jnp.bfloat16)
+
+
+def products_kernel(late, place, scale, *refs):
     out = refs[-1]
     core, y, z = place[0], place[1], place[2]
     n = out.shape[-1]
@@ -97,29 +106,41 @@
             jnp.bfloat16
         )
 
+    packed = (core == 1) & ((z < 8) != (y == 0))
+    partner = (core == 0) & (y == 1)
+
+    def four(first, kernel, left, steps):
+        total = product(left, steps)
+        for j in range(3):
+            store(first + j, kernel, total[:, j * n : (j + 1) * n])
+        return total[:, 3 * n :]
+
+    if late:
+        for kernel in range(2):
+            walk, far = refs[kernel : 8 + kernel : 2], refs[8 + kernel]
+            steps = jnp.concatenate([w[...] for w in walk], axis=1)
+            last = four(0, kernel, far[...], steps)
+
+            @pl.when(jnp.logical_not(packed | partner))
+            def _():
+                store(3, kernel, last)
+
+        return
     for slot in range(8):
         out[slot, 2 * n : 2 * n + EXTRA] = jnp.zeros((EXTRA, n), jnp.bfloat16)
-    packed = (core == 1) & ((z < 8) != (y == 0))
     for kernel in range(2):
-        walk, near, far = refs[kernel : 10 + kernel : 2], refs[10 + kernel], refs[12 + kernel]
+        walk, near = refs[kernel : 10 + kernel : 2], refs[10 + kernel]
         steps = jnp.concatenate([w[...] for w in walk[1:]], axis=1)
 
-        def four(first, left):
-            total = product(left, steps)
-            for j in range(4):
-                store(first + j, kernel, total[:, j * n : (j + 1) * n])
-
-        four(0, far[...])
-
         @pl.when(core == 0)
         def _():
-            four(4, near[...])
+            store(7, kernel, four(4, kernel, near[...], steps))
 
         @pl.when(core == 1)
         def _():
-            four(4, walk[0][...])
-
-        @pl.when((core == 0) & (y == 1))
+            store(7, kernel, four(4, kernel, walk[0][...], steps))
+
+        @pl.when(partner)
         def _():
             store(3, kernel, product(near[...], walk[0][...]))
 
@@ -162,27 +183,29 @@
     own = pl.pallas_call(
         features_kernel,
         out_shape=(values, values),
-        in_specs=[pl.BlockSpec(memory_space=pl.ANY)] * 2,
+        in_specs=[pl.BlockSpec(memory_space=pltpu.HBM)] * 2,
         out_specs=(VMEM, VMEM),
         scratch_shapes=[
             pltpu.VMEM((draws, n), jnp.bfloat16),
             pltpu.VMEM((draws, n), jnp.bfloat16),
-            pltpu.SemaphoreType.DMA((2,)),
+            pltpu.SemaphoreType.DMA((2, PIECES)),
         ],
-        compiler_params=PARAMS,
+        compiler_params=pltpu.CompilerParams(vmem_limit_bytes=60 * 1024 * 1024),
     )(field, backward)
 
     step = [
         (c * 16 + z, c * 16 + (z + 1 - 2 * c) % 16) for c in range(2) for z in range(16)
     ]
-    chains = [lax.all_gather(part, "c", axis=0, tiled=True) for part in own]
-    start, walk = chains, list(chains)
+    start = chains = [lax.all_gather(part, "c", axis=0, tiled=True) for part in own]
+    walk = list(chains)
     for j in range(4):
         chains = [lax.ppermute(chain, ("c", "z"), step) for chain in chains]
+        if j == 0:
+            start, chains[1] = lax.optimization_barrier((start, chains[1]))
+            near = [lax.ppermute(part, "yl", [(0, 1), (1, 0)]) for part in start]
+        if j == 2:
+            near, chains[1] = lax.optimization_barrier((near, chains[1]))
         walk += chains
-        if j == 0:
-            start = lax.optimization_barrier((start, chains))[0]
-    near = [lax.ppermute(part, "yl", [(0, 1), (1, 0)]) for part in start]
     cross = [(0, 2), (1, 3), (2, 1), (3, 0)]
     far = [lax.ppermute(chain, ("c", "yl"), cross) for chain in chains]
 
@@ -191,13 +214,27 @@
     scale = lax.dynamic_slice_in_dim(
         jnp.asarray(scales), lax.axis_index(("yh", "x")), 1
     )
+    shape = jax.ShapeDtypeStruct((8, 2 * n + EXTRA, n), jnp.bfloat16)
+    cost = pl.CostEstimate(
+        flops=32 * n * n * draws, bytes_accessed=28 * n * draws, transcendentals=0
+    )
     partial = pl.pallas_call(
-        products_kernel,
-        out_shape=jax.ShapeDtypeStruct((8, 2 * n + EXTRA, n), jnp.bfloat16),
-        in_specs=[SMEM, SMEM] + [VMEM] * 14,
+        functools.partial(products_kernel, False),
+        out_shape=shape,
+        in_specs=[SMEM, SMEM] + [VMEM] * 12,
         out_specs=VMEM,
         compiler_params=PARAMS,
-    )(place, scale, *walk, *near, *far)
+        cost_estimate=cost,
+    )(place, scale, *walk, *near)
+    partial = pl.pallas_call(
+        functools.partial(products_kernel, True),
+        out_shape=shape,
+        in_specs=[SMEM, SMEM] + [VMEM] * 11,
+        out_specs=VMEM,
+        input_output_aliases={12: 0},
+        compiler_params=PARAMS,
+        cost_estimate=cost,
+    )(place, scale, *walk[2:], *far, partial)
     partial = lax.all_to_all(partial, ("yh", "x"), 0, 0, tiled=True)
     block = jnp.sum(partial.astype(jnp.float32) / scales[:, None, None], axis=0)
     block = block[: 2 * n + 8]

time: 124 us -> 121 us (0.976)
  the two profiles are of different devices: /device:TPU:7 before, /device:TPU:6 now
where the time goes in v3:
time: 121 us; the launch traced here: 120 us
  waiting for transfers between devices  40.9 us (34%)
  starting transfers between devices  36.9 us (30%)
  blocking collectives  28.2 us (23%)
  Pallas kernels  8.37 us (7%)
  local copies, waits for them, and re-layouts  4.78 us (4%)
    ppermute x8, waiting for transfers between devices, on_device(): chains = [lax.ppermute(chain, ('c', 'z'), step) for chain in chains]  17.6 us
    ppermute x8, starting transfers between devices, on_device(): chains = [lax.ppermute(chain, ('c', 'z'), step) for chain in chains]  17.2 us
    all_to_all x1, blocking collectives, on_device(): partial = lax.all_to_all(partial, ('yh', 'x'), 0, 0, tiled=True)  16.6 us
    all_gather x2, blocking collectives, on_device(): lax.all_gather(part, 'c', axis=0, tiled=True)  11.6 us
    ppermute x2, waiting for transfers between devices, on_device(): near = [lax.ppermute(part, 'yl', [(0, 1), (1, 0)]) for part in start]  9.66 us
    ppermute x1, starting transfers between devices, on_device(): a = lax.ppermute(block, AXES, perms[0])  8.16 us
    ppermute x1, waiting for transfers between devices, on_device(): b = lax.ppermute(block, AXES, perms[1])  6.61 us
    ppermute x2, starting transfers between devices, on_device(): near = [lax.ppermute(part, 'yl', [(0, 1), (1, 0)]) for part in start]  5.84 us
  transfers between devices with their start and end apart: 14, of which 10 were waited for; matrix products, arithmetic and copies ran while one was open for 1% of the time, Pallas kernels for 2%

profile of v3, /device:TPU:6, one launch (start us, length us, event | category | flops | bytes accessed | tf_op | source)
XLA Modules:
  0.0 120.3 jit_solution(12150544844018778684)
XLA Ops:
  0.6 1.8 %shard_map.68 = (bf16[768,128]{1,0:T(8,128)(2,1)}, bf16[768,128]{1,0:T(8,128)(2,1)}) custom-call(bf16[768,128]{1,0:T(8,128)(2,1)} %field.1, bf16[768,128]{1,0:T(8,128)(2,1)} %backward.1), custom_call_target="tpu_custom_call" | custom-call | tf_op jit(solution)/shard_map/pallas_call | solution.py:183
  2.5 2.4 %all_gather.7.refs_1_ = bf16[1536,128]{1,0:T(8,128)(2,1)S(1)} all-gather(bf16[768,128]{1,0:T(8,128)(2,1)} %get-tuple-element.11), channel_id=1, replica_groups=mesh['yh'=2,'x'=4,'c'=2,'yl'=2,'z'=16] {'c'}, dimensions={0}, use_global_device_ids=true | all-gather | bytes 589824 | tf_op jit(solution)/shard_map/all_gather | solution.py:199
  4.9 3.8 %collective-permute-start.1 = (bf16[1536,128]{1,0:T(8,128)(2,1)S(1)}, bf16[1536,128]{1,0:T(8,128)(2,1)S(1)}, u32[]{:S(2)}, u32[]{:S(2)}) collective-permute-start(bf16[1536,128]{1,0:T(8,128)(2,1)S(1)} %all_gather.7.refs_1_), channel_id=1, source_target_pairs={{0,1},{1,2},{2,3},{3,4},{4,5},{5,6},{6,7},{7,8},{8,9},{9,10},{10,1... | collective-permute-start | bytes 1179656 | tf_op jit(solution)/shard_map/ppermute | solution.py:202
  8.7 9.2 %all_gather.6.refs_0_ = bf16[1536,128]{1,0:T(8,128)(2,1)S(1)} all-gather(bf16[768,128]{1,0:T(8,128)(2,1)S(1)} %copy-done.4), channel_id=1, replica_groups=mesh['yh'=2,'x'=4,'c'=2,'yl'=2,'z'=16] {'c'}, dimensions={0}, use_global_device_ids=true | all-gather | bytes 589824 | tf_op jit(solution)/shard_map/all_gather | solution.py:199
  17.9 1.9 %collective-permute-start = (bf16[1536,128]{1,0:T(8,128)(2,1)S(1)}, bf16[1536,128]{1,0:T(8,128)(2,1)S(1)}, u32[]{:S(2)}, u32[]{:S(2)}) collective-permute-start(bf16[1536,128]{1,0:T(8,128)(2,1)S(1)} %all_gather.6.refs_0_), channel_id=1, source_target_pairs={{0,1},{1,2},{2,3},{3,4},{4,5},{5,6},{6,7},{7,8},{8,9},{9,10},{10,1... | collective-permute-start | bytes 1179656 | tf_op jit(solution)/shard_map/ppermute | solution.py:202
  19.8 2.2 %collective-permute-done.1.refs_3_.refs_1_ = bf16[1536,128]{1,0:T(8,128)(2,1)S(1)} collective-permute-done((bf16[1536,128]{1,0:T(8,128)(2,1)S(1)}, bf16[1536,128]{1,0:T(8,128)(2,1)S(1)}, u32[]{:S(2)}, u32[]{:S(2)}) %collective-permute-start.1) | collective-permute-done | bytes 393248 | tf_op jit(solution)/shard_map/ppermute | solution.py:202
  22.0 1.9 %collective-permute-start.3 = (bf16[1536,128]{1,0:T(8,128)(2,1)S(1)}, bf16[1536,128]{1,0:T(8,128)(2,1)S(1)}, u32[]{:S(2)}, u32[]{:S(2)}) collective-permute-start(bf16[1536,128]{1,0:T(8,128)(2,1)S(1)} %collective-permute-done.1.refs_3_.refs_1_), channel_id=1, source_target_pairs={{0,1},{1,2},{2,3},{3,4},{4,5},{5,6},{6,7},{7,8},{8,9},{9,10},{10,1... | collective-permute-start | bytes 1179656 | tf_op jit(solution)/shard_map/ppermute | solution.py:202
  23.9 4.8 %collective-permute-done.refs_2_.refs_0_ = bf16[1536,128]{1,0:T(8,128)(2,1)S(1)} collective-permute-done((bf16[1536,128]{1,0:T(8,128)(2,1)S(1)}, bf16[1536,128]{1,0:T(8,128)(2,1)S(1)}, u32[]{:S(2)}, u32[]{:S(2)}) %collective-permute-start) | collective-permute-done | bytes 393248 | tf_op jit(solution)/shard_map/ppermute | solution.py:202
  28.7 1.9 %collective-permute-start.2 = (bf16[1536,128]{1,0:T(8,128)(2,1)S(1)}, bf16[1536,128]{1,0:T(8,128)(2,1)S(1)}, u32[]{:S(2)}, u32[]{:S(2)}) collective-permute-start(bf16[1536,128]{1,0:T(8,128)(2,1)S(1)} %collective-permute-done.refs_2_.refs_0_), channel_id=1, source_target_pairs={{0,1},{1,2},{2,3},{3,4},{4,5},{5,6},{6,7},{7,8},{8,9},{9,10},{10,1... | collective-permute-start | bytes 1179656 | tf_op jit(solution)/shard_map/ppermute | solution.py:202
  30.7 3.5 %collective-permute-start.5 = (bf16[1536,128]{1,0:T(8,128)(2,1)S(1)}, bf16[1536,128]{1,0:T(8,128)(2,1)S(1)}, u32[]{:S(2)}, u32[]{:S(2)}) collective-permute-start(bf16[1536,128]{1,0:T(8,128)(2,1)S(1)} %all_gather.6.refs_0_), channel_id=1, source_target_pairs={{0,16},{16,0},{1,17},{17,1},{2,18},{18,2},{3,19},{19,3},{4,20},{20... | collective-permute-start | bytes 1179656 | tf_op jit(solution)/shard_map/ppermute | solution.py:205
  34.2 2.4 %collective-permute-start.6 = (bf16[1536,128]{1,0:T(8,128)(2,1)S(1)}, bf16[1536,128]{1,0:T(8,128)(2,1)S(1)}, u32[]{:S(2)}, u32[]{:S(2)}) collective-permute-start(bf16[1536,128]{1,0:T(8,128)(2,1)S(1)} %all_gather.7.refs_1_), channel_id=1, source_target_pairs={{0,16},{16,0},{1,17},{17,1},{2,18},{18,2},{3,19},{19,3},{4,20},{20... | collective-permute-start | bytes 1179656 | tf_op jit(solution)/shard_map/ppermute | solution.py:205
  36.5 1.9 %collective-permute-start.7 = (bf16[1536,128]{1,0:T(8,128)(2,1)S(1)}, bf16[1536,128]{1,0:T(8,128)(2,1)S(1)}, u32[]{:S(2)}, u32[]{:S(2)}) collective-permute-start(bf16[1536,128]{1,0:T(8,128)(2,1)S(1)} %collective-permute-done.3.refs_5_.refs_3_), channel_id=1, source_target_pairs={{0,1},{1,2},{2,3},{3,4},{4,5},{5,6},{6,7},{7,8},{8,9},{9,10},{10,1... | collective-permute-start | bytes 1179656 | tf_op jit(solution)/shard_map/ppermute | solution.py:202
  38.5 1.2 collective-permute-done.2.refs_4_.refs_2_
  39.6 1.9 %collective-permute-start.4 = (bf16[1536,128]{1,0:T(8,128)(2,1)S(1)}, bf16[1536,128]{1,0:T(8,128)(2,1)S(1)}, u32[]{:S(2)}, u32[]{:S(2)}) collective-permute-start(bf16[1536,128]{1,0:T(8,128)(2,1)S(1)} %collective-permute-done.2.refs_4_.refs_2_), channel_id=1, source_target_pairs={{0,1},{1,2},{2,3},{3,4},{4,5},{5,6},{6,7},{7,8},{8,9},{9,10},{10,1... | collective-permute-start | bytes 1179656 | tf_op jit(solution)/shard_map/ppermute | solution.py:202
  41.5 3.0 %collective-permute-done.5.refs_10_ = bf16[1536,128]{1,0:T(8,128)(2,1)S(1)} collective-permute-done((bf16[1536,128]{1,0:T(8,128)(2,1)S(1)}, bf16[1536,128]{1,0:T(8,128)(2,1)S(1)}, u32[]{:S(2)}, u32[]{:S(2)}) %collective-permute-start.5) | collective-permute-done | bytes 393248 | tf_op jit(solution)/shard_map/ppermute | solution.py:205
  45.3 6.6 %collective-permute-done.6.refs_11_ = bf16[1536,128]{1,0:T(8,128)(2,1)S(1)} collective-permute-done((bf16[1536,128]{1,0:T(8,128)(2,1)S(1)}, bf16[1536,128]{1,0:T(8,128)(2,1)S(1)}, u32[]{:S(2)}, u32[]{:S(2)}) %collective-permute-start.6) | collective-permute-done | bytes 393248 | tf_op jit(solution)/shard_map/ppermute | solution.py:205
  52.7 1.9 %collective-permute-start.9 = (bf16[1536,128]{1,0:T(8,128)(2,1)S(1)}, bf16[1536,128]{1,0:T(8,128)(2,1)S(1)}, u32[]{:S(2)}, u32[]{:S(2)}) collective-permute-start(bf16[1536,128]{1,0:T(8,128)(2,1)S(1)} %collective-permute-done.7.refs_7_.refs_5_), channel_id=1, source_target_pairs={{0,1},{1,2},{2,3},{3,4},{4,5},{5,6},{6,7},{7,8},{8,9},{9,10},{10,1... | collective-permute-start | bytes 1179656 | tf_op jit(solution)/shard_map/ppermute | solution.py:202
  54.6 1.9 %collective-permute-start.8 = (bf16[1536,128]{1,0:T(8,128)(2,1)S(1)}, bf16[1536,128]{1,0:T(8,128)(2,1)}, u32[]{:S(2)}, u32[]{:S(2)}) collective-permute-start(bf16[1536,128]{1,0:T(8,128)(2,1)S(1)} %collective-permute-done.4.refs_6_.refs_4_), channel_id=1, source_target_pairs={{0,1},{1,2},{2,3},{3,4},{4,5},{5,6},{6,7},{7,8},{8,9},{9,10},{10,1... | collective-permute-start | bytes 1179656 | tf_op jit(solution)/shard_map/ppermute | solution.py:202
  56.6 7.0 %collective-permute-done.9.refs_9_.refs_7_ = bf16[1536,128]{1,0:T(8,128)(2,1)S(1)} collective-permute-done((bf16[1536,128]{1,0:T(8,128)(2,1)S(1)}, bf16[1536,128]{1,0:T(8,128)(2,1)S(1)}, u32[]{:S(2)}, u32[]{:S(2)}) %collective-permute-start.9) | collective-permute-done | bytes 393248 | tf_op jit(solution)/shard_map/ppermute | solution.py:202
  63.6 1.9 %collective-permute-start.11 = (bf16[1536,128]{1,0:T(8,128)(2,1)S(1)}, bf16[1536,128]{1,0:T(8,128)(2,1)}, u32[]{:S(2)}, u32[]{:S(2)}) collective-permute-start(bf16[1536,128]{1,0:T(8,128)(2,1)S(1)} %collective-permute-done.9.refs_9_.refs_7_), channel_id=1, source_target_pairs={{0,32},{16,48},{32,16},{48,0},{1,33},{17,49},{33,17},{49,1},{2,34}... | collective-permute-start | bytes 1179656 | tf_op jit(solution)/shard_map/ppermute | solution.py:210
  65.5 2.4 %collective-permute-done.8.refs_8_.refs_6_ = bf16[1536,128]{1,0:T(8,128)(2,1)} collective-permute-done((bf16[1536,128]{1,0:T(8,128)(2,1)S(1)}, bf16[1536,128]{1,0:T(8,128)(2,1)}, u32[]{:S(2)}, u32[]{:S(2)}) %collective-permute-start.8) | collective-permute-done | bytes 393248 | tf_op jit(solution)/shard_map/ppermute | solution.py:202
  67.9 1.9 %collective-permute-start.10 = (bf16[1536,128]{1,0:T(8,128)(2,1)}, bf16[1536,128]{1,0:T(8,128)(2,1)}, u32[]{:S(2)}, u32[]{:S(2)}) collective-permute-start(bf16[1536,128]{1,0:T(8,128)(2,1)} %collective-permute-done.8.refs_8_.refs_6_), channel_id=1, source_target_pairs={{0,32},{16,48},{32,16},{48,0},{1,33},{17,49},{33,17},{49,1},{2,34}... | collective-permute-start | bytes 1179656 | tf_op jit(solution)/shard_map/ppermute | solution.py:210
  70.5 1.0 copy-done.1
  72.5 2.6 %shard_map.69.refs_10_ = bf16[8,272,128]{2,1,0:T(8,128)(2,1)S(1)} custom-call(s32[3]{0:T(128)S(1)} %pad_add_fusion.place, f32[1]{0:T(128)} %dynamic_slice.8.scale, bf16[1536,128]{1,0:T(8,128)(2,1)S(1)} %all_gather.6.refs_0_, bf16[1536,128]{1,0:T(8,128)(2,1)S(1)} %all_gather.7.refs_1_, bf16[1536,128]{1,0:T(8,128)(2,1)S(1)} %collective-permute-done.refs_2_.refs_0_, ...), custom_call_target="tpu_custom_call" | custom-call | flops 402653184 | bytes 2752512 | tf_op jit(solution)/shard_map/pallas_call | solution.py:221
  75.1 2.2 %collective-permute-done.10.refs_8_ = bf16[1536,128]{1,0:T(8,128)(2,1)} collective-permute-done((bf16[1536,128]{1,0:T(8,128)(2,1)}, bf16[1536,128]{1,0:T(8,128)(2,1)}, u32[]{:S(2)}, u32[]{:S(2)}) %collective-permute-start.10) | collective-permute-done | bytes 393248 | tf_op jit(solution)/shard_map/ppermute | solution.py:210
  77.3 2.6 %shard_map.70 = bf16[8,272,128]{2,1,0:T(8,128)(2,1)S(1)} custom-call(s32[3]{0:T(128)S(1)} %pad_add_fusion.place, f32[1]{0:T(128)} %dynamic_slice.8.scale, bf16[1536,128]{1,0:T(8,128)(2,1)S(1)} %collective-permute-done.refs_2_.refs_0_, bf16[1536,128]{1,0:T(8,128)(2,1)S(1)} %collective-permute-done.1.refs_3_.refs_1_, ...), custom_call_target="tpu_custom_call", output_to_operand_aliasing={{}: (12, {})} | custom-call | flops 402653184 | bytes 2752512 | tf_op jit(solution)/shard_map/pallas_call | solution.py:229
  79.9 16.6 %all_to_all.5 = bf16[8,272,128]{2,1,0:T(8,128)(2,1)S(1)} all-to-all(bf16[8,272,128]{2,1,0:T(8,128)(2,1)S(1)} %shard_map.70), channel_id=1, replica_groups=mesh['yh'=2,'x'=4,'c'=2,'yl'=2,'z'=16] {'yh','x'}, dimensions={0} | all-to-all | bytes 1114112 | tf_op jit(solution)/shard_map/all_to_all | solution.py:238
  96.8 8.2 %collective-permute-start.12 = (f32[264,128]{1,0:T(8,128)S(1)}, f32[264,128]{1,0:T(8,128)S(1)}, u32[]{:S(2)}, u32[]{:S(2)}) collective-permute-start(f32[264,128]{1,0:T(8,128)S(1)} %slice.4), channel_id=1, source_target_pairs={{0,244},{1,21},{2,22},{3,55},{4,56},{5,89},{6,90},{7,123},{8,124},... | collective-permute-start | bytes 405512 | tf_op jit(solution)/shard_map/ppermute | solution.py:243
  104.9 1.9 %collective-permute-start.13 = (f32[264,128]{1,0:T(8,128)S(1)}, f32[264,128]{1,0:T(8,128)S(1)}, u32[]{:S(2)}, u32[]{:S(2)}) collective-permute-start(f32[264,128]{1,0:T(8,128)S(1)} %slice.4), channel_id=1, source_target_pairs={{0,335},{1,320},{2,353},{3,354},{4,387},{5,388},{6,421},{7,422},{8... | collective-permute-start | bytes 405512 | tf_op jit(solution)/shard_map/ppermute | solution.py:244
  107.6 4.7 %collective-permute-done.12.a = f32[264,128]{1,0:T(8,128)S(1)} collective-permute-done((f32[264,128]{1,0:T(8,128)S(1)}, f32[264,128]{1,0:T(8,128)S(1)}, u32[]{:S(2)}, u32[]{:S(2)}) %collective-permute-start.12) | collective-permute-done | bytes 135200 | tf_op jit(solution)/shard_map/ppermute | solution.py:243
  112.3 6.6 %collective-permute-done.13.b = f32[264,128]{1,0:T(8,128)S(1)} collective-permute-done((f32[264,128]{1,0:T(8,128)S(1)}, f32[264,128]{1,0:T(8,128)S(1)}, u32[]{:S(2)}, u32[]{:S(2)}) %collective-permute-start.13) | collective-permute-done | bytes 135200 | tf_op jit(solution)/shard_map/ppermute | solution.py:244
  118.9 1.4 %shard_map.71 = (f32[128,256]{1,0:T(8,128)}, f32[128,256]{1,0:T(8,128)}) custom-call(s32[4]{0:T(128)S(1)} %dynamic-slice_bitcast_fusion.todo, f32[264,128]{1,0:T(8,128)S(1)} %collective-permute-done.12.a, f32[264,128]{1,0:T(8,128)S(1)} %collective-permute-done.13.b), custom_call_target="tpu_custom_call" | custom-call | tf_op jit(solution)/shard_map/pallas_call | solution.py:249
  (22 shorter events, 4.0 us)
Async XLA Ops:
  2.4 6.3 %copy-start.4 = (bf16[768,128]{1,0:T(8,128)(2,1)S(1)}, bf16[768,128]{1,0:T(8,128)(2,1)}, u32[]{:S(2)}) copy-start(bf16[768,128]{1,0:T(8,128)(2,1)} %get-tuple-element.10) | copy-start | bytes 589828
  2.4 67.4 %copy-start.6 = (f32[8]{0:T(128)S(1)}, f32[8]{0:T(128)}, u32[]{:S(2)}) copy-start(f32[8]{0:T(128)} %constant.50.clone) | copy-start | bytes 100
  4.9 17.1 %collective-permute-start.1 = (bf16[1536,128]{1,0:T(8,128)(2,1)S(1)}, bf16[1536,128]{1,0:T(8,128)(2,1)S(1)}, u32[]{:S(2)}, u32[]{:S(2)}) collective-permute-start(bf16[1536,128]{1,0:T(8,128)(2,1)S(1)} %all_gather.7.refs_1_), channel_id=1, source_target_pairs={{0,1},{1,2},{2,3},{3,4},{4,5},{5,6},{6,7},{7,8},{8,9},{9,10},{10,1... | collective-permute-start | bytes 1179656 | tf_op jit(solution)/shard_map/ppermute | solution.py:202
  17.9 10.9 %collective-permute-start = (bf16[1536,128]{1,0:T(8,128)(2,1)S(1)}, bf16[1536,128]{1,0:T(8,128)(2,1)S(1)}, u32[]{:S(2)}, u32[]{:S(2)}) collective-permute-start(bf16[1536,128]{1,0:T(8,128)(2,1)S(1)} %all_gather.6.refs_0_), channel_id=1, source_target_pairs={{0,1},{1,2},{2,3},{3,4},{4,5},{5,6},{6,7},{7,8},{8,9},{9,10},{10,1... | collective-permute-start | bytes 1179656 | tf_op jit(solution)/shard_map/ppermute | solution.py:202
  22.0 14.5 %collective-permute-start.3 = (bf16[1536,128]{1,0:T(8,128)(2,1)S(1)}, bf16[1536,128]{1,0:T(8,128)(2,1)S(1)}, u32[]{:S(2)}, u32[]{:S(2)}) collective-permute-start(bf16[1536,128]{1,0:T(8,128)(2,1)S(1)} %collective-permute-done.1.refs_3_.refs_1_), channel_id=1, source_target_pairs={{0,1},{1,2},{2,3},{3,4},{4,5},{5,6},{6,7},{7,8},{8,9},{9,10},{10,1... | collective-permute-start | bytes 1179656 | tf_op jit(solution)/shard_map/ppermute | solution.py:202
  28.7 10.9 %collective-permute-start.2 = (bf16[1536,128]{1,0:T(8,128)(2,1)S(1)}, bf16[1536,128]{1,0:T(8,128)(2,1)S(1)}, u32[]{:S(2)}, u32[]{:S(2)}) collective-permute-start(bf16[1536,128]{1,0:T(8,128)(2,1)S(1)} %collective-permute-done.refs_2_.refs_0_), channel_id=1, source_target_pairs={{0,1},{1,2},{2,3},{3,4},{4,5},{5,6},{6,7},{7,8},{8,9},{9,10},{10,1... | collective-permute-start | bytes 1179656 | tf_op jit(solution)/shard_map/ppermute | solution.py:202
  30.7 13.9 %collective-permute-start.5 = (bf16[1536,128]{1,0:T(8,128)(2,1)S(1)}, bf16[1536,128]{1,0:T(8,128)(2,1)S(1)}, u32[]{:S(2)}, u32[]{:S(2)}) collective-permute-start(bf16[1536,128]{1,0:T(8,128)(2,1)S(1)} %all_gather.6.refs_0_), channel_id=1, source_target_pairs={{0,16},{16,0},{1,17},{17,1},{2,18},{18,2},{3,19},{19,3},{4,20},{20... | collective-permute-start | bytes 1179656 | tf_op jit(solution)/shard_map/ppermute | solution.py:205
  34.2 17.8 %collective-permute-start.6 = (bf16[1536,128]{1,0:T(8,128)(2,1)S(1)}, bf16[1536,128]{1,0:T(8,128)(2,1)S(1)}, u32[]{:S(2)}, u32[]{:S(2)}) collective-permute-start(bf16[1536,128]{1,0:T(8,128)(2,1)S(1)} %all_gather.7.refs_1_), channel_id=1, source_target_pairs={{0,16},{16,0},{1,17},{17,1},{2,18},{18,2},{3,19},{19,3},{4,20},{20... | collective-permute-start | bytes 1179656 | tf_op jit(solution)/shard_map/ppermute | solution.py:205
  36.5 16.2 %collective-permute-start.7 = (bf16[1536,128]{1,0:T(8,128)(2,1)S(1)}, bf16[1536,128]{1,0:T(8,128)(2,1)S(1)}, u32[]{:S(2)}, u32[]{:S(2)}) collective-permute-start(bf16[1536,128]{1,0:T(8,128)(2,1)S(1)} %collective-permute-done.3.refs_5_.refs_3_), channel_id=1, source_target_pairs={{0,1},{1,2},{2,3},{3,4},{4,5},{5,6},{6,7},{7,8},{8,9},{9,10},{10,1... | collective-permute-start | bytes 1179656 | tf_op jit(solution)/shard_map/ppermute | solution.py:202
  39.6 15.0 %collective-permute-start.4 = (bf16[1536,128]{1,0:T(8,128)(2,1)S(1)}, bf16[1536,128]{1,0:T(8,128)(2,1)S(1)}, u32[]{:S(2)}, u32[]{:S(2)}) collective-permute-start(bf16[1536,128]{1,0:T(8,128)(2,1)S(1)} %collective-permute-done.2.refs_4_.refs_2_), channel_id=1, source_target_pairs={{0,1},{1,2},{2,3},{3,4},{4,5},{5,6},{6,7},{7,8},{8,9},{9,10},{10,1... | collective-permute-start | bytes 1179656 | tf_op jit(solution)/shard_map/ppermute | solution.py:202
  44.5 0.7 copy-start
  51.9 0.8 copy-start.2
  52.7 10.9 %collective-permute-start.9 = (bf16[1536,128]{1,0:T(8,128)(2,1)S(1)}, bf16[1536,128]{1,0:T(8,128)(2,1)S(1)}, u32[]{:S(2)}, u32[]{:S(2)}) collective-permute-start(bf16[1536,128]{1,0:T(8,128)(2,1)S(1)} %collective-permute-done.7.refs_7_.refs_5_), channel_id=1, source_target_pairs={{0,1},{1,2},{2,3},{3,4},{4,5},{5,6},{6,7},{7,8},{8,9},{9,10},{10,1... | collective-permute-start | bytes 1179656 | tf_op jit(solution)/shard_map/ppermute | solution.py:202
  54.6 13.3 %collective-permute-start.8 = (bf16[1536,128]{1,0:T(8,128)(2,1)S(1)}, bf16[1536,128]{1,0:T(8,128)(2,1)}, u32[]{:S(2)}, u32[]{:S(2)}) collective-permute-start(bf16[1536,128]{1,0:T(8,128)(2,1)S(1)} %collective-permute-done.4.refs_6_.refs_4_), channel_id=1, source_target_pairs={{0,1},{1,2},{2,3},{3,4},{4,5},{5,6},{6,7},{7,8},{8,9},{9,10},{10,1... | collective-permute-start | bytes 1179656 | tf_op jit(solution)/shard_map/ppermute | solution.py:202
  63.6 11.5 %collective-permute-start.11 = (bf16[1536,128]{1,0:T(8,128)(2,1)S(1)}, bf16[1536,128]{1,0:T(8,128)(2,1)}, u32[]{:S(2)}, u32[]{:S(2)}) collective-permute-start(bf16[1536,128]{1,0:T(8,128)(2,1)S(1)} %collective-permute-done.9.refs_9_.refs_7_), channel_id=1, source_target_pairs={{0,32},{16,48},{32,16},{48,0},{1,33},{17,49},{33,17},{49,1},{2,34}... | collective-permute-start | bytes 1179656 | tf_op jit(solution)/shard_map/ppermute | solution.py:210
  67.9 9.4 %collective-permute-start.10 = (bf16[1536,128]{1,0:T(8,128)(2,1)}, bf16[1536,128]{1,0:T(8,128)(2,1)}, u32[]{:S(2)}, u32[]{:S(2)}) collective-permute-start(bf16[1536,128]{1,0:T(8,128)(2,1)} %collective-permute-done.8.refs_8_.refs_6_), channel_id=1, source_target_pairs={{0,32},{16,48},{32,16},{48,0},{1,33},{17,49},{33,17},{49,1},{2,34}... | collective-permute-start | bytes 1179656 | tf_op jit(solution)/shard_map/ppermute | solution.py:210
  70.5 1.0 copy-start.1
  71.5 1.0 copy-start.3
  79.9 16.6 %copy-start.5 = (f32[8]{0:T(128)S(1)}, f32[8]{0:T(128)}, u32[]{:S(2)}) copy-start(f32[8]{0:T(128)} %constant.54) | copy-start | bytes 100
  96.8 15.5 %collective-permute-start.12 = (f32[264,128]{1,0:T(8,128)S(1)}, f32[264,128]{1,0:T(8,128)S(1)}, u32[]{:S(2)}, u32[]{:S(2)}) collective-permute-start(f32[264,128]{1,0:T(8,128)S(1)} %slice.4), channel_id=1, source_target_pairs={{0,244},{1,21},{2,22},{3,55},{4,56},{5,89},{6,90},{7,123},{8,124},... | collective-permute-start | bytes 405512 | tf_op jit(solution)/shard_map/ppermute | solution.py:243
  104.9 14.0 %collective-permute-start.13 = (f32[264,128]{1,0:T(8,128)S(1)}, f32[264,128]{1,0:T(8,128)S(1)}, u32[]{:S(2)}, u32[]{:S(2)}) collective-permute-start(f32[264,128]{1,0:T(8,128)S(1)} %slice.4), channel_id=1, source_target_pairs={{0,335},{1,320},{2,353},{3,354},{4,387},{5,388},{6,421},{7,422},{8... | collective-permute-start | bytes 405512 | tf_op jit(solution)/shard_map/ppermute | solution.py:244

commit v4 on v3

--- a/solution.py
+++ b/solution.py
@@ -65,7 +65,7 @@
     return perms, table
 
 
-def features_kernel(field, backward, activity, signal, f, b, sems):
+def features_kernel(field, backward, activity, signal, both, f, b, sems):
     rows = field.shape[0] // PIECES
     copies = []
     for piece in range(PIECES):
@@ -83,10 +83,10 @@
         for copy in copies[piece]:
             copy.wait()
         wide = jnp.tanh(f[part, :].astype(jnp.float32))
-        activity[part, :] = wide.astype(jnp.bfloat16)
-        signal[part, :] = (
-            (1.0 - wide * wide) * b[part, :].astype(jnp.float32)
-        ).astype(jnp.bfloat16)
+        gated = (1.0 - wide * wide) * b[part, :].astype(jnp.float32)
+        for i, (out, value) in enumerate(((activity, wide), (signal, gated))):
+            out[part, :] = value.astype(jnp.bfloat16)
+            both[i, part, :] = value.astype(jnp.bfloat16)
 
 
 def products_kernel(late, place, scale, *refs):
@@ -129,12 +129,18 @@
     for slot in range(8):
         out[slot, 2 * n : 2 * n + EXTRA] = jnp.zeros((EXTRA, n), jnp.bfloat16)
     for kernel in range(2):
-        walk, near = refs[kernel : 10 + kernel : 2], refs[10 + kernel]
+        walk, gathered = refs[kernel : 10 + kernel : 2], refs[10]
+        rows = gathered.shape[1] // 4
+        near = [
+            gathered[kernel, pl.ds(pl.multiple_of((2 * c + 1 - y) * rows, rows), rows)]
+            for c in range(2)
+        ]
+        near = jnp.concatenate(near, axis=0)
         steps = jnp.concatenate([w[...] for w in walk[1:]], axis=1)
 
         @pl.when(core == 0)
         def _():
-            store(7, kernel, four(4, kernel, near[...], steps))
+            store(7, kernel, four(4, kernel, near, steps))
 
         @pl.when(core == 1)
         def _():
@@ -142,12 +148,12 @@
 
         @pl.when(partner)
         def _():
-            store(3, kernel, product(near[...], walk[0][...]))
+            store(3, kernel, product(near, walk[0][...]))
 
         @pl.when(packed)
         def _():
             own = product(walk[0][...], walk[0][...])
-            other = product(near[...], near[...])
+            other = product(near, near)
             high = jnp.where(y == 0, own, other)
             low = jnp.where(y == 0, other, own)
             store(3, kernel, jnp.where(row <= col, high, low))
@@ -180,11 +186,11 @@
     draws, n = field.shape
     total_draws = draws * 16
     values = jax.ShapeDtypeStruct((draws, n), jnp.bfloat16)
-    own = pl.pallas_call(
+    *own, both = pl.pallas_call(
         features_kernel,
-        out_shape=(values, values),
+        out_shape=(values, values, jax.ShapeDtypeStruct((2, draws, n), jnp.bfloat16)),
         in_specs=[pl.BlockSpec(memory_space=pltpu.HBM)] * 2,
-        out_specs=(VMEM, VMEM),
+        out_specs=(VMEM,) * 3,
         scratch_shapes=[
             pltpu.VMEM((draws, n), jnp.bfloat16),
             pltpu.VMEM((draws, n), jnp.bfloat16),
@@ -196,15 +202,11 @@
     step = [
         (c * 16 + z, c * 16 + (z + 1 - 2 * c) % 16) for c in range(2) for z in range(16)
     ]
-    start = chains = [lax.all_gather(part, "c", axis=0, tiled=True) for part in own]
+    chains = [lax.all_gather(part, "c", axis=0, tiled=True) for part in own]
+    near = lax.all_gather(both, ("c", "yl"), axis=1, tiled=True)
     walk = list(chains)
-    for j in range(4):
+    for _ in range(4):
         chains = [lax.ppermute(chain, ("c", "z"), step) for chain in chains]
-        if j == 0:
-            start, chains[1] = lax.optimization_barrier((start, chains[1]))
-            near = [lax.ppermute(part, "yl", [(0, 1), (1, 0)]) for part in start]
-        if j == 2:
-            near, chains[1] = lax.optimization_barrier((near, chains[1]))
         walk += chains
     cross = [(0, 2), (1, 3), (2, 1), (3, 0)]
     far = [lax.ppermute(chain, ("c", "yl"), cross) for chain in chains]
@@ -221,11 +223,11 @@
     partial = pl.pallas_call(
         functools.partial(products_kernel, False),
         out_shape=shape,
-        in_specs=[SMEM, SMEM] + [VMEM] * 12,
+        in_specs=[SMEM, SMEM] + [VMEM] * 11,
         out_specs=VMEM,
         compiler_params=PARAMS,
         cost_estimate=cost,
-    )(place, scale, *walk, *near)
+    )(place, scale, *walk, near)
     partial = pl.pallas_call(
         functools.partial(products_kernel, True),
         out_shape=shape,

time: 121 us -> 126 us (1.041)
  between operations: 0.89 us -> 14.2 us
  starting transfers between devices: 36.9 us -> 30.7 us
  local copies, waits for them, and re-layouts: 4.78 us -> 2.79 us
    ppermute x8, waiting for transfers between devices: 17.6 us -> 28.2 us  [on_device(): chains = [lax.ppermute(chain, ('c', 'z'), step) for chain in chains]]
    ppermute x2 -> x0, waiting for transfers between devices: 9.66 us -> none  [on_device(): near = [lax.ppermute(part, 'yl', [(0, 1), (1, 0)]) for part in start]]
    ppermute x2 -> x0, starting transfers between devices: 5.84 us -> none  [on_device(): near = [lax.ppermute(part, 'yl', [(0, 1), (1, 0)]) for part in start]]
    unnamed x14 -> x8, local copies, waits for them, and re-layouts: 3.51 us -> 1.43 us
    ppermute x1, waiting for transfers between devices: 6.61 us -> 5.16 us  [on_device(): b = lax.ppermute(block, AXES, perms[1])]
  transfers between devices with their start and end apart: 14 -> 13, of which waited for: 10 -> 11; matrix products, arithmetic and copies ran while one was open for 1% -> 1% of each run, Pallas kernels for 2% -> 2%
where the time goes in v4:
time: 126 us
  waiting for transfers between devices  40.9 us (32%)
  starting transfers between devices  30.7 us (24%)
  blocking collectives  28 us (22%)
  between operations  14.2 us (11%)
  Pallas kernels  8.7 us (7%)
  local copies, waits for them, and re-layouts  2.79 us (2%)
    ppermute x8, waiting for transfers between devices, on_device(): chains = [lax.ppermute(chain, ('c', 'z'), step) for chain in chains]  28.2 us
    ppermute x8, starting transfers between devices, on_device(): chains = [lax.ppermute(chain, ('c', 'z'), step) for chain in chains]  17.2 us
    all_to_all x1, blocking collectives, on_device(): partial = lax.all_to_all(partial, ('yh', 'x'), 0, 0, tiled=True)  16.4 us
    all_gather x2, blocking collectives, on_device(): chains = [lax.all_gather(part, 'c', axis=0, tiled=True) for part in own]  11.6 us
    ppermute x1, starting transfers between devices, on_device(): a = lax.ppermute(block, AXES, perms[0])  7.71 us
    ppermute x1, waiting for transfers between devices, on_device(): b = lax.ppermute(block, AXES, perms[1])  5.16 us
    ppermute x1, waiting for transfers between devices, on_device(): a = lax.ppermute(block, AXES, perms[0])  4.83 us
    ppermute x2, starting transfers between devices, on_device(): far = [lax.ppermute(chain, ('c', 'yl'), cross) for chain in chains]  3.82 us
  transfers between devices with their start and end apart: 13, of which 11 were waited for; matrix products, arithmetic and copies ran while one was open for 1% of the time, Pallas kernels for 2%

profile of v4, /device:TPU:6, one launch (start us, length us, event | category | flops | bytes accessed | tf_op | source)
XLA Modules:
  0.0 125.5 jit_solution(12583187490776039339)
XLA Ops:
  7.2 1.9 %shard_map.68 = (bf16[768,128]{1,0:T(8,128)(2,1)}, bf16[768,128]{1,0:T(8,128)(2,1)}, bf16[2,768,128]{2,1,0:T(8,128)(2,1)}) custom-call(bf16[768,128]{1,0:T(8,128)(2,1)} %field.1, bf16[768,128]{1,0:T(8,128)(2,1)} %backward.1), custom_call_target="tpu_custom_call" | custom-call | tf_op jit(solution)/shard_map/pallas_call | solution.py:189
  9.2 2.4 %all_gather.9.refs_0_ = bf16[1536,128]{1,0:T(8,128)(2,1)S(1)} all-gather(bf16[768,128]{1,0:T(8,128)(2,1)} %get-tuple-element.5), channel_id=1, replica_groups=mesh['yh'=2,'x'=4,'c'=2,'yl'=2,'z'=16] {'c'}, dimensions={0}, use_global_device_ids=true | all-gather | bytes 589824 | tf_op jit(solution)/shard_map/all_gather | solution.py:205
  11.6 3.8 %collective-permute-start = (bf16[1536,128]{1,0:T(8,128)(2,1)S(1)}, bf16[1536,128]{1,0:T(8,128)(2,1)S(1)}, u32[]{:S(2)}, u32[]{:S(2)}) collective-permute-start(bf16[1536,128]{1,0:T(8,128)(2,1)S(1)} %all_gather.9.refs_0_), channel_id=1, source_target_pairs={{0,1},{1,2},{2,3},{3,4},{4,5},{5,6},{6,7},{7,8},{8,9},{9,10},{10,1... | collective-permute-start | bytes 1179656 | tf_op jit(solution)/shard_map/ppermute | solution.py:209
  15.5 9.2 %all_gather.10.refs_1_ = bf16[1536,128]{1,0:T(8,128)(2,1)S(1)} all-gather(bf16[768,128]{1,0:T(8,128)(2,1)S(1)} %copy-done.1), channel_id=1, replica_groups=mesh['yh'=2,'x'=4,'c'=2,'yl'=2,'z'=16] {'c'}, dimensions={0}, use_global_device_ids=true | all-gather | bytes 589824 | tf_op jit(solution)/shard_map/all_gather | solution.py:205
  24.6 1.9 %collective-permute-start.1 = (bf16[1536,128]{1,0:T(8,128)(2,1)S(1)}, bf16[1536,128]{1,0:T(8,128)(2,1)S(1)}, u32[]{:S(2)}, u32[]{:S(2)}) collective-permute-start(bf16[1536,128]{1,0:T(8,128)(2,1)S(1)} %all_gather.10.refs_1_), channel_id=1, source_target_pairs={{0,1},{1,2},{2,3},{3,4},{4,5},{5,6},{6,7},{7,8},{8,9},{9,10},{10,1... | collective-permute-start | bytes 1179656 | tf_op jit(solution)/shard_map/ppermute | solution.py:209
  26.5 2.2 %collective-permute-done.refs_2_.refs_0_ = bf16[1536,128]{1,0:T(8,128)(2,1)S(1)} collective-permute-done((bf16[1536,128]{1,0:T(8,128)(2,1)S(1)}, bf16[1536,128]{1,0:T(8,128)(2,1)S(1)}, u32[]{:S(2)}, u32[]{:S(2)}) %collective-permute-start) | collective-permute-done | bytes 393248 | tf_op jit(solution)/shard_map/ppermute | solution.py:209
  28.8 1.9 %collective-permute-start.2 = (bf16[1536,128]{1,0:T(8,128)(2,1)S(1)}, bf16[1536,128]{1,0:T(8,128)(2,1)S(1)}, u32[]{:S(2)}, u32[]{:S(2)}) collective-permute-start(bf16[1536,128]{1,0:T(8,128)(2,1)S(1)} %collective-permute-done.refs_2_.refs_0_), channel_id=1, source_target_pairs={{0,1},{1,2},{2,3},{3,4},{4,5},{5,6},{6,7},{7,8},{8,9},{9,10},{10,1... | collective-permute-start | bytes 1179656 | tf_op jit(solution)/shard_map/ppermute | solution.py:209
  30.7 4.8 %collective-permute-done.1.refs_3_.refs_1_ = bf16[1536,128]{1,0:T(8,128)(2,1)S(1)} collective-permute-done((bf16[1536,128]{1,0:T(8,128)(2,1)S(1)}, bf16[1536,128]{1,0:T(8,128)(2,1)S(1)}, u32[]{:S(2)}, u32[]{:S(2)}) %collective-permute-start.1) | collective-permute-done | bytes 393248 | tf_op jit(solution)/shard_map/ppermute | solution.py:209
  35.5 1.9 %collective-permute-start.3 = (bf16[1536,128]{1,0:T(8,128)(2,1)S(1)}, bf16[1536,128]{1,0:T(8,128)(2,1)S(1)}, u32[]{:S(2)}, u32[]{:S(2)}) collective-permute-start(bf16[1536,128]{1,0:T(8,128)(2,1)S(1)} %collective-permute-done.1.refs_3_.refs_1_), channel_id=1, source_target_pairs={{0,1},{1,2},{2,3},{3,4},{4,5},{5,6},{6,7},{7,8},{8,9},{9,10},{10,1... | collective-permute-start | bytes 1179656 | tf_op jit(solution)/shard_map/ppermute | solution.py:209
  37.4 2.3 %collective-permute-done.2.refs_4_.refs_2_ = bf16[1536,128]{1,0:T(8,128)(2,1)S(1)} collective-permute-done((bf16[1536,128]{1,0:T(8,128)(2,1)S(1)}, bf16[1536,128]{1,0:T(8,128)(2,1)S(1)}, u32[]{:S(2)}, u32[]{:S(2)}) %collective-permute-start.2) | collective-permute-done | bytes 393248 | tf_op jit(solution)/shard_map/ppermute | solution.py:209
  39.7 1.9 %collective-permute-start.4 = (bf16[1536,128]{1,0:T(8,128)(2,1)S(1)}, bf16[1536,128]{1,0:T(8,128)(2,1)S(1)}, u32[]{:S(2)}, u32[]{:S(2)}) collective-permute-start(bf16[1536,128]{1,0:T(8,128)(2,1)S(1)} %collective-permute-done.2.refs_4_.refs_2_), channel_id=1, source_target_pairs={{0,1},{1,2},{2,3},{3,4},{4,5},{5,6},{6,7},{7,8},{8,9},{9,10},{10,1... | collective-permute-start | bytes 1179656 | tf_op jit(solution)/shard_map/ppermute | solution.py:209
  41.6 4.7 %collective-permute-done.3.refs_5_.refs_3_ = bf16[1536,128]{1,0:T(8,128)(2,1)S(1)} collective-permute-done((bf16[1536,128]{1,0:T(8,128)(2,1)S(1)}, bf16[1536,128]{1,0:T(8,128)(2,1)S(1)}, u32[]{:S(2)}, u32[]{:S(2)}) %collective-permute-start.3) | collective-permute-done | bytes 393248 | tf_op jit(solution)/shard_map/ppermute | solution.py:209
  46.4 1.9 %collective-permute-start.5 = (bf16[1536,128]{1,0:T(8,128)(2,1)S(1)}, bf16[1536,128]{1,0:T(8,128)(2,1)S(1)}, u32[]{:S(2)}, u32[]{:S(2)}) collective-permute-start(bf16[1536,128]{1,0:T(8,128)(2,1)S(1)} %collective-permute-done.3.refs_5_.refs_3_), channel_id=1, source_target_pairs={{0,1},{1,2},{2,3},{3,4},{4,5},{5,6},{6,7},{7,8},{8,9},{9,10},{10,1... | collective-permute-start | bytes 1179656 | tf_op jit(solution)/shard_map/ppermute | solution.py:209
  48.3 2.3 %collective-permute-done.4.refs_6_.refs_4_ = bf16[1536,128]{1,0:T(8,128)(2,1)S(1)} collective-permute-done((bf16[1536,128]{1,0:T(8,128)(2,1)S(1)}, bf16[1536,128]{1,0:T(8,128)(2,1)S(1)}, u32[]{:S(2)}, u32[]{:S(2)}) %collective-permute-start.4) | collective-permute-done | bytes 393248 | tf_op jit(solution)/shard_map/ppermute | solution.py:209
  50.6 1.9 %collective-permute-start.6 = (bf16[1536,128]{1,0:T(8,128)(2,1)S(1)}, bf16[1536,128]{1,0:T(8,128)(2,1)S(1)}, u32[]{:S(2)}, u32[]{:S(2)}) collective-permute-start(bf16[1536,128]{1,0:T(8,128)(2,1)S(1)} %collective-permute-done.4.refs_6_.refs_4_), channel_id=1, source_target_pairs={{0,1},{1,2},{2,3},{3,4},{4,5},{5,6},{6,7},{7,8},{8,9},{9,10},{10,1... | collective-permute-start | bytes 1179656 | tf_op jit(solution)/shard_map/ppermute | solution.py:209
  52.5 4.7 %collective-permute-done.5.refs_7_.refs_5_ = bf16[1536,128]{1,0:T(8,128)(2,1)S(1)} collective-permute-done((bf16[1536,128]{1,0:T(8,128)(2,1)S(1)}, bf16[1536,128]{1,0:T(8,128)(2,1)S(1)}, u32[]{:S(2)}, u32[]{:S(2)}) %collective-permute-start.5) | collective-permute-done | bytes 393248 | tf_op jit(solution)/shard_map/ppermute | solution.py:209
  57.2 1.9 %collective-permute-start.7 = (bf16[1536,128]{1,0:T(8,128)(2,1)S(1)}, bf16[1536,128]{1,0:T(8,128)(2,1)}, u32[]{:S(2)}, u32[]{:S(2)}) collective-permute-start(bf16[1536,128]{1,0:T(8,128)(2,1)S(1)} %collective-permute-done.5.refs_7_.refs_5_), channel_id=1, source_target_pairs={{0,1},{1,2},{2,3},{3,4},{4,5},{5,6},{6,7},{7,8},{8,9},{9,10},{10,1... | collective-permute-start | bytes 1179656 | tf_op jit(solution)/shard_map/ppermute | solution.py:209
  59.1 2.3 %collective-permute-done.6.refs_8_.refs_6_ = bf16[1536,128]{1,0:T(8,128)(2,1)S(1)} collective-permute-done((bf16[1536,128]{1,0:T(8,128)(2,1)S(1)}, bf16[1536,128]{1,0:T(8,128)(2,1)S(1)}, u32[]{:S(2)}, u32[]{:S(2)}) %collective-permute-start.6) | collective-permute-done | bytes 393248 | tf_op jit(solution)/shard_map/ppermute | solution.py:209
  61.4 1.9 %collective-permute-start.8 = (bf16[1536,128]{1,0:T(8,128)(2,1)S(1)}, bf16[1536,128]{1,0:T(8,128)(2,1)}, u32[]{:S(2)}, u32[]{:S(2)}) collective-permute-start(bf16[1536,128]{1,0:T(8,128)(2,1)S(1)} %collective-permute-done.6.refs_8_.refs_6_), channel_id=1, source_target_pairs={{0,32},{16,48},{32,16},{48,0},{1,33},{17,49},{33,17},{49,1},{2,34}... | collective-permute-start | bytes 1179656 | tf_op jit(solution)/shard_map/ppermute | solution.py:212
  63.4 4.8 %collective-permute-done.7.refs_9_.refs_7_ = bf16[1536,128]{1,0:T(8,128)(2,1)} collective-permute-done((bf16[1536,128]{1,0:T(8,128)(2,1)S(1)}, bf16[1536,128]{1,0:T(8,128)(2,1)}, u32[]{:S(2)}, u32[]{:S(2)}) %collective-permute-start.7) | collective-permute-done | bytes 393248 | tf_op jit(solution)/shard_map/ppermute | solution.py:209
  68.2 1.9 %collective-permute-start.9 = (bf16[1536,128]{1,0:T(8,128)(2,1)}, bf16[1536,128]{1,0:T(8,128)(2,1)}, u32[]{:S(2)}, u32[]{:S(2)}) collective-permute-start(bf16[1536,128]{1,0:T(8,128)(2,1)} %collective-permute-done.7.refs_9_.refs_7_), channel_id=1, source_target_pairs={{0,32},{16,48},{32,16},{48,0},{1,33},{17,49},{33,17},{49,1},{2,34}... | collective-permute-start | bytes 1179656 | tf_op jit(solution)/shard_map/ppermute | solution.py:212
  70.9 1.4 %copy-done = bf16[2,3072,128]{2,1,0:T(8,128)(2,1)S(1)} copy-done((bf16[2,3072,128]{2,1,0:T(8,128)(2,1)S(1)}, bf16[2,3072,128]{2,1,0:T(8,128)(2,1)}, u32[]{:S(2)}) %copy-start) | copy-done | bytes 1572888
  72.3 2.7 %shard_map.69.refs_10_ = bf16[8,272,128]{2,1,0:T(8,128)(2,1)S(1)} custom-call(s32[3]{0:T(128)S(1)} %pad_add_fusion.place, f32[1]{0:T(128)} %dynamic_slice.8.scale, bf16[1536,128]{1,0:T(8,128)(2,1)S(1)} %all_gather.9.refs_0_, bf16[1536,128]{1,0:T(8,128)(2,1)S(1)} %all_gather.10.refs_1_, bf16[1536,128]{1,0:T(8,128)(2,1)S(1)} %collective-permute-done.refs_2_.refs_0_, ...), custom_call_target="tpu_custom_call" | custom-call | flops 402653184 | bytes 2752512 | tf_op jit(solution)/shard_map/pallas_call | solution.py:223
  75.0 2.6 %collective-permute-done.9.refs_9_ = bf16[1536,128]{1,0:T(8,128)(2,1)} collective-permute-done((bf16[1536,128]{1,0:T(8,128)(2,1)}, bf16[1536,128]{1,0:T(8,128)(2,1)}, u32[]{:S(2)}, u32[]{:S(2)}) %collective-permute-start.9) | collective-permute-done | bytes 393248 | tf_op jit(solution)/shard_map/ppermute | solution.py:212
  77.6 2.7 %shard_map.70 = bf16[8,272,128]{2,1,0:T(8,128)(2,1)S(1)} custom-call(s32[3]{0:T(128)S(1)} %pad_add_fusion.place, f32[1]{0:T(128)} %dynamic_slice.8.scale, bf16[1536,128]{1,0:T(8,128)(2,1)S(1)} %collective-permute-done.refs_2_.refs_0_, bf16[1536,128]{1,0:T(8,128)(2,1)S(1)} %collective-permute-done.1.refs_3_.refs_1_, ...), custom_call_target="tpu_custom_call", output_to_operand_aliasing={{}: (12, {})} | custom-call | flops 402653184 | bytes 2752512 | tf_op jit(solution)/shard_map/pallas_call | solution.py:231
  80.3 16.4 %all_to_all.5 = bf16[8,272,128]{2,1,0:T(8,128)(2,1)S(1)} all-to-all(bf16[8,272,128]{2,1,0:T(8,128)(2,1)S(1)} %shard_map.70), channel_id=1, replica_groups=mesh['yh'=2,'x'=4,'c'=2,'yl'=2,'z'=16] {'yh','x'}, dimensions={0} | all-to-all | bytes 1114112 | tf_op jit(solution)/shard_map/all_to_all | solution.py:240
  96.9 7.7 %collective-permute-start.10 = (f32[264,128]{1,0:T(8,128)S(1)}, f32[264,128]{1,0:T(8,128)S(1)}, u32[]{:S(2)}, u32[]{:S(2)}) collective-permute-start(f32[264,128]{1,0:T(8,128)S(1)} %slice.4), channel_id=1, source_target_pairs={{0,244},{1,21},{2,22},{3,55},{4,56},{5,89},{6,90},{7,123},{8,124},... | collective-permute-start | bytes 405512 | tf_op jit(solution)/shard_map/ppermute | solution.py:245
  104.7 1.9 %collective-permute-start.11 = (f32[264,128]{1,0:T(8,128)S(1)}, f32[264,128]{1,0:T(8,128)S(1)}, u32[]{:S(2)}, u32[]{:S(2)}) collective-permute-start(f32[264,128]{1,0:T(8,128)S(1)} %slice.4), channel_id=1, source_target_pairs={{0,335},{1,320},{2,353},{3,354},{4,387},{5,388},{6,421},{7,422},{8... | collective-permute-start | bytes 405512 | tf_op jit(solution)/shard_map/ppermute | solution.py:246
  106.6 0.7 dynamic-slice_bitcast_fusion.todo
  107.3 4.8 %collective-permute-done.10.a = f32[264,128]{1,0:T(8,128)S(1)} collective-permute-done((f32[264,128]{1,0:T(8,128)S(1)}, f32[264,128]{1,0:T(8,128)S(1)}, u32[]{:S(2)}, u32[]{:S(2)}) %collective-permute-start.10) | collective-permute-done | bytes 135200 | tf_op jit(solution)/shard_map/ppermute | solution.py:245
  112.1 5.2 %collective-permute-done.11.b = f32[264,128]{1,0:T(8,128)S(1)} collective-permute-done((f32[264,128]{1,0:T(8,128)S(1)}, f32[264,128]{1,0:T(8,128)S(1)}, u32[]{:S(2)}, u32[]{:S(2)}) %collective-permute-start.11) | collective-permute-done | bytes 135200 | tf_op jit(solution)/shard_map/ppermute | solution.py:246
  117.3 1.4 %shard_map.71 = (f32[128,256]{1,0:T(8,128)}, f32[128,256]{1,0:T(8,128)}) custom-call(s32[4]{0:T(128)S(1)} %dynamic-slice_bitcast_fusion.todo, f32[264,128]{1,0:T(8,128)S(1)} %collective-permute-done.10.a, f32[264,128]{1,0:T(8,128)S(1)} %collective-permute-done.11.b), custom_call_target="tpu_custom_call" | custom-call | tf_op jit(solution)/shard_map/pallas_call | solution.py:251
  (15 shorter events, 1.0 us)
Async XLA Ops:
  7.2 63.0 %copy-start.3 = (f32[8]{0:T(128)S(1)}, f32[8]{0:T(128)}, u32[]{:S(2)}) copy-start(f32[8]{0:T(128)} %constant.50.clone) | copy-start | bytes 100
  7.2 63.7 %all-gather.2.cloned.1.call-start = ((), (), s32[]{:S(2)}) async-start(), calls=%async_computation.1 | async-start | bytes 1966080 | tf_op jit(solution)/shard_map/all_gather | solution.py:206
  9.2 6.3 %copy-start.1 = (bf16[768,128]{1,0:T(8,128)(2,1)S(1)}, bf16[768,128]{1,0:T(8,128)(2,1)}, u32[]{:S(2)}) copy-start(bf16[768,128]{1,0:T(8,128)(2,1)} %get-tuple-element.6) | copy-start | bytes 589828
  11.6 17.1 %collective-permute-start = (bf16[1536,128]{1,0:T(8,128)(2,1)S(1)}, bf16[1536,128]{1,0:T(8,128)(2,1)S(1)}, u32[]{:S(2)}, u32[]{:S(2)}) collective-permute-start(bf16[1536,128]{1,0:T(8,128)(2,1)S(1)} %all_gather.9.refs_0_), channel_id=1, source_target_pairs={{0,1},{1,2},{2,3},{3,4},{4,5},{5,6},{6,7},{7,8},{8,9},{9,10},{10,1... | collective-permute-start | bytes 1179656 | tf_op jit(solution)/shard_map/ppermute | solution.py:209
  24.6 10.9 %collective-permute-start.1 = (bf16[1536,128]{1,0:T(8,128)(2,1)S(1)}, bf16[1536,128]{1,0:T(8,128)(2,1)S(1)}, u32[]{:S(2)}, u32[]{:S(2)}) collective-permute-start(bf16[1536,128]{1,0:T(8,128)(2,1)S(1)} %all_gather.10.refs_1_), channel_id=1, source_target_pairs={{0,1},{1,2},{2,3},{3,4},{4,5},{5,6},{6,7},{7,8},{8,9},{9,10},{10,1... | collective-permute-start | bytes 1179656 | tf_op jit(solution)/shard_map/ppermute | solution.py:209
  28.8 10.9 %collective-permute-start.2 = (bf16[1536,128]{1,0:T(8,128)(2,1)S(1)}, bf16[1536,128]{1,0:T(8,128)(2,1)S(1)}, u32[]{:S(2)}, u32[]{:S(2)}) collective-permute-start(bf16[1536,128]{1,0:T(8,128)(2,1)S(1)} %collective-permute-done.refs_2_.refs_0_), channel_id=1, source_target_pairs={{0,1},{1,2},{2,3},{3,4},{4,5},{5,6},{6,7},{7,8},{8,9},{9,10},{10,1... | collective-permute-start | bytes 1179656 | tf_op jit(solution)/shard_map/ppermute | solution.py:209
  35.5 10.9 %collective-permute-start.3 = (bf16[1536,128]{1,0:T(8,128)(2,1)S(1)}, bf16[1536,128]{1,0:T(8,128)(2,1)S(1)}, u32[]{:S(2)}, u32[]{:S(2)}) collective-permute-start(bf16[1536,128]{1,0:T(8,128)(2,1)S(1)} %collective-permute-done.1.refs_3_.refs_1_), channel_id=1, source_target_pairs={{0,1},{1,2},{2,3},{3,4},{4,5},{5,6},{6,7},{7,8},{8,9},{9,10},{10,1... | collective-permute-start | bytes 1179656 | tf_op jit(solution)/shard_map/ppermute | solution.py:209
  39.7 10.9 %collective-permute-start.4 = (bf16[1536,128]{1,0:T(8,128)(2,1)S(1)}, bf16[1536,128]{1,0:T(8,128)(2,1)S(1)}, u32[]{:S(2)}, u32[]{:S(2)}) collective-permute-start(bf16[1536,128]{1,0:T(8,128)(2,1)S(1)} %collective-permute-done.2.refs_4_.refs_2_), channel_id=1, source_target_pairs={{0,1},{1,2},{2,3},{3,4},{4,5},{5,6},{6,7},{7,8},{8,9},{9,10},{10,1... | collective-permute-start | bytes 1179656 | tf_op jit(solution)/shard_map/ppermute | solution.py:209
  46.4 10.9 %collective-permute-start.5 = (bf16[1536,128]{1,0:T(8,128)(2,1)S(1)}, bf16[1536,128]{1,0:T(8,128)(2,1)S(1)}, u32[]{:S(2)}, u32[]{:S(2)}) collective-permute-start(bf16[1536,128]{1,0:T(8,128)(2,1)S(1)} %collective-permute-done.3.refs_5_.refs_3_), channel_id=1, source_target_pairs={{0,1},{1,2},{2,3},{3,4},{4,5},{5,6},{6,7},{7,8},{8,9},{9,10},{10,1... | collective-permute-start | bytes 1179656 | tf_op jit(solution)/shard_map/ppermute | solution.py:209
  50.6 10.9 %collective-permute-start.6 = (bf16[1536,128]{1,0:T(8,128)(2,1)S(1)}, bf16[1536,128]{1,0:T(8,128)(2,1)S(1)}, u32[]{:S(2)}, u32[]{:S(2)}) collective-permute-start(bf16[1536,128]{1,0:T(8,128)(2,1)S(1)} %collective-permute-done.4.refs_6_.refs_4_), channel_id=1, source_target_pairs={{0,1},{1,2},{2,3},{3,4},{4,5},{5,6},{6,7},{7,8},{8,9},{9,10},{10,1... | collective-permute-start | bytes 1179656 | tf_op jit(solution)/shard_map/ppermute | solution.py:209
  57.2 11.0 %collective-permute-start.7 = (bf16[1536,128]{1,0:T(8,128)(2,1)S(1)}, bf16[1536,128]{1,0:T(8,128)(2,1)}, u32[]{:S(2)}, u32[]{:S(2)}) collective-permute-start(bf16[1536,128]{1,0:T(8,128)(2,1)S(1)} %collective-permute-done.5.refs_7_.refs_5_), channel_id=1, source_target_pairs={{0,1},{1,2},{2,3},{3,4},{4,5},{5,6},{6,7},{7,8},{8,9},{9,10},{10,1... | collective-permute-start | bytes 1179656 | tf_op jit(solution)/shard_map/ppermute | solution.py:209
  61.4 13.5 %collective-permute-start.8 = (bf16[1536,128]{1,0:T(8,128)(2,1)S(1)}, bf16[1536,128]{1,0:T(8,128)(2,1)}, u32[]{:S(2)}, u32[]{:S(2)}) collective-permute-start(bf16[1536,128]{1,0:T(8,128)(2,1)S(1)} %collective-permute-done.6.refs_8_.refs_6_), channel_id=1, source_target_pairs={{0,32},{16,48},{32,16},{48,0},{1,33},{17,49},{33,17},{49,1},{2,34}... | collective-permute-start | bytes 1179656 | tf_op jit(solution)/shard_map/ppermute | solution.py:212
  68.2 9.4 %collective-permute-start.9 = (bf16[1536,128]{1,0:T(8,128)(2,1)}, bf16[1536,128]{1,0:T(8,128)(2,1)}, u32[]{:S(2)}, u32[]{:S(2)}) collective-permute-start(bf16[1536,128]{1,0:T(8,128)(2,1)} %collective-permute-done.7.refs_9_.refs_7_), channel_id=1, source_target_pairs={{0,32},{16,48},{32,16},{48,0},{1,33},{17,49},{33,17},{49,1},{2,34}... | collective-permute-start | bytes 1179656 | tf_op jit(solution)/shard_map/ppermute | solution.py:212
  70.9 1.4 %copy-start = (bf16[2,3072,128]{2,1,0:T(8,128)(2,1)S(1)}, bf16[2,3072,128]{2,1,0:T(8,128)(2,1)}, u32[]{:S(2)}) copy-start(bf16[2,3072,128]{2,1,0:T(8,128)(2,1)} %all-gather.2.cloned.1.call-done.refs_10_) | copy-start | bytes 4718596
  80.3 16.4 %copy-start.2 = (f32[8]{0:T(128)S(1)}, f32[8]{0:T(128)}, u32[]{:S(2)}) copy-start(f32[8]{0:T(128)} %constant.54) | copy-start | bytes 100
  96.9 15.2 %collective-permute-start.10 = (f32[264,128]{1,0:T(8,128)S(1)}, f32[264,128]{1,0:T(8,128)S(1)}, u32[]{:S(2)}, u32[]{:S(2)}) collective-permute-start(f32[264,128]{1,0:T(8,128)S(1)} %slice.4), channel_id=1, source_target_pairs={{0,244},{1,21},{2,22},{3,55},{4,56},{5,89},{6,90},{7,123},{8,124},... | collective-permute-start | bytes 405512 | tf_op jit(solution)/shard_map/ppermute | solution.py:245
  104.7 12.6 %collective-permute-start.11 = (f32[264,128]{1,0:T(8,128)S(1)}, f32[264,128]{1,0:T(8,128)S(1)}, u32[]{:S(2)}, u32[]{:S(2)}) collective-permute-start(f32[264,128]{1,0:T(8,128)S(1)} %slice.4), channel_id=1, source_target_pairs={{0,335},{1,320},{2,353},{3,354},{4,387},{5,388},{6,421},{7,422},{8... | collective-permute-start | bytes 405512 | tf_op jit(solution)/shard_map/ppermute | solution.py:246
Sparse Core Ops, SparseCore 0:
  10.1 49.9 all-gather.1

commit v5 on v3

--- a/solution.py
+++ b/solution.py
@@ -65,7 +65,7 @@
     return perms, table
 
 
-def features_kernel(field, backward, activity, signal, f, b, sems):
+def features_kernel(field, backward, both, f, b, sems):
     rows = field.shape[0] // PIECES
     copies = []
     for piece in range(PIECES):
@@ -83,79 +83,88 @@
         for copy in copies[piece]:
             copy.wait()
         wide = jnp.tanh(f[part, :].astype(jnp.float32))
-        activity[part, :] = wide.astype(jnp.bfloat16)
-        signal[part, :] = (
-            (1.0 - wide * wide) * b[part, :].astype(jnp.float32)
-        ).astype(jnp.bfloat16)
-
-
-def products_kernel(late, place, scale, *refs):
-    out = refs[-1]
+        gated = (1.0 - wide * wide) * b[part, :].astype(jnp.float32)
+        both[0, part, :] = wide.astype(jnp.bfloat16)
+        both[1, part, :] = gated.astype(jnp.bfloat16)
+
+
+def product(left, right):
+    return lax.dot_general(
+        left, right, (((0,), (0,)), ((), ())), preferred_element_type=jnp.float32
+    )
+
+
+def store(out, scale, slot, kernel, total):
+    n = out.shape[-1]
+    for j in range(total.shape[1] // n):
+        block = total[:, j * n : (j + 1) * n] * scale[0]
+        out[slot + j, kernel * n : (kernel + 1) * n] = block.astype(jnp.bfloat16)
+
+
+def cases(place):
     core, y, z = place[0], place[1], place[2]
+    return (core == 1) & ((z < 8) != (y == 0)), (core == 0) & (y == 1)
+
+
+def near_kernel(place, scale, *refs):
+    first, second, near, (out, steps) = refs[0:5], refs[5:10], refs[10:12], refs[12:]
+    core, y = place[0], place[1]
+    packed, partner = cases(place)
     n = out.shape[-1]
-    row = lax.broadcasted_iota(jnp.int32, (n, n), 0)
-    col = lax.broadcasted_iota(jnp.int32, (n, n), 1)
-
-    def product(left, right):
-        return lax.dot_general(
-            left, right, (((0,), (0,)), ((), ())), preferred_element_type=jnp.float32
-        )
-
-    def store(slot, kernel, total):
-        out[slot, kernel * n : (kernel + 1) * n] = (total * scale[0]).astype(
-            jnp.bfloat16
-        )
-
-    packed = (core == 1) & ((z < 8) != (y == 0))
-    partner = (core == 0) & (y == 1)
-
-    def four(first, kernel, left, steps):
-        total = product(left, steps)
-        for j in range(3):
-            store(first + j, kernel, total[:, j * n : (j + 1) * n])
-        return total[:, 3 * n :]
-
-    if late:
-        for kernel in range(2):
-            walk, far = refs[kernel : 8 + kernel : 2], refs[8 + kernel]
-            steps = jnp.concatenate([w[...] for w in walk], axis=1)
-            last = four(0, kernel, far[...], steps)
-
-            @pl.when(jnp.logical_not(packed | partner))
-            def _():
-                store(3, kernel, last)
-
-        return
+    rows = near[0].shape[1]
     for slot in range(8):
         out[slot, 2 * n : 2 * n + EXTRA] = jnp.zeros((EXTRA, n), jnp.bfloat16)
     for kernel in range(2):
-        walk, near = refs[kernel : 10 + kernel : 2], refs[10 + kernel]
-        steps = jnp.concatenate([w[...] for w in walk[1:]], axis=1)
+        for i, chain in enumerate((first, second)):
+            for j in range(4):
+                steps[kernel, i * rows : (i + 1) * rows, j * n : (j + 1) * n] = chain[
+                    j + 1
+                ][kernel]
+
+        def own(kernel=kernel):
+            return jnp.concatenate([first[0][kernel], second[0][kernel]], axis=0)
+
+        def other(kernel=kernel):
+            return jnp.concatenate([near[0][kernel], near[1][kernel]], axis=0)
 
         @pl.when(core == 0)
         def _():
-            store(7, kernel, four(4, kernel, near[...], steps))
+            store(out, scale, 4, kernel, product(other(), steps[kernel]))
 
         @pl.when(core == 1)
         def _():
-            store(7, kernel, four(4, kernel, walk[0][...], steps))
+            store(out, scale, 4, kernel, product(own(), steps[kernel]))
 
         @pl.when(partner)
         def _():
-            store(3, kernel, product(near[...], walk[0][...]))
+            store(out, scale, 3, kernel, product(other(), own()))
 
         @pl.when(packed)
         def _():
-            own = product(walk[0][...], walk[0][...])
-            other = product(near[...], near[...])
-            high = jnp.where(y == 0, own, other)
-            low = jnp.where(y == 0, other, own)
-            store(3, kernel, jnp.where(row <= col, high, low))
+            mine, yours = product(own(), own()), product(other(), other())
+            high = jnp.where(y == 0, mine, yours)
+            low = jnp.where(y == 0, yours, mine)
+            row = lax.broadcasted_iota(jnp.int32, (n, n), 0)
+            col = lax.broadcasted_iota(jnp.int32, (n, n), 1)
+            store(out, scale, 3, kernel, jnp.where(row <= col, high, low))
             diagonal = jnp.sum(jnp.where(row == col, low, 0.0), axis=0, keepdims=True)
             line = lax.broadcasted_iota(jnp.int32, (EXTRA, n), 0)
             extra = out[3, 2 * n : 2 * n + EXTRA].astype(jnp.float32)
             extra = jnp.where(line == kernel, diagonal * scale[0], extra)
             out[3, 2 * n : 2 * n + EXTRA] = extra.astype(jnp.bfloat16)
+
+
+def far_kernel(place, scale, steps, first, second, _, out):
+    packed, partner = cases(place)
+    n = out.shape[-1]
+    for kernel in range(2):
+        far = jnp.concatenate([first[kernel], second[kernel]], axis=0)
+        total = product(far, steps[kernel])
+        store(out, scale, 0, kernel, total[:, : 3 * n])
+
+        @pl.when(jnp.logical_not(packed | partner))
+        def _():
+            store(out, scale, 3, kernel, total[:, 3 * n :])
 
 
 def place_kernel(total_draws, todo, a, b, feature, gradient):
@@ -179,12 +188,11 @@
 def on_device(field, backward):
     draws, n = field.shape
     total_draws = draws * 16
-    values = jax.ShapeDtypeStruct((draws, n), jnp.bfloat16)
-    own = pl.pallas_call(
+    both = pl.pallas_call(
         features_kernel,
-        out_shape=(values, values),
+        out_shape=jax.ShapeDtypeStruct((2, draws, n), jnp.bfloat16),
         in_specs=[pl.BlockSpec(memory_space=pltpu.HBM)] * 2,
-        out_specs=(VMEM, VMEM),
+        out_specs=VMEM,
         scratch_shapes=[
             pltpu.VMEM((draws, n), jnp.bfloat16),
             pltpu.VMEM((draws, n), jnp.bfloat16),
@@ -193,19 +201,25 @@
         compiler_params=pltpu.CompilerParams(vmem_limit_bytes=60 * 1024 * 1024),
     )(field, backward)
 
+    swap = [(0, 1), (1, 0)]
     step = [
         (c * 16 + z, c * 16 + (z + 1 - 2 * c) % 16) for c in range(2) for z in range(16)
     ]
-    start = chains = [lax.all_gather(part, "c", axis=0, tiled=True) for part in own]
-    walk = list(chains)
+    chains = [both, lax.ppermute(both, "c", swap)]
+    walk = [[chain] for chain in chains]
+    near = [both]
     for j in range(4):
         chains = [lax.ppermute(chain, ("c", "z"), step) for chain in chains]
         if j == 0:
-            start, chains[1] = lax.optimization_barrier((start, chains[1]))
-            near = [lax.ppermute(part, "yl", [(0, 1), (1, 0)]) for part in start]
+            near[0], chains[1] = lax.optimization_barrier((near[0], chains[1]))
+            near = [lax.ppermute(near[0], "yl", swap)]
         if j == 2:
-            near, chains[1] = lax.optimization_barrier((near, chains[1]))
-        walk += chains
+            near[0], chains[1] = lax.optimization_barrier((near[0], chains[1]))
+            near.append(lax.ppermute(near[0], "c", swap))
+        if j == 3:
+            near[1], chains[1] = lax.optimization_barrier((near[1], chains[1]))
+        for chain, blocks in zip(chains, walk):
+            blocks.append(chain)
     cross = [(0, 2), (1, 3), (2, 1), (3, 0)]
     far = [lax.ppermute(chain, ("c", "yl"), cross) for chain in chains]
 
@@ -218,23 +232,23 @@
     cost = pl.CostEstimate(
         flops=32 * n * n * draws, bytes_accessed=28 * n * draws, transcendentals=0
     )
-    partial = pl.pallas_call(
-        functools.partial(products_kernel, False),
-        out_shape=shape,
+    partial, steps = pl.pallas_call(
+        near_kernel,
+        out_shape=(shape, jax.ShapeDtypeStruct((2, 2 * draws, 4 * n), jnp.bfloat16)),
         in_specs=[SMEM, SMEM] + [VMEM] * 12,
-        out_specs=VMEM,
+        out_specs=(VMEM, VMEM),
         compiler_params=PARAMS,
         cost_estimate=cost,
-    )(place, scale, *walk, *near)
+    )(place, scale, *walk[0], *walk[1], *near)
     partial = pl.pallas_call(
-        functools.partial(products_kernel, True),
+        far_kernel,
         out_shape=shape,
-        in_specs=[SMEM, SMEM] + [VMEM] * 11,
+        in_specs=[SMEM, SMEM] + [VMEM] * 4,
         out_specs=VMEM,
-        input_output_aliases={12: 0},
+        input_output_aliases={5: 0},
         compiler_params=PARAMS,
         cost_estimate=cost,
-    )(place, scale, *walk[2:], *far, partial)
+    )(place, scale, steps, far[1], far[0], partial)
     partial = lax.all_to_all(partial, ("yh", "x"), 0, 0, tiled=True)
     block = jnp.sum(partial.astype(jnp.float32) / scales[:, None, None], axis=0)
     block = block[: 2 * n + 8]

time: 121 us -> 116 us (0.959)
  blocking collectives: 28.2 us -> 17.5 us
  starting transfers between devices: 36.9 us -> 41.2 us
    all_gather x2 -> x0, blocking collectives: 11.6 us -> none  [on_device(): lax.all_gather(part, 'c', axis=0, tiled=True)]
    ppermute x8, waiting for transfers between devices: 17.6 us -> 26.4 us  [on_device(): chains = [lax.ppermute(chain, ('c', 'z'), step) for chain in chains]]
    ppermute x2 -> x3, waiting for transfers between devices: 9.66 us -> 3.06 us  [the longest x1 3.06 us: on_device(): near = [lax.ppermute(near[0], 'yl', swap)]]
    ppermute x8, starting transfers between devices: 17.2 us -> 19.1 us  [on_device(): chains = [lax.ppermute(chain, ('c', 'z'), step) for chain in chains]]
    ppermute x2 -> x3, starting transfers between devices: 5.84 us -> 7.31 us  [the longest x1 3.48 us: on_device(): near = [lax.ppermute(near[0], 'yl', swap)]]
    unnamed x14 -> x8, local copies, waits for them, and re-layouts: 3.51 us -> 2.74 us
  transfers between devices with their start and end apart: 14 -> 15, of which waited for: 10 -> 11; matrix products, arithmetic and copies ran while one was open for 1% -> 2% of each run, Pallas kernels for 2% -> 3%
where the time goes in v5:
time: 116 us; the launch traced here: 115 us
  waiting for transfers between devices  41.9 us (36%)
  starting transfers between devices  41.2 us (36%)
  blocking collectives  17.5 us (15%)
  Pallas kernels  8.83 us (8%)
  local copies, waits for them, and re-layouts  4.76 us (4%)
    ppermute x8, waiting for transfers between devices, on_device(): chains = [lax.ppermute(chain, ('c', 'z'), step) for chain in chains]  26.4 us
    ppermute x8, starting transfers between devices, on_device(): chains = [lax.ppermute(chain, ('c', 'z'), step) for chain in chains]  19.1 us
    all_to_all x1, blocking collectives, on_device(): partial = lax.all_to_all(partial, ('yh', 'x'), 0, 0, tiled=True)  17.5 us
    ppermute x1, starting transfers between devices, on_device(): a = lax.ppermute(block, AXES, perms[0])  8.35 us
    ppermute x1, waiting for transfers between devices, on_device(): b = lax.ppermute(block, AXES, perms[1])  6.24 us
    ppermute x1, waiting for transfers between devices, on_device(): a = lax.ppermute(block, AXES, perms[0])  5.1 us
    ppermute x2, starting transfers between devices, on_device(): far = [lax.ppermute(chain, ('c', 'yl'), cross) for chain in chains]  4.46 us
    ppermute x1, starting transfers between devices, on_device(): near = [lax.ppermute(near[0], 'yl', swap)]  3.48 us
  transfers between devices with their start and end apart: 15, of which 11 were waited for; matrix products, arithmetic and copies ran while one was open for 2% of the time, Pallas kernels for 3%

profile of v5, /device:TPU:6, one launch (start us, length us, event | category | flops | bytes accessed | tf_op | source)
XLA Modules:
  0.0 115.3 jit_solution(17015394324036686350)
XLA Ops:
  0.6 1.8 %shard_map.68.refs_0_ = bf16[2,768,128]{2,1,0:T(8,128)(2,1)} custom-call(bf16[768,128]{1,0:T(8,128)(2,1)} %field.1, bf16[768,128]{1,0:T(8,128)(2,1)} %backward.1), custom_call_target="tpu_custom_call" | custom-call | tf_op jit(solution)/shard_map/pallas_call | solution.py:191
  2.4 1.9 %collective-permute-start.4 = (bf16[2,768,128]{2,1,0:T(8,128)(2,1)}, bf16[2,768,128]{2,1,0:T(8,128)(2,1)S(1)}, u32[]{:S(2)}, u32[]{:S(2)}) collective-permute-start(bf16[2,768,128]{2,1,0:T(8,128)(2,1)} %shard_map.68.refs_0_), channel_id=1, source_target_pairs={{0,32},{32,0},{1,33},{33,1},{2,34},{34,2},{3,35},{35,3},{4,36},{36... | collective-permute-start | bytes 1179656 | tf_op jit(solution)/shard_map/ppermute | solution.py:208
  4.4 3.8 %collective-permute-start = (bf16[2,768,128]{2,1,0:T(8,128)(2,1)}, bf16[2,768,128]{2,1,0:T(8,128)(2,1)S(1)}, u32[]{:S(2)}, u32[]{:S(2)}) collective-permute-start(bf16[2,768,128]{2,1,0:T(8,128)(2,1)} %shard_map.68.refs_0_), channel_id=1, source_target_pairs={{0,1},{1,2},{2,3},{3,4},{4,5},{5,6},{6,7},{7,8},{8,9},{9,10},{10,1... | collective-permute-start | bytes 1179656 | tf_op jit(solution)/shard_map/ppermute | solution.py:212
  8.2 3.8 %collective-permute-start.5 = (bf16[2,768,128]{2,1,0:T(8,128)(2,1)S(1)}, bf16[2,768,128]{2,1,0:T(8,128)(2,1)S(1)}, u32[]{:S(2)}, u32[]{:S(2)}) collective-permute-start(bf16[2,768,128]{2,1,0:T(8,128)(2,1)S(1)} %collective-permute-done.4.refs_5_), channel_id=1, source_target_pairs={{0,1},{1,2},{2,3},{3,4},{4,5},{5,6},{6,7},{7,8},{8,9},{9,10},{10,1... | collective-permute-start | bytes 1179656 | tf_op jit(solution)/shard_map/ppermute | solution.py:212
  12.1 9.7 %collective-permute-done.refs_1_ = bf16[2,768,128]{2,1,0:T(8,128)(2,1)S(1)} collective-permute-done((bf16[2,768,128]{2,1,0:T(8,128)(2,1)}, bf16[2,768,128]{2,1,0:T(8,128)(2,1)S(1)}, u32[]{:S(2)}, u32[]{:S(2)}) %collective-permute-start) | collective-permute-done | bytes 393248 | tf_op jit(solution)/shard_map/ppermute | solution.py:212
  21.7 1.9 %collective-permute-start.1 = (bf16[2,768,128]{2,1,0:T(8,128)(2,1)S(1)}, bf16[2,768,128]{2,1,0:T(8,128)(2,1)S(1)}, u32[]{:S(2)}, u32[]{:S(2)}) collective-permute-start(bf16[2,768,128]{2,1,0:T(8,128)(2,1)S(1)} %collective-permute-done.refs_1_), channel_id=1, source_target_pairs={{0,1},{1,2},{2,3},{3,4},{4,5},{5,6},{6,7},{7,8},{8,9},{9,10},{10,1... | collective-permute-start | bytes 1179656 | tf_op jit(solution)/shard_map/ppermute | solution.py:212
  23.7 2.3 %collective-permute-done.5.refs_6_ = bf16[2,768,128]{2,1,0:T(8,128)(2,1)S(1)} collective-permute-done((bf16[2,768,128]{2,1,0:T(8,128)(2,1)S(1)}, bf16[2,768,128]{2,1,0:T(8,128)(2,1)S(1)}, u32[]{:S(2)}, u32[]{:S(2)}) %collective-permute-start.5) | collective-permute-done | bytes 393248 | tf_op jit(solution)/shard_map/ppermute | solution.py:212
  26.0 1.9 %collective-permute-start.6 = (bf16[2,768,128]{2,1,0:T(8,128)(2,1)S(1)}, bf16[2,768,128]{2,1,0:T(8,128)(2,1)S(1)}, u32[]{:S(2)}, u32[]{:S(2)}) collective-permute-start(bf16[2,768,128]{2,1,0:T(8,128)(2,1)S(1)} %collective-permute-done.5.refs_6_), channel_id=1, source_target_pairs={{0,1},{1,2},{2,3},{3,4},{4,5},{5,6},{6,7},{7,8},{8,9},{9,10},{10,1... | collective-permute-start | bytes 1179656 | tf_op jit(solution)/shard_map/ppermute | solution.py:212
  27.9 4.7 %collective-permute-done.1.refs_2_ = bf16[2,768,128]{2,1,0:T(8,128)(2,1)S(1)} collective-permute-done((bf16[2,768,128]{2,1,0:T(8,128)(2,1)S(1)}, bf16[2,768,128]{2,1,0:T(8,128)(2,1)S(1)}, u32[]{:S(2)}, u32[]{:S(2)}) %collective-permute-start.1) | collective-permute-done | bytes 393248 | tf_op jit(solution)/shard_map/ppermute | solution.py:212
  32.6 1.9 %collective-permute-start.2 = (bf16[2,768,128]{2,1,0:T(8,128)(2,1)S(1)}, bf16[2,768,128]{2,1,0:T(8,128)(2,1)S(1)}, u32[]{:S(2)}, u32[]{:S(2)}) collective-permute-start(bf16[2,768,128]{2,1,0:T(8,128)(2,1)S(1)} %collective-permute-done.1.refs_2_), channel_id=1, source_target_pairs={{0,1},{1,2},{2,3},{3,4},{4,5},{5,6},{6,7},{7,8},{8,9},{9,10},{10,1... | collective-permute-start | bytes 1179656 | tf_op jit(solution)/shard_map/ppermute | solution.py:212
  34.5 3.5 %collective-permute-start.7 = (bf16[2,768,128]{2,1,0:T(8,128)(2,1)}, bf16[2,768,128]{2,1,0:T(8,128)(2,1)S(1)}, u32[]{:S(2)}, u32[]{:S(2)}) collective-permute-start(bf16[2,768,128]{2,1,0:T(8,128)(2,1)} %shard_map.68.refs_0_), channel_id=1, source_target_pairs={{0,16},{16,0},{1,17},{17,1},{2,18},{18,2},{3,19},{19,3},{4,20},{20... | collective-permute-start | bytes 1179656 | tf_op jit(solution)/shard_map/ppermute | solution.py:215
  38.0 1.9 %collective-permute-start.8 = (bf16[2,768,128]{2,1,0:T(8,128)(2,1)S(1)}, bf16[2,768,128]{2,1,0:T(8,128)(2,1)S(1)}, u32[]{:S(2)}, u32[]{:S(2)}) collective-permute-start(bf16[2,768,128]{2,1,0:T(8,128)(2,1)S(1)} %collective-permute-done.6.refs_7_), channel_id=1, source_target_pairs={{0,1},{1,2},{2,3},{3,4},{4,5},{5,6},{6,7},{7,8},{8,9},{9,10},{10,1... | collective-permute-start | bytes 1179656 | tf_op jit(solution)/shard_map/ppermute | solution.py:212
  40.0 3.5 %collective-permute-done.2.refs_3_ = bf16[2,768,128]{2,1,0:T(8,128)(2,1)S(1)} collective-permute-done((bf16[2,768,128]{2,1,0:T(8,128)(2,1)S(1)}, bf16[2,768,128]{2,1,0:T(8,128)(2,1)S(1)}, u32[]{:S(2)}, u32[]{:S(2)}) %collective-permute-start.2) | collective-permute-done | bytes 393248 | tf_op jit(solution)/shard_map/ppermute | solution.py:212
  43.5 1.9 %collective-permute-start.3 = (bf16[2,768,128]{2,1,0:T(8,128)(2,1)S(1)}, bf16[2,768,128]{2,1,0:T(8,128)(2,1)S(1)}, u32[]{:S(2)}, u32[]{:S(2)}) collective-permute-start(bf16[2,768,128]{2,1,0:T(8,128)(2,1)S(1)} %collective-permute-done.2.refs_3_), channel_id=1, source_target_pairs={{0,1},{1,2},{2,3},{3,4},{4,5},{5,6},{6,7},{7,8},{8,9},{9,10},{10,1... | collective-permute-start | bytes 1179656 | tf_op jit(solution)/shard_map/ppermute | solution.py:212
  45.4 3.1 %collective-permute-done.7.refs_10_ = bf16[2,768,128]{2,1,0:T(8,128)(2,1)S(1)} collective-permute-done((bf16[2,768,128]{2,1,0:T(8,128)(2,1)}, bf16[2,768,128]{2,1,0:T(8,128)(2,1)S(1)}, u32[]{:S(2)}, u32[]{:S(2)}) %collective-permute-start.7) | collective-permute-done | bytes 393248 | tf_op jit(solution)/shard_map/ppermute | solution.py:215
  48.9 1.9 %collective-permute-start.9 = (bf16[2,768,128]{2,1,0:T(8,128)(2,1)S(1)}, bf16[2,768,128]{2,1,0:T(8,128)(2,1)S(1)}, u32[]{:S(2)}, u32[]{:S(2)}) collective-permute-start(bf16[2,768,128]{2,1,0:T(8,128)(2,1)S(1)} %collective-permute-done.7.refs_10_), channel_id=1, source_target_pairs={{0,32},{32,0},{1,33},{33,1},{2,34},{34,2},{3,35},{35,3},{4,36},{36... | collective-permute-start | bytes 1179656 | tf_op jit(solution)/shard_map/ppermute | solution.py:218
  50.8 1.9 %collective-permute-start.10 = (bf16[2,768,128]{2,1,0:T(8,128)(2,1)S(1)}, bf16[2,768,128]{2,1,0:T(8,128)(2,1)}, u32[]{:S(2)}, u32[]{:S(2)}) collective-permute-start(bf16[2,768,128]{2,1,0:T(8,128)(2,1)S(1)} %collective-permute-done.8.refs_8_), channel_id=1, source_target_pairs={{0,1},{1,2},{2,3},{3,4},{4,5},{5,6},{6,7},{7,8},{8,9},{9,10},{10,1... | collective-permute-start | bytes 1179656 | tf_op jit(solution)/shard_map/ppermute | solution.py:212
  52.8 1.6 %collective-permute-done.3.refs_4_ = bf16[2,768,128]{2,1,0:T(8,128)(2,1)S(1)} collective-permute-done((bf16[2,768,128]{2,1,0:T(8,128)(2,1)S(1)}, bf16[2,768,128]{2,1,0:T(8,128)(2,1)S(1)}, u32[]{:S(2)}, u32[]{:S(2)}) %collective-permute-start.3) | collective-permute-done | bytes 393248 | tf_op jit(solution)/shard_map/ppermute | solution.py:212
  54.3 2.5 %collective-permute-start.12 = (bf16[2,768,128]{2,1,0:T(8,128)(2,1)S(1)}, bf16[2,768,128]{2,1,0:T(8,128)(2,1)}, u32[]{:S(2)}, u32[]{:S(2)}) collective-permute-start(bf16[2,768,128]{2,1,0:T(8,128)(2,1)S(1)} %collective-permute-done.3.refs_4_), channel_id=1, source_target_pairs={{0,32},{16,48},{32,16},{48,0},{1,33},{17,49},{33,17},{49,1},{2,34}... | collective-permute-start | bytes 1179656 | tf_op jit(solution)/shard_map/ppermute | solution.py:224
  57.7 4.2 %collective-permute-done.10.refs_9_ = bf16[2,768,128]{2,1,0:T(8,128)(2,1)} collective-permute-done((bf16[2,768,128]{2,1,0:T(8,128)(2,1)S(1)}, bf16[2,768,128]{2,1,0:T(8,128)(2,1)}, u32[]{:S(2)}, u32[]{:S(2)}) %collective-permute-start.10) | collective-permute-done | bytes 393248 | tf_op jit(solution)/shard_map/ppermute | solution.py:212
  61.8 1.9 %collective-permute-start.11 = (bf16[2,768,128]{2,1,0:T(8,128)(2,1)}, bf16[2,768,128]{2,1,0:T(8,128)(2,1)}, u32[]{:S(2)}, u32[]{:S(2)}) collective-permute-start(bf16[2,768,128]{2,1,0:T(8,128)(2,1)} %collective-permute-done.10.refs_9_), channel_id=1, source_target_pairs={{0,32},{16,48},{32,16},{48,0},{1,33},{17,49},{33,17},{49,1},{2,34}... | collective-permute-start | bytes 1179656 | tf_op jit(solution)/shard_map/ppermute | solution.py:224
  63.7 1.3 %dynamic_slice.8.scale = f32[1]{0:T(128)} dynamic-slice(f32[8]{0:T(128)} %constant.50.clone, s32[]{:T(128)S(6)} %select_n.8), dynamic_slice_sizes={1} | dynamic-slice | bytes 12 | tf_op jit(solution)/shard_map/dynamic_slice | solution.py:228
  65.1 1.0 copy-done
  67.1 3.0 %shard_map.69 = (bf16[8,272,128]{2,1,0:T(8,128)(2,1)S(1)}, bf16[2,1536,512]{2,1,0:T(8,128)(2,1)S(1)}) custom-call(s32[3]{0:T(128)S(1)} %pad_add_fusion.place, f32[1]{0:T(128)} %dynamic_slice.8.scale, bf16[2,768,128]{2,1,0:T(8,128)(2,1)S(1)} %copy-done, bf16[2,768,128]{2,1,0:T(8,128)(2,1)S(1)} %collective-permute-done.refs_1_, ...), custom_call_target="tpu_custom_call" | custom-call | flops 402653184 | bytes 2752512 | tf_op jit(solution)/shard_map/pallas_call | solution.py:235
  70.2 1.0 collective-permute-done.11.first
  71.2 2.6 %shard_map.70 = bf16[8,272,128]{2,1,0:T(8,128)(2,1)S(1)} custom-call(s32[3]{0:T(128)S(1)} %pad_add_fusion.place, f32[1]{0:T(128)} %dynamic_slice.8.scale, bf16[2,1536,512]{2,1,0:T(8,128)(2,1)S(1)} %get-tuple-element.16.steps, bf16[2,768,128]{2,1,0:T(8,128)(2,1)} %collective-permute-done.11.first, ...), custom_call_target="tpu_custom_call", output_to_operand_aliasing={{}: (5, {})} | custom-call | flops 402653184 | bytes 2752512 | tf_op jit(solution)/shard_map/pallas_call | solution.py:243
  73.8 17.5 %all_to_all.5 = bf16[8,272,128]{2,1,0:T(8,128)(2,1)S(1)} all-to-all(bf16[8,272,128]{2,1,0:T(8,128)(2,1)S(1)} %shard_map.70), channel_id=1, replica_groups=mesh['yh'=2,'x'=4,'c'=2,'yl'=2,'z'=16] {'yh','x'}, dimensions={0} | all-to-all | bytes 1114112 | tf_op jit(solution)/shard_map/all_to_all | solution.py:252
  91.5 8.4 %collective-permute-start.13 = (f32[264,128]{1,0:T(8,128)S(1)}, f32[264,128]{1,0:T(8,128)S(1)}, u32[]{:S(2)}, u32[]{:S(2)}) collective-permute-start(f32[264,128]{1,0:T(8,128)S(1)} %slice.4), channel_id=1, source_target_pairs={{0,244},{1,21},{2,22},{3,55},{4,56},{5,89},{6,90},{7,123},{8,124},... | collective-permute-start | bytes 405512 | tf_op jit(solution)/shard_map/ppermute | solution.py:257
  99.9 1.9 %collective-permute-start.14 = (f32[264,128]{1,0:T(8,128)S(1)}, f32[264,128]{1,0:T(8,128)S(1)}, u32[]{:S(2)}, u32[]{:S(2)}) collective-permute-start(f32[264,128]{1,0:T(8,128)S(1)} %slice.4), channel_id=1, source_target_pairs={{0,335},{1,320},{2,353},{3,354},{4,387},{5,388},{6,421},{7,422},{8... | collective-permute-start | bytes 405512 | tf_op jit(solution)/shard_map/ppermute | solution.py:258
  102.5 5.1 %collective-permute-done.13.a = f32[264,128]{1,0:T(8,128)S(1)} collective-permute-done((f32[264,128]{1,0:T(8,128)S(1)}, f32[264,128]{1,0:T(8,128)S(1)}, u32[]{:S(2)}, u32[]{:S(2)}) %collective-permute-start.13) | collective-permute-done | bytes 135200 | tf_op jit(solution)/shard_map/ppermute | solution.py:257
  107.6 6.2 %collective-permute-done.14.b = f32[264,128]{1,0:T(8,128)S(1)} collective-permute-done((f32[264,128]{1,0:T(8,128)S(1)}, f32[264,128]{1,0:T(8,128)S(1)}, u32[]{:S(2)}, u32[]{:S(2)}) %collective-permute-start.14) | collective-permute-done | bytes 135200 | tf_op jit(solution)/shard_map/ppermute | solution.py:258
  113.9 1.4 %shard_map.71 = (f32[128,256]{1,0:T(8,128)}, f32[128,256]{1,0:T(8,128)}) custom-call(s32[4]{0:T(128)S(1)} %dynamic-slice_bitcast_fusion.todo, f32[264,128]{1,0:T(8,128)S(1)} %collective-permute-done.13.a, f32[264,128]{1,0:T(8,128)S(1)} %collective-permute-done.14.b), custom_call_target="tpu_custom_call" | custom-call | tf_op jit(solution)/shard_map/pallas_call | solution.py:263
  (16 shorter events, 3.2 us)
Async XLA Ops:
  2.4 5.8 %collective-permute-start.4 = (bf16[2,768,128]{2,1,0:T(8,128)(2,1)}, bf16[2,768,128]{2,1,0:T(8,128)(2,1)S(1)}, u32[]{:S(2)}, u32[]{:S(2)}) collective-permute-start(bf16[2,768,128]{2,1,0:T(8,128)(2,1)} %shard_map.68.refs_0_), channel_id=1, source_target_pairs={{0,32},{32,0},{1,33},{33,1},{2,34},{34,2},{3,35},{35,3},{4,36},{36... | collective-permute-start | bytes 1179656 | tf_op jit(solution)/shard_map/ppermute | solution.py:208
  4.4 17.4 %collective-permute-start = (bf16[2,768,128]{2,1,0:T(8,128)(2,1)}, bf16[2,768,128]{2,1,0:T(8,128)(2,1)S(1)}, u32[]{:S(2)}, u32[]{:S(2)}) collective-permute-start(bf16[2,768,128]{2,1,0:T(8,128)(2,1)} %shard_map.68.refs_0_), channel_id=1, source_target_pairs={{0,1},{1,2},{2,3},{3,4},{4,5},{5,6},{6,7},{7,8},{8,9},{9,10},{10,1... | collective-permute-start | bytes 1179656 | tf_op jit(solution)/shard_map/ppermute | solution.py:212
  8.2 17.7 %collective-permute-start.5 = (bf16[2,768,128]{2,1,0:T(8,128)(2,1)S(1)}, bf16[2,768,128]{2,1,0:T(8,128)(2,1)S(1)}, u32[]{:S(2)}, u32[]{:S(2)}) collective-permute-start(bf16[2,768,128]{2,1,0:T(8,128)(2,1)S(1)} %collective-permute-done.4.refs_5_), channel_id=1, source_target_pairs={{0,1},{1,2},{2,3},{3,4},{4,5},{5,6},{6,7},{7,8},{8,9},{9,10},{10,1... | collective-permute-start | bytes 1179656 | tf_op jit(solution)/shard_map/ppermute | solution.py:212
  21.7 10.9 %collective-permute-start.1 = (bf16[2,768,128]{2,1,0:T(8,128)(2,1)S(1)}, bf16[2,768,128]{2,1,0:T(8,128)(2,1)S(1)}, u32[]{:S(2)}, u32[]{:S(2)}) collective-permute-start(bf16[2,768,128]{2,1,0:T(8,128)(2,1)S(1)} %collective-permute-done.refs_1_), channel_id=1, source_target_pairs={{0,1},{1,2},{2,3},{3,4},{4,5},{5,6},{6,7},{7,8},{8,9},{9,10},{10,1... | collective-permute-start | bytes 1179656 | tf_op jit(solution)/shard_map/ppermute | solution.py:212
  26.0 12.1 %collective-permute-start.6 = (bf16[2,768,128]{2,1,0:T(8,128)(2,1)S(1)}, bf16[2,768,128]{2,1,0:T(8,128)(2,1)S(1)}, u32[]{:S(2)}, u32[]{:S(2)}) collective-permute-start(bf16[2,768,128]{2,1,0:T(8,128)(2,1)S(1)} %collective-permute-done.5.refs_6_), channel_id=1, source_target_pairs={{0,1},{1,2},{2,3},{3,4},{4,5},{5,6},{6,7},{7,8},{8,9},{9,10},{10,1... | collective-permute-start | bytes 1179656 | tf_op jit(solution)/shard_map/ppermute | solution.py:212
  32.6 10.9 %collective-permute-start.2 = (bf16[2,768,128]{2,1,0:T(8,128)(2,1)S(1)}, bf16[2,768,128]{2,1,0:T(8,128)(2,1)S(1)}, u32[]{:S(2)}, u32[]{:S(2)}) collective-permute-start(bf16[2,768,128]{2,1,0:T(8,128)(2,1)S(1)} %collective-permute-done.1.refs_2_), channel_id=1, source_target_pairs={{0,1},{1,2},{2,3},{3,4},{4,5},{5,6},{6,7},{7,8},{8,9},{9,10},{10,1... | collective-permute-start | bytes 1179656 | tf_op jit(solution)/shard_map/ppermute | solution.py:212
  34.5 13.9 %collective-permute-start.7 = (bf16[2,768,128]{2,1,0:T(8,128)(2,1)}, bf16[2,768,128]{2,1,0:T(8,128)(2,1)S(1)}, u32[]{:S(2)}, u32[]{:S(2)}) collective-permute-start(bf16[2,768,128]{2,1,0:T(8,128)(2,1)} %shard_map.68.refs_0_), channel_id=1, source_target_pairs={{0,16},{16,0},{1,17},{17,1},{2,18},{18,2},{3,19},{19,3},{4,20},{20... | collective-permute-start | bytes 1179656 | tf_op jit(solution)/shard_map/ppermute | solution.py:215
  38.0 10.9 %collective-permute-start.8 = (bf16[2,768,128]{2,1,0:T(8,128)(2,1)S(1)}, bf16[2,768,128]{2,1,0:T(8,128)(2,1)S(1)}, u32[]{:S(2)}, u32[]{:S(2)}) collective-permute-start(bf16[2,768,128]{2,1,0:T(8,128)(2,1)S(1)} %collective-permute-done.6.refs_7_), channel_id=1, source_target_pairs={{0,1},{1,2},{2,3},{3,4},{4,5},{5,6},{6,7},{7,8},{8,9},{9,10},{10,1... | collective-permute-start | bytes 1179656 | tf_op jit(solution)/shard_map/ppermute | solution.py:212
  43.5 10.9 %collective-permute-start.3 = (bf16[2,768,128]{2,1,0:T(8,128)(2,1)S(1)}, bf16[2,768,128]{2,1,0:T(8,128)(2,1)S(1)}, u32[]{:S(2)}, u32[]{:S(2)}) collective-permute-start(bf16[2,768,128]{2,1,0:T(8,128)(2,1)S(1)} %collective-permute-done.2.refs_3_), channel_id=1, source_target_pairs={{0,1},{1,2},{2,3},{3,4},{4,5},{5,6},{6,7},{7,8},{8,9},{9,10},{10,1... | collective-permute-start | bytes 1179656 | tf_op jit(solution)/shard_map/ppermute | solution.py:212
  48.9 8.0 %collective-permute-start.9 = (bf16[2,768,128]{2,1,0:T(8,128)(2,1)S(1)}, bf16[2,768,128]{2,1,0:T(8,128)(2,1)S(1)}, u32[]{:S(2)}, u32[]{:S(2)}) collective-permute-start(bf16[2,768,128]{2,1,0:T(8,128)(2,1)S(1)} %collective-permute-done.7.refs_10_), channel_id=1, source_target_pairs={{0,32},{32,0},{1,33},{33,1},{2,34},{34,2},{3,35},{35,3},{4,36},{36... | collective-permute-start | bytes 1179656 | tf_op jit(solution)/shard_map/ppermute | solution.py:218
  50.8 11.0 %collective-permute-start.10 = (bf16[2,768,128]{2,1,0:T(8,128)(2,1)S(1)}, bf16[2,768,128]{2,1,0:T(8,128)(2,1)}, u32[]{:S(2)}, u32[]{:S(2)}) collective-permute-start(bf16[2,768,128]{2,1,0:T(8,128)(2,1)S(1)} %collective-permute-done.8.refs_8_), channel_id=1, source_target_pairs={{0,1},{1,2},{2,3},{3,4},{4,5},{5,6},{6,7},{7,8},{8,9},{9,10},{10,1... | collective-permute-start | bytes 1179656 | tf_op jit(solution)/shard_map/ppermute | solution.py:212
  54.3 15.8 %collective-permute-start.12 = (bf16[2,768,128]{2,1,0:T(8,128)(2,1)S(1)}, bf16[2,768,128]{2,1,0:T(8,128)(2,1)}, u32[]{:S(2)}, u32[]{:S(2)}) collective-permute-start(bf16[2,768,128]{2,1,0:T(8,128)(2,1)S(1)} %collective-permute-done.3.refs_4_), channel_id=1, source_target_pairs={{0,32},{16,48},{32,16},{48,0},{1,33},{17,49},{33,17},{49,1},{2,34}... | collective-permute-start | bytes 1179656 | tf_op jit(solution)/shard_map/ppermute | solution.py:224
  56.9 0.7 copy-start.1
  61.8 9.4 %collective-permute-start.11 = (bf16[2,768,128]{2,1,0:T(8,128)(2,1)}, bf16[2,768,128]{2,1,0:T(8,128)(2,1)}, u32[]{:S(2)}, u32[]{:S(2)}) collective-permute-start(bf16[2,768,128]{2,1,0:T(8,128)(2,1)} %collective-permute-done.10.refs_9_), channel_id=1, source_target_pairs={{0,32},{16,48},{32,16},{48,0},{1,33},{17,49},{33,17},{49,1},{2,34}... | collective-permute-start | bytes 1179656 | tf_op jit(solution)/shard_map/ppermute | solution.py:224
  65.1 1.0 copy-start
  66.1 1.0 copy-start.2
  73.8 17.5 %copy-start.3 = (f32[8]{0:T(128)S(1)}, f32[8]{0:T(128)}, u32[]{:S(2)}) copy-start(f32[8]{0:T(128)} %constant.54) | copy-start | bytes 100
  91.5 16.1 %collective-permute-start.13 = (f32[264,128]{1,0:T(8,128)S(1)}, f32[264,128]{1,0:T(8,128)S(1)}, u32[]{:S(2)}, u32[]{:S(2)}) collective-permute-start(f32[264,128]{1,0:T(8,128)S(1)} %slice.4), channel_id=1, source_target_pairs={{0,244},{1,21},{2,22},{3,55},{4,56},{5,89},{6,90},{7,123},{8,124},... | collective-permute-start | bytes 405512 | tf_op jit(solution)/shard_map/ppermute | solution.py:257
  99.9 14.0 %collective-permute-start.14 = (f32[264,128]{1,0:T(8,128)S(1)}, f32[264,128]{1,0:T(8,128)S(1)}, u32[]{:S(2)}, u32[]{:S(2)}) collective-permute-start(f32[264,128]{1,0:T(8,128)S(1)} %slice.4), channel_id=1, source_target_pairs={{0,335},{1,320},{2,353},{3,354},{4,387},{5,388},{6,421},{7,422},{8... | collective-permute-start | bytes 405512 | tf_op jit(solution)/shard_map/ppermute | solution.py:258

commit v6 on v5

--- a/solution.py
+++ b/solution.py
@@ -97,7 +97,7 @@
 def store(out, scale, slot, kernel, total):
     n = out.shape[-1]
     for j in range(total.shape[1] // n):
-        block = total[:, j * n : (j + 1) * n] * scale[0]
+        block = total[:, j * n : (j + 1) * n] * scale
         out[slot + j, kernel * n : (kernel + 1) * n] = block.astype(jnp.bfloat16)
 
 
@@ -106,9 +106,9 @@
     return (core == 1) & ((z < 8) != (y == 0)), (core == 0) & (y == 1)
 
 
-def near_kernel(place, scale, *refs):
-    first, second, near, (out, steps) = refs[0:5], refs[5:10], refs[10:12], refs[12:]
-    core, y = place[0], place[1]
+def early_kernel(place, scales, *refs):
+    first, second, near, (out, left, steps) = refs[0:4], refs[4:8], refs[8:10], refs[10:]
+    core, y, scale = place[0], place[1], scales[place[3]]
     packed, partner = cases(place)
     n = out.shape[-1]
     rows = near[0].shape[1]
@@ -116,10 +116,9 @@
         out[slot, 2 * n : 2 * n + EXTRA] = jnp.zeros((EXTRA, n), jnp.bfloat16)
     for kernel in range(2):
         for i, chain in enumerate((first, second)):
-            for j in range(4):
-                steps[kernel, i * rows : (i + 1) * rows, j * n : (j + 1) * n] = chain[
-                    j + 1
-                ][kernel]
+            part = pl.ds(i * rows, rows)
+            for j in range(3):
+                steps[kernel, part, j * n : (j + 1) * n] = chain[j + 1][kernel]
 
         def own(kernel=kernel):
             return jnp.concatenate([first[0][kernel], second[0][kernel]], axis=0)
@@ -129,11 +128,14 @@
 
         @pl.when(core == 0)
         def _():
-            store(out, scale, 4, kernel, product(other(), steps[kernel]))
+            left[kernel] = other()
 
         @pl.when(core == 1)
         def _():
-            store(out, scale, 4, kernel, product(own(), steps[kernel]))
+            left[kernel] = own()
+
+        total = product(left[kernel], steps[kernel, :, 0 : 3 * n])
+        store(out, scale, 4, kernel, total)
 
         @pl.when(partner)
         def _():
@@ -150,16 +152,29 @@
             diagonal = jnp.sum(jnp.where(row == col, low, 0.0), axis=0, keepdims=True)
             line = lax.broadcasted_iota(jnp.int32, (EXTRA, n), 0)
             extra = out[3, 2 * n : 2 * n + EXTRA].astype(jnp.float32)
-            extra = jnp.where(line == kernel, diagonal * scale[0], extra)
+            extra = jnp.where(line == kernel, diagonal * scale, extra)
             out[3, 2 * n : 2 * n + EXTRA] = extra.astype(jnp.bfloat16)
 
 
-def far_kernel(place, scale, steps, first, second, _, out):
+def middle_kernel(place, scales, first, second, far, left, _, __, out, steps, total):
+    scale = scales[place[3]]
+    n = out.shape[-1]
+    rows = far.shape[1]
+    for kernel in range(2):
+        for i, chain in enumerate((first, second)):
+            steps[kernel, i * rows : (i + 1) * rows, 3 * n :] = chain[kernel]
+        total[kernel] = product(far[kernel], steps[kernel, rows:])
+        last = product(left[kernel], steps[kernel, :, 3 * n :])
+        store(out, scale, 7, kernel, last)
+
+
+def late_kernel(place, scales, far, steps, part, _, out):
+    scale = scales[place[3]]
     packed, partner = cases(place)
     n = out.shape[-1]
+    rows = far.shape[1]
     for kernel in range(2):
-        far = jnp.concatenate([first[kernel], second[kernel]], axis=0)
-        total = product(far, steps[kernel])
+        total = part[kernel] + product(far[kernel], steps[kernel, 0:rows])
         store(out, scale, 0, kernel, total[:, : 3 * n])
 
         @pl.when(jnp.logical_not(packed | partner))
@@ -201,54 +216,75 @@
         compiler_params=pltpu.CompilerParams(vmem_limit_bytes=60 * 1024 * 1024),
     )(field, backward)
 
-    swap = [(0, 1), (1, 0)]
-    step = [
-        (c * 16 + z, c * 16 + (z + 1 - 2 * c) % 16) for c in range(2) for z in range(16)
+    step, first_step = [], []
+    for c in range(2):
+        for z in range(16):
+            step.append((c * 16 + z, c * 16 + (z + 1 - 2 * c) % 16))
+            first_step.append((c * 16 + z, (1 - c) * 16 + (z + 2 * c - 1) % 16))
+    place = jnp.stack([lax.axis_index(a) for a in ("c", "yl", "z", ("yh", "x"))])
+    scales = np.exp2(np.arange(8) / 8).astype(np.float32)
+    shape = jax.ShapeDtypeStruct((8, 2 * n + EXTRA, n), jnp.bfloat16)
+    left_shape = jax.ShapeDtypeStruct((2, 2 * draws, n), jnp.bfloat16)
+    steps_shape = jax.ShapeDtypeStruct((2, 2 * draws, 4 * n), jnp.bfloat16)
+    total_shape = jax.ShapeDtypeStruct((2, n, 4 * n), jnp.float32)
+
+    def call(kernel, out_shape, *args, aliases={}, flops=1):
+        return pl.pallas_call(
+            kernel,
+            out_shape=out_shape,
+            in_specs=[SMEM, SMEM] + [VMEM] * len(args),
+            out_specs=jax.tree.map(lambda _: VMEM, out_shape),
+            input_output_aliases=aliases,
+            compiler_params=PARAMS,
+            cost_estimate=pl.CostEstimate(
+                flops=flops * 8 * n * n * draws,
+                bytes_accessed=28 * n * draws,
+                transcendentals=0,
+            ),
+        )(place, jnp.asarray(scales), *args)
+
+    chains = [
+        lax.ppermute(both, ("c", "z"), step),
+        lax.ppermute(both, ("c", "z"), first_step),
     ]
-    chains = [both, lax.ppermute(both, "c", swap)]
-    walk = [[chain] for chain in chains]
-    near = [both]
+    walk = [[], []]
     for j in range(4):
-        chains = [lax.ppermute(chain, ("c", "z"), step) for chain in chains]
+        if j:
+            chains = [lax.ppermute(chain, ("c", "z"), step) for chain in chains]
         if j == 0:
-            near[0], chains[1] = lax.optimization_barrier((near[0], chains[1]))
-            near = [lax.ppermute(near[0], "yl", swap)]
+            own, chains[1] = lax.optimization_barrier((both, chains[1]))
+            near = [lax.ppermute(own, "yl", [(0, 1), (1, 0)])]
+        if j == 1:
+            own, near[0], chains[1] = lax.optimization_barrier(
+                (own, near[0], chains[1])
+            )
+            near.append(
+                lax.ppermute(own, ("c", "yl"), [(0, 3), (1, 2), (2, 1), (3, 0)])
+            )
+            other = lax.ppermute(own, "c", [(0, 1), (1, 0)])
         if j == 2:
-            near[0], chains[1] = lax.optimization_barrier((near[0], chains[1]))
-            near.append(lax.ppermute(near[0], "c", swap))
+            near[1], chains[1] = lax.optimization_barrier((near[1], chains[1]))
         if j == 3:
-            near[1], chains[1] = lax.optimization_barrier((near[1], chains[1]))
+            partial, left, steps = call(
+                early_kernel,
+                (shape, left_shape, steps_shape),
+                *(both, *walk[0], other, *walk[1], *near),
+                flops=4,
+            )
+            partial, chains[0] = lax.optimization_barrier((partial, chains[0]))
         for chain, blocks in zip(chains, walk):
             blocks.append(chain)
     cross = [(0, 2), (1, 3), (2, 1), (3, 0)]
     far = [lax.ppermute(chain, ("c", "yl"), cross) for chain in chains]
 
-    place = jnp.stack([lax.axis_index("c"), lax.axis_index("yl"), lax.axis_index("z")])
-    scales = np.exp2(np.arange(8) / 8).astype(np.float32)
-    scale = lax.dynamic_slice_in_dim(
-        jnp.asarray(scales), lax.axis_index(("yh", "x")), 1
+    partial, steps, total = call(
+        middle_kernel,
+        (shape, steps_shape, total_shape),
+        *(*chains, far[0], left, partial, steps),
+        aliases={6: 0, 7: 1},
+        flops=3,
     )
-    shape = jax.ShapeDtypeStruct((8, 2 * n + EXTRA, n), jnp.bfloat16)
-    cost = pl.CostEstimate(
-        flops=32 * n * n * draws, bytes_accessed=28 * n * draws, transcendentals=0
-    )
-    partial, steps = pl.pallas_call(
-        near_kernel,
-        out_shape=(shape, jax.ShapeDtypeStruct((2, 2 * draws, 4 * n), jnp.bfloat16)),
-        in_specs=[SMEM, SMEM] + [VMEM] * 12,
-        out_specs=(VMEM, VMEM),
-        compiler_params=PARAMS,
-        cost_estimate=cost,
-    )(place, scale, *walk[0], *walk[1], *near)
-    partial = pl.pallas_call(
-        far_kernel,
-        out_shape=shape,
-        in_specs=[SMEM, SMEM] + [VMEM] * 4,
-        out_specs=VMEM,
-        input_output_aliases={5: 0},
-        compiler_params=PARAMS,
-        cost_estimate=cost,
-    )(place, scale, steps, far[1], far[0], partial)
+    partial = call(late_kernel, shape, far[1], steps, total, partial, aliases={5: 0}, flops=2)
     partial = lax.all_to_all(partial, ("yh", "x"), 0, 0, tiled=True)
     block = jnp.sum(partial.astype(jnp.float32) / scales[:, None, None], axis=0)
     block = block[: 2 * n + 8]

time: 116 us -> 115 us (level)
  the two profiles are of different devices: /device:TPU:6 before, /device:TPU:9 now
where the time goes in v6:
time: 115 us; the launch traced here: 114 us
  starting transfers between devices  62.6 us (54%)
  waiting for transfers between devices  21.5 us (19%)
  blocking collectives  16.2 us (14%)
  Pallas kernels  8.76 us (8%)
  local copies, waits for them, and re-layouts  4.12 us (4%)
    ppermute x6, starting transfers between devices, on_device(): chains = [lax.ppermute(chain, ('c', 'z'), step) for chain in chains]  22.5 us
    all_to_all x1, blocking collectives, on_device(): partial = lax.all_to_all(partial, ('yh', 'x'), 0, 0, tiled=True)  16.2 us
    ppermute x1, starting transfers between devices, on_device(): lax.ppermute(both, ('c', 'z'), step)  11.1 us
    ppermute x1, starting transfers between devices, on_device(): b = lax.ppermute(block, AXES, perms[1])  7.58 us
    ppermute x1, waiting for transfers between devices, on_device(): b = lax.ppermute(block, AXES, perms[1])  7.5 us
    ppermute x1, starting transfers between devices, on_device(): a = lax.ppermute(block, AXES, perms[0])  7.35 us
    ppermute x2, waiting for transfers between devices, on_device(): far = [lax.ppermute(chain, ('c', 'yl'), cross) for chain in chains]  5.61 us
    pallas_call x3, Pallas kernels, call(): pl.pallas_call(kernel, out_shape=out_shape, in_specs=[SMEM, SMEM] + [VMEM...  5.6 us
  transfers between devices with their start and end apart: 15, of which 6 were waited for; matrix products, arithmetic and copies ran while one was open for 1% of the time, Pallas kernels for 4%

profile of v6, /device:TPU:9, one launch (start us, length us, event | category | flops | bytes accessed | tf_op | source)
XLA Modules:
  0.0 114.3 jit_solution(12318643841632960618)
XLA Ops:
  0.6 1.8 %shard_map.68.refs_0_ = bf16[2,768,128]{2,1,0:T(8,128)(2,1)} custom-call(bf16[768,128]{1,0:T(8,128)(2,1)} %field.1, bf16[768,128]{1,0:T(8,128)(2,1)} %backward.1), custom_call_target="tpu_custom_call" | custom-call | tf_op jit(solution)/shard_map/pallas_call | solution.py:206
  2.4 11.1 %collective-permute-start.7 = (bf16[2,768,128]{2,1,0:T(8,128)(2,1)}, bf16[2,768,128]{2,1,0:T(8,128)(2,1)S(1)}, u32[]{:S(2)}, u32[]{:S(2)}) collective-permute-start(bf16[2,768,128]{2,1,0:T(8,128)(2,1)} %shard_map.68.refs_0_), channel_id=1, source_target_pairs={{0,1},{1,2},{2,3},{3,4},{4,5},{5,6},{6,7},{7,8},{8,9},{9,10},{10,1... | collective-permute-start | bytes 1179656 | tf_op jit(solution)/shard_map/ppermute | solution.py:247
  13.6 1.9 %collective-permute-start = (bf16[2,768,128]{2,1,0:T(8,128)(2,1)}, bf16[2,768,128]{2,1,0:T(8,128)(2,1)S(1)}, u32[]{:S(2)}, u32[]{:S(2)}) collective-permute-start(bf16[2,768,128]{2,1,0:T(8,128)(2,1)} %shard_map.68.refs_0_), channel_id=1, source_target_pairs={{0,47},{1,32},{2,33},{3,34},{4,35},{5,36},{6,37},{7,38},{8,39},{9,... | collective-permute-start | bytes 1179656 | tf_op jit(solution)/shard_map/ppermute | solution.py:248
  15.5 4.0 %collective-permute-done.7.refs_1_ = bf16[2,768,128]{2,1,0:T(8,128)(2,1)S(1)} collective-permute-done((bf16[2,768,128]{2,1,0:T(8,128)(2,1)}, bf16[2,768,128]{2,1,0:T(8,128)(2,1)S(1)}, u32[]{:S(2)}, u32[]{:S(2)}) %collective-permute-start.7) | collective-permute-done | bytes 393248 | tf_op jit(solution)/shard_map/ppermute | solution.py:247
  19.5 4.9 %collective-permute-start.8 = (bf16[2,768,128]{2,1,0:T(8,128)(2,1)S(1)}, bf16[2,768,128]{2,1,0:T(8,128)(2,1)S(1)}, u32[]{:S(2)}, u32[]{:S(2)}) collective-permute-start(bf16[2,768,128]{2,1,0:T(8,128)(2,1)S(1)} %collective-permute-done.7.refs_1_), channel_id=1, source_target_pairs={{0,1},{1,2},{2,3},{3,4},{4,5},{5,6},{6,7},{7,8},{8,9},{9,10},{10,1... | collective-permute-start | bytes 1179656 | tf_op jit(solution)/shard_map/ppermute | solution.py:253
  24.4 2.1 %collective-permute-start.1 = (bf16[2,768,128]{2,1,0:T(8,128)(2,1)}, bf16[2,768,128]{2,1,0:T(8,128)(2,1)S(1)}, u32[]{:S(2)}, u32[]{:S(2)}) collective-permute-start(bf16[2,768,128]{2,1,0:T(8,128)(2,1)} %shard_map.68.refs_0_), channel_id=1, source_target_pairs={{0,16},{16,0},{1,17},{17,1},{2,18},{18,2},{3,19},{19,3},{4,20},{20... | collective-permute-start | bytes 1179656 | tf_op jit(solution)/shard_map/ppermute | solution.py:256
  26.5 3.3 %collective-permute-start.2 = (bf16[2,768,128]{2,1,0:T(8,128)(2,1)S(1)}, bf16[2,768,128]{2,1,0:T(8,128)(2,1)S(1)}, u32[]{:S(2)}, u32[]{:S(2)}) collective-permute-start(bf16[2,768,128]{2,1,0:T(8,128)(2,1)S(1)} %collective-permute-done.refs_5_), channel_id=1, source_target_pairs={{0,1},{1,2},{2,3},{3,4},{4,5},{5,6},{6,7},{7,8},{8,9},{9,10},{10,1... | collective-permute-start | bytes 1179656 | tf_op jit(solution)/shard_map/ppermute | solution.py:253
  29.8 4.3 %collective-permute-start.9 = (bf16[2,768,128]{2,1,0:T(8,128)(2,1)S(1)}, bf16[2,768,128]{2,1,0:T(8,128)(2,1)S(1)}, u32[]{:S(2)}, u32[]{:S(2)}) collective-permute-start(bf16[2,768,128]{2,1,0:T(8,128)(2,1)S(1)} %collective-permute-done.8.refs_2_), channel_id=1, source_target_pairs={{0,1},{1,2},{2,3},{3,4},{4,5},{5,6},{6,7},{7,8},{8,9},{9,10},{10,1... | collective-permute-start | bytes 1179656 | tf_op jit(solution)/shard_map/ppermute | solution.py:253
  34.1 2.8 %collective-permute-done.1.refs_8_ = bf16[2,768,128]{2,1,0:T(8,128)(2,1)S(1)} collective-permute-done((bf16[2,768,128]{2,1,0:T(8,128)(2,1)}, bf16[2,768,128]{2,1,0:T(8,128)(2,1)S(1)}, u32[]{:S(2)}, u32[]{:S(2)}) %collective-permute-start.1) | collective-permute-done | bytes 393248 | tf_op jit(solution)/shard_map/ppermute | solution.py:256
  36.9 4.2 %collective-permute-start.3 = (bf16[2,768,128]{2,1,0:T(8,128)(2,1)}, bf16[2,768,128]{2,1,0:T(8,128)(2,1)S(1)}, u32[]{:S(2)}, u32[]{:S(2)}) collective-permute-start(bf16[2,768,128]{2,1,0:T(8,128)(2,1)} %shard_map.68.refs_0_), channel_id=1, source_target_pairs={{0,48},{16,32},{32,16},{48,0},{1,49},{17,33},{33,17},{49,1},{2,50}... | collective-permute-start | bytes 1179656 | tf_op jit(solution)/shard_map/ppermute | solution.py:262
  41.1 3.6 %collective-permute-start.4 = (bf16[2,768,128]{2,1,0:T(8,128)(2,1)S(1)}, bf16[2,768,128]{2,1,0:T(8,128)(2,1)S(1)}, u32[]{:S(2)}, u32[]{:S(2)}) collective-permute-start(bf16[2,768,128]{2,1,0:T(8,128)(2,1)S(1)} %collective-permute-done.2.refs_6_), channel_id=1, source_target_pairs={{0,1},{1,2},{2,3},{3,4},{4,5},{5,6},{6,7},{7,8},{8,9},{9,10},{10,1... | collective-permute-start | bytes 1179656 | tf_op jit(solution)/shard_map/ppermute | solution.py:253
  44.7 1.9 %collective-permute-start.10 = (bf16[2,768,128]{2,1,0:T(8,128)(2,1)}, bf16[2,768,128]{2,1,0:T(8,128)(2,1)}, u32[]{:S(2)}, u32[]{:S(2)}) collective-permute-start(bf16[2,768,128]{2,1,0:T(8,128)(2,1)} %shard_map.68.refs_0_), channel_id=1, source_target_pairs={{0,32},{32,0},{1,33},{33,1},{2,34},{34,2},{3,35},{35,3},{4,36},{36... | collective-permute-start | bytes 1179656 | tf_op jit(solution)/shard_map/ppermute | solution.py:264
  46.7 2.9 %collective-permute-start.11 = (bf16[2,768,128]{2,1,0:T(8,128)(2,1)S(1)}, bf16[2,768,128]{2,1,0:T(8,128)(2,1)S(1)}, u32[]{:S(2)}, u32[]{:S(2)}) collective-permute-start(bf16[2,768,128]{2,1,0:T(8,128)(2,1)S(1)} %collective-permute-done.9.refs_3_), channel_id=1, source_target_pairs={{0,1},{1,2},{2,3},{3,4},{4,5},{5,6},{6,7},{7,8},{8,9},{9,10},{10,1... | collective-permute-start | bytes 1179656 | tf_op jit(solution)/shard_map/ppermute | solution.py:253
  49.6 1.5 %collective-permute-done.3.refs_9_ = bf16[2,768,128]{2,1,0:T(8,128)(2,1)S(1)} collective-permute-done((bf16[2,768,128]{2,1,0:T(8,128)(2,1)}, bf16[2,768,128]{2,1,0:T(8,128)(2,1)S(1)}, u32[]{:S(2)}, u32[]{:S(2)}) %collective-permute-start.3) | collective-permute-done | bytes 393248 | tf_op jit(solution)/shard_map/ppermute | solution.py:262
  51.1 0.8 copy-done.1
  51.9 3.5 %collective-permute-start.5 = (bf16[2,768,128]{2,1,0:T(8,128)(2,1)S(1)}, bf16[2,768,128]{2,1,0:T(8,128)(2,1)S(1)}, u32[]{:S(2)}, u32[]{:S(2)}) collective-permute-start(bf16[2,768,128]{2,1,0:T(8,128)(2,1)S(1)} %collective-permute-done.4.refs_7_), channel_id=1, source_target_pairs={{0,1},{1,2},{2,3},{3,4},{4,5},{5,6},{6,7},{7,8},{8,9},{9,10},{10,1... | collective-permute-start | bytes 1179656 | tf_op jit(solution)/shard_map/ppermute | solution.py:253
  55.5 1.0 copy-done
  56.5 1.0 copy-done.2
  57.5 0.7 copy-done.3
  58.1 3.2 %shard_map.69 = (bf16[8,272,128]{2,1,0:T(8,128)(2,1)S(1)}, bf16[2,1536,128]{2,1,0:T(8,128)(2,1)S(1)}, bf16[2,1536,512]{2,1,0:T(8,128)(2,1)S(1)}) custom-call(s32[4]{0:T(128)S(1)} %pad_add_fusion.place, f32[8]{0:T(128)S(1)} %copy-done.3, bf16[2,768,128]{2,1,0:T(8,128)(2,1)S(1)} %copy-done, bf16[2,768,128]{2,1,0:T(8,128)(2,1)S(1)} %collective-permute-done.7.refs_1_, ...), custom_call_target="tpu_custom_call" | custom-call | flops 402653184 | bytes 2752512 | tf_op jit(solution)/shard_map/pallas_call | solution.py:232
  61.3 1.9 %collective-permute-start.12 = (bf16[2,768,128]{2,1,0:T(8,128)(2,1)S(1)}, bf16[2,768,128]{2,1,0:T(8,128)(2,1)S(1)}, u32[]{:S(2)}, u32[]{:S(2)}) collective-permute-start(bf16[2,768,128]{2,1,0:T(8,128)(2,1)S(1)} %collective-permute-done.11.first), channel_id=1, source_target_pairs={{0,32},{16,48},{32,16},{48,0},{1,33},{17,49},{33,17},{49,1},{2,34}... | collective-permute-start | bytes 1179656 | tf_op jit(solution)/shard_map/ppermute | solution.py:278
  63.3 2.0 %collective-permute-start.6 = (bf16[2,768,128]{2,1,0:T(8,128)(2,1)S(1)}, bf16[2,768,128]{2,1,0:T(8,128)(2,1)S(1)}, u32[]{:S(2)}, u32[]{:S(2)}) collective-permute-start(bf16[2,768,128]{2,1,0:T(8,128)(2,1)S(1)} %collective-permute-done.5.second), channel_id=1, source_target_pairs={{0,32},{16,48},{32,16},{48,0},{1,33},{17,49},{33,17},{49,1},{2,34}... | collective-permute-start | bytes 1179656 | tf_op jit(solution)/shard_map/ppermute | solution.py:278
  65.3 2.7 %collective-permute-done.12.far = bf16[2,768,128]{2,1,0:T(8,128)(2,1)S(1)} collective-permute-done((bf16[2,768,128]{2,1,0:T(8,128)(2,1)S(1)}, bf16[2,768,128]{2,1,0:T(8,128)(2,1)S(1)}, u32[]{:S(2)}, u32[]{:S(2)}) %collective-permute-start.12) | collective-permute-done | bytes 393248 | tf_op jit(solution)/shard_map/ppermute | solution.py:278
  68.0 1.3 %shard_map.70 = (bf16[8,272,128]{2,1,0:T(8,128)(2,1)S(1)}, bf16[2,1536,512]{2,1,0:T(8,128)(2,1)S(1)}, f32[2,128,512]{2,1,0:T(8,128)S(1)}) custom-call(s32[4]{0:T(128)S(1)} %pad_add_fusion.place, f32[8]{0:T(128)S(1)} %copy-done.3, bf16[2,768,128]{2,1,0:T(8,128)(2,1)S(1)} %collective-permute-done.11.first, ...), custom_call_target="tpu_custom_call", output_to_operand_aliasing={{0}: (6, {}), {1}: (7, {})} | custom-call | flops 301989888 | bytes 2752512 | tf_op jit(solution)/shard_map/pallas_call | solution.py:232
  69.2 2.9 %collective-permute-done.6.far = bf16[2,768,128]{2,1,0:T(8,128)(2,1)S(1)} collective-permute-done((bf16[2,768,128]{2,1,0:T(8,128)(2,1)S(1)}, bf16[2,768,128]{2,1,0:T(8,128)(2,1)S(1)}, u32[]{:S(2)}, u32[]{:S(2)}) %collective-permute-start.6) | collective-permute-done | bytes 393248 | tf_op jit(solution)/shard_map/ppermute | solution.py:278
  72.2 1.1 shard_map.71
  73.3 16.2 %all_to_all.5 = bf16[8,272,128]{2,1,0:T(8,128)(2,1)S(1)} all-to-all(bf16[8,272,128]{2,1,0:T(8,128)(2,1)S(1)} %shard_map.71), channel_id=1, replica_groups=mesh['yh'=2,'x'=4,'c'=2,'yl'=2,'z'=16] {'yh','x'}, dimensions={0} | all-to-all | bytes 1114112 | tf_op jit(solution)/shard_map/all_to_all | solution.py:288
  89.7 7.4 %collective-permute-start.13 = (f32[264,128]{1,0:T(8,128)S(1)}, f32[264,128]{1,0:T(8,128)S(1)}, u32[]{:S(2)}, u32[]{:S(2)}) collective-permute-start(f32[264,128]{1,0:T(8,128)S(1)} %slice.4), channel_id=1, source_target_pairs={{0,244},{1,21},{2,22},{3,55},{4,56},{5,89},{6,90},{7,123},{8,124},... | collective-permute-start | bytes 405512 | tf_op jit(solution)/shard_map/ppermute | solution.py:293
  97.1 7.6 %collective-permute-start.14 = (f32[264,128]{1,0:T(8,128)S(1)}, f32[264,128]{1,0:T(8,128)S(1)}, u32[]{:S(2)}, u32[]{:S(2)}) collective-permute-start(f32[264,128]{1,0:T(8,128)S(1)} %slice.4), channel_id=1, source_target_pairs={{0,335},{1,320},{2,353},{3,354},{4,387},{5,388},{6,421},{7,422},{8... | collective-permute-start | bytes 405512 | tf_op jit(solution)/shard_map/ppermute | solution.py:294
  104.7 0.7 dynamic-slice_bitcast_fusion.todo
  105.4 7.5 %collective-permute-done.14.b = f32[264,128]{1,0:T(8,128)S(1)} collective-permute-done((f32[264,128]{1,0:T(8,128)S(1)}, f32[264,128]{1,0:T(8,128)S(1)}, u32[]{:S(2)}, u32[]{:S(2)}) %collective-permute-start.14) | collective-permute-done | bytes 135200 | tf_op jit(solution)/shard_map/ppermute | solution.py:294
  112.9 1.4 %shard_map.72 = (f32[128,256]{1,0:T(8,128)}, f32[128,256]{1,0:T(8,128)}) custom-call(s32[4]{0:T(128)S(1)} %dynamic-slice_bitcast_fusion.todo, f32[264,128]{1,0:T(8,128)S(1)} %collective-permute-done.13.a, f32[264,128]{1,0:T(8,128)S(1)} %collective-permute-done.14.b), custom_call_target="tpu_custom_call" | custom-call | tf_op jit(solution)/shard_map/pallas_call | solution.py:299
  (18 shorter events, 0.3 us)
Async XLA Ops:
  2.4 17.1 %collective-permute-start.7 = (bf16[2,768,128]{2,1,0:T(8,128)(2,1)}, bf16[2,768,128]{2,1,0:T(8,128)(2,1)S(1)}, u32[]{:S(2)}, u32[]{:S(2)}) collective-permute-start(bf16[2,768,128]{2,1,0:T(8,128)(2,1)} %shard_map.68.refs_0_), channel_id=1, source_target_pairs={{0,1},{1,2},{2,3},{3,4},{4,5},{5,6},{6,7},{7,8},{8,9},{9,10},{10,1... | collective-permute-start | bytes 1179656 | tf_op jit(solution)/shard_map/ppermute | solution.py:247
  13.6 10.9 %collective-permute-start = (bf16[2,768,128]{2,1,0:T(8,128)(2,1)}, bf16[2,768,128]{2,1,0:T(8,128)(2,1)S(1)}, u32[]{:S(2)}, u32[]{:S(2)}) collective-permute-start(bf16[2,768,128]{2,1,0:T(8,128)(2,1)} %shard_map.68.refs_0_), channel_id=1, source_target_pairs={{0,47},{1,32},{2,33},{3,34},{4,35},{5,36},{6,37},{7,38},{8,39},{9,... | collective-permute-start | bytes 1179656 | tf_op jit(solution)/shard_map/ppermute | solution.py:248
  19.5 10.3 %collective-permute-start.8 = (bf16[2,768,128]{2,1,0:T(8,128)(2,1)S(1)}, bf16[2,768,128]{2,1,0:T(8,128)(2,1)S(1)}, u32[]{:S(2)}, u32[]{:S(2)}) collective-permute-start(bf16[2,768,128]{2,1,0:T(8,128)(2,1)S(1)} %collective-permute-done.7.refs_1_), channel_id=1, source_target_pairs={{0,1},{1,2},{2,3},{3,4},{4,5},{5,6},{6,7},{7,8},{8,9},{9,10},{10,1... | collective-permute-start | bytes 1179656 | tf_op jit(solution)/shard_map/ppermute | solution.py:253
  24.4 12.5 %collective-permute-start.1 = (bf16[2,768,128]{2,1,0:T(8,128)(2,1)}, bf16[2,768,128]{2,1,0:T(8,128)(2,1)S(1)}, u32[]{:S(2)}, u32[]{:S(2)}) collective-permute-start(bf16[2,768,128]{2,1,0:T(8,128)(2,1)} %shard_map.68.refs_0_), channel_id=1, source_target_pairs={{0,16},{16,0},{1,17},{17,1},{2,18},{18,2},{3,19},{19,3},{4,20},{20... | collective-permute-start | bytes 1179656 | tf_op jit(solution)/shard_map/ppermute | solution.py:256
  26.5 10.4 %collective-permute-start.2 = (bf16[2,768,128]{2,1,0:T(8,128)(2,1)S(1)}, bf16[2,768,128]{2,1,0:T(8,128)(2,1)S(1)}, u32[]{:S(2)}, u32[]{:S(2)}) collective-permute-start(bf16[2,768,128]{2,1,0:T(8,128)(2,1)S(1)} %collective-permute-done.refs_5_), channel_id=1, source_target_pairs={{0,1},{1,2},{2,3},{3,4},{4,5},{5,6},{6,7},{7,8},{8,9},{9,10},{10,1... | collective-permute-start | bytes 1179656 | tf_op jit(solution)/shard_map/ppermute | solution.py:253
  29.8 16.9 %collective-permute-start.9 = (bf16[2,768,128]{2,1,0:T(8,128)(2,1)S(1)}, bf16[2,768,128]{2,1,0:T(8,128)(2,1)S(1)}, u32[]{:S(2)}, u32[]{:S(2)}) collective-permute-start(bf16[2,768,128]{2,1,0:T(8,128)(2,1)S(1)} %collective-permute-done.8.refs_2_), channel_id=1, source_target_pairs={{0,1},{1,2},{2,3},{3,4},{4,5},{5,6},{6,7},{7,8},{8,9},{9,10},{10,1... | collective-permute-start | bytes 1179656 | tf_op jit(solution)/shard_map/ppermute | solution.py:253
  36.9 14.2 %collective-permute-start.3 = (bf16[2,768,128]{2,1,0:T(8,128)(2,1)}, bf16[2,768,128]{2,1,0:T(8,128)(2,1)S(1)}, u32[]{:S(2)}, u32[]{:S(2)}) collective-permute-start(bf16[2,768,128]{2,1,0:T(8,128)(2,1)} %shard_map.68.refs_0_), channel_id=1, source_target_pairs={{0,48},{16,32},{32,16},{48,0},{1,49},{17,33},{33,17},{49,1},{2,50}... | collective-permute-start | bytes 1179656 | tf_op jit(solution)/shard_map/ppermute | solution.py:262
  41.1 10.8 %collective-permute-start.4 = (bf16[2,768,128]{2,1,0:T(8,128)(2,1)S(1)}, bf16[2,768,128]{2,1,0:T(8,128)(2,1)S(1)}, u32[]{:S(2)}, u32[]{:S(2)}) collective-permute-start(bf16[2,768,128]{2,1,0:T(8,128)(2,1)S(1)} %collective-permute-done.2.refs_6_), channel_id=1, source_target_pairs={{0,1},{1,2},{2,3},{3,4},{4,5},{5,6},{6,7},{7,8},{8,9},{9,10},{10,1... | collective-permute-start | bytes 1179656 | tf_op jit(solution)/shard_map/ppermute | solution.py:253
  44.7 10.7 %collective-permute-start.10 = (bf16[2,768,128]{2,1,0:T(8,128)(2,1)}, bf16[2,768,128]{2,1,0:T(8,128)(2,1)}, u32[]{:S(2)}, u32[]{:S(2)}) collective-permute-start(bf16[2,768,128]{2,1,0:T(8,128)(2,1)} %shard_map.68.refs_0_), channel_id=1, source_target_pairs={{0,32},{32,0},{1,33},{33,1},{2,34},{34,2},{3,35},{35,3},{4,36},{36... | collective-permute-start | bytes 1179656 | tf_op jit(solution)/shard_map/ppermute | solution.py:264
  46.7 14.6 %collective-permute-start.11 = (bf16[2,768,128]{2,1,0:T(8,128)(2,1)S(1)}, bf16[2,768,128]{2,1,0:T(8,128)(2,1)S(1)}, u32[]{:S(2)}, u32[]{:S(2)}) collective-permute-start(bf16[2,768,128]{2,1,0:T(8,128)(2,1)S(1)} %collective-permute-done.9.refs_3_), channel_id=1, source_target_pairs={{0,1},{1,2},{2,3},{3,4},{4,5},{5,6},{6,7},{7,8},{8,9},{9,10},{10,1... | collective-permute-start | bytes 1179656 | tf_op jit(solution)/shard_map/ppermute | solution.py:253
  51.1 0.8 copy-start.1
  51.9 11.4 %collective-permute-start.5 = (bf16[2,768,128]{2,1,0:T(8,128)(2,1)S(1)}, bf16[2,768,128]{2,1,0:T(8,128)(2,1)S(1)}, u32[]{:S(2)}, u32[]{:S(2)}) collective-permute-start(bf16[2,768,128]{2,1,0:T(8,128)(2,1)S(1)} %collective-permute-done.4.refs_7_), channel_id=1, source_target_pairs={{0,1},{1,2},{2,3},{3,4},{4,5},{5,6},{6,7},{7,8},{8,9},{9,10},{10,1... | collective-permute-start | bytes 1179656 | tf_op jit(solution)/shard_map/ppermute | solution.py:253
  55.5 1.0 copy-start
  56.5 1.0 copy-start.2
  57.5 0.7 copy-start.3
  61.3 6.6 %collective-permute-start.12 = (bf16[2,768,128]{2,1,0:T(8,128)(2,1)S(1)}, bf16[2,768,128]{2,1,0:T(8,128)(2,1)S(1)}, u32[]{:S(2)}, u32[]{:S(2)}) collective-permute-start(bf16[2,768,128]{2,1,0:T(8,128)(2,1)S(1)} %collective-permute-done.11.first), channel_id=1, source_target_pairs={{0,32},{16,48},{32,16},{48,0},{1,33},{17,49},{33,17},{49,1},{2,34}... | collective-permute-start | bytes 1179656 | tf_op jit(solution)/shard_map/ppermute | solution.py:278
  63.3 8.9 %collective-permute-start.6 = (bf16[2,768,128]{2,1,0:T(8,128)(2,1)S(1)}, bf16[2,768,128]{2,1,0:T(8,128)(2,1)S(1)}, u32[]{:S(2)}, u32[]{:S(2)}) collective-permute-start(bf16[2,768,128]{2,1,0:T(8,128)(2,1)S(1)} %collective-permute-done.5.second), channel_id=1, source_target_pairs={{0,32},{16,48},{32,16},{48,0},{1,33},{17,49},{33,17},{49,1},{2,34}... | collective-permute-start | bytes 1179656 | tf_op jit(solution)/shard_map/ppermute | solution.py:278
  73.3 16.2 %copy-start.4 = (f32[8]{0:T(128)S(1)}, f32[8]{0:T(128)}, u32[]{:S(2)}) copy-start(f32[8]{0:T(128)} %constant.51) | copy-start | bytes 100
  89.7 15.7 %collective-permute-start.13 = (f32[264,128]{1,0:T(8,128)S(1)}, f32[264,128]{1,0:T(8,128)S(1)}, u32[]{:S(2)}, u32[]{:S(2)}) collective-permute-start(f32[264,128]{1,0:T(8,128)S(1)} %slice.4), channel_id=1, source_target_pairs={{0,244},{1,21},{2,22},{3,55},{4,56},{5,89},{6,90},{7,123},{8,124},... | collective-permute-start | bytes 405512 | tf_op jit(solution)/shard_map/ppermute | solution.py:293
  97.1 15.8 %collective-permute-start.14 = (f32[264,128]{1,0:T(8,128)S(1)}, f32[264,128]{1,0:T(8,128)S(1)}, u32[]{:S(2)}, u32[]{:S(2)}) collective-permute-start(f32[264,128]{1,0:T(8,128)S(1)} %slice.4), channel_id=1, source_target_pairs={{0,335},{1,320},{2,353},{3,354},{4,387},{5,388},{6,421},{7,422},{8... | collective-permute-start | bytes 405512 | tf_op jit(solution)/shard_map/ppermute | solution.py:294

commit v7 on v6

--- a/solution.py
+++ b/solution.py
@@ -28,13 +28,17 @@
 def homes(yh, x, c, yl, z):
     slot = yh * 4 + x
     if c == 0:
-        left, right = (1 - yl, z if slot > 3 else z + 4), (yl, z - slot % 4 - 1)
+        left = (yl, z) if slot > 3 else (1 - yl, z + 4)
+        right = (yl, z - slot % 4 - 1)
         if slot == 3 and yl == 1:
-            left, right = (0, z), (1, z)
+            right = (yl, z)
     else:
-        left, right = (yl, z if slot > 3 else z - 4), (yl, z + slot % 4 + 1)
+        left = (1 - yl, z) if slot > 3 else (yl, z - 4)
+        right = (yl, z + slot % 4 + 1)
         if slot == 3 and (z < 8) != (yl == 0):
             return [home(0, z, 0, z) + (2,), home(1, z, 1, z) + (3,)]
+        if slot == 7 and yl == 0:
+            right = (yl, z)
     left, right = (left[0], left[1] % 16), (right[0], right[1] % 16)
     return [home(*left, *right) + (0,), home(*right, *left) + (1,)]
 
@@ -103,13 +107,13 @@
 
 def cases(place):
     core, y, z = place[0], place[1], place[2]
-    return (core == 1) & ((z < 8) != (y == 0)), (core == 0) & (y == 1)
+    return (core == 1) & ((z < 8) != (y == 0)), (core == 1) & (y == 0), (core == 0) & (y == 1)
 
 
 def early_kernel(place, scales, *refs):
     first, second, near, (out, left, steps) = refs[0:4], refs[4:8], refs[8:10], refs[10:]
     core, y, scale = place[0], place[1], scales[place[3]]
-    packed, partner = cases(place)
+    packed, same, _ = cases(place)
     n = out.shape[-1]
     rows = near[0].shape[1]
     for slot in range(8):
@@ -128,18 +132,18 @@
 
         @pl.when(core == 0)
         def _():
+            left[kernel] = own()
+
+        @pl.when(core == 1)
+        def _():
             left[kernel] = other()
-
-        @pl.when(core == 1)
-        def _():
-            left[kernel] = own()
 
         total = product(left[kernel], steps[kernel, :, 0 : 3 * n])
         store(out, scale, 4, kernel, total)
 
-        @pl.when(partner)
-        def _():
-            store(out, scale, 3, kernel, product(other(), own()))
+        @pl.when(same)
+        def _():
+            store(out, scale, 7, kernel, product(other(), own()))
 
         @pl.when(packed)
         def _():
@@ -158,26 +162,37 @@
 
 def middle_kernel(place, scales, first, second, far, left, _, __, out, steps, total):
     scale = scales[place[3]]
+    _, same, turned = cases(place)
     n = out.shape[-1]
     rows = far.shape[1]
     for kernel in range(2):
-        for i, chain in enumerate((first, second)):
-            steps[kernel, i * rows : (i + 1) * rows, 3 * n :] = chain[kernel]
+        last = jnp.concatenate([first[kernel], second[kernel]], axis=0)
+
+        @pl.when(jnp.logical_not(same))
+        def _():
+            store(out, scale, 7, kernel, product(left[kernel], last))
+
+        @pl.when(turned)
+        def _():
+            steps[kernel, :, 3 * n :] = left[kernel]
+
+        @pl.when(jnp.logical_not(turned))
+        def _():
+            steps[kernel, :, 3 * n :] = last
+
         total[kernel] = product(far[kernel], steps[kernel, rows:])
-        last = product(left[kernel], steps[kernel, :, 3 * n :])
-        store(out, scale, 7, kernel, last)
 
 
 def late_kernel(place, scales, far, steps, part, _, out):
     scale = scales[place[3]]
-    packed, partner = cases(place)
+    packed, _, _ = cases(place)
     n = out.shape[-1]
     rows = far.shape[1]
     for kernel in range(2):
         total = part[kernel] + product(far[kernel], steps[kernel, 0:rows])
         store(out, scale, 0, kernel, total[:, : 3 * n])
 
-        @pl.when(jnp.logical_not(packed | partner))
+        @pl.when(jnp.logical_not(packed))
         def _():
             store(out, scale, 3, kernel, total[:, 3 * n :])
 
@@ -252,16 +267,14 @@
         if j:
             chains = [lax.ppermute(chain, ("c", "z"), step) for chain in chains]
         if j == 0:
+            other = lax.ppermute(both, "c", [(0, 1), (1, 0)])
+            other, chains[1] = lax.optimization_barrier((other, chains[1]))
             own, chains[1] = lax.optimization_barrier((both, chains[1]))
-            near = [lax.ppermute(own, "yl", [(0, 1), (1, 0)])]
+            near = [lax.ppermute(own, ("c", "yl"), [(2, 3), (3, 2)])]
         if j == 1:
-            own, near[0], chains[1] = lax.optimization_barrier(
-                (own, near[0], chains[1])
-            )
-            near.append(
-                lax.ppermute(own, ("c", "yl"), [(0, 3), (1, 2), (2, 1), (3, 0)])
-            )
-            other = lax.ppermute(own, "c", [(0, 1), (1, 0)])
+            own, chains[1] = lax.optimization_barrier((both, chains[1]))
+            near.append(lax.ppermute(own, ("c", "yl"), [(0, 3), (1, 2)]))
+            near[0], chains[1] = lax.optimization_barrier((near[0], chains[1]))
         if j == 2:
             near[1], chains[1] = lax.optimization_barrier((near[1], chains[1]))
         if j == 3:
@@ -271,7 +284,7 @@
                 *(both, *walk[0], other, *walk[1], *near),
                 flops=4,
             )
-            partial, chains[0] = lax.optimization_barrier((partial, chains[0]))
+            partial, chains[1] = lax.optimization_barrier((partial, chains[1]))
         for chain, blocks in zip(chains, walk):
             blocks.append(chain)
     cross = [(0, 2), (1, 3), (2, 1), (3, 0)]

time: 115 us -> 110 us (0.957)
  the two profiles are of different devices: /device:TPU:9 before, /device:TPU:7 now
where the time goes in v7:
time: 110 us; the launch traced here: 109 us
  starting transfers between devices  64.7 us (59%)
  waiting for transfers between devices  15.7 us (14%)
  blocking collectives  14.7 us (13%)
  Pallas kernels  8.62 us (8%)
  local copies, waits for them, and re-layouts  4.11 us (4%)
    ppermute x6, starting transfers between devices, on_device(): chains = [lax.ppermute(chain, ('c', 'z'), step) for chain in chains]  22 us
    all_to_all x1, blocking collectives, on_device(): partial = lax.all_to_all(partial, ('yh', 'x'), 0, 0, tiled=True)  14.7 us
    ppermute x1, starting transfers between devices, on_device(): lax.ppermute(both, ('c', 'z'), step)  11.1 us
    ppermute x1, starting transfers between devices, on_device(): b = lax.ppermute(block, AXES, perms[1])  10.9 us
    ppermute x2, starting transfers between devices, on_device(): far = [lax.ppermute(chain, ('c', 'yl'), cross) for chain in chains]  6.48 us
    pallas_call x3, Pallas kernels, call(): pl.pallas_call(kernel, out_shape=out_shape, in_specs=[SMEM, SMEM] + [VMEM...  5.44 us
    ppermute x1, starting transfers between devices, on_device(): a = lax.ppermute(block, AXES, perms[0])  4.74 us
    unnamed x10, local copies, waits for them, and re-layouts  3.4 us
  transfers between devices with their start and end apart: 15, of which 7 were waited for; matrix products, arithmetic and copies ran while one was open for 1% of the time, Pallas kernels for 4%

profile of v7, /device:TPU:7, one launch (start us, length us, event | category | flops | bytes accessed | tf_op | source)
XLA Modules:
  0.0 109.0 jit_solution(12620501385468118183)
XLA Ops:
  0.6 1.8 %shard_map.68.refs_0_ = bf16[2,768,128]{2,1,0:T(8,128)(2,1)} custom-call(bf16[768,128]{1,0:T(8,128)(2,1)} %field.1, bf16[768,128]{1,0:T(8,128)(2,1)} %backward.1), custom_call_target="tpu_custom_call" | custom-call | tf_op jit(solution)/shard_map/pallas_call | solution.py:221
  2.4 11.1 %collective-permute-start = (bf16[2,768,128]{2,1,0:T(8,128)(2,1)}, bf16[2,768,128]{2,1,0:T(8,128)(2,1)S(1)}, u32[]{:S(2)}, u32[]{:S(2)}) collective-permute-start(bf16[2,768,128]{2,1,0:T(8,128)(2,1)} %shard_map.68.refs_0_), channel_id=1, source_target_pairs={{0,1},{1,2},{2,3},{3,4},{4,5},{5,6},{6,7},{7,8},{8,9},{9,10},{10,1... | collective-permute-start | bytes 1179656 | tf_op jit(solution)/shard_map/ppermute | solution.py:262
  13.6 1.9 %collective-permute-start.4 = (bf16[2,768,128]{2,1,0:T(8,128)(2,1)}, bf16[2,768,128]{2,1,0:T(8,128)(2,1)S(1)}, u32[]{:S(2)}, u32[]{:S(2)}) collective-permute-start(bf16[2,768,128]{2,1,0:T(8,128)(2,1)} %shard_map.68.refs_0_), channel_id=1, source_target_pairs={{0,47},{1,32},{2,33},{3,34},{4,35},{5,36},{6,37},{7,38},{8,39},{9,... | collective-permute-start | bytes 1179656 | tf_op jit(solution)/shard_map/ppermute | solution.py:263
  15.5 3.0 %collective-permute-start.3 = (bf16[2,768,128]{2,1,0:T(8,128)(2,1)}, bf16[2,768,128]{2,1,0:T(8,128)(2,1)S(1)}, u32[]{:S(2)}, u32[]{:S(2)}) collective-permute-start(bf16[2,768,128]{2,1,0:T(8,128)(2,1)} %shard_map.68.refs_0_), channel_id=1, source_target_pairs={{0,32},{32,0},{1,33},{33,1},{2,34},{34,2},{3,35},{35,3},{4,36},{36... | collective-permute-start | bytes 1179656 | tf_op jit(solution)/shard_map/ppermute | solution.py:270
  18.5 1.0 collective-permute-done.refs_1_
  19.5 4.9 %collective-permute-start.1 = (bf16[2,768,128]{2,1,0:T(8,128)(2,1)S(1)}, bf16[2,768,128]{2,1,0:T(8,128)(2,1)S(1)}, u32[]{:S(2)}, u32[]{:S(2)}) collective-permute-start(bf16[2,768,128]{2,1,0:T(8,128)(2,1)S(1)} %collective-permute-done.refs_1_), channel_id=1, source_target_pairs={{0,1},{1,2},{2,3},{3,4},{4,5},{5,6},{6,7},{7,8},{8,9},{9,10},{10,1... | collective-permute-start | bytes 1179656 | tf_op jit(solution)/shard_map/ppermute | solution.py:268
  24.4 3.3 %collective-permute-start.6 = (bf16[2,768,128]{2,1,0:T(8,128)(2,1)S(1)}, bf16[2,768,128]{2,1,0:T(8,128)(2,1)S(1)}, u32[]{:S(2)}, u32[]{:S(2)}) collective-permute-start(bf16[2,768,128]{2,1,0:T(8,128)(2,1)S(1)} %collective-permute-done.4.refs_5_), channel_id=1, source_target_pairs={{0,1},{1,2},{2,3},{3,4},{4,5},{5,6},{6,7},{7,8},{8,9},{9,10},{10,1... | collective-permute-start | bytes 1179656 | tf_op jit(solution)/shard_map/ppermute | solution.py:268
  27.7 3.2 %collective-permute-start.5 = (bf16[2,768,128]{2,1,0:T(8,128)(2,1)}, bf16[2,768,128]{2,1,0:T(8,128)(2,1)S(1)}, u32[]{:S(2)}, u32[]{:S(2)}) collective-permute-start(bf16[2,768,128]{2,1,0:T(8,128)(2,1)} %shard_map.68.refs_0_), channel_id=1, source_target_pairs={{32,48},{48,32},{33,49},{49,33},{34,50},{50,34},{35,51},{51,35},{3... | collective-permute-start | bytes 1179656 | tf_op jit(solution)/shard_map/ppermute | solution.py:273
  30.9 3.2 %collective-permute-start.2 = (bf16[2,768,128]{2,1,0:T(8,128)(2,1)S(1)}, bf16[2,768,128]{2,1,0:T(8,128)(2,1)S(1)}, u32[]{:S(2)}, u32[]{:S(2)}) collective-permute-start(bf16[2,768,128]{2,1,0:T(8,128)(2,1)S(1)} %collective-permute-done.1.refs_2_), channel_id=1, source_target_pairs={{0,1},{1,2},{2,3},{3,4},{4,5},{5,6},{6,7},{7,8},{8,9},{9,10},{10,1... | collective-permute-start | bytes 1179656 | tf_op jit(solution)/shard_map/ppermute | solution.py:268
  34.2 2.6 %collective-permute-done.5.refs_8_ = bf16[2,768,128]{2,1,0:T(8,128)(2,1)S(1)} collective-permute-done((bf16[2,768,128]{2,1,0:T(8,128)(2,1)}, bf16[2,768,128]{2,1,0:T(8,128)(2,1)S(1)}, u32[]{:S(2)}, u32[]{:S(2)}) %collective-permute-start.5) | collective-permute-done | bytes 393248 | tf_op jit(solution)/shard_map/ppermute | solution.py:273
  36.7 1.9 %collective-permute-start.8 = (bf16[2,768,128]{2,1,0:T(8,128)(2,1)S(1)}, bf16[2,768,128]{2,1,0:T(8,128)(2,1)S(1)}, u32[]{:S(2)}, u32[]{:S(2)}) collective-permute-start(bf16[2,768,128]{2,1,0:T(8,128)(2,1)S(1)} %collective-permute-done.6.refs_6_), channel_id=1, source_target_pairs={{0,1},{1,2},{2,3},{3,4},{4,5},{5,6},{6,7},{7,8},{8,9},{9,10},{10,1... | collective-permute-start | bytes 1179656 | tf_op jit(solution)/shard_map/ppermute | solution.py:268
  38.7 1.3 %collective-permute-start.7 = (bf16[2,768,128]{2,1,0:T(8,128)(2,1)}, bf16[2,768,128]{2,1,0:T(8,128)(2,1)S(1)}, u32[]{:S(2)}, u32[]{:S(2)}) collective-permute-start(bf16[2,768,128]{2,1,0:T(8,128)(2,1)} %shard_map.68.refs_0_), channel_id=1, source_target_pairs={{0,48},{16,32},{1,49},{17,33},{2,50},{18,34},{3,51},{19,35},{4,52}... | collective-permute-start | bytes 1179656 | tf_op jit(solution)/shard_map/ppermute | solution.py:276
  40.0 3.9 %collective-permute-start.11 = (bf16[2,768,128]{2,1,0:T(8,128)(2,1)S(1)}, bf16[2,768,128]{2,1,0:T(8,128)(2,1)S(1)}, u32[]{:S(2)}, u32[]{:S(2)}) collective-permute-start(bf16[2,768,128]{2,1,0:T(8,128)(2,1)S(1)} %collective-permute-done.2.refs_3_), channel_id=1, source_target_pairs={{0,1},{1,2},{2,3},{3,4},{4,5},{5,6},{6,7},{7,8},{8,9},{9,10},{10,1... | collective-permute-start | bytes 1179656 | tf_op jit(solution)/shard_map/ppermute | solution.py:268
  43.9 1.7 %collective-permute-done.8.refs_7_ = bf16[2,768,128]{2,1,0:T(8,128)(2,1)S(1)} collective-permute-done((bf16[2,768,128]{2,1,0:T(8,128)(2,1)S(1)}, bf16[2,768,128]{2,1,0:T(8,128)(2,1)S(1)}, u32[]{:S(2)}, u32[]{:S(2)}) %collective-permute-start.8) | collective-permute-done | bytes 393248 | tf_op jit(solution)/shard_map/ppermute | solution.py:268
  45.5 2.7 %collective-permute-done.7.refs_9_ = bf16[2,768,128]{2,1,0:T(8,128)(2,1)S(1)} collective-permute-done((bf16[2,768,128]{2,1,0:T(8,128)(2,1)}, bf16[2,768,128]{2,1,0:T(8,128)(2,1)S(1)}, u32[]{:S(2)}, u32[]{:S(2)}) %collective-permute-start.7) | collective-permute-done | bytes 393248 | tf_op jit(solution)/shard_map/ppermute | solution.py:276
  48.3 0.8 copy-done.1
  49.0 4.8 %collective-permute-start.9 = (bf16[2,768,128]{2,1,0:T(8,128)(2,1)S(1)}, bf16[2,768,128]{2,1,0:T(8,128)(2,1)}, u32[]{:S(2)}, u32[]{:S(2)}) collective-permute-start(bf16[2,768,128]{2,1,0:T(8,128)(2,1)S(1)} %collective-permute-done.8.refs_7_), channel_id=1, source_target_pairs={{0,1},{1,2},{2,3},{3,4},{4,5},{5,6},{6,7},{7,8},{8,9},{9,10},{10,1... | collective-permute-start | bytes 1179656 | tf_op jit(solution)/shard_map/ppermute | solution.py:268
  54.0 4.6 %collective-permute-start.12 = (bf16[2,768,128]{2,1,0:T(8,128)(2,1)S(1)}, bf16[2,768,128]{2,1,0:T(8,128)(2,1)S(1)}, u32[]{:S(2)}, u32[]{:S(2)}) collective-permute-start(bf16[2,768,128]{2,1,0:T(8,128)(2,1)S(1)} %collective-permute-done.11.first), channel_id=1, source_target_pairs={{0,32},{16,48},{32,16},{48,0},{1,33},{17,49},{33,17},{49,1},{2,34}... | collective-permute-start | bytes 1179656 | tf_op jit(solution)/shard_map/ppermute | solution.py:291
  58.5 1.0 copy-done
  59.5 1.0 copy-done.2
  61.2 2.5 %shard_map.69 = (bf16[8,272,128]{2,1,0:T(8,128)(2,1)S(1)}, bf16[2,1536,128]{2,1,0:T(8,128)(2,1)S(1)}, bf16[2,1536,512]{2,1,0:T(8,128)(2,1)S(1)}) custom-call(s32[4]{0:T(128)S(1)} %pad_add_fusion.place, f32[8]{0:T(128)S(1)} %copy-done.3, bf16[2,768,128]{2,1,0:T(8,128)(2,1)S(1)} %copy-done, bf16[2,768,128]{2,1,0:T(8,128)(2,1)S(1)} %collective-permute-done.refs_1_, ...), custom_call_target="tpu_custom_call" | custom-call | flops 402653184 | bytes 2752512 | tf_op jit(solution)/shard_map/pallas_call | solution.py:247
  63.7 1.9 %collective-permute-start.10 = (bf16[2,768,128]{2,1,0:T(8,128)(2,1)}, bf16[2,768,128]{2,1,0:T(8,128)(2,1)S(1)}, u32[]{:S(2)}, u32[]{:S(2)}) collective-permute-start(bf16[2,768,128]{2,1,0:T(8,128)(2,1)} %collective-permute-done.9.second), channel_id=1, source_target_pairs={{0,32},{16,48},{32,16},{48,0},{1,33},{17,49},{33,17},{49,1},{2,34}... | collective-permute-start | bytes 1179656 | tf_op jit(solution)/shard_map/ppermute | solution.py:291
  65.6 1.8 %shard_map.70 = (bf16[8,272,128]{2,1,0:T(8,128)(2,1)S(1)}, bf16[2,1536,512]{2,1,0:T(8,128)(2,1)S(1)}, f32[2,128,512]{2,1,0:T(8,128)S(1)}) custom-call(s32[4]{0:T(128)S(1)} %pad_add_fusion.place, f32[8]{0:T(128)S(1)} %copy-done.3, bf16[2,768,128]{2,1,0:T(8,128)(2,1)S(1)} %collective-permute-done.11.first, ...), custom_call_target="tpu_custom_call", output_to_operand_aliasing={{0}: (6, {}), {1}: (7, {})} | custom-call | flops 301989888 | bytes 2752512 | tf_op jit(solution)/shard_map/pallas_call | solution.py:247
  67.5 3.2 %collective-permute-done.10.far = bf16[2,768,128]{2,1,0:T(8,128)(2,1)S(1)} collective-permute-done((bf16[2,768,128]{2,1,0:T(8,128)(2,1)}, bf16[2,768,128]{2,1,0:T(8,128)(2,1)S(1)}, u32[]{:S(2)}, u32[]{:S(2)}) %collective-permute-start.10) | collective-permute-done | bytes 393248 | tf_op jit(solution)/shard_map/ppermute | solution.py:291
  70.6 1.1 %shard_map.71 = bf16[8,272,128]{2,1,0:T(8,128)(2,1)S(1)} custom-call(s32[4]{0:T(128)S(1)} %pad_add_fusion.place, f32[8]{0:T(128)S(1)} %copy-done.3, bf16[2,768,128]{2,1,0:T(8,128)(2,1)S(1)} %collective-permute-done.10.far, bf16[2,1536,512]{2,1,0:T(8,128)(2,1)S(1)} %get-tuple-element.35.steps, ...), custom_call_target="tpu_custom_call", output_to_operand_aliasing={{}: (5, {})} | custom-call | flops 201326592 | bytes 2752512 | tf_op jit(solution)/shard_map/pallas_call | solution.py:247
  71.8 14.7 %all_to_all.5 = bf16[8,272,128]{2,1,0:T(8,128)(2,1)S(1)} all-to-all(bf16[8,272,128]{2,1,0:T(8,128)(2,1)S(1)} %shard_map.71), channel_id=1, replica_groups=mesh['yh'=2,'x'=4,'c'=2,'yl'=2,'z'=16] {'yh','x'}, dimensions={0} | all-to-all | bytes 1114112 | tf_op jit(solution)/shard_map/all_to_all | solution.py:301
  86.7 10.9 %collective-permute-start.14 = (f32[264,128]{1,0:T(8,128)S(1)}, f32[264,128]{1,0:T(8,128)S(1)}, u32[]{:S(2)}, u32[]{:S(2)}) collective-permute-start(f32[264,128]{1,0:T(8,128)S(1)} %slice.4), channel_id=1, source_target_pairs={{0,335},{1,320},{2,353},{3,354},{4,387},{5,388},{6,421},{7,422},{8... | collective-permute-start | bytes 405512 | tf_op jit(solution)/shard_map/ppermute | solution.py:307
  97.6 4.7 %collective-permute-start.13 = (f32[264,128]{1,0:T(8,128)S(1)}, f32[264,128]{1,0:T(8,128)S(1)}, u32[]{:S(2)}, u32[]{:S(2)}) collective-permute-start(f32[264,128]{1,0:T(8,128)S(1)} %slice.4), channel_id=1, source_target_pairs={{0,244},{1,21},{2,22},{3,55},{4,56},{5,89},{6,90},{7,123},{8,124},... | collective-permute-start | bytes 405512 | tf_op jit(solution)/shard_map/ppermute | solution.py:306
  102.4 0.7 dynamic-slice_bitcast_fusion.todo
  103.1 1.3 %collective-permute-done.14.b = f32[264,128]{1,0:T(8,128)S(1)} collective-permute-done((f32[264,128]{1,0:T(8,128)S(1)}, f32[264,128]{1,0:T(8,128)S(1)}, u32[]{:S(2)}, u32[]{:S(2)}) %collective-permute-start.14) | collective-permute-done | bytes 135200 | tf_op jit(solution)/shard_map/ppermute | solution.py:307
  104.4 3.2 %collective-permute-done.13.a = f32[264,128]{1,0:T(8,128)S(1)} collective-permute-done((f32[264,128]{1,0:T(8,128)S(1)}, f32[264,128]{1,0:T(8,128)S(1)}, u32[]{:S(2)}, u32[]{:S(2)}) %collective-permute-start.13) | collective-permute-done | bytes 135200 | tf_op jit(solution)/shard_map/ppermute | solution.py:306
  107.6 1.4 %shard_map.72 = (f32[128,256]{1,0:T(8,128)}, f32[128,256]{1,0:T(8,128)}) custom-call(s32[4]{0:T(128)S(1)} %dynamic-slice_bitcast_fusion.todo, f32[264,128]{1,0:T(8,128)S(1)} %collective-permute-done.13.a, f32[264,128]{1,0:T(8,128)S(1)} %collective-permute-done.14.b), custom_call_target="tpu_custom_call" | custom-call | tf_op jit(solution)/shard_map/pallas_call | solution.py:312
  (18 shorter events, 1.0 us)
Async XLA Ops:
  2.4 17.1 %collective-permute-start = (bf16[2,768,128]{2,1,0:T(8,128)(2,1)}, bf16[2,768,128]{2,1,0:T(8,128)(2,1)S(1)}, u32[]{:S(2)}, u32[]{:S(2)}) collective-permute-start(bf16[2,768,128]{2,1,0:T(8,128)(2,1)} %shard_map.68.refs_0_), channel_id=1, source_target_pairs={{0,1},{1,2},{2,3},{3,4},{4,5},{5,6},{6,7},{7,8},{8,9},{9,10},{10,1... | collective-permute-start | bytes 1179656 | tf_op jit(solution)/shard_map/ppermute | solution.py:262
  13.6 10.9 %collective-permute-start.4 = (bf16[2,768,128]{2,1,0:T(8,128)(2,1)}, bf16[2,768,128]{2,1,0:T(8,128)(2,1)S(1)}, u32[]{:S(2)}, u32[]{:S(2)}) collective-permute-start(bf16[2,768,128]{2,1,0:T(8,128)(2,1)} %shard_map.68.refs_0_), channel_id=1, source_target_pairs={{0,47},{1,32},{2,33},{3,34},{4,35},{5,36},{6,37},{7,38},{8,39},{9,... | collective-permute-start | bytes 1179656 | tf_op jit(solution)/shard_map/ppermute | solution.py:263
  15.5 8.9 %collective-permute-start.3 = (bf16[2,768,128]{2,1,0:T(8,128)(2,1)}, bf16[2,768,128]{2,1,0:T(8,128)(2,1)S(1)}, u32[]{:S(2)}, u32[]{:S(2)}) collective-permute-start(bf16[2,768,128]{2,1,0:T(8,128)(2,1)} %shard_map.68.refs_0_), channel_id=1, source_target_pairs={{0,32},{32,0},{1,33},{33,1},{2,34},{34,2},{3,35},{35,3},{4,36},{36... | collective-permute-start | bytes 1179656 | tf_op jit(solution)/shard_map/ppermute | solution.py:270
  19.5 11.4 %collective-permute-start.1 = (bf16[2,768,128]{2,1,0:T(8,128)(2,1)S(1)}, bf16[2,768,128]{2,1,0:T(8,128)(2,1)S(1)}, u32[]{:S(2)}, u32[]{:S(2)}) collective-permute-start(bf16[2,768,128]{2,1,0:T(8,128)(2,1)S(1)} %collective-permute-done.refs_1_), channel_id=1, source_target_pairs={{0,1},{1,2},{2,3},{3,4},{4,5},{5,6},{6,7},{7,8},{8,9},{9,10},{10,1... | collective-permute-start | bytes 1179656 | tf_op jit(solution)/shard_map/ppermute | solution.py:268
  24.4 9.7 %collective-permute-start.6 = (bf16[2,768,128]{2,1,0:T(8,128)(2,1)S(1)}, bf16[2,768,128]{2,1,0:T(8,128)(2,1)S(1)}, u32[]{:S(2)}, u32[]{:S(2)}) collective-permute-start(bf16[2,768,128]{2,1,0:T(8,128)(2,1)S(1)} %collective-permute-done.4.refs_5_), channel_id=1, source_target_pairs={{0,1},{1,2},{2,3},{3,4},{4,5},{5,6},{6,7},{7,8},{8,9},{9,10},{10,1... | collective-permute-start | bytes 1179656 | tf_op jit(solution)/shard_map/ppermute | solution.py:268
  27.7 9.0 %collective-permute-start.5 = (bf16[2,768,128]{2,1,0:T(8,128)(2,1)}, bf16[2,768,128]{2,1,0:T(8,128)(2,1)S(1)}, u32[]{:S(2)}, u32[]{:S(2)}) collective-permute-start(bf16[2,768,128]{2,1,0:T(8,128)(2,1)} %shard_map.68.refs_0_), channel_id=1, source_target_pairs={{32,48},{48,32},{33,49},{49,33},{34,50},{50,34},{35,51},{51,35},{3... | collective-permute-start | bytes 1179656 | tf_op jit(solution)/shard_map/ppermute | solution.py:273
  30.9 9.0 %collective-permute-start.2 = (bf16[2,768,128]{2,1,0:T(8,128)(2,1)S(1)}, bf16[2,768,128]{2,1,0:T(8,128)(2,1)S(1)}, u32[]{:S(2)}, u32[]{:S(2)}) collective-permute-start(bf16[2,768,128]{2,1,0:T(8,128)(2,1)S(1)} %collective-permute-done.1.refs_2_), channel_id=1, source_target_pairs={{0,1},{1,2},{2,3},{3,4},{4,5},{5,6},{6,7},{7,8},{8,9},{9,10},{10,1... | collective-permute-start | bytes 1179656 | tf_op jit(solution)/shard_map/ppermute | solution.py:268
  36.7 8.8 %collective-permute-start.8 = (bf16[2,768,128]{2,1,0:T(8,128)(2,1)S(1)}, bf16[2,768,128]{2,1,0:T(8,128)(2,1)S(1)}, u32[]{:S(2)}, u32[]{:S(2)}) collective-permute-start(bf16[2,768,128]{2,1,0:T(8,128)(2,1)S(1)} %collective-permute-done.6.refs_6_), channel_id=1, source_target_pairs={{0,1},{1,2},{2,3},{3,4},{4,5},{5,6},{6,7},{7,8},{8,9},{9,10},{10,1... | collective-permute-start | bytes 1179656 | tf_op jit(solution)/shard_map/ppermute | solution.py:268
  38.7 9.6 %collective-permute-start.7 = (bf16[2,768,128]{2,1,0:T(8,128)(2,1)}, bf16[2,768,128]{2,1,0:T(8,128)(2,1)S(1)}, u32[]{:S(2)}, u32[]{:S(2)}) collective-permute-start(bf16[2,768,128]{2,1,0:T(8,128)(2,1)} %shard_map.68.refs_0_), channel_id=1, source_target_pairs={{0,48},{16,32},{1,49},{17,33},{2,50},{18,34},{3,51},{19,35},{4,52}... | collective-permute-start | bytes 1179656 | tf_op jit(solution)/shard_map/ppermute | solution.py:276
  40.0 14.0 %collective-permute-start.11 = (bf16[2,768,128]{2,1,0:T(8,128)(2,1)S(1)}, bf16[2,768,128]{2,1,0:T(8,128)(2,1)S(1)}, u32[]{:S(2)}, u32[]{:S(2)}) collective-permute-start(bf16[2,768,128]{2,1,0:T(8,128)(2,1)S(1)} %collective-permute-done.2.refs_3_), channel_id=1, source_target_pairs={{0,1},{1,2},{2,3},{3,4},{4,5},{5,6},{6,7},{7,8},{8,9},{9,10},{10,1... | collective-permute-start | bytes 1179656 | tf_op jit(solution)/shard_map/ppermute | solution.py:268
  48.3 0.8 copy-start.1
  49.0 14.7 %collective-permute-start.9 = (bf16[2,768,128]{2,1,0:T(8,128)(2,1)S(1)}, bf16[2,768,128]{2,1,0:T(8,128)(2,1)}, u32[]{:S(2)}, u32[]{:S(2)}) collective-permute-start(bf16[2,768,128]{2,1,0:T(8,128)(2,1)S(1)} %collective-permute-done.8.refs_7_), channel_id=1, source_target_pairs={{0,1},{1,2},{2,3},{3,4},{4,5},{5,6},{6,7},{7,8},{8,9},{9,10},{10,1... | collective-permute-start | bytes 1179656 | tf_op jit(solution)/shard_map/ppermute | solution.py:268
  54.0 11.7 %collective-permute-start.12 = (bf16[2,768,128]{2,1,0:T(8,128)(2,1)S(1)}, bf16[2,768,128]{2,1,0:T(8,128)(2,1)S(1)}, u32[]{:S(2)}, u32[]{:S(2)}) collective-permute-start(bf16[2,768,128]{2,1,0:T(8,128)(2,1)S(1)} %collective-permute-done.11.first), channel_id=1, source_target_pairs={{0,32},{16,48},{32,16},{48,0},{1,33},{17,49},{33,17},{49,1},{2,34}... | collective-permute-start | bytes 1179656 | tf_op jit(solution)/shard_map/ppermute | solution.py:291
  58.5 1.0 copy-start
  59.5 1.0 copy-start.2
  60.5 0.7 copy-start.3
  63.7 6.9 %collective-permute-start.10 = (bf16[2,768,128]{2,1,0:T(8,128)(2,1)}, bf16[2,768,128]{2,1,0:T(8,128)(2,1)S(1)}, u32[]{:S(2)}, u32[]{:S(2)}) collective-permute-start(bf16[2,768,128]{2,1,0:T(8,128)(2,1)} %collective-permute-done.9.second), channel_id=1, source_target_pairs={{0,32},{16,48},{32,16},{48,0},{1,33},{17,49},{33,17},{49,1},{2,34}... | collective-permute-start | bytes 1179656 | tf_op jit(solution)/shard_map/ppermute | solution.py:291
  71.8 14.7 %copy-start.4 = (f32[8]{0:T(128)S(1)}, f32[8]{0:T(128)}, u32[]{:S(2)}) copy-start(f32[8]{0:T(128)} %constant.51) | copy-start | bytes 100
  86.7 17.7 %collective-permute-start.14 = (f32[264,128]{1,0:T(8,128)S(1)}, f32[264,128]{1,0:T(8,128)S(1)}, u32[]{:S(2)}, u32[]{:S(2)}) collective-permute-start(f32[264,128]{1,0:T(8,128)S(1)} %slice.4), channel_id=1, source_target_pairs={{0,335},{1,320},{2,353},{3,354},{4,387},{5,388},{6,421},{7,422},{8... | collective-permute-start | bytes 405512 | tf_op jit(solution)/shard_map/ppermute | solution.py:307
  97.6 10.0 %collective-permute-start.13 = (f32[264,128]{1,0:T(8,128)S(1)}, f32[264,128]{1,0:T(8,128)S(1)}, u32[]{:S(2)}, u32[]{:S(2)}) collective-permute-start(f32[264,128]{1,0:T(8,128)S(1)} %slice.4), channel_id=1, source_target_pairs={{0,244},{1,21},{2,22},{3,55},{4,56},{5,89},{6,90},{7,123},{8,124},... | collective-permute-start | bytes 405512 | tf_op jit(solution)/shard_map/ppermute | solution.py:306

commit v8 on v7

--- a/solution.py
+++ b/solution.py
@@ -11,6 +11,8 @@
 AXES = ("yh", "x", "c", "yl", "z")
 SIZES = (2, 4, 2, 2, 16)
 PIECES = 4
+SCALES = [float(np.float32(2 ** (i / 8))) for i in range(8)]
+TOP = 14.0
 EXTRA = 16
 VMEM = pl.BlockSpec(memory_space=pltpu.VMEM)
 SMEM = pl.BlockSpec(memory_space=pltpu.SMEM)
@@ -98,6 +100,13 @@
     )
 
 
+def scale_of(place):
+    scale = jnp.float32(SCALES[0])
+    for i in range(1, len(SCALES)):
+        scale = jnp.where(place[3] == i, SCALES[i], scale)
+    return scale
+
+
 def store(out, scale, slot, kernel, total):
     n = out.shape[-1]
     for j in range(total.shape[1] // n):
@@ -110,9 +119,9 @@
     return (core == 1) & ((z < 8) != (y == 0)), (core == 1) & (y == 0), (core == 0) & (y == 1)
 
 
-def early_kernel(place, scales, *refs):
+def early_kernel(place, *refs):
     first, second, near, (out, left, steps) = refs[0:4], refs[4:8], refs[8:10], refs[10:]
-    core, y, scale = place[0], place[1], scales[place[3]]
+    core, y, scale = place[0], place[1], scale_of(place)
     packed, same, _ = cases(place)
     n = out.shape[-1]
     rows = near[0].shape[1]
@@ -160,8 +169,8 @@
             out[3, 2 * n : 2 * n + EXTRA] = extra.astype(jnp.bfloat16)
 
 
-def middle_kernel(place, scales, first, second, far, left, _, __, out, steps, total):
-    scale = scales[place[3]]
+def middle_kernel(place, first, second, far, left, _, __, out, steps, total):
+    scale = scale_of(place)
     _, same, turned = cases(place)
     n = out.shape[-1]
     rows = far.shape[1]
@@ -183,8 +192,9 @@
         total[kernel] = product(far[kernel], steps[kernel, rows:])
 
 
-def late_kernel(place, scales, far, steps, part, _, out):
-    scale = scales[place[3]]
+def late_kernel(place, far, steps, part, partial, out):
+    out[...] = partial[...]
+    scale = scale_of(place)
     packed, _, _ = cases(place)
     n = out.shape[-1]
     rows = far.shape[1]
@@ -195,6 +205,27 @@
         @pl.when(jnp.logical_not(packed))
         def _():
             store(out, scale, 3, kernel, total[:, 3 * n :])
+
+
+def sum_kernel(parts, out):
+    n = out.shape[-1]
+    total = sum(
+        parts[i].astype(jnp.float32) * (1 / scale) for i, scale in enumerate(SCALES)
+    )
+    line = lax.broadcasted_iota(jnp.int32, (8, n), 0)
+    extra = total[2 * n : 2 * n + 8]
+    for kernel in range(2):
+        block = total[kernel * n : (kernel + 1) * n]
+        diagonal = total[2 * n + kernel : 2 * n + kernel + 1]
+        most = jnp.maximum(
+            jnp.max(jnp.abs(block), axis=0, keepdims=True), jnp.abs(diagonal)
+        )
+        power = jnp.ceil(jnp.log2(jnp.maximum(most, 1e-30)))
+        factor = jnp.exp2(TOP - power)
+        out[kernel * n : (kernel + 1) * n] = block * factor
+        extra = jnp.where(line == kernel, diagonal * factor, extra)
+        extra = jnp.where(line == 2 + kernel, power, extra)
+    out[2 * n :] = extra
 
 
 def place_kernel(total_draws, todo, a, b, feature, gradient):
@@ -203,10 +234,12 @@
     col = lax.broadcasted_iota(jnp.int32, (n, n), 1)
     for kernel, out in enumerate((feature, gradient)):
         block, line = pl.ds(kernel * n, n), pl.ds(2 * n + kernel, 1)
+        power = pl.ds(2 * n + 2 + kernel, 1)
         for half in range(2):
             second, mode = todo[2 * half] == 1, todo[2 * half + 1]
-            got = jnp.where(second, b[block, :], a[block, :])
-            extra = jnp.where(second, b[line, :], a[line, :])
+            factor = jnp.exp2(jnp.where(second, b[power, :], a[power, :]) - TOP)
+            got = jnp.where(second, b[block, :], a[block, :]) * factor
+            extra = jnp.where(second, b[line, :], a[line, :]) * factor
             turned = got.T
             lower = row > col
             plain = (mode == 0) | ((mode == 2) & (row <= col)) | ((mode == 3) & lower)
@@ -237,7 +270,6 @@
             step.append((c * 16 + z, c * 16 + (z + 1 - 2 * c) % 16))
             first_step.append((c * 16 + z, (1 - c) * 16 + (z + 2 * c - 1) % 16))
     place = jnp.stack([lax.axis_index(a) for a in ("c", "yl", "z", ("yh", "x"))])
-    scales = np.exp2(np.arange(8) / 8).astype(np.float32)
     shape = jax.ShapeDtypeStruct((8, 2 * n + EXTRA, n), jnp.bfloat16)
     left_shape = jax.ShapeDtypeStruct((2, 2 * draws, n), jnp.bfloat16)
     steps_shape = jax.ShapeDtypeStruct((2, 2 * draws, 4 * n), jnp.bfloat16)
@@ -247,7 +279,7 @@
         return pl.pallas_call(
             kernel,
             out_shape=out_shape,
-            in_specs=[SMEM, SMEM] + [VMEM] * len(args),
+            in_specs=[SMEM] + [VMEM] * len(args),
             out_specs=jax.tree.map(lambda _: VMEM, out_shape),
             input_output_aliases=aliases,
             compiler_params=PARAMS,
@@ -256,27 +288,26 @@
                 bytes_accessed=28 * n * draws,
                 transcendentals=0,
             ),
-        )(place, jnp.asarray(scales), *args)
+        )(place, *args)
 
     chains = [
         lax.ppermute(both, ("c", "z"), step),
         lax.ppermute(both, ("c", "z"), first_step),
     ]
     walk = [[], []]
+    other = lax.ppermute(both, "c", [(0, 1), (1, 0)])
+    partners = (("c", "yl"), [(2, 3), (3, 2)])
     for j in range(4):
         if j:
             chains = [lax.ppermute(chain, ("c", "z"), step) for chain in chains]
         if j == 0:
-            other = lax.ppermute(both, "c", [(0, 1), (1, 0)])
-            other, chains[1] = lax.optimization_barrier((other, chains[1]))
             own, chains[1] = lax.optimization_barrier((both, chains[1]))
-            near = [lax.ppermute(own, ("c", "yl"), [(2, 3), (3, 2)])]
+            near = [lax.ppermute(own, *partners)]
+            other, chains[0] = lax.optimization_barrier((other, chains[0]))
         if j == 1:
-            own, chains[1] = lax.optimization_barrier((both, chains[1]))
-            near.append(lax.ppermute(own, ("c", "yl"), [(0, 3), (1, 2)]))
+            again, chains[1] = lax.optimization_barrier((other, chains[1]))
+            near.append(lax.ppermute(again, *partners))
             near[0], chains[1] = lax.optimization_barrier((near[0], chains[1]))
-        if j == 2:
-            near[1], chains[1] = lax.optimization_barrier((near[1], chains[1]))
         if j == 3:
             partial, left, steps = call(
                 early_kernel,
@@ -294,17 +325,21 @@
         middle_kernel,
         (shape, steps_shape, total_shape),
         *(*chains, far[0], left, partial, steps),
-        aliases={6: 0, 7: 1},
+        aliases={5: 0, 6: 1},
         flops=3,
     )
-    partial = call(late_kernel, shape, far[1], steps, total, partial, aliases={5: 0}, flops=2)
+    partial = call(late_kernel, shape, far[1], steps, total, partial, flops=2)
     partial = lax.all_to_all(partial, ("yh", "x"), 0, 0, tiled=True)
-    block = jnp.sum(partial.astype(jnp.float32) / scales[:, None, None], axis=0)
-    block = block[: 2 * n + 8]
+    block = pl.pallas_call(
+        sum_kernel,
+        out_shape=jax.ShapeDtypeStruct((2 * n + 8, n), jnp.float32),
+        in_specs=[VMEM],
+        out_specs=VMEM,
+        compiler_params=PARAMS,
+    )(partial).astype(jnp.float16)
 
     perms, table = routes()
-    a = lax.ppermute(block, AXES, perms[0])
-    b = lax.ppermute(block, AXES, perms[1])
+    a, b = [lax.ppermute(block, AXES, p).astype(jnp.float32) for p in perms]
     todo = lax.dynamic_index_in_dim(
         jnp.asarray(table), lax.axis_index(AXES), 0, keepdims=False
     )

time: 110 us -> 107 us (0.973)
  blocking collectives: 14.7 us -> 0 us
  starting transfers between devices: 64.7 us -> 72.3 us
  waiting for transfers between devices: 15.7 us -> 21.4 us
  local copies, waits for them, and re-layouts: 4.11 us -> 1.69 us
    all_to_all x1 -> x0, blocking collectives: 14.7 us -> none  [on_device(): partial = lax.all_to_all(partial, ('yh', 'x'), 0, 0, tiled=True)]
    all_to_all x0 -> x1, waiting for transfers between devices: none -> 7.43 us  [on_device(): partial = lax.all_to_all(partial, ('yh', 'x'), 0, 0, tiled=True)]
    all_to_all x0 -> x1, starting transfers between devices: none -> 6.55 us  [on_device(): partial = lax.all_to_all(partial, ('yh', 'x'), 0, 0, tiled=True)]
    ppermute x4, waiting for transfers between devices: 9.86 us -> 5.95 us  [the longest x2 3.86 us: on_device(): a, b = [lax.ppermute(block, AXES, p).astype(jnp.float32) for p in perms]]
    ppermute x1, waiting for transfers between devices: 0.01 us -> 3.44 us  [on_device(): lax.ppermute(both, ('c', 'z'), first_step)]
    unnamed x10 -> x2, local copies, waits for them, and re-layouts: 3.4 us -> 0.99 us
    ppermute x4, starting transfers between devices: 20.1 us -> 22.1 us  [the longest x2 16.7 us: on_device(): a, b = [lax.ppermute(block, AXES, p).astype(jnp.float32) for p in perms]]
    ppermute x6, waiting for transfers between devices: 1.69 us -> 0.02 us  [on_device(): chains = [lax.ppermute(chain, ('c', 'z'), step) for chain in chains]]
  transfers between devices with their start and end apart: 15 -> 16, of which waited for: 7 -> 6; matrix products, arithmetic and copies ran while one was open for 1% -> 1% of each run, Pallas kernels for 4% -> 4%
where the time goes in v8:
time: 107 us; the launch traced here: 106 us
  starting transfers between devices  72.3 us (68%)
  waiting for transfers between devices  21.4 us (20%)
  Pallas kernels  9.67 us (9%)
  local copies, waits for them, and re-layouts  1.69 us (2%)
    ppermute x6, starting transfers between devices, on_device(): chains = [lax.ppermute(chain, ('c', 'z'), step) for chain in chains]  21.8 us
    ppermute x2, starting transfers between devices, on_device(): a, b = [lax.ppermute(block, AXES, p).astype(jnp.float32) for p in perms]  16.7 us
    ppermute x1, starting transfers between devices, on_device(): lax.ppermute(both, ('c', 'z'), step)  11.1 us
    all_to_all x1, waiting for transfers between devices, on_device(): partial = lax.all_to_all(partial, ('yh', 'x'), 0, 0, tiled=True)  7.43 us
    ppermute x2, starting transfers between devices, on_device(): far = [lax.ppermute(chain, ('c', 'yl'), cross) for chain in chains]  6.89 us
    all_to_all x1, starting transfers between devices, on_device(): partial = lax.all_to_all(partial, ('yh', 'x'), 0, 0, tiled=True)  6.55 us
    pallas_call x3, Pallas kernels, call(): pl.pallas_call(kernel, out_shape=out_shape, in_specs=[SMEM] + [VMEM] * le...  6.36 us
    ppermute x2, waiting for transfers between devices, on_device(): a, b = [lax.ppermute(block, AXES, p).astype(jnp.float32) for p in perms]  3.86 us
  transfers between devices with their start and end apart: 16, of which 6 were waited for; matrix products, arithmetic and copies ran while one was open for 1% of the time, Pallas kernels for 4%

profile of v8, /device:TPU:7, one launch (start us, length us, event | category | flops | bytes accessed | tf_op | source)
XLA Modules:
  0.0 106.0 jit_solution(13645763752062632774)
XLA Ops:
  0.6 1.8 %shard_map.50.refs_0_ = bf16[2,768,128]{2,1,0:T(8,128)(2,1)} custom-call(bf16[768,128]{1,0:T(8,128)(2,1)} %field.1, bf16[768,128]{1,0:T(8,128)(2,1)} %backward.1), custom_call_target="tpu_custom_call" | custom-call | tf_op jit(solution)/shard_map/pallas_call | solution.py:254
  2.4 11.1 %collective-permute-start.1 = (bf16[2,768,128]{2,1,0:T(8,128)(2,1)}, bf16[2,768,128]{2,1,0:T(8,128)(2,1)S(1)}, u32[]{:S(2)}, u32[]{:S(2)}) collective-permute-start(bf16[2,768,128]{2,1,0:T(8,128)(2,1)} %shard_map.50.refs_0_), channel_id=1, source_target_pairs={{0,1},{1,2},{2,3},{3,4},{4,5},{5,6},{6,7},{7,8},{8,9},{9,10},{10,1... | collective-permute-start | bytes 1179656 | tf_op jit(solution)/shard_map/ppermute | solution.py:294
  13.6 1.9 %collective-permute-start = (bf16[2,768,128]{2,1,0:T(8,128)(2,1)}, bf16[2,768,128]{2,1,0:T(8,128)(2,1)S(1)}, u32[]{:S(2)}, u32[]{:S(2)}) collective-permute-start(bf16[2,768,128]{2,1,0:T(8,128)(2,1)} %shard_map.50.refs_0_), channel_id=1, source_target_pairs={{0,32},{32,0},{1,33},{33,1},{2,34},{34,2},{3,35},{35,3},{4,36},{36... | collective-permute-start | bytes 1179656 | tf_op jit(solution)/shard_map/ppermute | solution.py:298
  15.5 1.9 %collective-permute-start.4 = (bf16[2,768,128]{2,1,0:T(8,128)(2,1)}, bf16[2,768,128]{2,1,0:T(8,128)(2,1)S(1)}, u32[]{:S(2)}, u32[]{:S(2)}) collective-permute-start(bf16[2,768,128]{2,1,0:T(8,128)(2,1)} %shard_map.50.refs_0_), channel_id=1, source_target_pairs={{0,47},{1,32},{2,33},{3,34},{4,35},{5,36},{6,37},{7,38},{8,39},{9,... | collective-permute-start | bytes 1179656 | tf_op jit(solution)/shard_map/ppermute | solution.py:295
  17.4 1.2 %collective-permute-done.1.refs_1_ = bf16[2,768,128]{2,1,0:T(8,128)(2,1)S(1)} collective-permute-done((bf16[2,768,128]{2,1,0:T(8,128)(2,1)}, bf16[2,768,128]{2,1,0:T(8,128)(2,1)S(1)}, u32[]{:S(2)}, u32[]{:S(2)}) %collective-permute-start.1) | collective-permute-done | bytes 393248 | tf_op jit(solution)/shard_map/ppermute | solution.py:294
  18.6 0.0 collective-permute-done.refs_4_
  18.6 4.9 %collective-permute-start.2 = (bf16[2,768,128]{2,1,0:T(8,128)(2,1)S(1)}, bf16[2,768,128]{2,1,0:T(8,128)(2,1)S(1)}, u32[]{:S(2)}, u32[]{:S(2)}) collective-permute-start(bf16[2,768,128]{2,1,0:T(8,128)(2,1)S(1)} %collective-permute-done.1.refs_1_), channel_id=1, source_target_pairs={{0,1},{1,2},{2,3},{3,4},{4,5},{5,6},{6,7},{7,8},{8,9},{9,10},{10,1... | collective-permute-start | bytes 1179656 | tf_op jit(solution)/shard_map/ppermute | solution.py:302
  23.5 3.4 %collective-permute-done.4.refs_5_ = bf16[2,768,128]{2,1,0:T(8,128)(2,1)S(1)} collective-permute-done((bf16[2,768,128]{2,1,0:T(8,128)(2,1)}, bf16[2,768,128]{2,1,0:T(8,128)(2,1)S(1)}, u32[]{:S(2)}, u32[]{:S(2)}) %collective-permute-start.4) | collective-permute-done | bytes 393248 | tf_op jit(solution)/shard_map/ppermute | solution.py:295
  26.9 1.9 %collective-permute-start.6 = (bf16[2,768,128]{2,1,0:T(8,128)(2,1)S(1)}, bf16[2,768,128]{2,1,0:T(8,128)(2,1)S(1)}, u32[]{:S(2)}, u32[]{:S(2)}) collective-permute-start(bf16[2,768,128]{2,1,0:T(8,128)(2,1)S(1)} %collective-permute-done.4.refs_5_), channel_id=1, source_target_pairs={{0,1},{1,2},{2,3},{3,4},{4,5},{5,6},{6,7},{7,8},{8,9},{9,10},{10,1... | collective-permute-start | bytes 1179656 | tf_op jit(solution)/shard_map/ppermute | solution.py:302
  28.9 3.2 %collective-permute-start.5 = (bf16[2,768,128]{2,1,0:T(8,128)(2,1)}, bf16[2,768,128]{2,1,0:T(8,128)(2,1)S(1)}, u32[]{:S(2)}, u32[]{:S(2)}) collective-permute-start(bf16[2,768,128]{2,1,0:T(8,128)(2,1)} %shard_map.50.refs_0_), channel_id=1, source_target_pairs={{32,48},{48,32},{33,49},{49,33},{34,50},{50,34},{35,51},{51,35},{3... | collective-permute-start | bytes 1179656 | tf_op jit(solution)/shard_map/ppermute | solution.py:305
  32.1 3.7 %collective-permute-start.3 = (bf16[2,768,128]{2,1,0:T(8,128)(2,1)S(1)}, bf16[2,768,128]{2,1,0:T(8,128)(2,1)S(1)}, u32[]{:S(2)}, u32[]{:S(2)}) collective-permute-start(bf16[2,768,128]{2,1,0:T(8,128)(2,1)S(1)} %collective-permute-done.2.refs_2_), channel_id=1, source_target_pairs={{0,1},{1,2},{2,3},{3,4},{4,5},{5,6},{6,7},{7,8},{8,9},{9,10},{10,1... | collective-permute-start | bytes 1179656 | tf_op jit(solution)/shard_map/ppermute | solution.py:302
  35.8 2.1 %collective-permute-done.5.refs_8_ = bf16[2,768,128]{2,1,0:T(8,128)(2,1)S(1)} collective-permute-done((bf16[2,768,128]{2,1,0:T(8,128)(2,1)}, bf16[2,768,128]{2,1,0:T(8,128)(2,1)S(1)}, u32[]{:S(2)}, u32[]{:S(2)}) %collective-permute-start.5) | collective-permute-done | bytes 393248 | tf_op jit(solution)/shard_map/ppermute | solution.py:305
  37.9 3.7 %collective-permute-start.7 = (bf16[2,768,128]{2,1,0:T(8,128)(2,1)S(1)}, bf16[2,768,128]{2,1,0:T(8,128)(2,1)}, u32[]{:S(2)}, u32[]{:S(2)}) collective-permute-start(bf16[2,768,128]{2,1,0:T(8,128)(2,1)S(1)} %collective-permute-done.6.refs_6_), channel_id=1, source_target_pairs={{0,1},{1,2},{2,3},{3,4},{4,5},{5,6},{6,7},{7,8},{8,9},{9,10},{10,1... | collective-permute-start | bytes 1179656 | tf_op jit(solution)/shard_map/ppermute | solution.py:302
  41.6 3.9 %collective-permute-start.11 = (bf16[2,768,128]{2,1,0:T(8,128)(2,1)S(1)}, bf16[2,768,128]{2,1,0:T(8,128)(2,1)S(1)}, u32[]{:S(2)}, u32[]{:S(2)}) collective-permute-start(bf16[2,768,128]{2,1,0:T(8,128)(2,1)S(1)} %collective-permute-done.3.refs_3_), channel_id=1, source_target_pairs={{0,1},{1,2},{2,3},{3,4},{4,5},{5,6},{6,7},{7,8},{8,9},{9,10},{10,1... | collective-permute-start | bytes 1179656 | tf_op jit(solution)/shard_map/ppermute | solution.py:302
  45.5 2.1 %collective-permute-start.8 = (bf16[2,768,128]{2,1,0:T(8,128)(2,1)S(1)}, bf16[2,768,128]{2,1,0:T(8,128)(2,1)}, u32[]{:S(2)}, u32[]{:S(2)}) collective-permute-start(bf16[2,768,128]{2,1,0:T(8,128)(2,1)S(1)} %collective-permute-done.refs_4_), channel_id=1, source_target_pairs={{32,48},{48,32},{33,49},{49,33},{34,50},{50,34},{35,51},{51,35},{3... | collective-permute-start | bytes 1179656 | tf_op jit(solution)/shard_map/ppermute | solution.py:309
  47.7 3.7 %collective-permute-start.9 = (bf16[2,768,128]{2,1,0:T(8,128)(2,1)}, bf16[2,768,128]{2,1,0:T(8,128)(2,1)S(1)}, u32[]{:S(2)}, u32[]{:S(2)}) collective-permute-start(bf16[2,768,128]{2,1,0:T(8,128)(2,1)} %collective-permute-done.7.refs_7_), channel_id=1, source_target_pairs={{0,1},{1,2},{2,3},{3,4},{4,5},{5,6},{6,7},{7,8},{8,9},{9,10},{10,1... | collective-permute-start | bytes 1179656 | tf_op jit(solution)/shard_map/ppermute | solution.py:302
  51.4 0.1 pad_add_fusion.place
  51.5 4.7 %collective-permute-start.12 = (bf16[2,768,128]{2,1,0:T(8,128)(2,1)S(1)}, bf16[2,768,128]{2,1,0:T(8,128)(2,1)S(1)}, u32[]{:S(2)}, u32[]{:S(2)}) collective-permute-start(bf16[2,768,128]{2,1,0:T(8,128)(2,1)S(1)} %collective-permute-done.11.first), channel_id=1, source_target_pairs={{0,32},{16,48},{32,16},{48,0},{1,33},{17,49},{33,17},{49,1},{2,34}... | collective-permute-start | bytes 1179656 | tf_op jit(solution)/shard_map/ppermute | solution.py:322
  56.2 1.0 copy-done
  57.2 3.1 %shard_map.51 = (bf16[8,272,128]{2,1,0:T(8,128)(2,1)S(1)}, bf16[2,1536,128]{2,1,0:T(8,128)(2,1)S(1)}, bf16[2,1536,512]{2,1,0:T(8,128)(2,1)S(1)}) custom-call(s32[4]{0:T(128)S(1)} %pad_add_fusion.place, bf16[2,768,128]{2,1,0:T(8,128)(2,1)S(1)} %copy-done, bf16[2,768,128]{2,1,0:T(8,128)(2,1)S(1)} %collective-permute-done.1.refs_1_, ...), custom_call_target="tpu_custom_call" | custom-call | flops 402653184 | bytes 2752512 | tf_op jit(solution)/shard_map/pallas_call | solution.py:279
  60.3 2.2 %collective-permute-start.10 = (bf16[2,768,128]{2,1,0:T(8,128)(2,1)S(1)}, bf16[2,768,128]{2,1,0:T(8,128)(2,1)S(1)}, u32[]{:S(2)}, u32[]{:S(2)}) collective-permute-start(bf16[2,768,128]{2,1,0:T(8,128)(2,1)S(1)} %collective-permute-done.9.second), channel_id=1, source_target_pairs={{0,32},{16,48},{32,16},{48,0},{1,33},{17,49},{33,17},{49,1},{2,34}... | collective-permute-start | bytes 1179656 | tf_op jit(solution)/shard_map/ppermute | solution.py:322
  62.5 1.3 %shard_map.52 = (bf16[8,272,128]{2,1,0:T(8,128)(2,1)S(1)}, bf16[2,1536,512]{2,1,0:T(8,128)(2,1)S(1)}, f32[2,128,512]{2,1,0:T(8,128)S(1)}) custom-call(s32[4]{0:T(128)S(1)} %pad_add_fusion.place, bf16[2,768,128]{2,1,0:T(8,128)(2,1)S(1)} %collective-permute-done.11.first, ...), custom_call_target="tpu_custom_call", output_to_operand_aliasing={{0}: (5, {}), {1}: (6, {})} | custom-call | flops 301989888 | bytes 2752512 | tf_op jit(solution)/shard_map/pallas_call | solution.py:279
  63.8 3.4 %collective-permute-done.10.far = bf16[2,768,128]{2,1,0:T(8,128)(2,1)S(1)} collective-permute-done((bf16[2,768,128]{2,1,0:T(8,128)(2,1)S(1)}, bf16[2,768,128]{2,1,0:T(8,128)(2,1)S(1)}, u32[]{:S(2)}, u32[]{:S(2)}) %collective-permute-start.10) | collective-permute-done | bytes 393248 | tf_op jit(solution)/shard_map/ppermute | solution.py:322
  67.2 2.0 %shard_map.53 = bf16[8,272,128]{2,1,0:T(8,128)(2,1)} custom-call(s32[4]{0:T(128)S(1)} %pad_add_fusion.place, bf16[2,768,128]{2,1,0:T(8,128)(2,1)S(1)} %collective-permute-done.10.far, bf16[2,1536,512]{2,1,0:T(8,128)(2,1)S(1)} %get-tuple-element.31.steps, f32[2,128,512]{2,1,0:T(8,128)S(1)} %get-tuple-element.32.part, ...), custom_call_target="tpu_custom_call" | custom-call | flops 201326592 | bytes 2752512 | tf_op jit(solution)/shard_map/pallas_call | solution.py:279
  69.2 6.5 %all-to-all-start = ((bf16[8,272,128]{2,1,0:T(8,128)(2,1)}), bf16[8,272,128]{2,1,0:T(8,128)(2,1)S(1)}, u32[]{:S(2)}, u32[]{:S(2)}) async-start(bf16[8,272,128]{2,1,0:T(8,128)(2,1)} %shard_map.53), calls=%async_computation | async-start | bytes 1114112 | tf_op jit(solution)/shard_map/all_to_all | solution.py:332
  75.7 7.4 %all-to-all-done.parts = bf16[8,272,128]{2,1,0:T(8,128)(2,1)S(1)} async-done(((bf16[8,272,128]{2,1,0:T(8,128)(2,1)}), bf16[8,272,128]{2,1,0:T(8,128)(2,1)S(1)}, u32[]{:S(2)}, u32[]{:S(2)}) %all-to-all-start) | async-done | bytes 557088 | tf_op jit(solution)/shard_map/all_to_all | solution.py:332
  83.2 0.1 shard_map.54
  83.3 12.1 %collective-permute-start.14 = (f16[264,128]{1,0:T(8,128)(2,1)S(1)}, f16[264,128]{1,0:T(8,128)(2,1)S(1)}, u32[]{:S(2)}, u32[]{:S(2)}) collective-permute-start(f16[264,128]{1,0:T(8,128)(2,1)S(1)} %convert_element_type.9), channel_id=1, source_target_pairs={{0,335},{1,320},{2,353},{3,354},{4,387},{5,388},{6,421},{7,422},{8... | collective-permute-start | bytes 202760 | tf_op jit(solution)/shard_map/ppermute | solution.py:342
  95.4 4.6 %collective-permute-start.13 = (f16[264,128]{1,0:T(8,128)(2,1)S(1)}, f16[264,128]{1,0:T(8,128)(2,1)S(1)}, u32[]{:S(2)}, u32[]{:S(2)}) collective-permute-start(f16[264,128]{1,0:T(8,128)(2,1)S(1)} %convert_element_type.9), channel_id=1, source_target_pairs={{0,244},{1,21},{2,22},{3,55},{4,56},{5,89},{6,90},{7,123},{8,124},... | collective-permute-start | bytes 202760 | tf_op jit(solution)/shard_map/ppermute | solution.py:342
  100.0 0.7 dynamic-slice_bitcast_fusion.todo
  100.8 3.9 %collective-permute-done.13 = f16[264,128]{1,0:T(8,128)(2,1)S(1)} collective-permute-done((f16[264,128]{1,0:T(8,128)(2,1)S(1)}, f16[264,128]{1,0:T(8,128)(2,1)S(1)}, u32[]{:S(2)}, u32[]{:S(2)}) %collective-permute-start.13) | collective-permute-done | bytes 67616 | tf_op jit(solution)/shard_map/ppermute | solution.py:342
  104.6 1.4 %shard_map.55 = (f32[128,256]{1,0:T(8,128)}, f32[128,256]{1,0:T(8,128)}) custom-call(s32[4]{0:T(128)S(1)} %dynamic-slice_bitcast_fusion.todo, f32[264,128]{1,0:T(8,128)S(1)} %convert_element_type.10.a, f32[264,128]{1,0:T(8,128)S(1)} %convert_element_type.11.b), custom_call_target="tpu_custom_call" | custom-call | tf_op jit(solution)/shard_map/pallas_call | solution.py:347
  (13 shorter events, 0.1 us)
Async XLA Ops:
  2.4 16.1 %collective-permute-start.1 = (bf16[2,768,128]{2,1,0:T(8,128)(2,1)}, bf16[2,768,128]{2,1,0:T(8,128)(2,1)S(1)}, u32[]{:S(2)}, u32[]{:S(2)}) collective-permute-start(bf16[2,768,128]{2,1,0:T(8,128)(2,1)} %shard_map.50.refs_0_), channel_id=1, source_target_pairs={{0,1},{1,2},{2,3},{3,4},{4,5},{5,6},{6,7},{7,8},{8,9},{9,10},{10,1... | collective-permute-start | bytes 1179656 | tf_op jit(solution)/shard_map/ppermute | solution.py:294
  13.6 5.0 %collective-permute-start = (bf16[2,768,128]{2,1,0:T(8,128)(2,1)}, bf16[2,768,128]{2,1,0:T(8,128)(2,1)S(1)}, u32[]{:S(2)}, u32[]{:S(2)}) collective-permute-start(bf16[2,768,128]{2,1,0:T(8,128)(2,1)} %shard_map.50.refs_0_), channel_id=1, source_target_pairs={{0,32},{32,0},{1,33},{33,1},{2,34},{34,2},{3,35},{35,3},{4,36},{36... | collective-permute-start | bytes 1179656 | tf_op jit(solution)/shard_map/ppermute | solution.py:298
  15.5 11.4 %collective-permute-start.4 = (bf16[2,768,128]{2,1,0:T(8,128)(2,1)}, bf16[2,768,128]{2,1,0:T(8,128)(2,1)S(1)}, u32[]{:S(2)}, u32[]{:S(2)}) collective-permute-start(bf16[2,768,128]{2,1,0:T(8,128)(2,1)} %shard_map.50.refs_0_), channel_id=1, source_target_pairs={{0,47},{1,32},{2,33},{3,34},{4,35},{5,36},{6,37},{7,38},{8,39},{9,... | collective-permute-start | bytes 1179656 | tf_op jit(solution)/shard_map/ppermute | solution.py:295
  18.6 13.5 %collective-permute-start.2 = (bf16[2,768,128]{2,1,0:T(8,128)(2,1)S(1)}, bf16[2,768,128]{2,1,0:T(8,128)(2,1)S(1)}, u32[]{:S(2)}, u32[]{:S(2)}) collective-permute-start(bf16[2,768,128]{2,1,0:T(8,128)(2,1)S(1)} %collective-permute-done.1.refs_1_), channel_id=1, source_target_pairs={{0,1},{1,2},{2,3},{3,4},{4,5},{5,6},{6,7},{7,8},{8,9},{9,10},{10,1... | collective-permute-start | bytes 1179656 | tf_op jit(solution)/shard_map/ppermute | solution.py:302
  26.9 8.8 %collective-permute-start.6 = (bf16[2,768,128]{2,1,0:T(8,128)(2,1)S(1)}, bf16[2,768,128]{2,1,0:T(8,128)(2,1)S(1)}, u32[]{:S(2)}, u32[]{:S(2)}) collective-permute-start(bf16[2,768,128]{2,1,0:T(8,128)(2,1)S(1)} %collective-permute-done.4.refs_5_), channel_id=1, source_target_pairs={{0,1},{1,2},{2,3},{3,4},{4,5},{5,6},{6,7},{7,8},{8,9},{9,10},{10,1... | collective-permute-start | bytes 1179656 | tf_op jit(solution)/shard_map/ppermute | solution.py:302
  28.9 9.0 %collective-permute-start.5 = (bf16[2,768,128]{2,1,0:T(8,128)(2,1)}, bf16[2,768,128]{2,1,0:T(8,128)(2,1)S(1)}, u32[]{:S(2)}, u32[]{:S(2)}) collective-permute-start(bf16[2,768,128]{2,1,0:T(8,128)(2,1)} %shard_map.50.refs_0_), channel_id=1, source_target_pairs={{32,48},{48,32},{33,49},{49,33},{34,50},{50,34},{35,51},{51,35},{3... | collective-permute-start | bytes 1179656 | tf_op jit(solution)/shard_map/ppermute | solution.py:305
  32.1 9.5 %collective-permute-start.3 = (bf16[2,768,128]{2,1,0:T(8,128)(2,1)S(1)}, bf16[2,768,128]{2,1,0:T(8,128)(2,1)S(1)}, u32[]{:S(2)}, u32[]{:S(2)}) collective-permute-start(bf16[2,768,128]{2,1,0:T(8,128)(2,1)S(1)} %collective-permute-done.2.refs_2_), channel_id=1, source_target_pairs={{0,1},{1,2},{2,3},{3,4},{4,5},{5,6},{6,7},{7,8},{8,9},{9,10},{10,1... | collective-permute-start | bytes 1179656 | tf_op jit(solution)/shard_map/ppermute | solution.py:302
  37.9 9.8 %collective-permute-start.7 = (bf16[2,768,128]{2,1,0:T(8,128)(2,1)S(1)}, bf16[2,768,128]{2,1,0:T(8,128)(2,1)}, u32[]{:S(2)}, u32[]{:S(2)}) collective-permute-start(bf16[2,768,128]{2,1,0:T(8,128)(2,1)S(1)} %collective-permute-done.6.refs_6_), channel_id=1, source_target_pairs={{0,1},{1,2},{2,3},{3,4},{4,5},{5,6},{6,7},{7,8},{8,9},{9,10},{10,1... | collective-permute-start | bytes 1179656 | tf_op jit(solution)/shard_map/ppermute | solution.py:302
  41.6 9.9 %collective-permute-start.11 = (bf16[2,768,128]{2,1,0:T(8,128)(2,1)S(1)}, bf16[2,768,128]{2,1,0:T(8,128)(2,1)S(1)}, u32[]{:S(2)}, u32[]{:S(2)}) collective-permute-start(bf16[2,768,128]{2,1,0:T(8,128)(2,1)S(1)} %collective-permute-done.3.refs_3_), channel_id=1, source_target_pairs={{0,1},{1,2},{2,3},{3,4},{4,5},{5,6},{6,7},{7,8},{8,9},{9,10},{10,1... | collective-permute-start | bytes 1179656 | tf_op jit(solution)/shard_map/ppermute | solution.py:302
  45.5 10.7 %collective-permute-start.8 = (bf16[2,768,128]{2,1,0:T(8,128)(2,1)S(1)}, bf16[2,768,128]{2,1,0:T(8,128)(2,1)}, u32[]{:S(2)}, u32[]{:S(2)}) collective-permute-start(bf16[2,768,128]{2,1,0:T(8,128)(2,1)S(1)} %collective-permute-done.refs_4_), channel_id=1, source_target_pairs={{32,48},{48,32},{33,49},{49,33},{34,50},{50,34},{35,51},{51,35},{3... | collective-permute-start | bytes 1179656 | tf_op jit(solution)/shard_map/ppermute | solution.py:309
  47.7 12.6 %collective-permute-start.9 = (bf16[2,768,128]{2,1,0:T(8,128)(2,1)}, bf16[2,768,128]{2,1,0:T(8,128)(2,1)S(1)}, u32[]{:S(2)}, u32[]{:S(2)}) collective-permute-start(bf16[2,768,128]{2,1,0:T(8,128)(2,1)} %collective-permute-done.7.refs_7_), channel_id=1, source_target_pairs={{0,1},{1,2},{2,3},{3,4},{4,5},{5,6},{6,7},{7,8},{8,9},{9,10},{10,1... | collective-permute-start | bytes 1179656 | tf_op jit(solution)/shard_map/ppermute | solution.py:302
  51.5 11.0 %collective-permute-start.12 = (bf16[2,768,128]{2,1,0:T(8,128)(2,1)S(1)}, bf16[2,768,128]{2,1,0:T(8,128)(2,1)S(1)}, u32[]{:S(2)}, u32[]{:S(2)}) collective-permute-start(bf16[2,768,128]{2,1,0:T(8,128)(2,1)S(1)} %collective-permute-done.11.first), channel_id=1, source_target_pairs={{0,32},{16,48},{32,16},{48,0},{1,33},{17,49},{33,17},{49,1},{2,34}... | collective-permute-start | bytes 1179656 | tf_op jit(solution)/shard_map/ppermute | solution.py:322
  56.2 1.0 copy-start
  60.3 6.9 %collective-permute-start.10 = (bf16[2,768,128]{2,1,0:T(8,128)(2,1)S(1)}, bf16[2,768,128]{2,1,0:T(8,128)(2,1)S(1)}, u32[]{:S(2)}, u32[]{:S(2)}) collective-permute-start(bf16[2,768,128]{2,1,0:T(8,128)(2,1)S(1)} %collective-permute-done.9.second), channel_id=1, source_target_pairs={{0,32},{16,48},{32,16},{48,0},{1,33},{17,49},{33,17},{49,1},{2,34}... | collective-permute-start | bytes 1179656 | tf_op jit(solution)/shard_map/ppermute | solution.py:322
  69.2 14.0 %all-to-all-start = ((bf16[8,272,128]{2,1,0:T(8,128)(2,1)}), bf16[8,272,128]{2,1,0:T(8,128)(2,1)S(1)}, u32[]{:S(2)}, u32[]{:S(2)}) async-start(bf16[8,272,128]{2,1,0:T(8,128)(2,1)} %shard_map.53), calls=%async_computation | async-start | bytes 1114112 | tf_op jit(solution)/shard_map/all_to_all | solution.py:332
  83.3 17.4 %collective-permute-start.14 = (f16[264,128]{1,0:T(8,128)(2,1)S(1)}, f16[264,128]{1,0:T(8,128)(2,1)S(1)}, u32[]{:S(2)}, u32[]{:S(2)}) collective-permute-start(f16[264,128]{1,0:T(8,128)(2,1)S(1)} %convert_element_type.9), channel_id=1, source_target_pairs={{0,335},{1,320},{2,353},{3,354},{4,387},{5,388},{6,421},{7,422},{8... | collective-permute-start | bytes 202760 | tf_op jit(solution)/shard_map/ppermute | solution.py:342
  95.4 9.2 %collective-permute-start.13 = (f16[264,128]{1,0:T(8,128)(2,1)S(1)}, f16[264,128]{1,0:T(8,128)(2,1)S(1)}, u32[]{:S(2)}, u32[]{:S(2)}) collective-permute-start(f16[264,128]{1,0:T(8,128)(2,1)S(1)} %convert_element_type.9), channel_id=1, source_target_pairs={{0,244},{1,21},{2,22},{3,55},{4,56},{5,89},{6,90},{7,123},{8,124},... | collective-permute-start | bytes 202760 | tf_op jit(solution)/shard_map/ppermute | solution.py:342

commit v9 on v8

--- a/solution.py
+++ b/solution.py
@@ -27,8 +27,12 @@
     return device_index(col_y, col_z // 4, col_z % 4 // 2, row_y, row_z), col_z % 2
 
 
+def rank_or_slot(i, core, y):
+    return i ^ (4 * (y ^ (1 - core)))
+
+
 def homes(yh, x, c, yl, z):
-    slot = yh * 4 + x
+    slot = rank_or_slot(yh * 4 + x, c, yl)
     if c == 0:
         left = (yl, z) if slot > 3 else (1 - yl, z + 4)
         right = (yl, z - slot % 4 - 1)
@@ -107,11 +111,12 @@
     return scale
 
 
-def store(out, scale, slot, kernel, total):
-    n = out.shape[-1]
+def store(out, place, slot, kernel, total):
+    n, scale = out.shape[-1], scale_of(place)
     for j in range(total.shape[1] // n):
         block = total[:, j * n : (j + 1) * n] * scale
-        out[slot + j, kernel * n : (kernel + 1) * n] = block.astype(jnp.bfloat16)
+        to = rank_or_slot(slot + j, place[0], place[1])
+        out[to, kernel * n : (kernel + 1) * n] = block.astype(jnp.bfloat16)
 
 
 def cases(place):
@@ -148,11 +153,11 @@
             left[kernel] = other()
 
         total = product(left[kernel], steps[kernel, :, 0 : 3 * n])
-        store(out, scale, 4, kernel, total)
+        store(out, place, 4, kernel, total)
 
         @pl.when(same)
         def _():
-            store(out, scale, 7, kernel, product(other(), own()))
+            store(out, place, 7, kernel, product(other(), own()))
 
         @pl.when(packed)
         def _():
@@ -161,16 +166,16 @@
             low = jnp.where(y == 0, yours, mine)
             row = lax.broadcasted_iota(jnp.int32, (n, n), 0)
             col = lax.broadcasted_iota(jnp.int32, (n, n), 1)
-            store(out, scale, 3, kernel, jnp.where(row <= col, high, low))
+            store(out, place, 3, kernel, jnp.where(row <= col, high, low))
             diagonal = jnp.sum(jnp.where(row == col, low, 0.0), axis=0, keepdims=True)
             line = lax.broadcasted_iota(jnp.int32, (EXTRA, n), 0)
-            extra = out[3, 2 * n : 2 * n + EXTRA].astype(jnp.float32)
+            to = rank_or_slot(3, core, y)
+            extra = out[to, 2 * n : 2 * n + EXTRA].astype(jnp.float32)
             extra = jnp.where(line == kernel, diagonal * scale, extra)
-            out[3, 2 * n : 2 * n + EXTRA] = extra.astype(jnp.bfloat16)
+            out[to, 2 * n : 2 * n + EXTRA] = extra.astype(jnp.bfloat16)
 
 
 def middle_kernel(place, first, second, far, left, _, __, out, steps, total):
-    scale = scale_of(place)
     _, same, turned = cases(place)
     n = out.shape[-1]
     rows = far.shape[1]
@@ -179,7 +184,7 @@
 
         @pl.when(jnp.logical_not(same))
         def _():
-            store(out, scale, 7, kernel, product(left[kernel], last))
+            store(out, place, 7, kernel, product(left[kernel], last))
 
         @pl.when(turned)
         def _():
@@ -192,19 +197,17 @@
         total[kernel] = product(far[kernel], steps[kernel, rows:])
 
 
-def late_kernel(place, far, steps, part, partial, out):
-    out[...] = partial[...]
-    scale = scale_of(place)
+def late_kernel(place, far, steps, part, _, out):
     packed, _, _ = cases(place)
     n = out.shape[-1]
     rows = far.shape[1]
     for kernel in range(2):
         total = part[kernel] + product(far[kernel], steps[kernel, 0:rows])
-        store(out, scale, 0, kernel, total[:, : 3 * n])
+        store(out, place, 0, kernel, total[:, : 3 * n])
 
         @pl.when(jnp.logical_not(packed))
         def _():
-            store(out, scale, 3, kernel, total[:, 3 * n :])
+            store(out, place, 3, kernel, total[:, 3 * n :])
 
 
 def sum_kernel(parts, out):
@@ -228,15 +231,16 @@
     out[2 * n :] = extra
 
 
-def place_kernel(total_draws, todo, a, b, feature, gradient):
+def place_kernel(total_draws, place, todo, a, b, feature, gradient):
     n = feature.shape[0]
     row = lax.broadcasted_iota(jnp.int32, (n, n), 0)
     col = lax.broadcasted_iota(jnp.int32, (n, n), 1)
+    code = todo[device_index(*[place[i] for i in range(5)])]
     for kernel, out in enumerate((feature, gradient)):
         block, line = pl.ds(kernel * n, n), pl.ds(2 * n + kernel, 1)
         power = pl.ds(2 * n + 2 + kernel, 1)
         for half in range(2):
-            second, mode = todo[2 * half] == 1, todo[2 * half + 1]
+            second, mode = code // 8**half % 2 == 1, code // 8**half // 2 % 4
             factor = jnp.exp2(jnp.where(second, b[power, :], a[power, :]) - TOP)
             got = jnp.where(second, b[block, :], a[block, :]) * factor
             extra = jnp.where(second, b[line, :], a[line, :]) * factor
@@ -328,7 +332,8 @@
         aliases={5: 0, 6: 1},
         flops=3,
     )
-    partial = call(late_kernel, shape, far[1], steps, total, partial, flops=2)
+    perms, table = routes()
+    partial = call(late_kernel, shape, far[1], steps, total, partial, aliases={4: 0}, flops=2)
     partial = lax.all_to_all(partial, ("yh", "x"), 0, 0, tiled=True)
     block = pl.pallas_call(
         sum_kernel,
@@ -338,19 +343,18 @@
         compiler_params=PARAMS,
     )(partial).astype(jnp.float16)
 
-    perms, table = routes()
     a, b = [lax.ppermute(block, AXES, p).astype(jnp.float32) for p in perms]
-    todo = lax.dynamic_index_in_dim(
-        jnp.asarray(table), lax.axis_index(AXES), 0, keepdims=False
-    )
+    codes = table[:, 0::2] + 2 * table[:, 1::2]
+    todo = jnp.asarray(codes[:, 0] + 8 * codes[:, 1])
+    where = jnp.stack([lax.axis_index(a) for a in AXES])
     out = jax.ShapeDtypeStruct((n, 2 * n), jnp.float32)
     return pl.pallas_call(
         functools.partial(place_kernel, total_draws),
         out_shape=(out, out),
-        in_specs=[SMEM, VMEM, VMEM],
+        in_specs=[SMEM, SMEM, VMEM, VMEM],
         out_specs=(VMEM, VMEM),
         compiler_params=PARAMS,
-    )(todo, a, b)
+    )(where, todo, a, b)
 
 
 def solution(mesh):

time: 107 us -> 105 us (0.981)
  the two profiles are of different devices: /device:TPU:7 before, /device:TPU:3 now
where the time goes in v9:
time: 105 us
  starting transfers between devices  60.5 us (58%)
  waiting for transfers between devices  17.9 us (17%)
  blocking collectives  15.3 us (15%)
  Pallas kernels  8.92 us (8%)
  local copies, waits for them, and re-layouts  1.08 us (1%)
    ppermute x6, starting transfers between devices, on_device(): chains = [lax.ppermute(chain, ('c', 'z'), step) for chain in chains]  21.8 us
    all_to_all x1, blocking collectives, on_device(): partial = lax.all_to_all(partial, ('yh', 'x'), 0, 0, tiled=True)  15.3 us
    ppermute x2, starting transfers between devices, on_device(): a, b = [lax.ppermute(block, AXES, p).astype(jnp.float32) for p in perms]  11.5 us
    ppermute x1, starting transfers between devices, on_device(): lax.ppermute(both, ('c', 'z'), step)  11.1 us
    ppermute x2, waiting for transfers between devices, on_device(): a, b = [lax.ppermute(block, AXES, p).astype(jnp.float32) for p in perms]  7.81 us
    ppermute x2, starting transfers between devices, on_device(): far = [lax.ppermute(chain, ('c', 'yl'), cross) for chain in chains]  6.89 us
    pallas_call x3, Pallas kernels, call(): pl.pallas_call(kernel, out_shape=out_shape, in_specs=[SMEM] + [VMEM] * le...  5.55 us
    ppermute x1, waiting for transfers between devices, on_device(): lax.ppermute(both, ('c', 'z'), first_step)  3.44 us
  transfers between devices with their start and end apart: 15, of which 6 were waited for; matrix products, arithmetic and copies ran while one was open for 0% of the time, Pallas kernels for 4%

profile of v9, /device:TPU:3, one launch (start us, length us, event | category | flops | bytes accessed | tf_op | source)
XLA Modules:
  0.0 104.7 jit_solution(7264406282921872413)
XLA Ops:
  0.6 1.8 %shard_map.50.refs_0_ = bf16[2,768,128]{2,1,0:T(8,128)(2,1)} custom-call(bf16[768,128]{1,0:T(8,128)(2,1)} %field.1, bf16[768,128]{1,0:T(8,128)(2,1)} %backward.1), custom_call_target="tpu_custom_call" | custom-call | tf_op jit(solution)/shard_map/pallas_call | solution.py:258
  2.4 11.1 %collective-permute-start.1 = (bf16[2,768,128]{2,1,0:T(8,128)(2,1)}, bf16[2,768,128]{2,1,0:T(8,128)(2,1)S(1)}, u32[]{:S(2)}, u32[]{:S(2)}) collective-permute-start(bf16[2,768,128]{2,1,0:T(8,128)(2,1)} %shard_map.50.refs_0_), channel_id=1, source_target_pairs={{0,1},{1,2},{2,3},{3,4},{4,5},{5,6},{6,7},{7,8},{8,9},{9,10},{10,1... | collective-permute-start | bytes 1179656 | tf_op jit(solution)/shard_map/ppermute | solution.py:298
  13.6 1.9 %collective-permute-start = (bf16[2,768,128]{2,1,0:T(8,128)(2,1)}, bf16[2,768,128]{2,1,0:T(8,128)(2,1)S(1)}, u32[]{:S(2)}, u32[]{:S(2)}) collective-permute-start(bf16[2,768,128]{2,1,0:T(8,128)(2,1)} %shard_map.50.refs_0_), channel_id=1, source_target_pairs={{0,32},{32,0},{1,33},{33,1},{2,34},{34,2},{3,35},{35,3},{4,36},{36... | collective-permute-start | bytes 1179656 | tf_op jit(solution)/shard_map/ppermute | solution.py:302
  15.5 1.9 %collective-permute-start.4 = (bf16[2,768,128]{2,1,0:T(8,128)(2,1)}, bf16[2,768,128]{2,1,0:T(8,128)(2,1)S(1)}, u32[]{:S(2)}, u32[]{:S(2)}) collective-permute-start(bf16[2,768,128]{2,1,0:T(8,128)(2,1)} %shard_map.50.refs_0_), channel_id=1, source_target_pairs={{0,47},{1,32},{2,33},{3,34},{4,35},{5,36},{6,37},{7,38},{8,39},{9,... | collective-permute-start | bytes 1179656 | tf_op jit(solution)/shard_map/ppermute | solution.py:299
  17.4 1.2 %collective-permute-done.1.refs_1_ = bf16[2,768,128]{2,1,0:T(8,128)(2,1)S(1)} collective-permute-done((bf16[2,768,128]{2,1,0:T(8,128)(2,1)}, bf16[2,768,128]{2,1,0:T(8,128)(2,1)S(1)}, u32[]{:S(2)}, u32[]{:S(2)}) %collective-permute-start.1) | collective-permute-done | bytes 393248 | tf_op jit(solution)/shard_map/ppermute | solution.py:298
  18.6 4.9 %collective-permute-start.2 = (bf16[2,768,128]{2,1,0:T(8,128)(2,1)S(1)}, bf16[2,768,128]{2,1,0:T(8,128)(2,1)S(1)}, u32[]{:S(2)}, u32[]{:S(2)}) collective-permute-start(bf16[2,768,128]{2,1,0:T(8,128)(2,1)S(1)} %collective-permute-done.1.refs_1_), channel_id=1, source_target_pairs={{0,1},{1,2},{2,3},{3,4},{4,5},{5,6},{6,7},{7,8},{8,9},{9,10},{10,1... | collective-permute-start | bytes 1179656 | tf_op jit(solution)/shard_map/ppermute | solution.py:306
  23.5 3.4 %collective-permute-done.4.refs_5_ = bf16[2,768,128]{2,1,0:T(8,128)(2,1)S(1)} collective-permute-done((bf16[2,768,128]{2,1,0:T(8,128)(2,1)}, bf16[2,768,128]{2,1,0:T(8,128)(2,1)S(1)}, u32[]{:S(2)}, u32[]{:S(2)}) %collective-permute-start.4) | collective-permute-done | bytes 393248 | tf_op jit(solution)/shard_map/ppermute | solution.py:299
  26.9 1.9 %collective-permute-start.6 = (bf16[2,768,128]{2,1,0:T(8,128)(2,1)S(1)}, bf16[2,768,128]{2,1,0:T(8,128)(2,1)S(1)}, u32[]{:S(2)}, u32[]{:S(2)}) collective-permute-start(bf16[2,768,128]{2,1,0:T(8,128)(2,1)S(1)} %collective-permute-done.4.refs_5_), channel_id=1, source_target_pairs={{0,1},{1,2},{2,3},{3,4},{4,5},{5,6},{6,7},{7,8},{8,9},{9,10},{10,1... | collective-permute-start | bytes 1179656 | tf_op jit(solution)/shard_map/ppermute | solution.py:306
  28.9 3.2 %collective-permute-start.5 = (bf16[2,768,128]{2,1,0:T(8,128)(2,1)}, bf16[2,768,128]{2,1,0:T(8,128)(2,1)S(1)}, u32[]{:S(2)}, u32[]{:S(2)}) collective-permute-start(bf16[2,768,128]{2,1,0:T(8,128)(2,1)} %shard_map.50.refs_0_), channel_id=1, source_target_pairs={{32,48},{48,32},{33,49},{49,33},{34,50},{50,34},{35,51},{51,35},{3... | collective-permute-start | bytes 1179656 | tf_op jit(solution)/shard_map/ppermute | solution.py:309
  32.1 0.0 collective-permute-done.2.refs_2_
  32.1 3.7 %collective-permute-start.3 = (bf16[2,768,128]{2,1,0:T(8,128)(2,1)S(1)}, bf16[2,768,128]{2,1,0:T(8,128)(2,1)S(1)}, u32[]{:S(2)}, u32[]{:S(2)}) collective-permute-start(bf16[2,768,128]{2,1,0:T(8,128)(2,1)S(1)} %collective-permute-done.2.refs_2_), channel_id=1, source_target_pairs={{0,1},{1,2},{2,3},{3,4},{4,5},{5,6},{6,7},{7,8},{8,9},{9,10},{10,1... | collective-permute-start | bytes 1179656 | tf_op jit(solution)/shard_map/ppermute | solution.py:306
  35.8 2.1 %collective-permute-done.5.refs_8_ = bf16[2,768,128]{2,1,0:T(8,128)(2,1)S(1)} collective-permute-done((bf16[2,768,128]{2,1,0:T(8,128)(2,1)}, bf16[2,768,128]{2,1,0:T(8,128)(2,1)S(1)}, u32[]{:S(2)}, u32[]{:S(2)}) %collective-permute-start.5) | collective-permute-done | bytes 393248 | tf_op jit(solution)/shard_map/ppermute | solution.py:309
  37.9 3.7 %collective-permute-start.7 = (bf16[2,768,128]{2,1,0:T(8,128)(2,1)S(1)}, bf16[2,768,128]{2,1,0:T(8,128)(2,1)}, u32[]{:S(2)}, u32[]{:S(2)}) collective-permute-start(bf16[2,768,128]{2,1,0:T(8,128)(2,1)S(1)} %collective-permute-done.6.refs_6_), channel_id=1, source_target_pairs={{0,1},{1,2},{2,3},{3,4},{4,5},{5,6},{6,7},{7,8},{8,9},{9,10},{10,1... | collective-permute-start | bytes 1179656 | tf_op jit(solution)/shard_map/ppermute | solution.py:306
  41.6 3.9 %collective-permute-start.11 = (bf16[2,768,128]{2,1,0:T(8,128)(2,1)S(1)}, bf16[2,768,128]{2,1,0:T(8,128)(2,1)S(1)}, u32[]{:S(2)}, u32[]{:S(2)}) collective-permute-start(bf16[2,768,128]{2,1,0:T(8,128)(2,1)S(1)} %collective-permute-done.3.refs_3_), channel_id=1, source_target_pairs={{0,1},{1,2},{2,3},{3,4},{4,5},{5,6},{6,7},{7,8},{8,9},{9,10},{10,1... | collective-permute-start | bytes 1179656 | tf_op jit(solution)/shard_map/ppermute | solution.py:306
  45.5 2.1 %collective-permute-start.8 = (bf16[2,768,128]{2,1,0:T(8,128)(2,1)S(1)}, bf16[2,768,128]{2,1,0:T(8,128)(2,1)}, u32[]{:S(2)}, u32[]{:S(2)}) collective-permute-start(bf16[2,768,128]{2,1,0:T(8,128)(2,1)S(1)} %collective-permute-done.refs_4_), channel_id=1, source_target_pairs={{32,48},{48,32},{33,49},{49,33},{34,50},{50,34},{35,51},{51,35},{3... | collective-permute-start | bytes 1179656 | tf_op jit(solution)/shard_map/ppermute | solution.py:313
  47.7 3.7 %collective-permute-start.9 = (bf16[2,768,128]{2,1,0:T(8,128)(2,1)}, bf16[2,768,128]{2,1,0:T(8,128)(2,1)S(1)}, u32[]{:S(2)}, u32[]{:S(2)}) collective-permute-start(bf16[2,768,128]{2,1,0:T(8,128)(2,1)} %collective-permute-done.7.refs_7_), channel_id=1, source_target_pairs={{0,1},{1,2},{2,3},{3,4},{4,5},{5,6},{6,7},{7,8},{8,9},{9,10},{10,1... | collective-permute-start | bytes 1179656 | tf_op jit(solution)/shard_map/ppermute | solution.py:306
  51.4 0.1 pad_add_fusion.place
  51.5 4.7 %collective-permute-start.12 = (bf16[2,768,128]{2,1,0:T(8,128)(2,1)S(1)}, bf16[2,768,128]{2,1,0:T(8,128)(2,1)S(1)}, u32[]{:S(2)}, u32[]{:S(2)}) collective-permute-start(bf16[2,768,128]{2,1,0:T(8,128)(2,1)S(1)} %collective-permute-done.11.first), channel_id=1, source_target_pairs={{0,32},{16,48},{32,16},{48,0},{1,33},{17,49},{33,17},{49,1},{2,34}... | collective-permute-start | bytes 1179656 | tf_op jit(solution)/shard_map/ppermute | solution.py:326
  56.2 1.0 copy-done
  57.2 3.1 %shard_map.51 = (bf16[8,272,128]{2,1,0:T(8,128)(2,1)S(1)}, bf16[2,1536,128]{2,1,0:T(8,128)(2,1)S(1)}, bf16[2,1536,512]{2,1,0:T(8,128)(2,1)S(1)}) custom-call(s32[4]{0:T(128)S(1)} %pad_add_fusion.place, bf16[2,768,128]{2,1,0:T(8,128)(2,1)S(1)} %copy-done, bf16[2,768,128]{2,1,0:T(8,128)(2,1)S(1)} %collective-permute-done.1.refs_1_, ...), custom_call_target="tpu_custom_call" | custom-call | flops 402653184 | bytes 2752512 | tf_op jit(solution)/shard_map/pallas_call | solution.py:283
  60.3 2.2 %collective-permute-start.10 = (bf16[2,768,128]{2,1,0:T(8,128)(2,1)S(1)}, bf16[2,768,128]{2,1,0:T(8,128)(2,1)S(1)}, u32[]{:S(2)}, u32[]{:S(2)}) collective-permute-start(bf16[2,768,128]{2,1,0:T(8,128)(2,1)S(1)} %collective-permute-done.9.second), channel_id=1, source_target_pairs={{0,32},{16,48},{32,16},{48,0},{1,33},{17,49},{33,17},{49,1},{2,34}... | collective-permute-start | bytes 1179656 | tf_op jit(solution)/shard_map/ppermute | solution.py:326
  62.5 1.3 %shard_map.52 = (bf16[8,272,128]{2,1,0:T(8,128)(2,1)S(1)}, bf16[2,1536,512]{2,1,0:T(8,128)(2,1)S(1)}, f32[2,128,512]{2,1,0:T(8,128)S(1)}) custom-call(s32[4]{0:T(128)S(1)} %pad_add_fusion.place, bf16[2,768,128]{2,1,0:T(8,128)(2,1)S(1)} %collective-permute-done.11.first, ...), custom_call_target="tpu_custom_call", output_to_operand_aliasing={{0}: (5, {}), {1}: (6, {})} | custom-call | flops 301989888 | bytes 2752512 | tf_op jit(solution)/shard_map/pallas_call | solution.py:283
  63.9 3.4 %collective-permute-done.10.far = bf16[2,768,128]{2,1,0:T(8,128)(2,1)S(1)} collective-permute-done((bf16[2,768,128]{2,1,0:T(8,128)(2,1)S(1)}, bf16[2,768,128]{2,1,0:T(8,128)(2,1)S(1)}, u32[]{:S(2)}, u32[]{:S(2)}) %collective-permute-start.10) | collective-permute-done | bytes 393248 | tf_op jit(solution)/shard_map/ppermute | solution.py:326
  67.2 1.1 %shard_map.53 = bf16[8,272,128]{2,1,0:T(8,128)(2,1)S(1)} custom-call(s32[4]{0:T(128)S(1)} %pad_add_fusion.place, bf16[2,768,128]{2,1,0:T(8,128)(2,1)S(1)} %collective-permute-done.10.far, bf16[2,1536,512]{2,1,0:T(8,128)(2,1)S(1)} %get-tuple-element.31.steps, f32[2,128,512]{2,1,0:T(8,128)S(1)} %get-tuple-element.32.part, ...), custom_call_target="tpu_custom_call", output_to_operand_aliasing={{}: (4, {})} | custom-call | flops 201326592 | bytes 2752512 | tf_op jit(solution)/shard_map/pallas_call | solution.py:283
  68.4 15.3 %all_to_all.5.parts = bf16[8,272,128]{2,1,0:T(8,128)(2,1)S(1)} all-to-all(bf16[8,272,128]{2,1,0:T(8,128)(2,1)S(1)} %shard_map.53), channel_id=1, replica_groups=mesh['yh'=2,'x'=4,'c'=2,'yl'=2,'z'=16] {'yh','x'}, dimensions={0} | all-to-all | bytes 1114112 | tf_op jit(solution)/shard_map/all_to_all | solution.py:337
  83.7 0.1 shard_map.54
  83.9 9.5 %collective-permute-start.14 = (f16[264,128]{1,0:T(8,128)(2,1)S(1)}, f16[264,128]{1,0:T(8,128)(2,1)S(1)}, u32[]{:S(2)}, u32[]{:S(2)}) collective-permute-start(f16[264,128]{1,0:T(8,128)(2,1)S(1)} %convert_element_type.9), channel_id=1, source_target_pairs={{0,15},{1,0},{2,33},{3,34},{4,67},{5,68},{6,101},{7,102},{8,135},{... | collective-permute-start | bytes 202760 | tf_op jit(solution)/shard_map/ppermute | solution.py:346
  93.4 1.9 %collective-permute-start.13 = (f16[264,128]{1,0:T(8,128)(2,1)S(1)}, f16[264,128]{1,0:T(8,128)(2,1)S(1)}, u32[]{:S(2)}, u32[]{:S(2)}) collective-permute-start(f16[264,128]{1,0:T(8,128)(2,1)S(1)} %convert_element_type.9), channel_id=1, source_target_pairs={{0,224},{1,1},{2,2},{3,35},{4,36},{5,69},{6,70},{7,103},{8,104},{9... | collective-permute-start | bytes 202760 | tf_op jit(solution)/shard_map/ppermute | solution.py:346
  95.4 0.1 stack.32.place
  95.4 0.5 collective-permute-done.14
  95.9 7.4 %collective-permute-done.13 = f16[264,128]{1,0:T(8,128)(2,1)S(1)} collective-permute-done((f16[264,128]{1,0:T(8,128)(2,1)S(1)}, f16[264,128]{1,0:T(8,128)(2,1)S(1)}, u32[]{:S(2)}, u32[]{:S(2)}) %collective-permute-start.13) | collective-permute-done | bytes 67616 | tf_op jit(solution)/shard_map/ppermute | solution.py:346
  103.3 1.4 %shard_map.55 = (f32[128,256]{1,0:T(8,128)}, f32[128,256]{1,0:T(8,128)}) custom-call(s32[5]{0:T(128)S(1)} %stack.32.place, s32[512]{0:T(512)S(1)} %copy-done.1, f32[264,128]{1,0:T(8,128)S(1)} %convert_element_type.10.a, f32[264,128]{1,0:T(8,128)S(1)} %convert_element_type.11.b), custom_call_target="tpu_custom_call" | custom-call | tf_op jit(solution)/shard_map/pallas_call | solution.py:351
  (14 shorter events, 0.1 us)
Async XLA Ops:
  2.4 16.1 %collective-permute-start.1 = (bf16[2,768,128]{2,1,0:T(8,128)(2,1)}, bf16[2,768,128]{2,1,0:T(8,128)(2,1)S(1)}, u32[]{:S(2)}, u32[]{:S(2)}) collective-permute-start(bf16[2,768,128]{2,1,0:T(8,128)(2,1)} %shard_map.50.refs_0_), channel_id=1, source_target_pairs={{0,1},{1,2},{2,3},{3,4},{4,5},{5,6},{6,7},{7,8},{8,9},{9,10},{10,1... | collective-permute-start | bytes 1179656 | tf_op jit(solution)/shard_map/ppermute | solution.py:298
  13.6 5.0 %collective-permute-start = (bf16[2,768,128]{2,1,0:T(8,128)(2,1)}, bf16[2,768,128]{2,1,0:T(8,128)(2,1)S(1)}, u32[]{:S(2)}, u32[]{:S(2)}) collective-permute-start(bf16[2,768,128]{2,1,0:T(8,128)(2,1)} %shard_map.50.refs_0_), channel_id=1, source_target_pairs={{0,32},{32,0},{1,33},{33,1},{2,34},{34,2},{3,35},{35,3},{4,36},{36... | collective-permute-start | bytes 1179656 | tf_op jit(solution)/shard_map/ppermute | solution.py:302
  15.5 11.4 %collective-permute-start.4 = (bf16[2,768,128]{2,1,0:T(8,128)(2,1)}, bf16[2,768,128]{2,1,0:T(8,128)(2,1)S(1)}, u32[]{:S(2)}, u32[]{:S(2)}) collective-permute-start(bf16[2,768,128]{2,1,0:T(8,128)(2,1)} %shard_map.50.refs_0_), channel_id=1, source_target_pairs={{0,47},{1,32},{2,33},{3,34},{4,35},{5,36},{6,37},{7,38},{8,39},{9,... | collective-permute-start | bytes 1179656 | tf_op jit(solution)/shard_map/ppermute | solution.py:299
  18.6 13.5 %collective-permute-start.2 = (bf16[2,768,128]{2,1,0:T(8,128)(2,1)S(1)}, bf16[2,768,128]{2,1,0:T(8,128)(2,1)S(1)}, u32[]{:S(2)}, u32[]{:S(2)}) collective-permute-start(bf16[2,768,128]{2,1,0:T(8,128)(2,1)S(1)} %collective-permute-done.1.refs_1_), channel_id=1, source_target_pairs={{0,1},{1,2},{2,3},{3,4},{4,5},{5,6},{6,7},{7,8},{8,9},{9,10},{10,1... | collective-permute-start | bytes 1179656 | tf_op jit(solution)/shard_map/ppermute | solution.py:306
  26.9 8.8 %collective-permute-start.6 = (bf16[2,768,128]{2,1,0:T(8,128)(2,1)S(1)}, bf16[2,768,128]{2,1,0:T(8,128)(2,1)S(1)}, u32[]{:S(2)}, u32[]{:S(2)}) collective-permute-start(bf16[2,768,128]{2,1,0:T(8,128)(2,1)S(1)} %collective-permute-done.4.refs_5_), channel_id=1, source_target_pairs={{0,1},{1,2},{2,3},{3,4},{4,5},{5,6},{6,7},{7,8},{8,9},{9,10},{10,1... | collective-permute-start | bytes 1179656 | tf_op jit(solution)/shard_map/ppermute | solution.py:306
  28.9 9.0 %collective-permute-start.5 = (bf16[2,768,128]{2,1,0:T(8,128)(2,1)}, bf16[2,768,128]{2,1,0:T(8,128)(2,1)S(1)}, u32[]{:S(2)}, u32[]{:S(2)}) collective-permute-start(bf16[2,768,128]{2,1,0:T(8,128)(2,1)} %shard_map.50.refs_0_), channel_id=1, source_target_pairs={{32,48},{48,32},{33,49},{49,33},{34,50},{50,34},{35,51},{51,35},{3... | collective-permute-start | bytes 1179656 | tf_op jit(solution)/shard_map/ppermute | solution.py:309
  32.1 9.5 %collective-permute-start.3 = (bf16[2,768,128]{2,1,0:T(8,128)(2,1)S(1)}, bf16[2,768,128]{2,1,0:T(8,128)(2,1)S(1)}, u32[]{:S(2)}, u32[]{:S(2)}) collective-permute-start(bf16[2,768,128]{2,1,0:T(8,128)(2,1)S(1)} %collective-permute-done.2.refs_2_), channel_id=1, source_target_pairs={{0,1},{1,2},{2,3},{3,4},{4,5},{5,6},{6,7},{7,8},{8,9},{9,10},{10,1... | collective-permute-start | bytes 1179656 | tf_op jit(solution)/shard_map/ppermute | solution.py:306
  37.9 9.8 %collective-permute-start.7 = (bf16[2,768,128]{2,1,0:T(8,128)(2,1)S(1)}, bf16[2,768,128]{2,1,0:T(8,128)(2,1)}, u32[]{:S(2)}, u32[]{:S(2)}) collective-permute-start(bf16[2,768,128]{2,1,0:T(8,128)(2,1)S(1)} %collective-permute-done.6.refs_6_), channel_id=1, source_target_pairs={{0,1},{1,2},{2,3},{3,4},{4,5},{5,6},{6,7},{7,8},{8,9},{9,10},{10,1... | collective-permute-start | bytes 1179656 | tf_op jit(solution)/shard_map/ppermute | solution.py:306
  41.6 9.9 %collective-permute-start.11 = (bf16[2,768,128]{2,1,0:T(8,128)(2,1)S(1)}, bf16[2,768,128]{2,1,0:T(8,128)(2,1)S(1)}, u32[]{:S(2)}, u32[]{:S(2)}) collective-permute-start(bf16[2,768,128]{2,1,0:T(8,128)(2,1)S(1)} %collective-permute-done.3.refs_3_), channel_id=1, source_target_pairs={{0,1},{1,2},{2,3},{3,4},{4,5},{5,6},{6,7},{7,8},{8,9},{9,10},{10,1... | collective-permute-start | bytes 1179656 | tf_op jit(solution)/shard_map/ppermute | solution.py:306
  45.5 10.7 %collective-permute-start.8 = (bf16[2,768,128]{2,1,0:T(8,128)(2,1)S(1)}, bf16[2,768,128]{2,1,0:T(8,128)(2,1)}, u32[]{:S(2)}, u32[]{:S(2)}) collective-permute-start(bf16[2,768,128]{2,1,0:T(8,128)(2,1)S(1)} %collective-permute-done.refs_4_), channel_id=1, source_target_pairs={{32,48},{48,32},{33,49},{49,33},{34,50},{50,34},{35,51},{51,35},{3... | collective-permute-start | bytes 1179656 | tf_op jit(solution)/shard_map/ppermute | solution.py:313
  47.7 12.6 %collective-permute-start.9 = (bf16[2,768,128]{2,1,0:T(8,128)(2,1)}, bf16[2,768,128]{2,1,0:T(8,128)(2,1)S(1)}, u32[]{:S(2)}, u32[]{:S(2)}) collective-permute-start(bf16[2,768,128]{2,1,0:T(8,128)(2,1)} %collective-permute-done.7.refs_7_), channel_id=1, source_target_pairs={{0,1},{1,2},{2,3},{3,4},{4,5},{5,6},{6,7},{7,8},{8,9},{9,10},{10,1... | collective-permute-start | bytes 1179656 | tf_op jit(solution)/shard_map/ppermute | solution.py:306
  51.5 11.0 %collective-permute-start.12 = (bf16[2,768,128]{2,1,0:T(8,128)(2,1)S(1)}, bf16[2,768,128]{2,1,0:T(8,128)(2,1)S(1)}, u32[]{:S(2)}, u32[]{:S(2)}) collective-permute-start(bf16[2,768,128]{2,1,0:T(8,128)(2,1)S(1)} %collective-permute-done.11.first), channel_id=1, source_target_pairs={{0,32},{16,48},{32,16},{48,0},{1,33},{17,49},{33,17},{49,1},{2,34}... | collective-permute-start | bytes 1179656 | tf_op jit(solution)/shard_map/ppermute | solution.py:326
  56.2 1.0 copy-start
  60.3 6.9 %collective-permute-start.10 = (bf16[2,768,128]{2,1,0:T(8,128)(2,1)S(1)}, bf16[2,768,128]{2,1,0:T(8,128)(2,1)S(1)}, u32[]{:S(2)}, u32[]{:S(2)}) collective-permute-start(bf16[2,768,128]{2,1,0:T(8,128)(2,1)S(1)} %collective-permute-done.9.second), channel_id=1, source_target_pairs={{0,32},{16,48},{32,16},{48,0},{1,33},{17,49},{33,17},{49,1},{2,34}... | collective-permute-start | bytes 1179656 | tf_op jit(solution)/shard_map/ppermute | solution.py:326
  67.2 36.1 %copy-start.1 = (s32[512]{0:T(512)S(1)}, s32[512]{0:T(512)}, u32[]{:S(2)}) copy-start(s32[512]{0:T(512)} %constant.27.clone.todo) | copy-start | bytes 6148
  83.9 12.0 %collective-permute-start.14 = (f16[264,128]{1,0:T(8,128)(2,1)S(1)}, f16[264,128]{1,0:T(8,128)(2,1)S(1)}, u32[]{:S(2)}, u32[]{:S(2)}) collective-permute-start(f16[264,128]{1,0:T(8,128)(2,1)S(1)} %convert_element_type.9), channel_id=1, source_target_pairs={{0,15},{1,0},{2,33},{3,34},{4,67},{5,68},{6,101},{7,102},{8,135},{... | collective-permute-start | bytes 202760 | tf_op jit(solution)/shard_map/ppermute | solution.py:346
  93.4 9.8 %collective-permute-start.13 = (f16[264,128]{1,0:T(8,128)(2,1)S(1)}, f16[264,128]{1,0:T(8,128)(2,1)S(1)}, u32[]{:S(2)}, u32[]{:S(2)}) collective-permute-start(f16[264,128]{1,0:T(8,128)(2,1)S(1)} %convert_element_type.9), channel_id=1, source_target_pairs={{0,224},{1,1},{2,2},{3,35},{4,36},{5,69},{6,70},{7,103},{8,104},{9... | collective-permute-start | bytes 202760 | tf_op jit(solution)/shard_map/ppermute | solution.py:346

commit v10 on v9

--- a/solution.py
+++ b/solution.py
@@ -57,15 +57,31 @@
     into = [[] for _ in range(512)]
     for e, edge in enumerate(edges):
         into[edge[1]].append(e)
+    def hops(e):
+        there = np.unravel_index(edges[e][0], SIZES), np.unravel_index(edges[e][1], SIZES)
+        (h0, x0, _, l0, z0), (h1, x1, _, l1, z1) = there
+        return sum(
+            min((p - q) % n, (q - p) % n)
+            for p, q, n in ((x0, x1, 4), (2 * h0 + l0, 2 * h1 + l1, 4), (z0, z1, 16))
+        )
+
     turn = [-1] * len(edges)
     for first in range(len(edges)):
-        e = first
+        e, ways = first, ([], [])
         while turn[e] < 0:
             turn[e] = 0
             pair = into[edges[e][1]]
             other = pair[0] + pair[1] - e
             turn[other] = 1
+            ways[0].append(e)
+            ways[1].append(other)
             e = other ^ 1
+        costs = [sum(map(hops, way)) for way in ways]
+        if ways[0] and costs[1] < costs[0]:
+            for e in ways[0]:
+                turn[e] = 1
+            for e in ways[1]:
+                turn[e] = 0
     perms = [[], []]
     table = np.zeros((512, 4), np.int32)
     for e, (source, to, half, mode) in enumerate(edges):

time: 105 us -> 104 us (level)
  the two profiles are of different devices: /device:TPU:3 before, /device:TPU:7 now
where the time goes in v10:
time: 104 us; the launch traced here: 103 us
  starting transfers between devices  63 us (61%)
  blocking collectives  14.6 us (14%)
  waiting for transfers between devices  14 us (13%)
  Pallas kernels  8.91 us (9%)
  local copies, waits for them, and re-layouts  1.08 us (1%)
    ppermute x6, starting transfers between devices, on_device(): chains = [lax.ppermute(chain, ('c', 'z'), step) for chain in chains]  21.8 us
    all_to_all x1, blocking collectives, on_device(): partial = lax.all_to_all(partial, ('yh', 'x'), 0, 0, tiled=True)  14.6 us
    ppermute x2, starting transfers between devices, on_device(): a, b = [lax.ppermute(block, AXES, p).astype(jnp.float32) for p in perms]  14 us
    ppermute x1, starting transfers between devices, on_device(): lax.ppermute(both, ('c', 'z'), step)  11.1 us
    ppermute x2, starting transfers between devices, on_device(): far = [lax.ppermute(chain, ('c', 'yl'), cross) for chain in chains]  6.9 us
    pallas_call x3, Pallas kernels, call(): pl.pallas_call(kernel, out_shape=out_shape, in_specs=[SMEM] + [VMEM] * le...  5.54 us
    ppermute x2, waiting for transfers between devices, on_device(): a, b = [lax.ppermute(block, AXES, p).astype(jnp.float32) for p in perms]  3.95 us
    ppermute x1, waiting for transfers between devices, on_device(): lax.ppermute(both, ('c', 'z'), first_step)  3.44 us
  transfers between devices with their start and end apart: 15, of which 5 were waited for; matrix products, arithmetic and copies ran while one was open for 0% of the time, Pallas kernels for 4%

profile of v10, /device:TPU:7, one launch (start us, length us, event | category | flops | bytes accessed | tf_op | source)
XLA Modules:
  0.0 102.7 jit_solution(16049548390688662851)
XLA Ops:
  0.6 1.8 %shard_map.50.refs_0_ = bf16[2,768,128]{2,1,0:T(8,128)(2,1)} custom-call(bf16[768,128]{1,0:T(8,128)(2,1)} %field.1, bf16[768,128]{1,0:T(8,128)(2,1)} %backward.1), custom_call_target="tpu_custom_call" | custom-call | tf_op jit(solution)/shard_map/pallas_call | solution.py:274
  2.4 11.1 %collective-permute-start.1 = (bf16[2,768,128]{2,1,0:T(8,128)(2,1)}, bf16[2,768,128]{2,1,0:T(8,128)(2,1)S(1)}, u32[]{:S(2)}, u32[]{:S(2)}) collective-permute-start(bf16[2,768,128]{2,1,0:T(8,128)(2,1)} %shard_map.50.refs_0_), channel_id=1, source_target_pairs={{0,1},{1,2},{2,3},{3,4},{4,5},{5,6},{6,7},{7,8},{8,9},{9,10},{10,1... | collective-permute-start | bytes 1179656 | tf_op jit(solution)/shard_map/ppermute | solution.py:314
  13.6 1.9 %collective-permute-start = (bf16[2,768,128]{2,1,0:T(8,128)(2,1)}, bf16[2,768,128]{2,1,0:T(8,128)(2,1)S(1)}, u32[]{:S(2)}, u32[]{:S(2)}) collective-permute-start(bf16[2,768,128]{2,1,0:T(8,128)(2,1)} %shard_map.50.refs_0_), channel_id=1, source_target_pairs={{0,32},{32,0},{1,33},{33,1},{2,34},{34,2},{3,35},{35,3},{4,36},{36... | collective-permute-start | bytes 1179656 | tf_op jit(solution)/shard_map/ppermute | solution.py:318
  15.5 1.9 %collective-permute-start.4 = (bf16[2,768,128]{2,1,0:T(8,128)(2,1)}, bf16[2,768,128]{2,1,0:T(8,128)(2,1)S(1)}, u32[]{:S(2)}, u32[]{:S(2)}) collective-permute-start(bf16[2,768,128]{2,1,0:T(8,128)(2,1)} %shard_map.50.refs_0_), channel_id=1, source_target_pairs={{0,47},{1,32},{2,33},{3,34},{4,35},{5,36},{6,37},{7,38},{8,39},{9,... | collective-permute-start | bytes 1179656 | tf_op jit(solution)/shard_map/ppermute | solution.py:315
  17.4 1.2 %collective-permute-done.1.refs_1_ = bf16[2,768,128]{2,1,0:T(8,128)(2,1)S(1)} collective-permute-done((bf16[2,768,128]{2,1,0:T(8,128)(2,1)}, bf16[2,768,128]{2,1,0:T(8,128)(2,1)S(1)}, u32[]{:S(2)}, u32[]{:S(2)}) %collective-permute-start.1) | collective-permute-done | bytes 393248 | tf_op jit(solution)/shard_map/ppermute | solution.py:314
  18.6 0.0 collective-permute-done.refs_4_
  18.6 4.9 %collective-permute-start.2 = (bf16[2,768,128]{2,1,0:T(8,128)(2,1)S(1)}, bf16[2,768,128]{2,1,0:T(8,128)(2,1)S(1)}, u32[]{:S(2)}, u32[]{:S(2)}) collective-permute-start(bf16[2,768,128]{2,1,0:T(8,128)(2,1)S(1)} %collective-permute-done.1.refs_1_), channel_id=1, source_target_pairs={{0,1},{1,2},{2,3},{3,4},{4,5},{5,6},{6,7},{7,8},{8,9},{9,10},{10,1... | collective-permute-start | bytes 1179656 | tf_op jit(solution)/shard_map/ppermute | solution.py:322
  23.5 3.4 %collective-permute-done.4.refs_5_ = bf16[2,768,128]{2,1,0:T(8,128)(2,1)S(1)} collective-permute-done((bf16[2,768,128]{2,1,0:T(8,128)(2,1)}, bf16[2,768,128]{2,1,0:T(8,128)(2,1)S(1)}, u32[]{:S(2)}, u32[]{:S(2)}) %collective-permute-start.4) | collective-permute-done | bytes 393248 | tf_op jit(solution)/shard_map/ppermute | solution.py:315
  26.9 1.9 %collective-permute-start.6 = (bf16[2,768,128]{2,1,0:T(8,128)(2,1)S(1)}, bf16[2,768,128]{2,1,0:T(8,128)(2,1)S(1)}, u32[]{:S(2)}, u32[]{:S(2)}) collective-permute-start(bf16[2,768,128]{2,1,0:T(8,128)(2,1)S(1)} %collective-permute-done.4.refs_5_), channel_id=1, source_target_pairs={{0,1},{1,2},{2,3},{3,4},{4,5},{5,6},{6,7},{7,8},{8,9},{9,10},{10,1... | collective-permute-start | bytes 1179656 | tf_op jit(solution)/shard_map/ppermute | solution.py:322
  28.9 3.2 %collective-permute-start.5 = (bf16[2,768,128]{2,1,0:T(8,128)(2,1)}, bf16[2,768,128]{2,1,0:T(8,128)(2,1)S(1)}, u32[]{:S(2)}, u32[]{:S(2)}) collective-permute-start(bf16[2,768,128]{2,1,0:T(8,128)(2,1)} %shard_map.50.refs_0_), channel_id=1, source_target_pairs={{32,48},{48,32},{33,49},{49,33},{34,50},{50,34},{35,51},{51,35},{3... | collective-permute-start | bytes 1179656 | tf_op jit(solution)/shard_map/ppermute | solution.py:325
  32.1 0.0 collective-permute-done.2.refs_2_
  32.1 3.7 %collective-permute-start.3 = (bf16[2,768,128]{2,1,0:T(8,128)(2,1)S(1)}, bf16[2,768,128]{2,1,0:T(8,128)(2,1)S(1)}, u32[]{:S(2)}, u32[]{:S(2)}) collective-permute-start(bf16[2,768,128]{2,1,0:T(8,128)(2,1)S(1)} %collective-permute-done.2.refs_2_), channel_id=1, source_target_pairs={{0,1},{1,2},{2,3},{3,4},{4,5},{5,6},{6,7},{7,8},{8,9},{9,10},{10,1... | collective-permute-start | bytes 1179656 | tf_op jit(solution)/shard_map/ppermute | solution.py:322
  35.8 2.1 %collective-permute-done.5.refs_8_ = bf16[2,768,128]{2,1,0:T(8,128)(2,1)S(1)} collective-permute-done((bf16[2,768,128]{2,1,0:T(8,128)(2,1)}, bf16[2,768,128]{2,1,0:T(8,128)(2,1)S(1)}, u32[]{:S(2)}, u32[]{:S(2)}) %collective-permute-start.5) | collective-permute-done | bytes 393248 | tf_op jit(solution)/shard_map/ppermute | solution.py:325
  37.9 3.7 %collective-permute-start.7 = (bf16[2,768,128]{2,1,0:T(8,128)(2,1)S(1)}, bf16[2,768,128]{2,1,0:T(8,128)(2,1)}, u32[]{:S(2)}, u32[]{:S(2)}) collective-permute-start(bf16[2,768,128]{2,1,0:T(8,128)(2,1)S(1)} %collective-permute-done.6.refs_6_), channel_id=1, source_target_pairs={{0,1},{1,2},{2,3},{3,4},{4,5},{5,6},{6,7},{7,8},{8,9},{9,10},{10,1... | collective-permute-start | bytes 1179656 | tf_op jit(solution)/shard_map/ppermute | solution.py:322
  41.6 3.9 %collective-permute-start.11 = (bf16[2,768,128]{2,1,0:T(8,128)(2,1)S(1)}, bf16[2,768,128]{2,1,0:T(8,128)(2,1)S(1)}, u32[]{:S(2)}, u32[]{:S(2)}) collective-permute-start(bf16[2,768,128]{2,1,0:T(8,128)(2,1)S(1)} %collective-permute-done.3.refs_3_), channel_id=1, source_target_pairs={{0,1},{1,2},{2,3},{3,4},{4,5},{5,6},{6,7},{7,8},{8,9},{9,10},{10,1... | collective-permute-start | bytes 1179656 | tf_op jit(solution)/shard_map/ppermute | solution.py:322
  45.5 2.1 %collective-permute-start.8 = (bf16[2,768,128]{2,1,0:T(8,128)(2,1)S(1)}, bf16[2,768,128]{2,1,0:T(8,128)(2,1)}, u32[]{:S(2)}, u32[]{:S(2)}) collective-permute-start(bf16[2,768,128]{2,1,0:T(8,128)(2,1)S(1)} %collective-permute-done.refs_4_), channel_id=1, source_target_pairs={{32,48},{48,32},{33,49},{49,33},{34,50},{50,34},{35,51},{51,35},{3... | collective-permute-start | bytes 1179656 | tf_op jit(solution)/shard_map/ppermute | solution.py:329
  47.7 3.7 %collective-permute-start.9 = (bf16[2,768,128]{2,1,0:T(8,128)(2,1)}, bf16[2,768,128]{2,1,0:T(8,128)(2,1)S(1)}, u32[]{:S(2)}, u32[]{:S(2)}) collective-permute-start(bf16[2,768,128]{2,1,0:T(8,128)(2,1)} %collective-permute-done.7.refs_7_), channel_id=1, source_target_pairs={{0,1},{1,2},{2,3},{3,4},{4,5},{5,6},{6,7},{7,8},{8,9},{9,10},{10,1... | collective-permute-start | bytes 1179656 | tf_op jit(solution)/shard_map/ppermute | solution.py:322
  51.4 0.1 pad_add_fusion.place
  51.5 4.7 %collective-permute-start.12 = (bf16[2,768,128]{2,1,0:T(8,128)(2,1)S(1)}, bf16[2,768,128]{2,1,0:T(8,128)(2,1)S(1)}, u32[]{:S(2)}, u32[]{:S(2)}) collective-permute-start(bf16[2,768,128]{2,1,0:T(8,128)(2,1)S(1)} %collective-permute-done.11.first), channel_id=1, source_target_pairs={{0,32},{16,48},{32,16},{48,0},{1,33},{17,49},{33,17},{49,1},{2,34}... | collective-permute-start | bytes 1179656 | tf_op jit(solution)/shard_map/ppermute | solution.py:342
  56.2 1.0 copy-done
  57.2 3.1 %shard_map.51 = (bf16[8,272,128]{2,1,0:T(8,128)(2,1)S(1)}, bf16[2,1536,128]{2,1,0:T(8,128)(2,1)S(1)}, bf16[2,1536,512]{2,1,0:T(8,128)(2,1)S(1)}) custom-call(s32[4]{0:T(128)S(1)} %pad_add_fusion.place, bf16[2,768,128]{2,1,0:T(8,128)(2,1)S(1)} %copy-done, bf16[2,768,128]{2,1,0:T(8,128)(2,1)S(1)} %collective-permute-done.1.refs_1_, ...), custom_call_target="tpu_custom_call" | custom-call | flops 402653184 | bytes 2752512 | tf_op jit(solution)/shard_map/pallas_call | solution.py:299
  60.3 2.2 %collective-permute-start.10 = (bf16[2,768,128]{2,1,0:T(8,128)(2,1)S(1)}, bf16[2,768,128]{2,1,0:T(8,128)(2,1)S(1)}, u32[]{:S(2)}, u32[]{:S(2)}) collective-permute-start(bf16[2,768,128]{2,1,0:T(8,128)(2,1)S(1)} %collective-permute-done.9.second), channel_id=1, source_target_pairs={{0,32},{16,48},{32,16},{48,0},{1,33},{17,49},{33,17},{49,1},{2,34}... | collective-permute-start | bytes 1179656 | tf_op jit(solution)/shard_map/ppermute | solution.py:342
  62.5 1.3 %shard_map.52 = (bf16[8,272,128]{2,1,0:T(8,128)(2,1)S(1)}, bf16[2,1536,512]{2,1,0:T(8,128)(2,1)S(1)}, f32[2,128,512]{2,1,0:T(8,128)S(1)}) custom-call(s32[4]{0:T(128)S(1)} %pad_add_fusion.place, bf16[2,768,128]{2,1,0:T(8,128)(2,1)S(1)} %collective-permute-done.11.first, ...), custom_call_target="tpu_custom_call", output_to_operand_aliasing={{0}: (5, {}), {1}: (6, {})} | custom-call | flops 301989888 | bytes 2752512 | tf_op jit(solution)/shard_map/pallas_call | solution.py:299
  63.9 3.4 %collective-permute-done.10.far = bf16[2,768,128]{2,1,0:T(8,128)(2,1)S(1)} collective-permute-done((bf16[2,768,128]{2,1,0:T(8,128)(2,1)S(1)}, bf16[2,768,128]{2,1,0:T(8,128)(2,1)S(1)}, u32[]{:S(2)}, u32[]{:S(2)}) %collective-permute-start.10) | collective-permute-done | bytes 393248 | tf_op jit(solution)/shard_map/ppermute | solution.py:342
  67.2 1.1 %shard_map.53 = bf16[8,272,128]{2,1,0:T(8,128)(2,1)S(1)} custom-call(s32[4]{0:T(128)S(1)} %pad_add_fusion.place, bf16[2,768,128]{2,1,0:T(8,128)(2,1)S(1)} %collective-permute-done.10.far, bf16[2,1536,512]{2,1,0:T(8,128)(2,1)S(1)} %get-tuple-element.31.steps, f32[2,128,512]{2,1,0:T(8,128)S(1)} %get-tuple-element.32.part, ...), custom_call_target="tpu_custom_call", output_to_operand_aliasing={{}: (4, {})} | custom-call | flops 201326592 | bytes 2752512 | tf_op jit(solution)/shard_map/pallas_call | solution.py:299
  68.4 14.6 %all_to_all.5.parts = bf16[8,272,128]{2,1,0:T(8,128)(2,1)S(1)} all-to-all(bf16[8,272,128]{2,1,0:T(8,128)(2,1)S(1)} %shard_map.53), channel_id=1, replica_groups=mesh['yh'=2,'x'=4,'c'=2,'yl'=2,'z'=16] {'yh','x'}, dimensions={0} | all-to-all | bytes 1114112 | tf_op jit(solution)/shard_map/all_to_all | solution.py:353
  83.0 0.1 shard_map.54
  83.2 11.2 %collective-permute-start.14 = (f16[264,128]{1,0:T(8,128)(2,1)S(1)}, f16[264,128]{1,0:T(8,128)(2,1)S(1)}, u32[]{:S(2)}, u32[]{:S(2)}) collective-permute-start(f16[264,128]{1,0:T(8,128)(2,1)S(1)} %convert_element_type.9), channel_id=1, source_target_pairs={{0,15},{1,0},{2,33},{3,34},{4,67},{5,68},{6,101},{7,102},{8,104},{... | collective-permute-start | bytes 202760 | tf_op jit(solution)/shard_map/ppermute | solution.py:362
  94.4 2.8 %collective-permute-start.13 = (f16[264,128]{1,0:T(8,128)(2,1)S(1)}, f16[264,128]{1,0:T(8,128)(2,1)S(1)}, u32[]{:S(2)}, u32[]{:S(2)}) collective-permute-start(f16[264,128]{1,0:T(8,128)(2,1)S(1)} %convert_element_type.9), channel_id=1, source_target_pairs={{0,224},{1,1},{2,2},{3,35},{4,36},{5,69},{6,70},{7,103},{8,135},{9... | collective-permute-start | bytes 202760 | tf_op jit(solution)/shard_map/ppermute | solution.py:362
  97.2 0.1 stack.32.place
  97.3 3.9 %collective-permute-done.13 = f16[264,128]{1,0:T(8,128)(2,1)S(1)} collective-permute-done((f16[264,128]{1,0:T(8,128)(2,1)S(1)}, f16[264,128]{1,0:T(8,128)(2,1)S(1)}, u32[]{:S(2)}, u32[]{:S(2)}) %collective-permute-start.13) | collective-permute-done | bytes 67616 | tf_op jit(solution)/shard_map/ppermute | solution.py:362
  101.2 1.4 %shard_map.55 = (f32[128,256]{1,0:T(8,128)}, f32[128,256]{1,0:T(8,128)}) custom-call(s32[5]{0:T(128)S(1)} %stack.32.place, s32[512]{0:T(512)S(1)} %copy-done.1, f32[264,128]{1,0:T(8,128)S(1)} %convert_element_type.10.a, f32[264,128]{1,0:T(8,128)S(1)} %convert_element_type.11.b), custom_call_target="tpu_custom_call" | custom-call | tf_op jit(solution)/shard_map/pallas_call | solution.py:367
  (14 shorter events, 0.1 us)
Async XLA Ops:
  2.4 16.1 %collective-permute-start.1 = (bf16[2,768,128]{2,1,0:T(8,128)(2,1)}, bf16[2,768,128]{2,1,0:T(8,128)(2,1)S(1)}, u32[]{:S(2)}, u32[]{:S(2)}) collective-permute-start(bf16[2,768,128]{2,1,0:T(8,128)(2,1)} %shard_map.50.refs_0_), channel_id=1, source_target_pairs={{0,1},{1,2},{2,3},{3,4},{4,5},{5,6},{6,7},{7,8},{8,9},{9,10},{10,1... | collective-permute-start | bytes 1179656 | tf_op jit(solution)/shard_map/ppermute | solution.py:314
  13.6 5.0 %collective-permute-start = (bf16[2,768,128]{2,1,0:T(8,128)(2,1)}, bf16[2,768,128]{2,1,0:T(8,128)(2,1)S(1)}, u32[]{:S(2)}, u32[]{:S(2)}) collective-permute-start(bf16[2,768,128]{2,1,0:T(8,128)(2,1)} %shard_map.50.refs_0_), channel_id=1, source_target_pairs={{0,32},{32,0},{1,33},{33,1},{2,34},{34,2},{3,35},{35,3},{4,36},{36... | collective-permute-start | bytes 1179656 | tf_op jit(solution)/shard_map/ppermute | solution.py:318
  15.5 11.4 %collective-permute-start.4 = (bf16[2,768,128]{2,1,0:T(8,128)(2,1)}, bf16[2,768,128]{2,1,0:T(8,128)(2,1)S(1)}, u32[]{:S(2)}, u32[]{:S(2)}) collective-permute-start(bf16[2,768,128]{2,1,0:T(8,128)(2,1)} %shard_map.50.refs_0_), channel_id=1, source_target_pairs={{0,47},{1,32},{2,33},{3,34},{4,35},{5,36},{6,37},{7,38},{8,39},{9,... | collective-permute-start | bytes 1179656 | tf_op jit(solution)/shard_map/ppermute | solution.py:315
  18.6 13.5 %collective-permute-start.2 = (bf16[2,768,128]{2,1,0:T(8,128)(2,1)S(1)}, bf16[2,768,128]{2,1,0:T(8,128)(2,1)S(1)}, u32[]{:S(2)}, u32[]{:S(2)}) collective-permute-start(bf16[2,768,128]{2,1,0:T(8,128)(2,1)S(1)} %collective-permute-done.1.refs_1_), channel_id=1, source_target_pairs={{0,1},{1,2},{2,3},{3,4},{4,5},{5,6},{6,7},{7,8},{8,9},{9,10},{10,1... | collective-permute-start | bytes 1179656 | tf_op jit(solution)/shard_map/ppermute | solution.py:322
  26.9 8.8 %collective-permute-start.6 = (bf16[2,768,128]{2,1,0:T(8,128)(2,1)S(1)}, bf16[2,768,128]{2,1,0:T(8,128)(2,1)S(1)}, u32[]{:S(2)}, u32[]{:S(2)}) collective-permute-start(bf16[2,768,128]{2,1,0:T(8,128)(2,1)S(1)} %collective-permute-done.4.refs_5_), channel_id=1, source_target_pairs={{0,1},{1,2},{2,3},{3,4},{4,5},{5,6},{6,7},{7,8},{8,9},{9,10},{10,1... | collective-permute-start | bytes 1179656 | tf_op jit(solution)/shard_map/ppermute | solution.py:322
  28.9 9.0 %collective-permute-start.5 = (bf16[2,768,128]{2,1,0:T(8,128)(2,1)}, bf16[2,768,128]{2,1,0:T(8,128)(2,1)S(1)}, u32[]{:S(2)}, u32[]{:S(2)}) collective-permute-start(bf16[2,768,128]{2,1,0:T(8,128)(2,1)} %shard_map.50.refs_0_), channel_id=1, source_target_pairs={{32,48},{48,32},{33,49},{49,33},{34,50},{50,34},{35,51},{51,35},{3... | collective-permute-start | bytes 1179656 | tf_op jit(solution)/shard_map/ppermute | solution.py:325
  32.1 9.5 %collective-permute-start.3 = (bf16[2,768,128]{2,1,0:T(8,128)(2,1)S(1)}, bf16[2,768,128]{2,1,0:T(8,128)(2,1)S(1)}, u32[]{:S(2)}, u32[]{:S(2)}) collective-permute-start(bf16[2,768,128]{2,1,0:T(8,128)(2,1)S(1)} %collective-permute-done.2.refs_2_), channel_id=1, source_target_pairs={{0,1},{1,2},{2,3},{3,4},{4,5},{5,6},{6,7},{7,8},{8,9},{9,10},{10,1... | collective-permute-start | bytes 1179656 | tf_op jit(solution)/shard_map/ppermute | solution.py:322
  37.9 9.8 %collective-permute-start.7 = (bf16[2,768,128]{2,1,0:T(8,128)(2,1)S(1)}, bf16[2,768,128]{2,1,0:T(8,128)(2,1)}, u32[]{:S(2)}, u32[]{:S(2)}) collective-permute-start(bf16[2,768,128]{2,1,0:T(8,128)(2,1)S(1)} %collective-permute-done.6.refs_6_), channel_id=1, source_target_pairs={{0,1},{1,2},{2,3},{3,4},{4,5},{5,6},{6,7},{7,8},{8,9},{9,10},{10,1... | collective-permute-start | bytes 1179656 | tf_op jit(solution)/shard_map/ppermute | solution.py:322
  41.6 9.9 %collective-permute-start.11 = (bf16[2,768,128]{2,1,0:T(8,128)(2,1)S(1)}, bf16[2,768,128]{2,1,0:T(8,128)(2,1)S(1)}, u32[]{:S(2)}, u32[]{:S(2)}) collective-permute-start(bf16[2,768,128]{2,1,0:T(8,128)(2,1)S(1)} %collective-permute-done.3.refs_3_), channel_id=1, source_target_pairs={{0,1},{1,2},{2,3},{3,4},{4,5},{5,6},{6,7},{7,8},{8,9},{9,10},{10,1... | collective-permute-start | bytes 1179656 | tf_op jit(solution)/shard_map/ppermute | solution.py:322
  45.5 10.7 %collective-permute-start.8 = (bf16[2,768,128]{2,1,0:T(8,128)(2,1)S(1)}, bf16[2,768,128]{2,1,0:T(8,128)(2,1)}, u32[]{:S(2)}, u32[]{:S(2)}) collective-permute-start(bf16[2,768,128]{2,1,0:T(8,128)(2,1)S(1)} %collective-permute-done.refs_4_), channel_id=1, source_target_pairs={{32,48},{48,32},{33,49},{49,33},{34,50},{50,34},{35,51},{51,35},{3... | collective-permute-start | bytes 1179656 | tf_op jit(solution)/shard_map/ppermute | solution.py:329
  47.7 12.6 %collective-permute-start.9 = (bf16[2,768,128]{2,1,0:T(8,128)(2,1)}, bf16[2,768,128]{2,1,0:T(8,128)(2,1)S(1)}, u32[]{:S(2)}, u32[]{:S(2)}) collective-permute-start(bf16[2,768,128]{2,1,0:T(8,128)(2,1)} %collective-permute-done.7.refs_7_), channel_id=1, source_target_pairs={{0,1},{1,2},{2,3},{3,4},{4,5},{5,6},{6,7},{7,8},{8,9},{9,10},{10,1... | collective-permute-start | bytes 1179656 | tf_op jit(solution)/shard_map/ppermute | solution.py:322
  51.5 11.0 %collective-permute-start.12 = (bf16[2,768,128]{2,1,0:T(8,128)(2,1)S(1)}, bf16[2,768,128]{2,1,0:T(8,128)(2,1)S(1)}, u32[]{:S(2)}, u32[]{:S(2)}) collective-permute-start(bf16[2,768,128]{2,1,0:T(8,128)(2,1)S(1)} %collective-permute-done.11.first), channel_id=1, source_target_pairs={{0,32},{16,48},{32,16},{48,0},{1,33},{17,49},{33,17},{49,1},{2,34}... | collective-permute-start | bytes 1179656 | tf_op jit(solution)/shard_map/ppermute | solution.py:342
  56.2 1.0 copy-start
  60.3 6.9 %collective-permute-start.10 = (bf16[2,768,128]{2,1,0:T(8,128)(2,1)S(1)}, bf16[2,768,128]{2,1,0:T(8,128)(2,1)S(1)}, u32[]{:S(2)}, u32[]{:S(2)}) collective-permute-start(bf16[2,768,128]{2,1,0:T(8,128)(2,1)S(1)} %collective-permute-done.9.second), channel_id=1, source_target_pairs={{0,32},{16,48},{32,16},{48,0},{1,33},{17,49},{33,17},{49,1},{2,34}... | collective-permute-start | bytes 1179656 | tf_op jit(solution)/shard_map/ppermute | solution.py:342
  67.2 34.0 %copy-start.1 = (s32[512]{0:T(512)S(1)}, s32[512]{0:T(512)}, u32[]{:S(2)}) copy-start(s32[512]{0:T(512)} %constant.27.clone.todo) | copy-start | bytes 6148
  83.2 14.1 %collective-permute-start.14 = (f16[264,128]{1,0:T(8,128)(2,1)S(1)}, f16[264,128]{1,0:T(8,128)(2,1)S(1)}, u32[]{:S(2)}, u32[]{:S(2)}) collective-permute-start(f16[264,128]{1,0:T(8,128)(2,1)S(1)} %convert_element_type.9), channel_id=1, source_target_pairs={{0,15},{1,0},{2,33},{3,34},{4,67},{5,68},{6,101},{7,102},{8,104},{... | collective-permute-start | bytes 202760 | tf_op jit(solution)/shard_map/ppermute | solution.py:362
  94.4 6.8 %collective-permute-start.13 = (f16[264,128]{1,0:T(8,128)(2,1)S(1)}, f16[264,128]{1,0:T(8,128)(2,1)S(1)}, u32[]{:S(2)}, u32[]{:S(2)}) collective-permute-start(f16[264,128]{1,0:T(8,128)(2,1)S(1)} %convert_element_type.9), channel_id=1, source_target_pairs={{0,224},{1,1},{2,2},{3,35},{4,36},{5,69},{6,70},{7,103},{8,135},{9... | collective-permute-start | bytes 202760 | tf_op jit(solution)/shard_map/ppermute | solution.py:362

commit v11 on v10

--- a/solution.py
+++ b/solution.py
@@ -91,9 +91,9 @@
     return perms, table
 
 
-def features_kernel(field, backward, both, f, b, sems):
+def features_kernel(field, backward, both, f, b, done, sems, out_sems):
     rows = field.shape[0] // PIECES
-    copies = []
+    copies, leaving = [], []
     for piece in range(PIECES):
         part = pl.ds(piece * rows, rows)
         copies.append(
@@ -110,8 +110,16 @@
             copy.wait()
         wide = jnp.tanh(f[part, :].astype(jnp.float32))
         gated = (1.0 - wide * wide) * b[part, :].astype(jnp.float32)
-        both[0, part, :] = wide.astype(jnp.bfloat16)
-        both[1, part, :] = gated.astype(jnp.bfloat16)
+        done[0, part, :] = wide.astype(jnp.bfloat16)
+        done[1, part, :] = gated.astype(jnp.bfloat16)
+        for i in range(2):
+            leave = pltpu.make_async_copy(
+                done.at[i, part], both.at[i, part], out_sems.at[i, piece]
+            )
+            leave.start()
+            leaving.append(leave)
+    for leave in leaving:
+        leave.wait()
 
 
 def product(left, right):
@@ -275,10 +283,12 @@
         features_kernel,
         out_shape=jax.ShapeDtypeStruct((2, draws, n), jnp.bfloat16),
         in_specs=[pl.BlockSpec(memory_space=pltpu.HBM)] * 2,
-        out_specs=VMEM,
+        out_specs=pl.BlockSpec(memory_space=pltpu.HBM),
         scratch_shapes=[
             pltpu.VMEM((draws, n), jnp.bfloat16),
             pltpu.VMEM((draws, n), jnp.bfloat16),
+            pltpu.VMEM((2, draws, n), jnp.bfloat16),
+            pltpu.SemaphoreType.DMA((2, PIECES)),
             pltpu.SemaphoreType.DMA((2, PIECES)),
         ],
         compiler_params=pltpu.CompilerParams(vmem_limit_bytes=60 * 1024 * 1024),

time: 104 us -> 104 us (level)
  no operation moved by 1% of the time
where the time goes in v11:
time: 104 us; the launch traced here: 103 us
  starting transfers between devices  63 us (61%)
  blocking collectives  14.6 us (14%)
  waiting for transfers between devices  14.1 us (14%)
  Pallas kernels  8.9 us (9%)
  local copies, waits for them, and re-layouts  1.08 us (1%)
    ppermute x6, starting transfers between devices, on_device(): chains = [lax.ppermute(chain, ('c', 'z'), step) for chain in chains]  21.8 us
    all_to_all x1, blocking collectives, on_device(): partial = lax.all_to_all(partial, ('yh', 'x'), 0, 0, tiled=True)  14.6 us
    ppermute x2, starting transfers between devices, on_device(): a, b = [lax.ppermute(block, AXES, p).astype(jnp.float32) for p in perms]  14 us
    ppermute x1, starting transfers between devices, on_device(): lax.ppermute(both, ('c', 'z'), step)  11.1 us
    ppermute x2, starting transfers between devices, on_device(): far = [lax.ppermute(chain, ('c', 'yl'), cross) for chain in chains]  6.9 us
    pallas_call x3, Pallas kernels, call(): pl.pallas_call(kernel, out_shape=out_shape, in_specs=[SMEM] + [VMEM] * le...  5.55 us
    ppermute x2, waiting for transfers between devices, on_device(): a, b = [lax.ppermute(block, AXES, p).astype(jnp.float32) for p in perms]  3.95 us
    ppermute x1, waiting for transfers between devices, on_device(): lax.ppermute(both, ('c', 'z'), first_step)  3.44 us
  transfers between devices with their start and end apart: 15, of which 5 were waited for; matrix products, arithmetic and copies ran while one was open for 0% of the time, Pallas kernels for 4%

profile of v11, /device:TPU:7, one launch (start us, length us, event | category | flops | bytes accessed | tf_op | source)
XLA Modules:
  0.0 102.7 jit_solution(17881406873453283238)
XLA Ops:
  0.6 1.8 %shard_map.50.refs_0_ = bf16[2,768,128]{2,1,0:T(8,128)(2,1)} custom-call(bf16[768,128]{1,0:T(8,128)(2,1)} %field.1, bf16[768,128]{1,0:T(8,128)(2,1)} %backward.1), custom_call_target="tpu_custom_call" | custom-call | tf_op jit(solution)/shard_map/pallas_call | solution.py:282
  2.4 11.1 %collective-permute-start.1 = (bf16[2,768,128]{2,1,0:T(8,128)(2,1)}, bf16[2,768,128]{2,1,0:T(8,128)(2,1)S(1)}, u32[]{:S(2)}, u32[]{:S(2)}) collective-permute-start(bf16[2,768,128]{2,1,0:T(8,128)(2,1)} %shard_map.50.refs_0_), channel_id=1, source_target_pairs={{0,1},{1,2},{2,3},{3,4},{4,5},{5,6},{6,7},{7,8},{8,9},{9,10},{10,1... | collective-permute-start | bytes 1179656 | tf_op jit(solution)/shard_map/ppermute | solution.py:324
  13.6 1.9 %collective-permute-start = (bf16[2,768,128]{2,1,0:T(8,128)(2,1)}, bf16[2,768,128]{2,1,0:T(8,128)(2,1)S(1)}, u32[]{:S(2)}, u32[]{:S(2)}) collective-permute-start(bf16[2,768,128]{2,1,0:T(8,128)(2,1)} %shard_map.50.refs_0_), channel_id=1, source_target_pairs={{0,32},{32,0},{1,33},{33,1},{2,34},{34,2},{3,35},{35,3},{4,36},{36... | collective-permute-start | bytes 1179656 | tf_op jit(solution)/shard_map/ppermute | solution.py:328
  15.5 1.9 %collective-permute-start.4 = (bf16[2,768,128]{2,1,0:T(8,128)(2,1)}, bf16[2,768,128]{2,1,0:T(8,128)(2,1)S(1)}, u32[]{:S(2)}, u32[]{:S(2)}) collective-permute-start(bf16[2,768,128]{2,1,0:T(8,128)(2,1)} %shard_map.50.refs_0_), channel_id=1, source_target_pairs={{0,47},{1,32},{2,33},{3,34},{4,35},{5,36},{6,37},{7,38},{8,39},{9,... | collective-permute-start | bytes 1179656 | tf_op jit(solution)/shard_map/ppermute | solution.py:325
  17.4 1.2 %collective-permute-done.1.refs_1_ = bf16[2,768,128]{2,1,0:T(8,128)(2,1)S(1)} collective-permute-done((bf16[2,768,128]{2,1,0:T(8,128)(2,1)}, bf16[2,768,128]{2,1,0:T(8,128)(2,1)S(1)}, u32[]{:S(2)}, u32[]{:S(2)}) %collective-permute-start.1) | collective-permute-done | bytes 393248 | tf_op jit(solution)/shard_map/ppermute | solution.py:324
  18.6 0.0 collective-permute-done.refs_4_
  18.6 4.9 %collective-permute-start.2 = (bf16[2,768,128]{2,1,0:T(8,128)(2,1)S(1)}, bf16[2,768,128]{2,1,0:T(8,128)(2,1)S(1)}, u32[]{:S(2)}, u32[]{:S(2)}) collective-permute-start(bf16[2,768,128]{2,1,0:T(8,128)(2,1)S(1)} %collective-permute-done.1.refs_1_), channel_id=1, source_target_pairs={{0,1},{1,2},{2,3},{3,4},{4,5},{5,6},{6,7},{7,8},{8,9},{9,10},{10,1... | collective-permute-start | bytes 1179656 | tf_op jit(solution)/shard_map/ppermute | solution.py:332
  23.5 3.4 %collective-permute-done.4.refs_5_ = bf16[2,768,128]{2,1,0:T(8,128)(2,1)S(1)} collective-permute-done((bf16[2,768,128]{2,1,0:T(8,128)(2,1)}, bf16[2,768,128]{2,1,0:T(8,128)(2,1)S(1)}, u32[]{:S(2)}, u32[]{:S(2)}) %collective-permute-start.4) | collective-permute-done | bytes 393248 | tf_op jit(solution)/shard_map/ppermute | solution.py:325
  26.9 1.9 %collective-permute-start.6 = (bf16[2,768,128]{2,1,0:T(8,128)(2,1)S(1)}, bf16[2,768,128]{2,1,0:T(8,128)(2,1)S(1)}, u32[]{:S(2)}, u32[]{:S(2)}) collective-permute-start(bf16[2,768,128]{2,1,0:T(8,128)(2,1)S(1)} %collective-permute-done.4.refs_5_), channel_id=1, source_target_pairs={{0,1},{1,2},{2,3},{3,4},{4,5},{5,6},{6,7},{7,8},{8,9},{9,10},{10,1... | collective-permute-start | bytes 1179656 | tf_op jit(solution)/shard_map/ppermute | solution.py:332
  28.8 3.2 %collective-permute-start.5 = (bf16[2,768,128]{2,1,0:T(8,128)(2,1)}, bf16[2,768,128]{2,1,0:T(8,128)(2,1)S(1)}, u32[]{:S(2)}, u32[]{:S(2)}) collective-permute-start(bf16[2,768,128]{2,1,0:T(8,128)(2,1)} %shard_map.50.refs_0_), channel_id=1, source_target_pairs={{32,48},{48,32},{33,49},{49,33},{34,50},{50,34},{35,51},{51,35},{3... | collective-permute-start | bytes 1179656 | tf_op jit(solution)/shard_map/ppermute | solution.py:335
  32.1 3.7 %collective-permute-start.3 = (bf16[2,768,128]{2,1,0:T(8,128)(2,1)S(1)}, bf16[2,768,128]{2,1,0:T(8,128)(2,1)S(1)}, u32[]{:S(2)}, u32[]{:S(2)}) collective-permute-start(bf16[2,768,128]{2,1,0:T(8,128)(2,1)S(1)} %collective-permute-done.2.refs_2_), channel_id=1, source_target_pairs={{0,1},{1,2},{2,3},{3,4},{4,5},{5,6},{6,7},{7,8},{8,9},{9,10},{10,1... | collective-permute-start | bytes 1179656 | tf_op jit(solution)/shard_map/ppermute | solution.py:332
  35.8 0.0 collective-permute-done.6.refs_6_
  35.8 2.1 %collective-permute-done.5.refs_8_ = bf16[2,768,128]{2,1,0:T(8,128)(2,1)S(1)} collective-permute-done((bf16[2,768,128]{2,1,0:T(8,128)(2,1)}, bf16[2,768,128]{2,1,0:T(8,128)(2,1)S(1)}, u32[]{:S(2)}, u32[]{:S(2)}) %collective-permute-start.5) | collective-permute-done | bytes 393248 | tf_op jit(solution)/shard_map/ppermute | solution.py:335
  37.9 3.7 %collective-permute-start.7 = (bf16[2,768,128]{2,1,0:T(8,128)(2,1)S(1)}, bf16[2,768,128]{2,1,0:T(8,128)(2,1)}, u32[]{:S(2)}, u32[]{:S(2)}) collective-permute-start(bf16[2,768,128]{2,1,0:T(8,128)(2,1)S(1)} %collective-permute-done.6.refs_6_), channel_id=1, source_target_pairs={{0,1},{1,2},{2,3},{3,4},{4,5},{5,6},{6,7},{7,8},{8,9},{9,10},{10,1... | collective-permute-start | bytes 1179656 | tf_op jit(solution)/shard_map/ppermute | solution.py:332
  41.6 3.9 %collective-permute-start.11 = (bf16[2,768,128]{2,1,0:T(8,128)(2,1)S(1)}, bf16[2,768,128]{2,1,0:T(8,128)(2,1)S(1)}, u32[]{:S(2)}, u32[]{:S(2)}) collective-permute-start(bf16[2,768,128]{2,1,0:T(8,128)(2,1)S(1)} %collective-permute-done.3.refs_3_), channel_id=1, source_target_pairs={{0,1},{1,2},{2,3},{3,4},{4,5},{5,6},{6,7},{7,8},{8,9},{9,10},{10,1... | collective-permute-start | bytes 1179656 | tf_op jit(solution)/shard_map/ppermute | solution.py:332
  45.5 2.1 %collective-permute-start.8 = (bf16[2,768,128]{2,1,0:T(8,128)(2,1)S(1)}, bf16[2,768,128]{2,1,0:T(8,128)(2,1)}, u32[]{:S(2)}, u32[]{:S(2)}) collective-permute-start(bf16[2,768,128]{2,1,0:T(8,128)(2,1)S(1)} %collective-permute-done.refs_4_), channel_id=1, source_target_pairs={{32,48},{48,32},{33,49},{49,33},{34,50},{50,34},{35,51},{51,35},{3... | collective-permute-start | bytes 1179656 | tf_op jit(solution)/shard_map/ppermute | solution.py:339
  47.6 3.7 %collective-permute-start.9 = (bf16[2,768,128]{2,1,0:T(8,128)(2,1)}, bf16[2,768,128]{2,1,0:T(8,128)(2,1)S(1)}, u32[]{:S(2)}, u32[]{:S(2)}) collective-permute-start(bf16[2,768,128]{2,1,0:T(8,128)(2,1)} %collective-permute-done.7.refs_7_), channel_id=1, source_target_pairs={{0,1},{1,2},{2,3},{3,4},{4,5},{5,6},{6,7},{7,8},{8,9},{9,10},{10,1... | collective-permute-start | bytes 1179656 | tf_op jit(solution)/shard_map/ppermute | solution.py:332
  51.4 0.1 pad_add_fusion.place
  51.5 4.7 %collective-permute-start.12 = (bf16[2,768,128]{2,1,0:T(8,128)(2,1)S(1)}, bf16[2,768,128]{2,1,0:T(8,128)(2,1)S(1)}, u32[]{:S(2)}, u32[]{:S(2)}) collective-permute-start(bf16[2,768,128]{2,1,0:T(8,128)(2,1)S(1)} %collective-permute-done.11.first), channel_id=1, source_target_pairs={{0,32},{16,48},{32,16},{48,0},{1,33},{17,49},{33,17},{49,1},{2,34}... | collective-permute-start | bytes 1179656 | tf_op jit(solution)/shard_map/ppermute | solution.py:352
  56.2 1.0 copy-done
  57.2 3.1 %shard_map.51 = (bf16[8,272,128]{2,1,0:T(8,128)(2,1)S(1)}, bf16[2,1536,128]{2,1,0:T(8,128)(2,1)S(1)}, bf16[2,1536,512]{2,1,0:T(8,128)(2,1)S(1)}) custom-call(s32[4]{0:T(128)S(1)} %pad_add_fusion.place, bf16[2,768,128]{2,1,0:T(8,128)(2,1)S(1)} %copy-done, bf16[2,768,128]{2,1,0:T(8,128)(2,1)S(1)} %collective-permute-done.1.refs_1_, ...), custom_call_target="tpu_custom_call" | custom-call | flops 402653184 | bytes 2752512 | tf_op jit(solution)/shard_map/pallas_call | solution.py:309
  60.3 2.2 %collective-permute-start.10 = (bf16[2,768,128]{2,1,0:T(8,128)(2,1)S(1)}, bf16[2,768,128]{2,1,0:T(8,128)(2,1)S(1)}, u32[]{:S(2)}, u32[]{:S(2)}) collective-permute-start(bf16[2,768,128]{2,1,0:T(8,128)(2,1)S(1)} %collective-permute-done.9.second), channel_id=1, source_target_pairs={{0,32},{16,48},{32,16},{48,0},{1,33},{17,49},{33,17},{49,1},{2,34}... | collective-permute-start | bytes 1179656 | tf_op jit(solution)/shard_map/ppermute | solution.py:352
  62.5 1.3 %shard_map.52 = (bf16[8,272,128]{2,1,0:T(8,128)(2,1)S(1)}, bf16[2,1536,512]{2,1,0:T(8,128)(2,1)S(1)}, f32[2,128,512]{2,1,0:T(8,128)S(1)}) custom-call(s32[4]{0:T(128)S(1)} %pad_add_fusion.place, bf16[2,768,128]{2,1,0:T(8,128)(2,1)S(1)} %collective-permute-done.11.first, ...), custom_call_target="tpu_custom_call", output_to_operand_aliasing={{0}: (5, {}), {1}: (6, {})} | custom-call | flops 301989888 | bytes 2752512 | tf_op jit(solution)/shard_map/pallas_call | solution.py:309
  63.8 3.4 %collective-permute-done.10.far = bf16[2,768,128]{2,1,0:T(8,128)(2,1)S(1)} collective-permute-done((bf16[2,768,128]{2,1,0:T(8,128)(2,1)S(1)}, bf16[2,768,128]{2,1,0:T(8,128)(2,1)S(1)}, u32[]{:S(2)}, u32[]{:S(2)}) %collective-permute-start.10) | collective-permute-done | bytes 393248 | tf_op jit(solution)/shard_map/ppermute | solution.py:352
  67.2 1.2 %shard_map.53 = bf16[8,272,128]{2,1,0:T(8,128)(2,1)S(1)} custom-call(s32[4]{0:T(128)S(1)} %pad_add_fusion.place, bf16[2,768,128]{2,1,0:T(8,128)(2,1)S(1)} %collective-permute-done.10.far, bf16[2,1536,512]{2,1,0:T(8,128)(2,1)S(1)} %get-tuple-element.31.steps, f32[2,128,512]{2,1,0:T(8,128)S(1)} %get-tuple-element.32.part, ...), custom_call_target="tpu_custom_call", output_to_operand_aliasing={{}: (4, {})} | custom-call | flops 201326592 | bytes 2752512 | tf_op jit(solution)/shard_map/pallas_call | solution.py:309
  68.4 14.6 %all_to_all.5.parts = bf16[8,272,128]{2,1,0:T(8,128)(2,1)S(1)} all-to-all(bf16[8,272,128]{2,1,0:T(8,128)(2,1)S(1)} %shard_map.53), channel_id=1, replica_groups=mesh['yh'=2,'x'=4,'c'=2,'yl'=2,'z'=16] {'yh','x'}, dimensions={0} | all-to-all | bytes 1114112 | tf_op jit(solution)/shard_map/all_to_all | solution.py:363
  83.0 0.1 shard_map.54
  83.1 11.2 %collective-permute-start.14 = (f16[264,128]{1,0:T(8,128)(2,1)S(1)}, f16[264,128]{1,0:T(8,128)(2,1)S(1)}, u32[]{:S(2)}, u32[]{:S(2)}) collective-permute-start(f16[264,128]{1,0:T(8,128)(2,1)S(1)} %convert_element_type.9), channel_id=1, source_target_pairs={{0,15},{1,0},{2,33},{3,34},{4,67},{5,68},{6,101},{7,102},{8,104},{... | collective-permute-start | bytes 202760 | tf_op jit(solution)/shard_map/ppermute | solution.py:372
  94.4 2.8 %collective-permute-start.13 = (f16[264,128]{1,0:T(8,128)(2,1)S(1)}, f16[264,128]{1,0:T(8,128)(2,1)S(1)}, u32[]{:S(2)}, u32[]{:S(2)}) collective-permute-start(f16[264,128]{1,0:T(8,128)(2,1)S(1)} %convert_element_type.9), channel_id=1, source_target_pairs={{0,224},{1,1},{2,2},{3,35},{4,36},{5,69},{6,70},{7,103},{8,135},{9... | collective-permute-start | bytes 202760 | tf_op jit(solution)/shard_map/ppermute | solution.py:372
  97.1 0.1 stack.32.place
  97.3 4.0 %collective-permute-done.13 = f16[264,128]{1,0:T(8,128)(2,1)S(1)} collective-permute-done((f16[264,128]{1,0:T(8,128)(2,1)S(1)}, f16[264,128]{1,0:T(8,128)(2,1)S(1)}, u32[]{:S(2)}, u32[]{:S(2)}) %collective-permute-start.13) | collective-permute-done | bytes 67616 | tf_op jit(solution)/shard_map/ppermute | solution.py:372
  101.2 1.4 %shard_map.55 = (f32[128,256]{1,0:T(8,128)}, f32[128,256]{1,0:T(8,128)}) custom-call(s32[5]{0:T(128)S(1)} %stack.32.place, s32[512]{0:T(512)S(1)} %copy-done.1, f32[264,128]{1,0:T(8,128)S(1)} %convert_element_type.10.a, f32[264,128]{1,0:T(8,128)S(1)} %convert_element_type.11.b), custom_call_target="tpu_custom_call" | custom-call | tf_op jit(solution)/shard_map/pallas_call | solution.py:377
  (14 shorter events, 0.1 us)
Async XLA Ops:
  2.4 16.1 %collective-permute-start.1 = (bf16[2,768,128]{2,1,0:T(8,128)(2,1)}, bf16[2,768,128]{2,1,0:T(8,128)(2,1)S(1)}, u32[]{:S(2)}, u32[]{:S(2)}) collective-permute-start(bf16[2,768,128]{2,1,0:T(8,128)(2,1)} %shard_map.50.refs_0_), channel_id=1, source_target_pairs={{0,1},{1,2},{2,3},{3,4},{4,5},{5,6},{6,7},{7,8},{8,9},{9,10},{10,1... | collective-permute-start | bytes 1179656 | tf_op jit(solution)/shard_map/ppermute | solution.py:324
  13.6 5.0 %collective-permute-start = (bf16[2,768,128]{2,1,0:T(8,128)(2,1)}, bf16[2,768,128]{2,1,0:T(8,128)(2,1)S(1)}, u32[]{:S(2)}, u32[]{:S(2)}) collective-permute-start(bf16[2,768,128]{2,1,0:T(8,128)(2,1)} %shard_map.50.refs_0_), channel_id=1, source_target_pairs={{0,32},{32,0},{1,33},{33,1},{2,34},{34,2},{3,35},{35,3},{4,36},{36... | collective-permute-start | bytes 1179656 | tf_op jit(solution)/shard_map/ppermute | solution.py:328
  15.5 11.4 %collective-permute-start.4 = (bf16[2,768,128]{2,1,0:T(8,128)(2,1)}, bf16[2,768,128]{2,1,0:T(8,128)(2,1)S(1)}, u32[]{:S(2)}, u32[]{:S(2)}) collective-permute-start(bf16[2,768,128]{2,1,0:T(8,128)(2,1)} %shard_map.50.refs_0_), channel_id=1, source_target_pairs={{0,47},{1,32},{2,33},{3,34},{4,35},{5,36},{6,37},{7,38},{8,39},{9,... | collective-permute-start | bytes 1179656 | tf_op jit(solution)/shard_map/ppermute | solution.py:325
  18.6 13.5 %collective-permute-start.2 = (bf16[2,768,128]{2,1,0:T(8,128)(2,1)S(1)}, bf16[2,768,128]{2,1,0:T(8,128)(2,1)S(1)}, u32[]{:S(2)}, u32[]{:S(2)}) collective-permute-start(bf16[2,768,128]{2,1,0:T(8,128)(2,1)S(1)} %collective-permute-done.1.refs_1_), channel_id=1, source_target_pairs={{0,1},{1,2},{2,3},{3,4},{4,5},{5,6},{6,7},{7,8},{8,9},{9,10},{10,1... | collective-permute-start | bytes 1179656 | tf_op jit(solution)/shard_map/ppermute | solution.py:332
  26.9 8.8 %collective-permute-start.6 = (bf16[2,768,128]{2,1,0:T(8,128)(2,1)S(1)}, bf16[2,768,128]{2,1,0:T(8,128)(2,1)S(1)}, u32[]{:S(2)}, u32[]{:S(2)}) collective-permute-start(bf16[2,768,128]{2,1,0:T(8,128)(2,1)S(1)} %collective-permute-done.4.refs_5_), channel_id=1, source_target_pairs={{0,1},{1,2},{2,3},{3,4},{4,5},{5,6},{6,7},{7,8},{8,9},{9,10},{10,1... | collective-permute-start | bytes 1179656 | tf_op jit(solution)/shard_map/ppermute | solution.py:332
  28.8 9.0 %collective-permute-start.5 = (bf16[2,768,128]{2,1,0:T(8,128)(2,1)}, bf16[2,768,128]{2,1,0:T(8,128)(2,1)S(1)}, u32[]{:S(2)}, u32[]{:S(2)}) collective-permute-start(bf16[2,768,128]{2,1,0:T(8,128)(2,1)} %shard_map.50.refs_0_), channel_id=1, source_target_pairs={{32,48},{48,32},{33,49},{49,33},{34,50},{50,34},{35,51},{51,35},{3... | collective-permute-start | bytes 1179656 | tf_op jit(solution)/shard_map/ppermute | solution.py:335
  32.1 9.5 %collective-permute-start.3 = (bf16[2,768,128]{2,1,0:T(8,128)(2,1)S(1)}, bf16[2,768,128]{2,1,0:T(8,128)(2,1)S(1)}, u32[]{:S(2)}, u32[]{:S(2)}) collective-permute-start(bf16[2,768,128]{2,1,0:T(8,128)(2,1)S(1)} %collective-permute-done.2.refs_2_), channel_id=1, source_target_pairs={{0,1},{1,2},{2,3},{3,4},{4,5},{5,6},{6,7},{7,8},{8,9},{9,10},{10,1... | collective-permute-start | bytes 1179656 | tf_op jit(solution)/shard_map/ppermute | solution.py:332
  37.9 9.8 %collective-permute-start.7 = (bf16[2,768,128]{2,1,0:T(8,128)(2,1)S(1)}, bf16[2,768,128]{2,1,0:T(8,128)(2,1)}, u32[]{:S(2)}, u32[]{:S(2)}) collective-permute-start(bf16[2,768,128]{2,1,0:T(8,128)(2,1)S(1)} %collective-permute-done.6.refs_6_), channel_id=1, source_target_pairs={{0,1},{1,2},{2,3},{3,4},{4,5},{5,6},{6,7},{7,8},{8,9},{9,10},{10,1... | collective-permute-start | bytes 1179656 | tf_op jit(solution)/shard_map/ppermute | solution.py:332
  41.6 9.9 %collective-permute-start.11 = (bf16[2,768,128]{2,1,0:T(8,128)(2,1)S(1)}, bf16[2,768,128]{2,1,0:T(8,128)(2,1)S(1)}, u32[]{:S(2)}, u32[]{:S(2)}) collective-permute-start(bf16[2,768,128]{2,1,0:T(8,128)(2,1)S(1)} %collective-permute-done.3.refs_3_), channel_id=1, source_target_pairs={{0,1},{1,2},{2,3},{3,4},{4,5},{5,6},{6,7},{7,8},{8,9},{9,10},{10,1... | collective-permute-start | bytes 1179656 | tf_op jit(solution)/shard_map/ppermute | solution.py:332
  45.5 10.7 %collective-permute-start.8 = (bf16[2,768,128]{2,1,0:T(8,128)(2,1)S(1)}, bf16[2,768,128]{2,1,0:T(8,128)(2,1)}, u32[]{:S(2)}, u32[]{:S(2)}) collective-permute-start(bf16[2,768,128]{2,1,0:T(8,128)(2,1)S(1)} %collective-permute-done.refs_4_), channel_id=1, source_target_pairs={{32,48},{48,32},{33,49},{49,33},{34,50},{50,34},{35,51},{51,35},{3... | collective-permute-start | bytes 1179656 | tf_op jit(solution)/shard_map/ppermute | solution.py:339
  47.6 12.6 %collective-permute-start.9 = (bf16[2,768,128]{2,1,0:T(8,128)(2,1)}, bf16[2,768,128]{2,1,0:T(8,128)(2,1)S(1)}, u32[]{:S(2)}, u32[]{:S(2)}) collective-permute-start(bf16[2,768,128]{2,1,0:T(8,128)(2,1)} %collective-permute-done.7.refs_7_), channel_id=1, source_target_pairs={{0,1},{1,2},{2,3},{3,4},{4,5},{5,6},{6,7},{7,8},{8,9},{9,10},{10,1... | collective-permute-start | bytes 1179656 | tf_op jit(solution)/shard_map/ppermute | solution.py:332
  51.5 11.0 %collective-permute-start.12 = (bf16[2,768,128]{2,1,0:T(8,128)(2,1)S(1)}, bf16[2,768,128]{2,1,0:T(8,128)(2,1)S(1)}, u32[]{:S(2)}, u32[]{:S(2)}) collective-permute-start(bf16[2,768,128]{2,1,0:T(8,128)(2,1)S(1)} %collective-permute-done.11.first), channel_id=1, source_target_pairs={{0,32},{16,48},{32,16},{48,0},{1,33},{17,49},{33,17},{49,1},{2,34}... | collective-permute-start | bytes 1179656 | tf_op jit(solution)/shard_map/ppermute | solution.py:352
  56.2 1.0 copy-start
  60.3 6.9 %collective-permute-start.10 = (bf16[2,768,128]{2,1,0:T(8,128)(2,1)S(1)}, bf16[2,768,128]{2,1,0:T(8,128)(2,1)S(1)}, u32[]{:S(2)}, u32[]{:S(2)}) collective-permute-start(bf16[2,768,128]{2,1,0:T(8,128)(2,1)S(1)} %collective-permute-done.9.second), channel_id=1, source_target_pairs={{0,32},{16,48},{32,16},{48,0},{1,33},{17,49},{33,17},{49,1},{2,34}... | collective-permute-start | bytes 1179656 | tf_op jit(solution)/shard_map/ppermute | solution.py:352
  67.2 34.0 %copy-start.1 = (s32[512]{0:T(512)S(1)}, s32[512]{0:T(512)}, u32[]{:S(2)}) copy-start(s32[512]{0:T(512)} %constant.27.clone.todo) | copy-start | bytes 6148
  83.1 14.1 %collective-permute-start.14 = (f16[264,128]{1,0:T(8,128)(2,1)S(1)}, f16[264,128]{1,0:T(8,128)(2,1)S(1)}, u32[]{:S(2)}, u32[]{:S(2)}) collective-permute-start(f16[264,128]{1,0:T(8,128)(2,1)S(1)} %convert_element_type.9), channel_id=1, source_target_pairs={{0,15},{1,0},{2,33},{3,34},{4,67},{5,68},{6,101},{7,102},{8,104},{... | collective-permute-start | bytes 202760 | tf_op jit(solution)/shard_map/ppermute | solution.py:372
  94.4 6.8 %collective-permute-start.13 = (f16[264,128]{1,0:T(8,128)(2,1)S(1)}, f16[264,128]{1,0:T(8,128)(2,1)S(1)}, u32[]{:S(2)}, u32[]{:S(2)}) collective-permute-start(f16[264,128]{1,0:T(8,128)(2,1)S(1)} %convert_element_type.9), channel_id=1, source_target_pairs={{0,224},{1,1},{2,2},{3,35},{4,36},{5,69},{6,70},{7,103},{8,135},{9... | collective-permute-start | bytes 202760 | tf_op jit(solution)/shard_map/ppermute | solution.py:372

commit v12 on v10

--- a/solution.py
+++ b/solution.py
@@ -10,7 +10,7 @@
 
 AXES = ("yh", "x", "c", "yl", "z")
 SIZES = (2, 4, 2, 2, 16)
-PIECES = 4
+PIECES = 2
 SCALES = [float(np.float32(2 ** (i / 8))) for i in range(8)]
 TOP = 14.0
 EXTRA = 16
@@ -61,8 +61,8 @@
         there = np.unravel_index(edges[e][0], SIZES), np.unravel_index(edges[e][1], SIZES)
         (h0, x0, _, l0, z0), (h1, x1, _, l1, z1) = there
         return sum(
-            min((p - q) % n, (q - p) % n)
-            for p, q, n in ((x0, x1, 4), (2 * h0 + l0, 2 * h1 + l1, 4), (z0, z1, 16))
+            w * min((p - q) % n, (q - p) % n)
+            for p, q, n, w in ((x0, x1, 4, 1), (2 * h0 + l0, 2 * h1 + l1, 4, 1), (z0, z1, 16, 2))
         )
 
     turn = [-1] * len(edges)

time: 104 us -> 104 us (level)
  no operation moved by 1% of the time
where the time goes in v12:
time: 104 us; the launch traced here: 103 us
  starting transfers between devices  63 us (61%)
  blocking collectives  14.6 us (14%)
  waiting for transfers between devices  14.1 us (14%)
  Pallas kernels  8.98 us (9%)
  local copies, waits for them, and re-layouts  1.08 us (1%)
    ppermute x6, starting transfers between devices, on_device(): chains = [lax.ppermute(chain, ('c', 'z'), step) for chain in chains]  21.8 us
    all_to_all x1, blocking collectives, on_device(): partial = lax.all_to_all(partial, ('yh', 'x'), 0, 0, tiled=True)  14.6 us
    ppermute x2, starting transfers between devices, on_device(): a, b = [lax.ppermute(block, AXES, p).astype(jnp.float32) for p in perms]  14 us
    ppermute x1, starting transfers between devices, on_device(): lax.ppermute(both, ('c', 'z'), step)  11.1 us
    ppermute x2, starting transfers between devices, on_device(): far = [lax.ppermute(chain, ('c', 'yl'), cross) for chain in chains]  6.9 us
    pallas_call x3, Pallas kernels, call(): pl.pallas_call(kernel, out_shape=out_shape, in_specs=[SMEM] + [VMEM] * le...  5.55 us
    ppermute x2, waiting for transfers between devices, on_device(): a, b = [lax.ppermute(block, AXES, p).astype(jnp.float32) for p in perms]  3.95 us
    ppermute x1, waiting for transfers between devices, on_device(): lax.ppermute(both, ('c', 'z'), first_step)  3.44 us
  transfers between devices with their start and end apart: 15, of which 5 were waited for; matrix products, arithmetic and copies ran while one was open for 0% of the time, Pallas kernels for 4%

profile of v12, /device:TPU:7, one launch (start us, length us, event | category | flops | bytes accessed | tf_op | source)
XLA Modules:
  0.0 102.8 jit_solution(15284402288884741883)
XLA Ops:
  0.6 1.9 %shard_map.50.refs_0_ = bf16[2,768,128]{2,1,0:T(8,128)(2,1)} custom-call(bf16[768,128]{1,0:T(8,128)(2,1)} %field.1, bf16[768,128]{1,0:T(8,128)(2,1)} %backward.1), custom_call_target="tpu_custom_call" | custom-call | tf_op jit(solution)/shard_map/pallas_call | solution.py:274
  2.5 11.1 %collective-permute-start.1 = (bf16[2,768,128]{2,1,0:T(8,128)(2,1)}, bf16[2,768,128]{2,1,0:T(8,128)(2,1)S(1)}, u32[]{:S(2)}, u32[]{:S(2)}) collective-permute-start(bf16[2,768,128]{2,1,0:T(8,128)(2,1)} %shard_map.50.refs_0_), channel_id=1, source_target_pairs={{0,1},{1,2},{2,3},{3,4},{4,5},{5,6},{6,7},{7,8},{8,9},{9,10},{10,1... | collective-permute-start | bytes 1179656 | tf_op jit(solution)/shard_map/ppermute | solution.py:314
  13.6 1.9 %collective-permute-start = (bf16[2,768,128]{2,1,0:T(8,128)(2,1)}, bf16[2,768,128]{2,1,0:T(8,128)(2,1)S(1)}, u32[]{:S(2)}, u32[]{:S(2)}) collective-permute-start(bf16[2,768,128]{2,1,0:T(8,128)(2,1)} %shard_map.50.refs_0_), channel_id=1, source_target_pairs={{0,32},{32,0},{1,33},{33,1},{2,34},{34,2},{3,35},{35,3},{4,36},{36... | collective-permute-start | bytes 1179656 | tf_op jit(solution)/shard_map/ppermute | solution.py:318
  15.6 1.9 %collective-permute-start.4 = (bf16[2,768,128]{2,1,0:T(8,128)(2,1)}, bf16[2,768,128]{2,1,0:T(8,128)(2,1)S(1)}, u32[]{:S(2)}, u32[]{:S(2)}) collective-permute-start(bf16[2,768,128]{2,1,0:T(8,128)(2,1)} %shard_map.50.refs_0_), channel_id=1, source_target_pairs={{0,47},{1,32},{2,33},{3,34},{4,35},{5,36},{6,37},{7,38},{8,39},{9,... | collective-permute-start | bytes 1179656 | tf_op jit(solution)/shard_map/ppermute | solution.py:315
  17.5 1.2 %collective-permute-done.1.refs_1_ = bf16[2,768,128]{2,1,0:T(8,128)(2,1)S(1)} collective-permute-done((bf16[2,768,128]{2,1,0:T(8,128)(2,1)}, bf16[2,768,128]{2,1,0:T(8,128)(2,1)S(1)}, u32[]{:S(2)}, u32[]{:S(2)}) %collective-permute-start.1) | collective-permute-done | bytes 393248 | tf_op jit(solution)/shard_map/ppermute | solution.py:314
  18.6 4.9 %collective-permute-start.2 = (bf16[2,768,128]{2,1,0:T(8,128)(2,1)S(1)}, bf16[2,768,128]{2,1,0:T(8,128)(2,1)S(1)}, u32[]{:S(2)}, u32[]{:S(2)}) collective-permute-start(bf16[2,768,128]{2,1,0:T(8,128)(2,1)S(1)} %collective-permute-done.1.refs_1_), channel_id=1, source_target_pairs={{0,1},{1,2},{2,3},{3,4},{4,5},{5,6},{6,7},{7,8},{8,9},{9,10},{10,1... | collective-permute-start | bytes 1179656 | tf_op jit(solution)/shard_map/ppermute | solution.py:322
  23.6 3.4 %collective-permute-done.4.refs_5_ = bf16[2,768,128]{2,1,0:T(8,128)(2,1)S(1)} collective-permute-done((bf16[2,768,128]{2,1,0:T(8,128)(2,1)}, bf16[2,768,128]{2,1,0:T(8,128)(2,1)S(1)}, u32[]{:S(2)}, u32[]{:S(2)}) %collective-permute-start.4) | collective-permute-done | bytes 393248 | tf_op jit(solution)/shard_map/ppermute | solution.py:315
  27.0 1.9 %collective-permute-start.6 = (bf16[2,768,128]{2,1,0:T(8,128)(2,1)S(1)}, bf16[2,768,128]{2,1,0:T(8,128)(2,1)S(1)}, u32[]{:S(2)}, u32[]{:S(2)}) collective-permute-start(bf16[2,768,128]{2,1,0:T(8,128)(2,1)S(1)} %collective-permute-done.4.refs_5_), channel_id=1, source_target_pairs={{0,1},{1,2},{2,3},{3,4},{4,5},{5,6},{6,7},{7,8},{8,9},{9,10},{10,1... | collective-permute-start | bytes 1179656 | tf_op jit(solution)/shard_map/ppermute | solution.py:322
  28.9 3.2 %collective-permute-start.5 = (bf16[2,768,128]{2,1,0:T(8,128)(2,1)}, bf16[2,768,128]{2,1,0:T(8,128)(2,1)S(1)}, u32[]{:S(2)}, u32[]{:S(2)}) collective-permute-start(bf16[2,768,128]{2,1,0:T(8,128)(2,1)} %shard_map.50.refs_0_), channel_id=1, source_target_pairs={{32,48},{48,32},{33,49},{49,33},{34,50},{50,34},{35,51},{51,35},{3... | collective-permute-start | bytes 1179656 | tf_op jit(solution)/shard_map/ppermute | solution.py:325
  32.1 0.0 collective-permute-done.2.refs_2_
  32.1 3.7 %collective-permute-start.3 = (bf16[2,768,128]{2,1,0:T(8,128)(2,1)S(1)}, bf16[2,768,128]{2,1,0:T(8,128)(2,1)S(1)}, u32[]{:S(2)}, u32[]{:S(2)}) collective-permute-start(bf16[2,768,128]{2,1,0:T(8,128)(2,1)S(1)} %collective-permute-done.2.refs_2_), channel_id=1, source_target_pairs={{0,1},{1,2},{2,3},{3,4},{4,5},{5,6},{6,7},{7,8},{8,9},{9,10},{10,1... | collective-permute-start | bytes 1179656 | tf_op jit(solution)/shard_map/ppermute | solution.py:322
  35.9 2.1 %collective-permute-done.5.refs_8_ = bf16[2,768,128]{2,1,0:T(8,128)(2,1)S(1)} collective-permute-done((bf16[2,768,128]{2,1,0:T(8,128)(2,1)}, bf16[2,768,128]{2,1,0:T(8,128)(2,1)S(1)}, u32[]{:S(2)}, u32[]{:S(2)}) %collective-permute-start.5) | collective-permute-done | bytes 393248 | tf_op jit(solution)/shard_map/ppermute | solution.py:325
  37.9 3.7 %collective-permute-start.7 = (bf16[2,768,128]{2,1,0:T(8,128)(2,1)S(1)}, bf16[2,768,128]{2,1,0:T(8,128)(2,1)}, u32[]{:S(2)}, u32[]{:S(2)}) collective-permute-start(bf16[2,768,128]{2,1,0:T(8,128)(2,1)S(1)} %collective-permute-done.6.refs_6_), channel_id=1, source_target_pairs={{0,1},{1,2},{2,3},{3,4},{4,5},{5,6},{6,7},{7,8},{8,9},{9,10},{10,1... | collective-permute-start | bytes 1179656 | tf_op jit(solution)/shard_map/ppermute | solution.py:322
  41.6 3.9 %collective-permute-start.11 = (bf16[2,768,128]{2,1,0:T(8,128)(2,1)S(1)}, bf16[2,768,128]{2,1,0:T(8,128)(2,1)S(1)}, u32[]{:S(2)}, u32[]{:S(2)}) collective-permute-start(bf16[2,768,128]{2,1,0:T(8,128)(2,1)S(1)} %collective-permute-done.3.refs_3_), channel_id=1, source_target_pairs={{0,1},{1,2},{2,3},{3,4},{4,5},{5,6},{6,7},{7,8},{8,9},{9,10},{10,1... | collective-permute-start | bytes 1179656 | tf_op jit(solution)/shard_map/ppermute | solution.py:322
  45.6 2.1 %collective-permute-start.8 = (bf16[2,768,128]{2,1,0:T(8,128)(2,1)S(1)}, bf16[2,768,128]{2,1,0:T(8,128)(2,1)}, u32[]{:S(2)}, u32[]{:S(2)}) collective-permute-start(bf16[2,768,128]{2,1,0:T(8,128)(2,1)S(1)} %collective-permute-done.refs_4_), channel_id=1, source_target_pairs={{32,48},{48,32},{33,49},{49,33},{34,50},{50,34},{35,51},{51,35},{3... | collective-permute-start | bytes 1179656 | tf_op jit(solution)/shard_map/ppermute | solution.py:329
  47.7 0.0 collective-permute-done.7.refs_7_
  47.7 3.7 %collective-permute-start.9 = (bf16[2,768,128]{2,1,0:T(8,128)(2,1)}, bf16[2,768,128]{2,1,0:T(8,128)(2,1)S(1)}, u32[]{:S(2)}, u32[]{:S(2)}) collective-permute-start(bf16[2,768,128]{2,1,0:T(8,128)(2,1)} %collective-permute-done.7.refs_7_), channel_id=1, source_target_pairs={{0,1},{1,2},{2,3},{3,4},{4,5},{5,6},{6,7},{7,8},{8,9},{9,10},{10,1... | collective-permute-start | bytes 1179656 | tf_op jit(solution)/shard_map/ppermute | solution.py:322
  51.5 0.1 pad_add_fusion.place
  51.6 4.7 %collective-permute-start.12 = (bf16[2,768,128]{2,1,0:T(8,128)(2,1)S(1)}, bf16[2,768,128]{2,1,0:T(8,128)(2,1)S(1)}, u32[]{:S(2)}, u32[]{:S(2)}) collective-permute-start(bf16[2,768,128]{2,1,0:T(8,128)(2,1)S(1)} %collective-permute-done.11.first), channel_id=1, source_target_pairs={{0,32},{16,48},{32,16},{48,0},{1,33},{17,49},{33,17},{49,1},{2,34}... | collective-permute-start | bytes 1179656 | tf_op jit(solution)/shard_map/ppermute | solution.py:342
  56.3 1.0 copy-done
  57.2 3.1 %shard_map.51 = (bf16[8,272,128]{2,1,0:T(8,128)(2,1)S(1)}, bf16[2,1536,128]{2,1,0:T(8,128)(2,1)S(1)}, bf16[2,1536,512]{2,1,0:T(8,128)(2,1)S(1)}) custom-call(s32[4]{0:T(128)S(1)} %pad_add_fusion.place, bf16[2,768,128]{2,1,0:T(8,128)(2,1)S(1)} %copy-done, bf16[2,768,128]{2,1,0:T(8,128)(2,1)S(1)} %collective-permute-done.1.refs_1_, ...), custom_call_target="tpu_custom_call" | custom-call | flops 402653184 | bytes 2752512 | tf_op jit(solution)/shard_map/pallas_call | solution.py:299
  60.4 2.2 %collective-permute-start.10 = (bf16[2,768,128]{2,1,0:T(8,128)(2,1)S(1)}, bf16[2,768,128]{2,1,0:T(8,128)(2,1)S(1)}, u32[]{:S(2)}, u32[]{:S(2)}) collective-permute-start(bf16[2,768,128]{2,1,0:T(8,128)(2,1)S(1)} %collective-permute-done.9.second), channel_id=1, source_target_pairs={{0,32},{16,48},{32,16},{48,0},{1,33},{17,49},{33,17},{49,1},{2,34}... | collective-permute-start | bytes 1179656 | tf_op jit(solution)/shard_map/ppermute | solution.py:342
  62.6 1.3 %shard_map.52 = (bf16[8,272,128]{2,1,0:T(8,128)(2,1)S(1)}, bf16[2,1536,512]{2,1,0:T(8,128)(2,1)S(1)}, f32[2,128,512]{2,1,0:T(8,128)S(1)}) custom-call(s32[4]{0:T(128)S(1)} %pad_add_fusion.place, bf16[2,768,128]{2,1,0:T(8,128)(2,1)S(1)} %collective-permute-done.11.first, ...), custom_call_target="tpu_custom_call", output_to_operand_aliasing={{0}: (5, {}), {1}: (6, {})} | custom-call | flops 301989888 | bytes 2752512 | tf_op jit(solution)/shard_map/pallas_call | solution.py:299
  63.9 3.4 %collective-permute-done.10.far = bf16[2,768,128]{2,1,0:T(8,128)(2,1)S(1)} collective-permute-done((bf16[2,768,128]{2,1,0:T(8,128)(2,1)S(1)}, bf16[2,768,128]{2,1,0:T(8,128)(2,1)S(1)}, u32[]{:S(2)}, u32[]{:S(2)}) %collective-permute-start.10) | collective-permute-done | bytes 393248 | tf_op jit(solution)/shard_map/ppermute | solution.py:342
  67.3 1.2 %shard_map.53 = bf16[8,272,128]{2,1,0:T(8,128)(2,1)S(1)} custom-call(s32[4]{0:T(128)S(1)} %pad_add_fusion.place, bf16[2,768,128]{2,1,0:T(8,128)(2,1)S(1)} %collective-permute-done.10.far, bf16[2,1536,512]{2,1,0:T(8,128)(2,1)S(1)} %get-tuple-element.31.steps, f32[2,128,512]{2,1,0:T(8,128)S(1)} %get-tuple-element.32.part, ...), custom_call_target="tpu_custom_call", output_to_operand_aliasing={{}: (4, {})} | custom-call | flops 201326592 | bytes 2752512 | tf_op jit(solution)/shard_map/pallas_call | solution.py:299
  68.5 14.6 %all_to_all.5.parts = bf16[8,272,128]{2,1,0:T(8,128)(2,1)S(1)} all-to-all(bf16[8,272,128]{2,1,0:T(8,128)(2,1)S(1)} %shard_map.53), channel_id=1, replica_groups=mesh['yh'=2,'x'=4,'c'=2,'yl'=2,'z'=16] {'yh','x'}, dimensions={0} | all-to-all | bytes 1114112 | tf_op jit(solution)/shard_map/all_to_all | solution.py:353
  83.1 0.1 shard_map.54
  83.2 11.2 %collective-permute-start.14 = (f16[264,128]{1,0:T(8,128)(2,1)S(1)}, f16[264,128]{1,0:T(8,128)(2,1)S(1)}, u32[]{:S(2)}, u32[]{:S(2)}) collective-permute-start(f16[264,128]{1,0:T(8,128)(2,1)S(1)} %convert_element_type.9), channel_id=1, source_target_pairs={{0,15},{1,0},{2,33},{3,34},{4,67},{5,68},{6,101},{7,102},{8,104},{... | collective-permute-start | bytes 202760 | tf_op jit(solution)/shard_map/ppermute | solution.py:362
  94.5 2.8 %collective-permute-start.13 = (f16[264,128]{1,0:T(8,128)(2,1)S(1)}, f16[264,128]{1,0:T(8,128)(2,1)S(1)}, u32[]{:S(2)}, u32[]{:S(2)}) collective-permute-start(f16[264,128]{1,0:T(8,128)(2,1)S(1)} %convert_element_type.9), channel_id=1, source_target_pairs={{0,224},{1,1},{2,2},{3,35},{4,36},{5,69},{6,70},{7,103},{8,135},{9... | collective-permute-start | bytes 202760 | tf_op jit(solution)/shard_map/ppermute | solution.py:362
  97.2 0.1 stack.32.place
  97.3 4.0 %collective-permute-done.13 = f16[264,128]{1,0:T(8,128)(2,1)S(1)} collective-permute-done((f16[264,128]{1,0:T(8,128)(2,1)S(1)}, f16[264,128]{1,0:T(8,128)(2,1)S(1)}, u32[]{:S(2)}, u32[]{:S(2)}) %collective-permute-start.13) | collective-permute-done | bytes 67616 | tf_op jit(solution)/shard_map/ppermute | solution.py:362
  101.3 1.4 %shard_map.55 = (f32[128,256]{1,0:T(8,128)}, f32[128,256]{1,0:T(8,128)}) custom-call(s32[5]{0:T(128)S(1)} %stack.32.place, s32[512]{0:T(512)S(1)} %copy-done.1, f32[264,128]{1,0:T(8,128)S(1)} %convert_element_type.10.a, f32[264,128]{1,0:T(8,128)S(1)} %convert_element_type.11.b), custom_call_target="tpu_custom_call" | custom-call | tf_op jit(solution)/shard_map/pallas_call | solution.py:367
  (14 shorter events, 0.1 us)
Async XLA Ops:
  2.5 16.1 %collective-permute-start.1 = (bf16[2,768,128]{2,1,0:T(8,128)(2,1)}, bf16[2,768,128]{2,1,0:T(8,128)(2,1)S(1)}, u32[]{:S(2)}, u32[]{:S(2)}) collective-permute-start(bf16[2,768,128]{2,1,0:T(8,128)(2,1)} %shard_map.50.refs_0_), channel_id=1, source_target_pairs={{0,1},{1,2},{2,3},{3,4},{4,5},{5,6},{6,7},{7,8},{8,9},{9,10},{10,1... | collective-permute-start | bytes 1179656 | tf_op jit(solution)/shard_map/ppermute | solution.py:314
  13.6 5.0 %collective-permute-start = (bf16[2,768,128]{2,1,0:T(8,128)(2,1)}, bf16[2,768,128]{2,1,0:T(8,128)(2,1)S(1)}, u32[]{:S(2)}, u32[]{:S(2)}) collective-permute-start(bf16[2,768,128]{2,1,0:T(8,128)(2,1)} %shard_map.50.refs_0_), channel_id=1, source_target_pairs={{0,32},{32,0},{1,33},{33,1},{2,34},{34,2},{3,35},{35,3},{4,36},{36... | collective-permute-start | bytes 1179656 | tf_op jit(solution)/shard_map/ppermute | solution.py:318
  15.6 11.4 %collective-permute-start.4 = (bf16[2,768,128]{2,1,0:T(8,128)(2,1)}, bf16[2,768,128]{2,1,0:T(8,128)(2,1)S(1)}, u32[]{:S(2)}, u32[]{:S(2)}) collective-permute-start(bf16[2,768,128]{2,1,0:T(8,128)(2,1)} %shard_map.50.refs_0_), channel_id=1, source_target_pairs={{0,47},{1,32},{2,33},{3,34},{4,35},{5,36},{6,37},{7,38},{8,39},{9,... | collective-permute-start | bytes 1179656 | tf_op jit(solution)/shard_map/ppermute | solution.py:315
  18.6 13.5 %collective-permute-start.2 = (bf16[2,768,128]{2,1,0:T(8,128)(2,1)S(1)}, bf16[2,768,128]{2,1,0:T(8,128)(2,1)S(1)}, u32[]{:S(2)}, u32[]{:S(2)}) collective-permute-start(bf16[2,768,128]{2,1,0:T(8,128)(2,1)S(1)} %collective-permute-done.1.refs_1_), channel_id=1, source_target_pairs={{0,1},{1,2},{2,3},{3,4},{4,5},{5,6},{6,7},{7,8},{8,9},{9,10},{10,1... | collective-permute-start | bytes 1179656 | tf_op jit(solution)/shard_map/ppermute | solution.py:322
  27.0 8.8 %collective-permute-start.6 = (bf16[2,768,128]{2,1,0:T(8,128)(2,1)S(1)}, bf16[2,768,128]{2,1,0:T(8,128)(2,1)S(1)}, u32[]{:S(2)}, u32[]{:S(2)}) collective-permute-start(bf16[2,768,128]{2,1,0:T(8,128)(2,1)S(1)} %collective-permute-done.4.refs_5_), channel_id=1, source_target_pairs={{0,1},{1,2},{2,3},{3,4},{4,5},{5,6},{6,7},{7,8},{8,9},{9,10},{10,1... | collective-permute-start | bytes 1179656 | tf_op jit(solution)/shard_map/ppermute | solution.py:322
  28.9 9.0 %collective-permute-start.5 = (bf16[2,768,128]{2,1,0:T(8,128)(2,1)}, bf16[2,768,128]{2,1,0:T(8,128)(2,1)S(1)}, u32[]{:S(2)}, u32[]{:S(2)}) collective-permute-start(bf16[2,768,128]{2,1,0:T(8,128)(2,1)} %shard_map.50.refs_0_), channel_id=1, source_target_pairs={{32,48},{48,32},{33,49},{49,33},{34,50},{50,34},{35,51},{51,35},{3... | collective-permute-start | bytes 1179656 | tf_op jit(solution)/shard_map/ppermute | solution.py:325
  32.1 9.5 %collective-permute-start.3 = (bf16[2,768,128]{2,1,0:T(8,128)(2,1)S(1)}, bf16[2,768,128]{2,1,0:T(8,128)(2,1)S(1)}, u32[]{:S(2)}, u32[]{:S(2)}) collective-permute-start(bf16[2,768,128]{2,1,0:T(8,128)(2,1)S(1)} %collective-permute-done.2.refs_2_), channel_id=1, source_target_pairs={{0,1},{1,2},{2,3},{3,4},{4,5},{5,6},{6,7},{7,8},{8,9},{9,10},{10,1... | collective-permute-start | bytes 1179656 | tf_op jit(solution)/shard_map/ppermute | solution.py:322
  37.9 9.8 %collective-permute-start.7 = (bf16[2,768,128]{2,1,0:T(8,128)(2,1)S(1)}, bf16[2,768,128]{2,1,0:T(8,128)(2,1)}, u32[]{:S(2)}, u32[]{:S(2)}) collective-permute-start(bf16[2,768,128]{2,1,0:T(8,128)(2,1)S(1)} %collective-permute-done.6.refs_6_), channel_id=1, source_target_pairs={{0,1},{1,2},{2,3},{3,4},{4,5},{5,6},{6,7},{7,8},{8,9},{9,10},{10,1... | collective-permute-start | bytes 1179656 | tf_op jit(solution)/shard_map/ppermute | solution.py:322
  41.6 9.9 %collective-permute-start.11 = (bf16[2,768,128]{2,1,0:T(8,128)(2,1)S(1)}, bf16[2,768,128]{2,1,0:T(8,128)(2,1)S(1)}, u32[]{:S(2)}, u32[]{:S(2)}) collective-permute-start(bf16[2,768,128]{2,1,0:T(8,128)(2,1)S(1)} %collective-permute-done.3.refs_3_), channel_id=1, source_target_pairs={{0,1},{1,2},{2,3},{3,4},{4,5},{5,6},{6,7},{7,8},{8,9},{9,10},{10,1... | collective-permute-start | bytes 1179656 | tf_op jit(solution)/shard_map/ppermute | solution.py:322
  45.6 10.7 %collective-permute-start.8 = (bf16[2,768,128]{2,1,0:T(8,128)(2,1)S(1)}, bf16[2,768,128]{2,1,0:T(8,128)(2,1)}, u32[]{:S(2)}, u32[]{:S(2)}) collective-permute-start(bf16[2,768,128]{2,1,0:T(8,128)(2,1)S(1)} %collective-permute-done.refs_4_), channel_id=1, source_target_pairs={{32,48},{48,32},{33,49},{49,33},{34,50},{50,34},{35,51},{51,35},{3... | collective-permute-start | bytes 1179656 | tf_op jit(solution)/shard_map/ppermute | solution.py:329
  47.7 12.6 %collective-permute-start.9 = (bf16[2,768,128]{2,1,0:T(8,128)(2,1)}, bf16[2,768,128]{2,1,0:T(8,128)(2,1)S(1)}, u32[]{:S(2)}, u32[]{:S(2)}) collective-permute-start(bf16[2,768,128]{2,1,0:T(8,128)(2,1)} %collective-permute-done.7.refs_7_), channel_id=1, source_target_pairs={{0,1},{1,2},{2,3},{3,4},{4,5},{5,6},{6,7},{7,8},{8,9},{9,10},{10,1... | collective-permute-start | bytes 1179656 | tf_op jit(solution)/shard_map/ppermute | solution.py:322
  51.6 11.0 %collective-permute-start.12 = (bf16[2,768,128]{2,1,0:T(8,128)(2,1)S(1)}, bf16[2,768,128]{2,1,0:T(8,128)(2,1)S(1)}, u32[]{:S(2)}, u32[]{:S(2)}) collective-permute-start(bf16[2,768,128]{2,1,0:T(8,128)(2,1)S(1)} %collective-permute-done.11.first), channel_id=1, source_target_pairs={{0,32},{16,48},{32,16},{48,0},{1,33},{17,49},{33,17},{49,1},{2,34}... | collective-permute-start | bytes 1179656 | tf_op jit(solution)/shard_map/ppermute | solution.py:342
  56.2 1.0 copy-start
  60.4 6.9 %collective-permute-start.10 = (bf16[2,768,128]{2,1,0:T(8,128)(2,1)S(1)}, bf16[2,768,128]{2,1,0:T(8,128)(2,1)S(1)}, u32[]{:S(2)}, u32[]{:S(2)}) collective-permute-start(bf16[2,768,128]{2,1,0:T(8,128)(2,1)S(1)} %collective-permute-done.9.second), channel_id=1, source_target_pairs={{0,32},{16,48},{32,16},{48,0},{1,33},{17,49},{33,17},{49,1},{2,34}... | collective-permute-start | bytes 1179656 | tf_op jit(solution)/shard_map/ppermute | solution.py:342
  67.3 34.0 %copy-start.1 = (s32[512]{0:T(512)S(1)}, s32[512]{0:T(512)}, u32[]{:S(2)}) copy-start(s32[512]{0:T(512)} %constant.27.clone.todo) | copy-start | bytes 6148
  83.2 14.1 %collective-permute-start.14 = (f16[264,128]{1,0:T(8,128)(2,1)S(1)}, f16[264,128]{1,0:T(8,128)(2,1)S(1)}, u32[]{:S(2)}, u32[]{:S(2)}) collective-permute-start(f16[264,128]{1,0:T(8,128)(2,1)S(1)} %convert_element_type.9), channel_id=1, source_target_pairs={{0,15},{1,0},{2,33},{3,34},{4,67},{5,68},{6,101},{7,102},{8,104},{... | collective-permute-start | bytes 202760 | tf_op jit(solution)/shard_map/ppermute | solution.py:362
  94.5 6.8 %collective-permute-start.13 = (f16[264,128]{1,0:T(8,128)(2,1)S(1)}, f16[264,128]{1,0:T(8,128)(2,1)S(1)}, u32[]{:S(2)}, u32[]{:S(2)}) collective-permute-start(f16[264,128]{1,0:T(8,128)(2,1)S(1)} %convert_element_type.9), channel_id=1, source_target_pairs={{0,224},{1,1},{2,2},{3,35},{4,36},{5,69},{6,70},{7,103},{8,135},{9... | collective-permute-start | bytes 202760 | tf_op jit(solution)/shard_map/ppermute | solution.py:362
